TPU v7x, 32 devices: a whole 2x2x4 slice. The times are simulated.
32 devices in a mesh: groups: 2 (over y), lev: 4 (over z), tm: 2 (over x), sub: 2 (over core).
Axes of the slice: x: 2, y: 2, z: 4, core: 2. Of those that a mesh axis runs over, the one named last changes fastest.
Arguments:
- level_field: float32 [32, 96, 16384], P(('groups', 'tm'), ('lev', 'sub')), parts along dimension 0, may hold values from -6 to 6
- tile_weight: float32 [64, 65536], P(None, ('lev', 'sub')), may hold values from -0.4 to 0.4
- tile_rows: int32 [1024], P(('lev', 'sub')), may hold values from 0 to 15
- tile_columns: int32 [1024], P(('lev', 'sub')), may hold values from 0 to 31
- live_count: int32 [8], P(('lev', 'sub')), may hold values from 16 to 128, as said below
- step_hour: int32 [16], P('tm'), may hold values from 0 to 1, as said below
Outputs:
- hourly: float32 [4, 96, 8192], P('groups', 'tm', ('lev', 'sub')), parts along dimension 0
There are 2 independent parts, one for each index of `groups`. A program takes and returns all parts, laid end to end along the dimension named above; an argument that names none is the same for every part. Nothing has to cross between parts.
Inputs may be any that keep to these rules, and one draw needn't show every extreme that they name: `live_count`: some shard has all 128 slots live in every draw, not always the same. `step_hour`: every hour has exactly 8 steps.
All inputs are finite; a program needn't handle non-finite values.
Results may differ from a plain program's by a relative error of at most 0.0003.
Values sent between devices are 32-bit elements; how exact they have to be, the bound alone decides.
No kernel may reach another device: no remote copies, remote signals or barrier semaphores. Data moves between devices by JAX's collectives and lax.ppermute only.
A program may use at most 128 MiB of HBM per device.

v0:
```python
import functools

import jax
import jax.numpy as jnp
from jax import lax
from jax.experimental import pallas as pl
from jax.experimental.pallas import tpu as pltpu
from jax.sharding import PartitionSpec as P

TILE = 64
HOURS = 2
CT_DEV = 32
PT_DEV = 16
SLOTS = 128
CELLS_DEV = CT_DEV * TILE
PIXELS_DEV = PT_DEV * TILE
LANES = 2 * TILE
MIB = 1 << 20

LIGHT = pl.CostEstimate(flops=1, bytes_accessed=1, transcendentals=0)
MEDIUM = pl.CostEstimate(flops=2_500_000_000, bytes_accessed=1, transcendentals=0)
HEAVY = pl.CostEstimate(flops=10_000_000_000, bytes_accessed=1, transcendentals=0)

NT = (((1,), (1,)), ((), ()))
NN = (((1,), (0,)), ((), ()))


def split(x):
    high = x.astype(jnp.bfloat16)
    return high, (x - high.astype(jnp.float32)).astype(jnp.bfloat16)


def dot(a, b, dims):
    return lax.dot_general(a, b, dims, preferred_element_type=jnp.float32)


GROUP = 8


def place_kernel(rows, columns, count, weights, *refs):
    high, low, total = refs[-3:]
    band = 128

    @pl.loop(0, PIXELS_DEV // band)
    def _(b):
        total[pl.ds(pl.multiple_of(b * band, band), band), :] = jnp.zeros((band, CELLS_DEV), jnp.float32)

    lane_half = lax.broadcasted_iota(jnp.int32, (TILE, LANES), 1) // TILE
    live = count[0]

    @pl.loop(0, (live + GROUP - 1) // GROUP)
    def _(g):
        for pair in range(GROUP // 2):
            lanes = pl.ds(pl.multiple_of((g * (GROUP // 2) + pair) * LANES, LANES), LANES)
            tiles = weights[:, lanes]
            turned = pltpu.roll(tiles, TILE, 1)
            for i in range(2):
                k = g * GROUP + pair * 2 + i
                row, column = rows[k], columns[k]
                side = jnp.where(k < live, column & 1, -1)
                tile = jnp.where(lane_half == i, tiles, turned)
                at = (
                    pl.ds(pl.multiple_of(row * TILE, TILE), TILE),
                    pl.ds(pl.multiple_of((column >> 1) * LANES, LANES), LANES),
                )
                total[at] = total[at] + jnp.where(lane_half == side, tile, 0.0)

    @pl.loop(0, PIXELS_DEV // band)
    def _(b):
        at = pl.ds(pl.multiple_of(b * band, band), band)
        high[at, :], low[at, :] = split(total[at, :])


def place_tiles(rows, columns, count, weights, *after):
    smem = pl.BlockSpec(memory_space=pltpu.SMEM)
    vmem = pl.BlockSpec(memory_space=pltpu.VMEM)
    half = jax.ShapeDtypeStruct((PIXELS_DEV, CELLS_DEV), jnp.bfloat16)
    return pl.pallas_call(
        place_kernel,
        out_shape=(half, half),
        in_specs=[smem, smem, smem, vmem] + [pl.BlockSpec(memory_space=pl.ANY)] * len(after),
        out_specs=(vmem, vmem),
        scratch_shapes=[pltpu.VMEM((PIXELS_DEV, CELLS_DEV), jnp.float32)],
        compiler_params=pltpu.CompilerParams(vmem_limit_bytes=28 * MIB),
        cost_estimate=HEAVY,
        name="place_tiles",
    )(rows, columns, count, weights, *after)


PIXEL_BLOCK = 256


def remap_blocks(x, high, low):
    m = x.shape[0]
    x_high, x_low = split(x)
    both = jnp.concatenate([x_high, x_low], axis=0)
    for start in range(0, PIXELS_DEV, PIXEL_BLOCK):
        at = slice(start, start + PIXEL_BLOCK)
        first = dot(both, high[at, :], NT)
        yield at, first[:m] + first[m:] + dot(x_high, low[at, :], NT)


def remap_call(kernel, inputs, after, out_rows, high, low, cost, name, scratch_rows=()):
    vmem = pl.BlockSpec(memory_space=pltpu.VMEM)
    return pl.pallas_call(
        kernel,
        out_shape=[jax.ShapeDtypeStruct((rows, PIXELS_DEV), jnp.float32) for rows in out_rows],
        in_specs=[vmem] * (len(inputs) + 2) + [pl.BlockSpec(memory_space=pl.ANY)] * len(after),
        out_specs=[vmem] * len(out_rows),
        scratch_shapes=[pltpu.VMEM((rows, PIXELS_DEV), jnp.float32) for rows in scratch_rows],
        compiler_params=pltpu.CompilerParams(vmem_limit_bytes=24 * MIB),
        cost_estimate=cost,
        name=name,
    )(*inputs, high, low, *after)


def remap_rows_kernel(x, high, low, out):
    for at, result in remap_blocks(x[...], high, low):
        out[:, at] = result


def unfold(block):
    levels = block.shape[0] // 2
    return jnp.concatenate([block[:levels], block[levels:]], axis=1)


def far_rows(same_sub, other_sub):
    even = lax.axis_index("sub") == 0
    blocks = [jnp.where(even, same_sub, other_sub), jnp.where(even, other_sub, same_sub)]
    return [unfold(block) for block in blocks]


def keeps_near():
    return lax.axis_index("tm") == lax.axis_index("lev") // 2


def near_rows(same_sub, other_sub):
    even = lax.axis_index("sub") == 0
    return [jnp.where(even, same_sub, other_sub), jnp.where(even, other_sub, same_sub)]


def by_hour(result, levels):
    pieces = [result[start : start + levels] for start in range(0, 2 * HOURS * levels, levels)]
    return jnp.concatenate([pieces[sub * HOURS + hour] for hour in range(HOURS) for sub in range(2)], axis=0)


def sort_out(near_result, far_result, keep, send):
    near = keeps_near()

    @pl.when(near)
    def _():
        keep[...], send[...] = near_result[...], far_result[...]

    @pl.when(jnp.logical_not(near))
    def _():
        keep[...], send[...] = far_result[...], near_result[...]


def remap_both_kernel(own, sibling, plain, high, low, *refs):
    keep, send, near_result, far_result = refs[-4:]
    rows = own.shape[0]
    blocks = near_rows(own[...], sibling[...]) + [plain[...]]
    for at, result in remap_blocks(jnp.concatenate(blocks, axis=0), high, low):
        near_result[:, at] = by_hour(result, rows // HOURS)
        far_result[:rows, at] = result[2 * rows :]
    far_result[rows:] = jnp.zeros((rows, PIXELS_DEV), jnp.float32)
    sort_out(near_result, far_result, keep, send)


def remap_near_kernel(near_same, near_other, far, high, low, *refs):
    keep, send, near_result, far_result = refs[-4:]
    rows = near_same.shape[0]
    blocks = near_rows(near_same[...], near_other[...]) + [far[...]]
    for at, result in remap_blocks(jnp.concatenate(blocks, axis=0), high, low):
        near_result[:, at] = by_hour(result, rows // HOURS)
        far_result[:rows, at] = result[2 * rows :]
    far_result[rows:] = jnp.zeros((rows, PIXELS_DEV), jnp.float32)
    sort_out(near_result, far_result, keep, send)


def remap_last_kernel(block, high, low, *refs):
    out = refs[-1]
    x = unfold(block[...])
    x = jnp.concatenate([x, jnp.zeros((out.shape[0] - x.shape[0], x.shape[1]), jnp.float32)], axis=0)
    for at, result in remap_blocks(x, high, low):
        out[:, at] = result


def hour_matrix(step_hour, levels, steps, hours, cuts):
    rows, columns = cuts * levels, cuts * 2 * levels * steps
    row = lax.broadcasted_iota(jnp.int32, (rows, columns), 0)
    column = lax.broadcasted_iota(jnp.int32, (rows, columns), 1)
    span = levels * steps
    near = jnp.full((rows, columns), -1, jnp.int32)
    for cut in range(cuts):
        for half in range(2):
            step = column - (cut * 2 + half) * span - (row - cut * levels) * steps
            inside = (row >= cut * levels) & (row < (cut + 1) * levels)
            inside = inside & (step >= 0) & (step < steps)
            near = jnp.where(inside, step, near)
    blocks = []
    for hour in hours:
        block = jnp.zeros((rows, columns), jnp.float32)
        for step in range(steps):
            block = jnp.where(near == step, jnp.where(step_hour[step] == hour, 1.0, 0.0), block)
        blocks.append(block)
    return jnp.concatenate(blocks, axis=0).astype(jnp.bfloat16)


def peer_shard(k, j):
    subs = lax.axis_size("sub")
    return (lax.axis_index("lev") ^ k) * subs + (lax.axis_index("sub") ^ j)


def field_copies(field, buffer, arrived, peers):
    copies = []
    for place, (k, j) in enumerate(peers):
        start = pl.multiple_of(peer_shard(k, j) * CELLS_DEV, CELLS_DEV)
        copy = pltpu.make_async_copy(
            field.at[:, :, pl.ds(start, CELLS_DEV)], buffer.at[place], arrived.at[place]
        )
        copy.start()
        copies.append(copy)
    return copies


def sums_kernel(plain, first, second, step_hour, field, *refs):
    *outs, buffer, arrived = refs
    _, levels, steps, cells = buffer.shape
    rows, cut = HOURS * levels, cells // 2
    copies = field_copies(field, buffer, arrived, [*plain, *first, second])
    me = lax.axis_index("tm")
    by_place = hour_matrix(step_hour, levels, steps, (1 - me, me), 2)
    by_hour = hour_matrix(step_hour, levels, steps, range(HOURS), 1)

    def halves(place):
        copies[place].wait()
        return split(buffer[place].reshape(levels * steps, cells))

    for place in range(len(plain)):
        outs[place][...] = dot(by_hour, jnp.concatenate(halves(place), axis=0), NN)
    theirs_first, mine_first, theirs_second, mine_second = outs[len(plain) :]
    for j in range(len(first) + 1):
        high, low = halves(len(plain) + j)
        stacked = [high[:, :cut], low[:, :cut], high[:, cut:], low[:, cut:]]
        result = dot(by_place, jnp.concatenate(stacked, axis=0), NN)
        if j < len(first):
            at = slice(j * rows, (j + 1) * rows)
            theirs_first[at], mine_first[at] = result[:rows], result[rows:]
        else:
            theirs_second[...], mine_second[...] = result[:rows], result[rows:]


def hour_sums(plain, first, second, step_hour, field):
    levels, steps, _ = field.shape
    rows, cut = HOURS * levels, CELLS_DEV // 2
    vmem = pl.BlockSpec(memory_space=pltpu.VMEM)
    shapes = [(rows, CELLS_DEV)] * len(plain) + [(len(first) * rows, cut)] * 2 + [(rows, cut)] * 2
    count = len(plain) + len(first) + 1
    outs = pl.pallas_call(
        functools.partial(sums_kernel, plain, first, second),
        out_shape=[jax.ShapeDtypeStruct(shape, jnp.float32) for shape in shapes],
        in_specs=[pl.BlockSpec(memory_space=pltpu.SMEM), pl.BlockSpec(memory_space=pl.ANY)],
        out_specs=[vmem] * len(shapes),
        scratch_shapes=[
            pltpu.VMEM((count, levels, steps, CELLS_DEV), jnp.float32),
            pltpu.SemaphoreType.DMA((count,)),
        ],
        compiler_params=pltpu.CompilerParams(vmem_limit_bytes=52 * MIB),
        cost_estimate=LIGHT,
        name="hour_sums",
    )(step_hour, field)
    return outs[: len(plain)], outs[len(plain) :]


def merge_kernel(mine, got, *refs):
    outs = refs[-(mine.shape[0] // refs[-1].shape[0]) :]
    rows = outs[0].shape[0]
    for place, out in enumerate(outs):
        at = slice(place * rows, (place + 1) * rows)
        out[...] = mine[at] + got[at]


def hold_kernel(x, *refs):
    refs[-1][...] = x[...]


def far_rows_kernel(same_sub, other_sub, out):
    out[...] = jnp.concatenate(far_rows(same_sub[...], other_sub[...]), axis=0)


def small_call(kernel, inputs, after, shapes, cost, name):
    vmem = pl.BlockSpec(memory_space=pltpu.VMEM)
    return pl.pallas_call(
        kernel,
        out_shape=[jax.ShapeDtypeStruct(shape, jnp.float32) for shape in shapes],
        in_specs=[vmem] * len(inputs) + [pl.BlockSpec(memory_space=pl.ANY)] * len(after),
        out_specs=[vmem] * len(shapes),
        compiler_params=pltpu.CompilerParams(vmem_limit_bytes=8 * MIB),
        cost_estimate=cost,
        name=name,
    )(*inputs, *after)


def finish_kernel(divisor, levels, chip, got_chip, one, got_one, last, got_last, out):
    me, lev, even = lax.axis_index("tm"), lax.axis_index("lev") % 2, lax.axis_index("sub") == 0
    rows = 2 * levels
    near = keeps_near()
    for hour in range(HOURS):
        same_at = pl.ds(pl.multiple_of((hour * 2 + lev) * rows, rows), rows)
        other_at = pl.ds(pl.multiple_of((hour * 2 + 1 - lev) * rows, rows), rows)

        @pl.when(near)
        def _():
            here = slice(hour * rows, (hour + 1) * rows)
            out[same_at, :] = (chip[here] + got_chip[here]) / divisor
            out[other_at, :] = (one[here] + got_one[here]) / divisor

        @pl.when(jnp.logical_not(near))
        def _():
            here = slice(hour * levels, (hour + 1) * levels)
            plain = chip[here] + got_chip[here]
            other = jnp.where(me == hour, last[:levels], got_last[:levels])
            pair = [jnp.where(even, plain, other), jnp.where(even, other, plain)]
            out[same_at, :] = jnp.concatenate(pair, axis=0) / divisor
            out[other_at, :] = jnp.where(me == hour, one[:rows], got_one[:rows]) / divisor


def finish(arrays, levels, divisor):
    call = functools.partial(finish_kernel, divisor, levels)
    shape = (2 * arrays[0].shape[0], PIXELS_DEV)
    return small_call(call, arrays, [], [shape], LIGHT, "finish")[0]


def hour_plan(level_field, tile_weight, tile_rows, tile_columns, live_count, step_hour):
    levs, subs, shards_tm = lax.axis_size("lev"), lax.axis_size("sub"), lax.axis_size("tm")
    half = levs // 2
    divisor = float(level_field.shape[0] * shards_tm // HOURS)
    field = jnp.transpose(level_field, (1, 0, 2))

    def to_peer(x, k, j):
        pairs = [(a * subs + b, (a ^ k) * subs + (b ^ j)) for a in range(levs) for b in range(subs)]
        return lax.ppermute(x, ("lev", "sub"), pairs)

    def swap(x):
        return lax.ppermute(x, "tm", [(0, 1), (1, 0)])

    plain = [(half, 0), (1, 0), (1, 1), (0, 1), (0, 0)]
    first, second = [(half + 1, j) for j in range(subs)], (half, 1)
    sums, (theirs_0, mine_0, theirs_1, mine_1) = hour_sums(plain, first, second, step_hour, field)
    rows = 2 * field.shape[0]
    folded = theirs_1.shape
    sibling = to_peer(sums[3], *plain[3])
    near_got = [to_peer(x, *peer) for x, peer in list(zip(sums, plain))[1:3]]
    got_0 = swap(theirs_0)
    plain_got = to_peer(sums[0], *plain[0])
    high, low = place_tiles(tile_rows, tile_columns, live_count, tile_weight, theirs_0)

    merged = small_call(
        merge_kernel, [mine_0, got_0], [high, sibling], [folded] * subs, LIGHT, "merge_first"
    )
    first_got = [to_peer(x, *peer) for x, peer in zip(merged, first)]
    theirs_1 = small_call(hold_kernel, [theirs_1], [plain_got, *merged], [folded], LIGHT, "hold")[0]
    got_1 = swap(theirs_1)
    both, send = remap_call(
        remap_both_kernel,
        [sums[4], sibling, plain_got],
        [theirs_1],
        [2 * rows] * 2,
        high,
        low,
        MEDIUM,
        "remap_both",
        [2 * rows] * 2,
    )
    got_both = swap(send)
    merged = small_call(
        merge_kernel, [mine_1, got_1], [both, near_got[0]], [folded], HEAVY, "merge_last"
    )
    second_got = to_peer(merged[0], *second)
    far = small_call(far_rows_kernel, first_got, [], [(rows, CELLS_DEV)], HEAVY, "far_rows")[0]
    one, send = remap_call(
        remap_near_kernel,
        [*near_got, far],
        [],
        [2 * rows] * 2,
        high,
        low,
        LIGHT,
        "remap_near",
        [2 * rows] * 2,
    )
    got_one = swap(send)
    padded = -(-rows // 32) * 16
    (last,) = remap_call(remap_last_kernel, [second_got], [one], [padded], high, low, HEAVY, "remap_last")
    got_last = swap(last)
    out = finish([both, got_both, one, got_one, last, got_last], rows // 2, divisor)
    return out.reshape(HOURS, out.shape[0] // HOURS, PIXELS_DEV)


def general_plan(level_field, tile_weight, tile_rows, tile_columns, live_count, step_hour):
    steps, levels, cells = level_field.shape
    shards = lax.axis_size("lev") * lax.axis_size("sub")
    divisor = float(steps * lax.axis_size("tm") // HOURS)
    hours = jnp.arange(HOURS, dtype=jnp.int32)
    table = (step_hour[None, :] == hours[:, None]).astype(jnp.float32)
    fields = level_field.reshape(steps, levels, shards, cells // shards)
    partial = jnp.einsum("hs,slgc->ghlc", table, fields, precision=lax.Precision.HIGHEST)
    regrouped = lax.all_to_all(partial, ("lev", "sub"), split_axis=0, concat_axis=0, tiled=True)
    rows = jnp.transpose(regrouped, (1, 0, 2, 3)).reshape(-1, cells // shards)
    high, low = place_tiles(tile_rows, tile_columns, live_count, tile_weight)
    (out,) = remap_call(remap_rows_kernel, [rows], [], [rows.shape[0]], high, low, LIGHT, "remap_rows")
    out = out.reshape(HOURS, shards * levels, PIXELS_DEV) / divisor
    return lax.psum_scatter(out, "tm", scatter_dimension=1, tiled=True)


def solution(mesh):
    sizes = mesh.shape
    paired = sizes["tm"] == HOURS and sizes["lev"] == 4 and sizes["sub"] == 2
    placed = (
        P(("groups", "tm"), ("lev", "sub"), None),
        P(None, ("lev", "sub")),
        P(("lev", "sub")),
        P(("lev", "sub")),
        P(("lev", "sub")),
        P("tm"),
    )
    return jax.shard_map(
        hour_plan if paired else general_plan,
        mesh=mesh,
        in_specs=placed,
        out_specs=P("groups", "tm", ("lev", "sub")),
        check_vma=False,
    )
```

profile of v0, /device:TPU:0, one launch (start us, length us, event | category | flops | bytes accessed | tf_op | source)
XLA Modules:
  0.0 41.2 jit_solution(15712005649160814385)
XLA Ops:
  0.0 0.7 %copy-done = s32[8]{0:T(128)S(1)} copy-done((s32[8]{0:T(128)S(1)}, s32[8]{0:T(128)}, u32[]{:S(2)}) %copy-start) | copy-done | bytes 56
  0.7 3.9 %hour_sums.1 = (f32[24,2048]{1,0:T(8,128)S(1)}, f32[24,2048]{1,0:T(8,128)S(1)}, f32[24,2048]{1,0:T(8,128)S(1)}, f32[24,2048]{1,0:T(8,128)S(1)}, f32[24,2048]{1,0...) custom-call(s32[8]{0:T(128)S(1)} %copy-done, ...), custom_call_target="tpu_custom_call" | custom-call | flops 1 | bytes 1 | tf_op jit(solution)/shard_map/hour_sums/pallas_call | solution.py:260
  4.6 0.5 %collective-permute-start = (f32[24,2048]{1,0:T(8,128)S(1)}, f32[24,2048]{1,0:T(8,128)S(1)}, u32[]{:S(2)}, u32[]{:S(2)}) collective-permute-start(f32[24,2048]{1,0:T(8,128)S(1)} %get-tuple-element.23), channel_id=1, source_target_pairs={{0,1},{1,0},{4,5},{5,4},{8,9},{9,8},{12,13},{13,12},{2,3},{3,2},{6... | collective-permute-start | bytes 589832 | tf_op jit(solution)/shard_map/ppermute | solution.py:343
  5.1 3.7 %collective-permute-start.1 = (f32[24,2048]{1,0:T(8,128)S(1)}, f32[24,2048]{1,0:T(8,128)S(1)}, u32[]{:S(2)}, u32[]{:S(2)}) collective-permute-start(f32[24,2048]{1,0:T(8,128)S(1)} %get-tuple-element.24), channel_id=1, source_target_pairs={{0,8},{1,9},{4,12},{5,13},{8,0},{9,1},{12,4},{13,5},{2,10},{3,11},... | collective-permute-start | bytes 589832 | tf_op jit(solution)/shard_map/ppermute | solution.py:343
  8.8 1.6 %collective-permute-start.4 = (f32[24,2048]{1,0:T(8,128)S(1)}, f32[24,2048]{1,0:T(8,128)S(1)}, u32[]{:S(2)}, u32[]{:S(2)}) collective-permute-start(f32[24,2048]{1,0:T(8,128)S(1)} %get-tuple-element.34), channel_id=1, source_target_pairs={{0,4},{1,5},{4,0},{5,1},{8,12},{9,13},{12,8},{13,9},{2,6},{3,7},{6... | collective-permute-start | bytes 589832 | tf_op jit(solution)/shard_map/ppermute | solution.py:343
  10.4 0.0 collective-permute-start.5
  10.4 1.5 %collective-permute-start.2 = (f32[48,1024]{1,0:T(8,128)S(1)}, f32[48,1024]{1,0:T(8,128)S(1)}, u32[]{:S(2)}, u32[]{:S(2)}) collective-permute-start(f32[48,1024]{1,0:T(8,128)S(1)} %get-tuple-element.25.refs_0_), channel_id=1, source_target_pairs={{0,2},{2,0},{1,3},{3,1},{4,6},{6,4},{5,7},{7,5},{8,10},{10,8},{9,1... | collective-permute-start | bytes 589832 | tf_op jit(solution)/shard_map/ppermute | solution.py:346
  12.5 0.0 copy-done.3
  12.5 4.3 %place_tiles.1 = (bf16[1024,2048]{1,0:T(8,128)(2,1)S(1)}, bf16[1024,2048]{1,0:T(8,128)(2,1)S(1)}) custom-call(s32[128]{0:T(128)S(1)} %copy-done.2, s32[128]{0:T(128)S(1)} %copy-done.3, s32[1]{0:T(128)S(6)} %copy.7.count, f32[64,8192]{1,0:T(8,128)S(1)} %copy-done.1, f32[48,1024]{1,0:T(8,128)S(1)} %get-tuple-element.25.refs_0_), custom_call_target="tpu_custom_call" | custom-call | flops 10000000000 | bytes 1 | tf_op jit(solution)/shard_map/place_tiles/pallas_call | solution.py:78
  16.9 0.0 collective-permute-done.refs_1_.sibling
  16.9 0.9 %collective-permute-done.2.got = f32[48,1024]{1,0:T(8,128)S(1)} collective-permute-done((f32[48,1024]{1,0:T(8,128)S(1)}, f32[48,1024]{1,0:T(8,128)S(1)}, u32[]{:S(2)}, u32[]{:S(2)}) %collective-permute-start.2) | collective-permute-done | bytes 196640 | tf_op jit(solution)/shard_map/ppermute | solution.py:346
  17.7 1.4 %collective-permute-start.6 = (f32[24,1024]{1,0:T(8,128)S(1)}, f32[24,1024]{1,0:T(8,128)S(1)}, u32[]{:S(2)}, u32[]{:S(2)}) collective-permute-start(f32[24,1024]{1,0:T(8,128)S(1)} %get-tuple-element.30.refs_1_), channel_id=1, source_target_pairs={{0,12},{1,13},{4,8},{5,9},{8,4},{9,5},{12,0},{13,1},{2,14},{3,15},... | collective-permute-start | bytes 294920 | tf_op jit(solution)/shard_map/ppermute | solution.py:343
  19.2 1.6 %collective-permute-start.7 = (f32[24,1024]{1,0:T(8,128)S(1)}, f32[24,1024]{1,0:T(8,128)S(1)}, u32[]{:S(2)}, u32[]{:S(2)}) collective-permute-start(f32[24,1024]{1,0:T(8,128)S(1)} %get-tuple-element.31.refs_2_), channel_id=1, source_target_pairs={{0,13},{1,12},{4,9},{5,8},{8,5},{9,4},{12,1},{13,0},{2,15},{3,14},... | collective-permute-start | bytes 294920 | tf_op jit(solution)/shard_map/ppermute | solution.py:343
  20.8 0.0 collective-permute-done.1.refs_0_.plain
  20.8 1.6 %collective-permute-start.9 = (f32[24,1024]{1,0:T(8,128)S(1)}, f32[24,1024]{1,0:T(8,128)S(1)}, u32[]{:S(2)}, u32[]{:S(2)}) collective-permute-start(f32[24,1024]{1,0:T(8,128)S(1)} %hold.1.refs_0_), channel_id=1, source_target_pairs={{0,2},{2,0},{1,3},{3,1},{4,6},{6,4},{5,7},{7,5},{8,10},{10,8},{9,1... | collective-permute-start | bytes 294920 | tf_op jit(solution)/shard_map/ppermute | solution.py:346
  22.3 2.7 %remap_both.1 = (f32[48,1024]{1,0:T(8,128)S(1)}, f32[48,1024]{1,0:T(8,128)S(1)}) custom-call(f32[24,2048]{1,0:T(8,128)S(1)} %get-tuple-element.22.own, f32[24,2048]{1,0:T(8,128)S(1)} %collective-permute-done.refs_1_.sibling, f32[24,2048]{1,0:T(8,128)S(1)} %collective-permute-done.1.refs_0_.plain, bf16[1024,2048]{1,0:T(8,128)(2,1)S(1)} %get-tuple-element.26.refs_0_.high, ...), custom_call_target="tpu_custom_call" | custom-call | flops 2500000000 | bytes 1 | tf_op jit(solution)/shard_map/remap_both/pallas_call | solution.py:105
  25.1 0.0 collective-permute-done.4.near_same.refs_1_
  25.1 0.6 %collective-permute-start.3 = (f32[48,1024]{1,0:T(8,128)S(1)}, f32[48,1024]{1,0:T(8,128)S(1)}, u32[]{:S(2)}, u32[]{:S(2)}) collective-permute-start(f32[48,1024]{1,0:T(8,128)S(1)} %get-tuple-element.33), channel_id=1, source_target_pairs={{0,2},{2,0},{1,3},{3,1},{4,6},{6,4},{5,7},{7,5},{8,10},{10,8},{9,1... | collective-permute-start | bytes 589832 | tf_op jit(solution)/shard_map/ppermute | solution.py:346
  25.7 0.8 %collective-permute-done.9.got = f32[24,1024]{1,0:T(8,128)S(1)} collective-permute-done((f32[24,1024]{1,0:T(8,128)S(1)}, f32[24,1024]{1,0:T(8,128)S(1)}, u32[]{:S(2)}, u32[]{:S(2)}) %collective-permute-start.9) | collective-permute-done | bytes 98336 | tf_op jit(solution)/shard_map/ppermute | solution.py:346
  26.5 0.1 collective-permute-start.10
  26.6 0.0 collective-permute-done.6.same_sub
  26.6 1.1 %collective-permute-done.7.other_sub = f32[24,1024]{1,0:T(8,128)S(1)} collective-permute-done((f32[24,1024]{1,0:T(8,128)S(1)}, f32[24,1024]{1,0:T(8,128)S(1)}, u32[]{:S(2)}, u32[]{:S(2)}) %collective-permute-start.7) | collective-permute-done | bytes 98336 | tf_op jit(solution)/shard_map/ppermute | solution.py:343
  27.7 0.0 collective-permute-done.5.near_other
  27.7 2.7 %remap_near.1 = (f32[48,1024]{1,0:T(8,128)S(1)}, f32[48,1024]{1,0:T(8,128)S(1)}) custom-call(f32[24,2048]{1,0:T(8,128)S(1)} %collective-permute-done.4.near_same.refs_1_, f32[24,2048]{1,0:T(8,128)S(1)} %collective-permute-done.5.near_other, f32[24,2048]{1,0:T(8,128)S(1)} %far_rows.1.far, bf16[1024,2048]{1,0:T(8,128)(2,1)S(1)} %get-tuple-element.26.refs_0_.high, ...), custom_call_target="tpu_custom_call" | custom-call | flops 1 | bytes 1 | tf_op jit(solution)/shard_map/remap_near/pallas_call | solution.py:105
  30.5 1.6 %collective-permute-start.8 = (f32[48,1024]{1,0:T(8,128)S(1)}, f32[48,1024]{1,0:T(8,128)S(1)}, u32[]{:S(2)}, u32[]{:S(2)}) collective-permute-start(f32[48,1024]{1,0:T(8,128)S(1)} %get-tuple-element.37), channel_id=1, source_target_pairs={{0,2},{2,0},{1,3},{3,1},{4,6},{6,4},{5,7},{7,5},{8,10},{10,8},{9,1... | collective-permute-start | bytes 589832 | tf_op jit(solution)/shard_map/ppermute | solution.py:346
  32.0 1.8 %collective-permute-done.10.block = f32[24,1024]{1,0:T(8,128)S(1)} collective-permute-done((f32[24,1024]{1,0:T(8,128)S(1)}, f32[24,1024]{1,0:T(8,128)S(1)}, u32[]{:S(2)}, u32[]{:S(2)}) %collective-permute-start.10) | collective-permute-done | bytes 98336 | tf_op jit(solution)/shard_map/ppermute | solution.py:343
  33.8 2.4 %remap_last.1.last = f32[16,1024]{1,0:T(8,128)S(1)} custom-call(f32[24,1024]{1,0:T(8,128)S(1)} %collective-permute-done.10.block, bf16[1024,2048]{1,0:T(8,128)(2,1)S(1)} %get-tuple-element.26.refs_0_.high, bf16[1024,2048]{1,0:T(8,128)(2,1)S(1)} %get-tuple-element.27.low, f32[48,1024]{1,0:T(8,128)S(1)} %get-tuple-element.36.refs_0_.one), custom_call_target="tpu_custom_call" | custom-call | flops 10000000000 | bytes 1 | tf_op jit(solution)/shard_map/remap_last/pallas_call | solution.py:105
  36.2 1.5 %collective-permute-start.11 = (f32[16,1024]{1,0:T(8,128)S(1)}, f32[16,1024]{1,0:T(8,128)S(1)}, u32[]{:S(2)}, u32[]{:S(2)}) collective-permute-start(f32[16,1024]{1,0:T(8,128)S(1)} %remap_last.1.last), channel_id=1, source_target_pairs={{0,2},{2,0},{1,3},{3,1},{4,6},{6,4},{5,7},{7,5},{8,10},{10,8},{9,1... | collective-permute-start | bytes 196616 | tf_op jit(solution)/shard_map/ppermute | solution.py:346
  37.7 0.0 collective-permute-done.3.got_chip
  37.7 2.8 %collective-permute-done.11.got_last = f32[16,1024]{1,0:T(8,128)S(1)} collective-permute-done((f32[16,1024]{1,0:T(8,128)S(1)}, f32[16,1024]{1,0:T(8,128)S(1)}, u32[]{:S(2)}, u32[]{:S(2)}) %collective-permute-start.11) | collective-permute-done | bytes 65568 | tf_op jit(solution)/shard_map/ppermute | solution.py:346
  40.4 0.0 collective-permute-done.8.got_one
  40.5 0.8 %finish.1 = f32[96,1024]{1,0:T(8,128)} custom-call(f32[48,1024]{1,0:T(8,128)S(1)} %get-tuple-element.32.refs_0_.chip, f32[48,1024]{1,0:T(8,128)S(1)} %collective-permute-done.3.got_chip, f32[48,1024]{1,0:T(8,128)S(1)} %get-tuple-element.36.refs_0_.one, f32[48,1024]{1,0:T(8,128)S(1)} %collective-permute-done.8.got_one, f32[16,1024]{1,0:T(8,128)S(1)} %remap_last.1.last, ...), custom_call_target="tpu_custom_call" | custom-call | flops 1 | bytes 1 | tf_op jit(solution)/shard_map/finish/pallas_call | solution.py:294
  (10 shorter events, 0.1 us)
Async XLA Ops:
  0.0 12.5 %copy-start.3 = (s32[128]{0:T(128)S(1)}, s32[128]{0:T(128)}, u32[]{:S(2)}) copy-start(s32[128]{0:T(128)} %columns.1) | copy-start | bytes 1540
  0.0 12.5 %copy-start.2 = (s32[128]{0:T(128)S(1)}, s32[128]{0:T(128)}, u32[]{:S(2)}) copy-start(s32[128]{0:T(128)} %rows.1) | copy-start | bytes 1540
  0.0 0.7 %copy-start = (s32[8]{0:T(128)S(1)}, s32[8]{0:T(128)}, u32[]{:S(2)}) copy-start(s32[8]{0:T(128)} %step_hour.1) | copy-start | bytes 100
  0.7 11.8 %copy-start.1 = (f32[64,8192]{1,0:T(8,128)S(1)}, f32[64,8192]{1,0:T(8,128)}, u32[]{:S(2)}) copy-start(f32[64,8192]{1,0:T(8,128)} %weights.1) | copy-start | bytes 6291460
  4.6 12.3 %collective-permute-start = (f32[24,2048]{1,0:T(8,128)S(1)}, f32[24,2048]{1,0:T(8,128)S(1)}, u32[]{:S(2)}, u32[]{:S(2)}) collective-permute-start(f32[24,2048]{1,0:T(8,128)S(1)} %get-tuple-element.23), channel_id=1, source_target_pairs={{0,1},{1,0},{4,5},{5,4},{8,9},{9,8},{12,13},{13,12},{2,3},{3,2},{6... | collective-permute-start | bytes 589832 | tf_op jit(solution)/shard_map/ppermute | solution.py:343
  5.1 15.6 %collective-permute-start.1 = (f32[24,2048]{1,0:T(8,128)S(1)}, f32[24,2048]{1,0:T(8,128)S(1)}, u32[]{:S(2)}, u32[]{:S(2)}) collective-permute-start(f32[24,2048]{1,0:T(8,128)S(1)} %get-tuple-element.24), channel_id=1, source_target_pairs={{0,8},{1,9},{4,12},{5,13},{8,0},{9,1},{12,4},{13,5},{2,10},{3,11},... | collective-permute-start | bytes 589832 | tf_op jit(solution)/shard_map/ppermute | solution.py:343
  8.8 16.3 %collective-permute-start.4 = (f32[24,2048]{1,0:T(8,128)S(1)}, f32[24,2048]{1,0:T(8,128)S(1)}, u32[]{:S(2)}, u32[]{:S(2)}) collective-permute-start(f32[24,2048]{1,0:T(8,128)S(1)} %get-tuple-element.34), channel_id=1, source_target_pairs={{0,4},{1,5},{4,0},{5,1},{8,12},{9,13},{12,8},{13,9},{2,6},{3,7},{6... | collective-permute-start | bytes 589832 | tf_op jit(solution)/shard_map/ppermute | solution.py:343
  10.4 17.4 %collective-permute-start.5 = (f32[24,2048]{1,0:T(8,128)S(1)}, f32[24,2048]{1,0:T(8,128)S(1)}, u32[]{:S(2)}, u32[]{:S(2)}) collective-permute-start(f32[24,2048]{1,0:T(8,128)S(1)} %get-tuple-element.35), channel_id=1, source_target_pairs={{0,5},{1,4},{4,1},{5,0},{8,13},{9,12},{12,9},{13,8},{2,7},{3,6},{6... | collective-permute-start | bytes 589832 | tf_op jit(solution)/shard_map/ppermute | solution.py:343
  10.4 7.4 %collective-permute-start.2 = (f32[48,1024]{1,0:T(8,128)S(1)}, f32[48,1024]{1,0:T(8,128)S(1)}, u32[]{:S(2)}, u32[]{:S(2)}) collective-permute-start(f32[48,1024]{1,0:T(8,128)S(1)} %get-tuple-element.25.refs_0_), channel_id=1, source_target_pairs={{0,2},{2,0},{1,3},{3,1},{4,6},{6,4},{5,7},{7,5},{8,10},{10,8},{9,1... | collective-permute-start | bytes 589832 | tf_op jit(solution)/shard_map/ppermute | solution.py:346
  17.7 8.8 %collective-permute-start.6 = (f32[24,1024]{1,0:T(8,128)S(1)}, f32[24,1024]{1,0:T(8,128)S(1)}, u32[]{:S(2)}, u32[]{:S(2)}) collective-permute-start(f32[24,1024]{1,0:T(8,128)S(1)} %get-tuple-element.30.refs_1_), channel_id=1, source_target_pairs={{0,12},{1,13},{4,8},{5,9},{8,4},{9,5},{12,0},{13,1},{2,14},{3,15},... | collective-permute-start | bytes 294920 | tf_op jit(solution)/shard_map/ppermute | solution.py:343
  19.2 8.5 %collective-permute-start.7 = (f32[24,1024]{1,0:T(8,128)S(1)}, f32[24,1024]{1,0:T(8,128)S(1)}, u32[]{:S(2)}, u32[]{:S(2)}) collective-permute-start(f32[24,1024]{1,0:T(8,128)S(1)} %get-tuple-element.31.refs_2_), channel_id=1, source_target_pairs={{0,13},{1,12},{4,9},{5,8},{8,5},{9,4},{12,1},{13,0},{2,15},{3,14},... | collective-permute-start | bytes 294920 | tf_op jit(solution)/shard_map/ppermute | solution.py:343
  20.8 5.7 %collective-permute-start.9 = (f32[24,1024]{1,0:T(8,128)S(1)}, f32[24,1024]{1,0:T(8,128)S(1)}, u32[]{:S(2)}, u32[]{:S(2)}) collective-permute-start(f32[24,1024]{1,0:T(8,128)S(1)} %hold.1.refs_0_), channel_id=1, source_target_pairs={{0,2},{2,0},{1,3},{3,1},{4,6},{6,4},{5,7},{7,5},{8,10},{10,8},{9,1... | collective-permute-start | bytes 294920 | tf_op jit(solution)/shard_map/ppermute | solution.py:346
  25.1 12.6 %collective-permute-start.3 = (f32[48,1024]{1,0:T(8,128)S(1)}, f32[48,1024]{1,0:T(8,128)S(1)}, u32[]{:S(2)}, u32[]{:S(2)}) collective-permute-start(f32[48,1024]{1,0:T(8,128)S(1)} %get-tuple-element.33), channel_id=1, source_target_pairs={{0,2},{2,0},{1,3},{3,1},{4,6},{6,4},{5,7},{7,5},{8,10},{10,8},{9,1... | collective-permute-start | bytes 589832 | tf_op jit(solution)/shard_map/ppermute | solution.py:346
  26.5 7.3 %collective-permute-start.10 = (f32[24,1024]{1,0:T(8,128)S(1)}, f32[24,1024]{1,0:T(8,128)S(1)}, u32[]{:S(2)}, u32[]{:S(2)}) collective-permute-start(f32[24,1024]{1,0:T(8,128)S(1)} %merge_last.1), channel_id=1, source_target_pairs={{0,9},{1,8},{4,13},{5,12},{8,1},{9,0},{12,5},{13,4},{2,11},{3,10},... | collective-permute-start | bytes 294920 | tf_op jit(solution)/shard_map/ppermute | solution.py:343
  30.5 10.0 %collective-permute-start.8 = (f32[48,1024]{1,0:T(8,128)S(1)}, f32[48,1024]{1,0:T(8,128)S(1)}, u32[]{:S(2)}, u32[]{:S(2)}) collective-permute-start(f32[48,1024]{1,0:T(8,128)S(1)} %get-tuple-element.37), channel_id=1, source_target_pairs={{0,2},{2,0},{1,3},{3,1},{4,6},{6,4},{5,7},{7,5},{8,10},{10,8},{9,1... | collective-permute-start | bytes 589832 | tf_op jit(solution)/shard_map/ppermute | solution.py:346
  36.2 4.3 %collective-permute-start.11 = (f32[16,1024]{1,0:T(8,128)S(1)}, f32[16,1024]{1,0:T(8,128)S(1)}, u32[]{:S(2)}, u32[]{:S(2)}) collective-permute-start(f32[16,1024]{1,0:T(8,128)S(1)} %remap_last.1.last), channel_id=1, source_target_pairs={{0,2},{2,0},{1,3},{3,1},{4,6},{6,4},{5,7},{7,5},{8,10},{10,8},{9,1... | collective-permute-start | bytes 196616 | tf_op jit(solution)/shard_map/ppermute | solution.py:346
where the time goes:
time: 41.4 us; the launch traced here: 41.2 us
  Pallas kernels  16.9 us (41%)
  starting transfers between devices  15.6 us (38%)
  waiting for transfers between devices  7.31 us (18%)
  between operations  0.77 us (2%)
  local copies, waits for them, and re-layouts  0.69 us (2%)
    ppermute x7, starting transfers between devices, to_peer(): return lax.ppermute(x, ('lev', 'sub'), pairs)  8.83 us
    pallas_call x3, Pallas kernels, remap_call(): pl.pallas_call(kernel, out_shape=[jax.ShapeDtypeStruct((rows, PIXELS_DEV)...  7.83 us
    ppermute x5, starting transfers between devices, swap(): return lax.ppermute(x, 'tm', [(0, 1), (1, 0)])  6.72 us
    ppermute x5, waiting for transfers between devices, swap(): return lax.ppermute(x, 'tm', [(0, 1), (1, 0)])  4.42 us
    pallas_call x1, Pallas kernels, place_tiles(): pl.pallas_call(place_kernel, out_shape=(half, half), in_specs=[smem, smem...  4.33 us
    pallas_call x1, Pallas kernels, hour_sums(): pl.pallas_call(functools.partial(sums_kernel, plain, first, second), out_...  3.9 us
    ppermute x7, waiting for transfers between devices, to_peer(): return lax.ppermute(x, ('lev', 'sub'), pairs)  2.89 us
    pallas_call x5, Pallas kernels, small_call(): pl.pallas_call(kernel, out_shape=[jax.ShapeDtypeStruct(shape, jnp.float32...  0.87 us
  transfers between devices with their start and end apart: 12, of which 5 were waited for; matrix products, arithmetic and copies ran while one was open for 0% of the time, Pallas kernels for 30%

commit v1 on v0

--- a/solution.py
+++ b/solution.py
@@ -273,20 +273,28 @@
     return outs[: len(plain)], outs[len(plain) :]
 
 
-def merge_kernel(mine, got, *refs):
-    outs = refs[-(mine.shape[0] // refs[-1].shape[0]) :]
-    rows = outs[0].shape[0]
-    for place, out in enumerate(outs):
-        at = slice(place * rows, (place + 1) * rows)
-        out[...] = mine[at] + got[at]
-
-
 def hold_kernel(x, *refs):
     refs[-1][...] = x[...]
 
 
-def far_rows_kernel(same_sub, other_sub, out):
-    out[...] = jnp.concatenate(far_rows(same_sub[...], other_sub[...]), axis=0)
+def merge_first_kernel(mine, got, held, *refs):
+    out, passed = refs[-2:]
+    rows = out.shape[0]
+    out[...] = mine[:rows] + got[:rows]
+    passed[...] = held[...]
+
+
+def merge_next_kernel(mine, got, *refs):
+    rows = refs[-1].shape[0]
+    refs[-1][...] = mine[rows:] + got[rows:]
+
+
+def merge_last_kernel(mine, got, *refs):
+    refs[-1][...] = mine[...] + got[...]
+
+
+def far_rows_kernel(same_sub, other_sub, *refs):
+    refs[-1][...] = jnp.concatenate(far_rows(same_sub[...], other_sub[...]), axis=0)
 
 
 def small_call(kernel, inputs, after, shapes, cost, name):
@@ -302,7 +310,11 @@
     )(*inputs, *after)
 
 
-def finish_kernel(divisor, levels, chip, got_chip, one, got_one, last, got_last, out):
+def sum_both_kernel(own, got, *refs):
+    refs[-1][...] = own[...] + got[...]
+
+
+def finish_kernel(divisor, levels, both, one, got_one, last, got_last, out):
     me, lev, even = lax.axis_index("tm"), lax.axis_index("lev") % 2, lax.axis_index("sub") == 0
     rows = 2 * levels
     near = keeps_near()
@@ -313,13 +325,12 @@
         @pl.when(near)
         def _():
             here = slice(hour * rows, (hour + 1) * rows)
-            out[same_at, :] = (chip[here] + got_chip[here]) / divisor
+            out[same_at, :] = both[here] / divisor
             out[other_at, :] = (one[here] + got_one[here]) / divisor
 
         @pl.when(jnp.logical_not(near))
         def _():
-            here = slice(hour * levels, (hour + 1) * levels)
-            plain = chip[here] + got_chip[here]
+            plain = both[hour * levels : (hour + 1) * levels]
             other = jnp.where(me == hour, last[:levels], got_last[:levels])
             pair = [jnp.where(even, plain, other), jnp.where(even, other, plain)]
             out[same_at, :] = jnp.concatenate(pair, axis=0) / divisor
@@ -356,16 +367,26 @@
     plain_got = to_peer(sums[0], *plain[0])
     high, low = place_tiles(tile_rows, tile_columns, live_count, tile_weight, theirs_0)
 
+    merged, theirs_1 = small_call(
+        merge_first_kernel,
+        [mine_0, got_0, theirs_1],
+        [high, sibling],
+        [folded] * 2,
+        LIGHT,
+        "merge_first",
+    )
+    got_1 = swap(theirs_1)
+    far_same = to_peer(merged, *first[0])
     merged = small_call(
-        merge_kernel, [mine_0, got_0], [high, sibling], [folded] * subs, LIGHT, "merge_first"
-    )
-    first_got = [to_peer(x, *peer) for x, peer in zip(merged, first)]
-    theirs_1 = small_call(hold_kernel, [theirs_1], [plain_got, *merged], [folded], LIGHT, "hold")[0]
-    got_1 = swap(theirs_1)
+        merge_next_kernel, [mine_0, got_0], [plain_got, merged], [folded], MEDIUM, "merge_next"
+    )
+    far_other = to_peer(merged[0], *first[1])
+    merged = small_call(merge_last_kernel, [mine_1, got_1], merged, [folded], LIGHT, "merge_last")
+    second_got = to_peer(merged[0], *second)
     both, send = remap_call(
         remap_both_kernel,
         [sums[4], sibling, plain_got],
-        [theirs_1],
+        merged,
         [2 * rows] * 2,
         high,
         low,
@@ -373,12 +394,9 @@
         "remap_both",
         [2 * rows] * 2,
     )
+    send = small_call(hold_kernel, [send], [near_got[0]], [send.shape], LIGHT, "hold")[0]
     got_both = swap(send)
-    merged = small_call(
-        merge_kernel, [mine_1, got_1], [both, near_got[0]], [folded], HEAVY, "merge_last"
-    )
-    second_got = to_peer(merged[0], *second)
-    far = small_call(far_rows_kernel, first_got, [], [(rows, CELLS_DEV)], HEAVY, "far_rows")[0]
+    far = small_call(far_rows_kernel, [far_same, far_other], [both], [(rows, CELLS_DEV)], HEAVY, "far_rows")[0]
     one, send = remap_call(
         remap_near_kernel,
         [*near_got, far],
@@ -391,10 +409,11 @@
         [2 * rows] * 2,
     )
     got_one = swap(send)
+    both = small_call(sum_both_kernel, [both, got_both], [one], [both.shape], LIGHT, "sum_both")[0]
     padded = -(-rows // 32) * 16
-    (last,) = remap_call(remap_last_kernel, [second_got], [one], [padded], high, low, HEAVY, "remap_last")
+    (last,) = remap_call(remap_last_kernel, [second_got], [both], [padded], high, low, HEAVY, "remap_last")
     got_last = swap(last)
-    out = finish([both, got_both, one, got_one, last, got_last], rows // 2, divisor)
+    out = finish([both, one, got_one, last, got_last], rows // 2, divisor)
     return out.reshape(HOURS, out.shape[0] // HOURS, PIXELS_DEV)
 
 

time: 41.4 us -> 42.6 us (1.029)
  the two profiles are of different devices: /device:TPU:0 before, /device:TPU:13 now
where the time goes in v1:
time: 42.6 us; the launch traced here: 42.5 us
  Pallas kernels  15.3 us (36%)
  starting transfers between devices  14.5 us (34%)
  waiting for transfers between devices  11.2 us (26%)
  between operations  0.78 us (2%)
  local copies, waits for them, and re-layouts  0.69 us (2%)
    ppermute x7, starting transfers between devices, to_peer(): return lax.ppermute(x, ('lev', 'sub'), pairs)  9.17 us
    pallas_call x3, Pallas kernels, remap_call(): pl.pallas_call(kernel, out_shape=[jax.ShapeDtypeStruct((rows, PIXELS_DEV)...  7.83 us
    ppermute x7, waiting for transfers between devices, to_peer(): return lax.ppermute(x, ('lev', 'sub'), pairs)  5.78 us
    ppermute x5, waiting for transfers between devices, swap(): return lax.ppermute(x, 'tm', [(0, 1), (1, 0)])  5.44 us
    ppermute x5, starting transfers between devices, swap(): return lax.ppermute(x, 'tm', [(0, 1), (1, 0)])  5.33 us
    pallas_call x1, Pallas kernels, hour_sums(): pl.pallas_call(functools.partial(sums_kernel, plain, first, second), out_...  3.9 us
    pallas_call x1, Pallas kernels, place_tiles(): pl.pallas_call(place_kernel, out_shape=(half, half), in_specs=[smem, smem...  2.65 us
    pallas_call x7, Pallas kernels, small_call(): pl.pallas_call(kernel, out_shape=[jax.ShapeDtypeStruct(shape, jnp.float32...  0.9 us
  transfers between devices with their start and end apart: 12, of which 4 were waited for; matrix products, arithmetic and copies ran while one was open for 0% of the time, Pallas kernels for 25%

profile of v1, /device:TPU:13, one launch (start us, length us, event | category | flops | bytes accessed | tf_op | source)
XLA Modules:
  0.0 42.5 jit_solution(7764430245210534283)
XLA Ops:
  0.0 0.7 %copy-done = s32[8]{0:T(128)S(1)} copy-done((s32[8]{0:T(128)S(1)}, s32[8]{0:T(128)}, u32[]{:S(2)}) %copy-start) | copy-done | bytes 56
  0.7 3.9 %hour_sums.1 = (f32[24,2048]{1,0:T(8,128)S(1)}, f32[24,2048]{1,0:T(8,128)S(1)}, f32[24,2048]{1,0:T(8,128)S(1)}, f32[24,2048]{1,0:T(8,128)S(1)}, f32[24,2048]{1,0...) custom-call(s32[8]{0:T(128)S(1)} %copy-done, ...), custom_call_target="tpu_custom_call" | custom-call | flops 1 | bytes 1 | tf_op jit(solution)/shard_map/hour_sums/pallas_call | solution.py:260
  4.6 0.7 %collective-permute-start = (f32[24,2048]{1,0:T(8,128)S(1)}, f32[24,2048]{1,0:T(8,128)S(1)}, u32[]{:S(2)}, u32[]{:S(2)}) collective-permute-start(f32[24,2048]{1,0:T(8,128)S(1)} %get-tuple-element.23), channel_id=1, source_target_pairs={{0,1},{1,0},{4,5},{5,4},{8,9},{9,8},{12,13},{13,12},{2,3},{3,2},{6... | collective-permute-start | bytes 589832 | tf_op jit(solution)/shard_map/ppermute | solution.py:354
  5.3 2.3 %collective-permute-start.1 = (f32[24,2048]{1,0:T(8,128)S(1)}, f32[24,2048]{1,0:T(8,128)S(1)}, u32[]{:S(2)}, u32[]{:S(2)}) collective-permute-start(f32[24,2048]{1,0:T(8,128)S(1)} %get-tuple-element.24), channel_id=1, source_target_pairs={{0,8},{1,9},{4,12},{5,13},{8,0},{9,1},{12,4},{13,5},{2,10},{3,11},... | collective-permute-start | bytes 589832 | tf_op jit(solution)/shard_map/ppermute | solution.py:354
  7.7 0.2 collective-permute-start.4
  7.8 1.8 %collective-permute-start.6 = (f32[24,2048]{1,0:T(8,128)S(1)}, f32[24,2048]{1,0:T(8,128)S(1)}, u32[]{:S(2)}, u32[]{:S(2)}) collective-permute-start(f32[24,2048]{1,0:T(8,128)S(1)} %get-tuple-element.36), channel_id=1, source_target_pairs={{0,5},{1,4},{4,1},{5,0},{8,13},{9,12},{12,9},{13,8},{2,7},{3,6},{6... | collective-permute-start | bytes 589832 | tf_op jit(solution)/shard_map/ppermute | solution.py:354
  9.6 1.2 %collective-permute-start.2 = (f32[48,1024]{1,0:T(8,128)S(1)}, f32[48,1024]{1,0:T(8,128)S(1)}, u32[]{:S(2)}, u32[]{:S(2)}) collective-permute-start(f32[48,1024]{1,0:T(8,128)S(1)} %get-tuple-element.25.refs_0_), channel_id=1, source_target_pairs={{0,2},{2,0},{1,3},{3,1},{4,6},{6,4},{5,7},{7,5},{8,10},{10,8},{9,1... | collective-permute-start | bytes 589832 | tf_op jit(solution)/shard_map/ppermute | solution.py:357
  11.5 0.0 copy-done.3
  11.5 2.7 %place_tiles.1 = (bf16[1024,2048]{1,0:T(8,128)(2,1)S(1)}, bf16[1024,2048]{1,0:T(8,128)(2,1)S(1)}) custom-call(s32[128]{0:T(128)S(1)} %copy-done.2, s32[128]{0:T(128)S(1)} %copy-done.3, s32[1]{0:T(128)S(6)} %copy.7.count, f32[64,8192]{1,0:T(8,128)S(1)} %copy-done.1, f32[48,1024]{1,0:T(8,128)S(1)} %get-tuple-element.25.refs_0_), custom_call_target="tpu_custom_call" | custom-call | flops 10000000000 | bytes 1 | tf_op jit(solution)/shard_map/place_tiles/pallas_call | solution.py:78
  14.2 0.0 collective-permute-done.refs_1_.sibling
  14.2 2.0 %collective-permute-done.2.got = f32[48,1024]{1,0:T(8,128)S(1)} collective-permute-done((f32[48,1024]{1,0:T(8,128)S(1)}, f32[48,1024]{1,0:T(8,128)S(1)}, u32[]{:S(2)}, u32[]{:S(2)}) %collective-permute-start.2) | collective-permute-done | bytes 196640 | tf_op jit(solution)/shard_map/ppermute | solution.py:357
  16.2 1.3 %collective-permute-start.3 = (f32[24,1024]{1,0:T(8,128)S(1)}, f32[24,1024]{1,0:T(8,128)S(1)}, u32[]{:S(2)}, u32[]{:S(2)}) collective-permute-start(f32[24,1024]{1,0:T(8,128)S(1)} %get-tuple-element.31), channel_id=1, source_target_pairs={{0,2},{2,0},{1,3},{3,1},{4,6},{6,4},{5,7},{7,5},{8,10},{10,8},{9,1... | collective-permute-start | bytes 294920 | tf_op jit(solution)/shard_map/ppermute | solution.py:357
  17.5 0.0 collective-permute-start.7
  17.5 0.0 collective-permute-done.1.refs_0_.plain
  17.5 2.7 %collective-permute-start.8 = (f32[24,1024]{1,0:T(8,128)S(1)}, f32[24,1024]{1,0:T(8,128)S(1)}, u32[]{:S(2)}, u32[]{:S(2)}) collective-permute-start(f32[24,1024]{1,0:T(8,128)S(1)} %merge_next.1.refs_0_), channel_id=1, source_target_pairs={{0,13},{1,12},{4,9},{5,8},{8,5},{9,4},{12,1},{13,0},{2,15},{3,14},... | collective-permute-start | bytes 294920 | tf_op jit(solution)/shard_map/ppermute | solution.py:354
  20.2 0.0 collective-permute-done.3.got
  20.3 1.4 %collective-permute-start.10 = (f32[24,1024]{1,0:T(8,128)S(1)}, f32[24,1024]{1,0:T(8,128)S(1)}, u32[]{:S(2)}, u32[]{:S(2)}) collective-permute-start(f32[24,1024]{1,0:T(8,128)S(1)} %merge_last.1.refs_0_), channel_id=1, source_target_pairs={{0,9},{1,8},{4,13},{5,12},{8,1},{9,0},{12,5},{13,4},{2,11},{3,10},... | collective-permute-start | bytes 294920 | tf_op jit(solution)/shard_map/ppermute | solution.py:354
  21.7 2.7 %remap_both.1 = (f32[48,1024]{1,0:T(8,128)S(1)}, f32[48,1024]{1,0:T(8,128)S(1)}) custom-call(f32[24,2048]{1,0:T(8,128)S(1)} %get-tuple-element.22.own, f32[24,2048]{1,0:T(8,128)S(1)} %collective-permute-done.refs_1_.sibling, f32[24,2048]{1,0:T(8,128)S(1)} %collective-permute-done.1.refs_0_.plain, bf16[1024,2048]{1,0:T(8,128)(2,1)S(1)} %get-tuple-element.26.refs_0_.high, ...), custom_call_target="tpu_custom_call" | custom-call | flops 2500000000 | bytes 1 | tf_op jit(solution)/shard_map/remap_both/pallas_call | solution.py:105
  24.4 0.0 collective-permute-done.4.refs_0_.near_same
  24.5 1.3 %collective-permute-start.5 = (f32[48,1024]{1,0:T(8,128)S(1)}, f32[48,1024]{1,0:T(8,128)S(1)}, u32[]{:S(2)}, u32[]{:S(2)}) collective-permute-start(f32[48,1024]{1,0:T(8,128)S(1)} %hold.1), channel_id=1, source_target_pairs={{0,2},{2,0},{1,3},{3,1},{4,6},{6,4},{5,7},{7,5},{8,10},{10,8},{9,1... | collective-permute-start | bytes 589832 | tf_op jit(solution)/shard_map/ppermute | solution.py:357
  25.7 5.8 %collective-permute-done.8.other_sub = f32[24,1024]{1,0:T(8,128)S(1)} collective-permute-done((f32[24,1024]{1,0:T(8,128)S(1)}, f32[24,1024]{1,0:T(8,128)S(1)}, u32[]{:S(2)}, u32[]{:S(2)}) %collective-permute-start.8) | collective-permute-done | bytes 98336 | tf_op jit(solution)/shard_map/ppermute | solution.py:354
  31.5 0.0 collective-permute-done.7.same_sub
  31.6 0.0 collective-permute-done.6.near_other
  31.6 2.7 %remap_near.1 = (f32[48,1024]{1,0:T(8,128)S(1)}, f32[48,1024]{1,0:T(8,128)S(1)}) custom-call(f32[24,2048]{1,0:T(8,128)S(1)} %collective-permute-done.4.refs_0_.near_same, f32[24,2048]{1,0:T(8,128)S(1)} %collective-permute-done.6.near_other, f32[24,2048]{1,0:T(8,128)S(1)} %far_rows.1.far, bf16[1024,2048]{1,0:T(8,128)(2,1)S(1)} %get-tuple-element.26.refs_0_.high, ...), custom_call_target="tpu_custom_call" | custom-call | flops 1 | bytes 1 | tf_op jit(solution)/shard_map/remap_near/pallas_call | solution.py:105
  34.3 0.6 %collective-permute-start.9 = (f32[48,1024]{1,0:T(8,128)S(1)}, f32[48,1024]{1,0:T(8,128)S(1)}, u32[]{:S(2)}, u32[]{:S(2)}) collective-permute-start(f32[48,1024]{1,0:T(8,128)S(1)} %get-tuple-element.38), channel_id=1, source_target_pairs={{0,2},{2,0},{1,3},{3,1},{4,6},{6,4},{5,7},{7,5},{8,10},{10,8},{9,1... | collective-permute-start | bytes 589832 | tf_op jit(solution)/shard_map/ppermute | solution.py:357
  34.9 0.0 collective-permute-done.5.got
  34.9 0.0 collective-permute-done.10.block
  35.0 2.4 %remap_last.1.last = f32[16,1024]{1,0:T(8,128)S(1)} custom-call(f32[24,1024]{1,0:T(8,128)S(1)} %collective-permute-done.10.block, bf16[1024,2048]{1,0:T(8,128)(2,1)S(1)} %get-tuple-element.26.refs_0_.high, bf16[1024,2048]{1,0:T(8,128)(2,1)S(1)} %get-tuple-element.27.low, f32[48,1024]{1,0:T(8,128)S(1)} %sum_both.1.refs_0_.both), custom_call_target="tpu_custom_call" | custom-call | flops 10000000000 | bytes 1 | tf_op jit(solution)/shard_map/remap_last/pallas_call | solution.py:105
  37.3 0.9 %collective-permute-start.11 = (f32[16,1024]{1,0:T(8,128)S(1)}, f32[16,1024]{1,0:T(8,128)S(1)}, u32[]{:S(2)}, u32[]{:S(2)}) collective-permute-start(f32[16,1024]{1,0:T(8,128)S(1)} %remap_last.1.last), channel_id=1, source_target_pairs={{0,2},{2,0},{1,3},{3,1},{4,6},{6,4},{5,7},{7,5},{8,10},{10,8},{9,1... | collective-permute-start | bytes 196616 | tf_op jit(solution)/shard_map/ppermute | solution.py:357
  38.3 3.0 %collective-permute-done.9.got_one = f32[48,1024]{1,0:T(8,128)S(1)} collective-permute-done((f32[48,1024]{1,0:T(8,128)S(1)}, f32[48,1024]{1,0:T(8,128)S(1)}, u32[]{:S(2)}, u32[]{:S(2)}) %collective-permute-start.9) | collective-permute-done | bytes 196640 | tf_op jit(solution)/shard_map/ppermute | solution.py:357
  41.2 0.4 %collective-permute-done.11.got_last = f32[16,1024]{1,0:T(8,128)S(1)} collective-permute-done((f32[16,1024]{1,0:T(8,128)S(1)}, f32[16,1024]{1,0:T(8,128)S(1)}, u32[]{:S(2)}, u32[]{:S(2)}) %collective-permute-start.11) | collective-permute-done | bytes 65568 | tf_op jit(solution)/shard_map/ppermute | solution.py:357
  41.7 0.8 %finish.1 = f32[96,1024]{1,0:T(8,128)} custom-call(f32[48,1024]{1,0:T(8,128)S(1)} %sum_both.1.refs_0_.both, f32[48,1024]{1,0:T(8,128)S(1)} %get-tuple-element.37.refs_0_.one, f32[48,1024]{1,0:T(8,128)S(1)} %collective-permute-done.9.got_one, f32[16,1024]{1,0:T(8,128)S(1)} %remap_last.1.last, f32[16,1024]{1,0:T(8,128)S(1)} %collective-permute-done.11.got_last), custom_call_target="tpu_custom_call" | custom-call | flops 1 | bytes 1 | tf_op jit(solution)/shard_map/finish/pallas_call | solution.py:302
  (12 shorter events, 0.1 us)
Async XLA Ops:
  0.0 11.5 %copy-start.3 = (s32[128]{0:T(128)S(1)}, s32[128]{0:T(128)}, u32[]{:S(2)}) copy-start(s32[128]{0:T(128)} %columns.1) | copy-start | bytes 1540
  0.0 11.5 %copy-start.2 = (s32[128]{0:T(128)S(1)}, s32[128]{0:T(128)}, u32[]{:S(2)}) copy-start(s32[128]{0:T(128)} %rows.1) | copy-start | bytes 1540
  0.0 0.7 %copy-start = (s32[8]{0:T(128)S(1)}, s32[8]{0:T(128)}, u32[]{:S(2)}) copy-start(s32[8]{0:T(128)} %step_hour.1) | copy-start | bytes 100
  0.7 10.8 %copy-start.1 = (f32[64,8192]{1,0:T(8,128)S(1)}, f32[64,8192]{1,0:T(8,128)}, u32[]{:S(2)}) copy-start(f32[64,8192]{1,0:T(8,128)} %weights.1) | copy-start | bytes 6291460
  4.6 9.6 %collective-permute-start = (f32[24,2048]{1,0:T(8,128)S(1)}, f32[24,2048]{1,0:T(8,128)S(1)}, u32[]{:S(2)}, u32[]{:S(2)}) collective-permute-start(f32[24,2048]{1,0:T(8,128)S(1)} %get-tuple-element.23), channel_id=1, source_target_pairs={{0,1},{1,0},{4,5},{5,4},{8,9},{9,8},{12,13},{13,12},{2,3},{3,2},{6... | collective-permute-start | bytes 589832 | tf_op jit(solution)/shard_map/ppermute | solution.py:354
  5.3 12.2 %collective-permute-start.1 = (f32[24,2048]{1,0:T(8,128)S(1)}, f32[24,2048]{1,0:T(8,128)S(1)}, u32[]{:S(2)}, u32[]{:S(2)}) collective-permute-start(f32[24,2048]{1,0:T(8,128)S(1)} %get-tuple-element.24), channel_id=1, source_target_pairs={{0,8},{1,9},{4,12},{5,13},{8,0},{9,1},{12,4},{13,5},{2,10},{3,11},... | collective-permute-start | bytes 589832 | tf_op jit(solution)/shard_map/ppermute | solution.py:354
  7.7 16.8 %collective-permute-start.4 = (f32[24,2048]{1,0:T(8,128)S(1)}, f32[24,2048]{1,0:T(8,128)S(1)}, u32[]{:S(2)}, u32[]{:S(2)}) collective-permute-start(f32[24,2048]{1,0:T(8,128)S(1)} %get-tuple-element.35), channel_id=1, source_target_pairs={{0,4},{1,5},{4,0},{5,1},{8,12},{9,13},{12,8},{13,9},{2,6},{3,7},{6... | collective-permute-start | bytes 589832 | tf_op jit(solution)/shard_map/ppermute | solution.py:354
  7.8 23.7 %collective-permute-start.6 = (f32[24,2048]{1,0:T(8,128)S(1)}, f32[24,2048]{1,0:T(8,128)S(1)}, u32[]{:S(2)}, u32[]{:S(2)}) collective-permute-start(f32[24,2048]{1,0:T(8,128)S(1)} %get-tuple-element.36), channel_id=1, source_target_pairs={{0,5},{1,4},{4,1},{5,0},{8,13},{9,12},{12,9},{13,8},{2,7},{3,6},{6... | collective-permute-start | bytes 589832 | tf_op jit(solution)/shard_map/ppermute | solution.py:354
  9.6 6.6 %collective-permute-start.2 = (f32[48,1024]{1,0:T(8,128)S(1)}, f32[48,1024]{1,0:T(8,128)S(1)}, u32[]{:S(2)}, u32[]{:S(2)}) collective-permute-start(f32[48,1024]{1,0:T(8,128)S(1)} %get-tuple-element.25.refs_0_), channel_id=1, source_target_pairs={{0,2},{2,0},{1,3},{3,1},{4,6},{6,4},{5,7},{7,5},{8,10},{10,8},{9,1... | collective-permute-start | bytes 589832 | tf_op jit(solution)/shard_map/ppermute | solution.py:357
  16.2 4.0 %collective-permute-start.3 = (f32[24,1024]{1,0:T(8,128)S(1)}, f32[24,1024]{1,0:T(8,128)S(1)}, u32[]{:S(2)}, u32[]{:S(2)}) collective-permute-start(f32[24,1024]{1,0:T(8,128)S(1)} %get-tuple-element.31), channel_id=1, source_target_pairs={{0,2},{2,0},{1,3},{3,1},{4,6},{6,4},{5,7},{7,5},{8,10},{10,8},{9,1... | collective-permute-start | bytes 294920 | tf_op jit(solution)/shard_map/ppermute | solution.py:357
  17.5 14.0 %collective-permute-start.7 = (f32[24,1024]{1,0:T(8,128)S(1)}, f32[24,1024]{1,0:T(8,128)S(1)}, u32[]{:S(2)}, u32[]{:S(2)}) collective-permute-start(f32[24,1024]{1,0:T(8,128)S(1)} %get-tuple-element.32.refs_1_), channel_id=1, source_target_pairs={{0,12},{1,13},{4,8},{5,9},{8,4},{9,5},{12,0},{13,1},{2,14},{3,15},... | collective-permute-start | bytes 294920 | tf_op jit(solution)/shard_map/ppermute | solution.py:354
  17.5 14.0 %collective-permute-start.8 = (f32[24,1024]{1,0:T(8,128)S(1)}, f32[24,1024]{1,0:T(8,128)S(1)}, u32[]{:S(2)}, u32[]{:S(2)}) collective-permute-start(f32[24,1024]{1,0:T(8,128)S(1)} %merge_next.1.refs_0_), channel_id=1, source_target_pairs={{0,13},{1,12},{4,9},{5,8},{8,5},{9,4},{12,1},{13,0},{2,15},{3,14},... | collective-permute-start | bytes 294920 | tf_op jit(solution)/shard_map/ppermute | solution.py:354
  20.3 14.7 %collective-permute-start.10 = (f32[24,1024]{1,0:T(8,128)S(1)}, f32[24,1024]{1,0:T(8,128)S(1)}, u32[]{:S(2)}, u32[]{:S(2)}) collective-permute-start(f32[24,1024]{1,0:T(8,128)S(1)} %merge_last.1.refs_0_), channel_id=1, source_target_pairs={{0,9},{1,8},{4,13},{5,12},{8,1},{9,0},{12,5},{13,4},{2,11},{3,10},... | collective-permute-start | bytes 294920 | tf_op jit(solution)/shard_map/ppermute | solution.py:354
  24.5 10.5 %collective-permute-start.5 = (f32[48,1024]{1,0:T(8,128)S(1)}, f32[48,1024]{1,0:T(8,128)S(1)}, u32[]{:S(2)}, u32[]{:S(2)}) collective-permute-start(f32[48,1024]{1,0:T(8,128)S(1)} %hold.1), channel_id=1, source_target_pairs={{0,2},{2,0},{1,3},{3,1},{4,6},{6,4},{5,7},{7,5},{8,10},{10,8},{9,1... | collective-permute-start | bytes 589832 | tf_op jit(solution)/shard_map/ppermute | solution.py:357
  34.3 6.9 %collective-permute-start.9 = (f32[48,1024]{1,0:T(8,128)S(1)}, f32[48,1024]{1,0:T(8,128)S(1)}, u32[]{:S(2)}, u32[]{:S(2)}) collective-permute-start(f32[48,1024]{1,0:T(8,128)S(1)} %get-tuple-element.38), channel_id=1, source_target_pairs={{0,2},{2,0},{1,3},{3,1},{4,6},{6,4},{5,7},{7,5},{8,10},{10,8},{9,1... | collective-permute-start | bytes 589832 | tf_op jit(solution)/shard_map/ppermute | solution.py:357
  37.3 4.4 %collective-permute-start.11 = (f32[16,1024]{1,0:T(8,128)S(1)}, f32[16,1024]{1,0:T(8,128)S(1)}, u32[]{:S(2)}, u32[]{:S(2)}) collective-permute-start(f32[16,1024]{1,0:T(8,128)S(1)} %remap_last.1.last), channel_id=1, source_target_pairs={{0,2},{2,0},{1,3},{3,1},{4,6},{6,4},{5,7},{7,5},{8,10},{10,8},{9,1... | collective-permute-start | bytes 196616 | tf_op jit(solution)/shard_map/ppermute | solution.py:357

commit v2 on v0

--- a/solution.py
+++ b/solution.py
@@ -186,25 +186,42 @@
         out[:, at] = result
 
 
-def hour_matrix(step_hour, levels, steps, hours, cuts):
-    rows, columns = cuts * levels, cuts * 2 * levels * steps
-    row = lax.broadcasted_iota(jnp.int32, (rows, columns), 0)
-    column = lax.broadcasted_iota(jnp.int32, (rows, columns), 1)
-    span = levels * steps
-    near = jnp.full((rows, columns), -1, jnp.int32)
-    for cut in range(cuts):
-        for half in range(2):
-            step = column - (cut * 2 + half) * span - (row - cut * levels) * steps
-            inside = (row >= cut * levels) & (row < (cut + 1) * levels)
-            inside = inside & (step >= 0) & (step < steps)
-            near = jnp.where(inside, step, near)
-    blocks = []
-    for hour in hours:
-        block = jnp.zeros((rows, columns), jnp.float32)
-        for step in range(steps):
-            block = jnp.where(near == step, jnp.where(step_hour[step] == hour, 1.0, 0.0), block)
-        blocks.append(block)
-    return jnp.concatenate(blocks, axis=0).astype(jnp.bfloat16)
+def hour_weights(step_hour, steps, hours, width):
+    row = lax.broadcasted_iota(jnp.int32, (steps, width), 0)
+    first = jnp.zeros((steps, width), jnp.float32)
+    second = jnp.zeros((steps, width), jnp.float32)
+    for step in range(steps):
+        first = jnp.where(row == step, jnp.where(step_hour[step] == hours[0], 1.0, 0.0), first)
+        second = jnp.where(row == step, jnp.where(step_hour[step] == hours[1], 1.0, 0.0), second)
+    upper = row < steps // 2
+    return jnp.where(upper, first, second), jnp.where(upper, second, first)
+
+
+def turn(x, rows):
+    return pltpu.roll(x, rows % x.shape[0], 0)
+
+
+def join(a, b, bit):
+    clear = (lax.broadcasted_iota(jnp.int32, a.shape, 0) & bit) == 0
+    kept, moved = jnp.where(clear, a, b), jnp.where(clear, b, a)
+    return kept + jnp.where(clear, turn(moved, -bit), turn(moved, bit))
+
+
+def sum_steps(block, weights):
+    def halve(x):
+        return x * weights[0] + turn(x * weights[1], 4)
+
+    def four(level):
+        a, b, c, d = (halve(block(level + i)) for i in range(4))
+        return join(join(a, c, 2), join(b, d, 2), 1)
+
+    return four
+
+
+def pack(pieces):
+    upper = lax.broadcasted_iota(jnp.int32, pieces[0][0].shape, 0) < 4
+    at_half = [x if half == place % 2 else turn(x, 4) for place, (x, half) in enumerate(pieces)]
+    return [jnp.where(upper, a, b) for a, b in zip(at_half[::2], at_half[1::2])]
 
 
 def peer_shard(k, j):
@@ -224,31 +241,51 @@
     return copies
 
 
+SUM_WIDTH = 512
+
+
 def sums_kernel(plain, first, second, step_hour, field, *refs):
     *outs, buffer, arrived = refs
     _, levels, steps, cells = buffer.shape
     rows, cut = HOURS * levels, cells // 2
     copies = field_copies(field, buffer, arrived, [*plain, *first, second])
     me = lax.axis_index("tm")
-    by_place = hour_matrix(step_hour, levels, steps, (1 - me, me), 2)
-    by_hour = hour_matrix(step_hour, levels, steps, range(HOURS), 1)
-
-    def halves(place):
+    groups = range(0, levels, 4)
+
+    def summed(place, start, width, weights):
+        four = sum_steps(lambda level: buffer[place, level, :, pl.ds(start, width)], weights)
+        return [four(level) for level in groups]
+
+    def store(out, offset, start, width, pieces):
+        for place, x in enumerate(pack(pieces)):
+            out[offset + place * 8 : offset + place * 8 + 8, pl.ds(start, width)] = x
+
+    weights = hour_weights(step_hour, steps, range(HOURS), SUM_WIDTH)
+    for place in range(len(plain)):
         copies[place].wait()
-        return split(buffer[place].reshape(levels * steps, cells))
-
-    for place in range(len(plain)):
-        outs[place][...] = dot(by_hour, jnp.concatenate(halves(place), axis=0), NN)
+
+        @pl.loop(0, cells // SUM_WIDTH)
+        def _(i):
+            start = pl.multiple_of(i * SUM_WIDTH, SUM_WIDTH)
+            sums = summed(place, start, SUM_WIDTH, weights)
+            pieces = [(x, half) for half in range(HOURS) for x in sums]
+            store(outs[place], 0, start, SUM_WIDTH, pieces)
+
     theirs_first, mine_first, theirs_second, mine_second = outs[len(plain) :]
+    width = SUM_WIDTH // 2
+    weights = hour_weights(step_hour, steps, (1 - me, me), width)
     for j in range(len(first) + 1):
-        high, low = halves(len(plain) + j)
-        stacked = [high[:, :cut], low[:, :cut], high[:, cut:], low[:, cut:]]
-        result = dot(by_place, jnp.concatenate(stacked, axis=0), NN)
-        if j < len(first):
-            at = slice(j * rows, (j + 1) * rows)
-            theirs_first[at], mine_first[at] = result[:rows], result[rows:]
-        else:
-            theirs_second[...], mine_second[...] = result[:rows], result[rows:]
+        place = len(plain) + j
+        copies[place].wait()
+        offset = j * rows if j < len(first) else 0
+        theirs, mine = (theirs_first, mine_first) if j < len(first) else (theirs_second, mine_second)
+
+        @pl.loop(0, cut // width)
+        def _(i):
+            start = pl.multiple_of(i * width, width)
+            sums = summed(place, start, width, weights) + summed(place, cut + start, width, weights)
+            store(theirs, offset, start, width, [(x, 0) for x in sums])
+            store(mine, offset, start, width, [(x, 1) for x in sums])
 
 
 def hour_sums(plain, first, second, step_hour, field):
@@ -417,6 +454,12 @@
 def solution(mesh):
     sizes = mesh.shape
     paired = sizes["tm"] == HOURS and sizes["lev"] == 4 and sizes["sub"] == 2
+
+    def body(level_field, *others):
+        steps, levels, _ = level_field.shape
+        suits = paired and steps == 8 and levels % 4 == 0
+        return (hour_plan if suits else general_plan)(level_field, *others)
+
     placed = (
         P(("groups", "tm"), ("lev", "sub"), None),
         P(None, ("lev", "sub")),
@@ -426,7 +469,7 @@
         P("tm"),
     )
     return jax.shard_map(
-        hour_plan if paired else general_plan,
+        body,
         mesh=mesh,
         in_specs=placed,
         out_specs=P("groups", "tm", ("lev", "sub")),

time: 41.4 us -> 41.4 us (level)
  Pallas kernels: 16.9 us -> 15.2 us
  waiting for transfers between devices: 7.31 us -> 8.99 us
    ppermute x5, waiting for transfers between devices: 4.42 us -> 6.1 us  [swap(): return lax.ppermute(x, 'tm', [(0, 1), (1, 0)])]
    pallas_call x1, Pallas kernels: 4.33 us -> 2.65 us  [place_tiles(): pl.pallas_call(place_kernel, out_shape=(half, half), in_specs=[smem, smem...]
  transfers between devices with their start and end apart: 12 -> 12, of which waited for: 5 -> 5; matrix products, arithmetic and copies ran while one was open for 0% -> 0% of each run, Pallas kernels for 30% -> 26%
where the time goes in v2:
time: 41.4 us; the launch traced here: 41.2 us
  starting transfers between devices  15.5 us (37%)
  Pallas kernels  15.2 us (37%)
  waiting for transfers between devices  8.99 us (22%)
  between operations  0.77 us (2%)
  local copies, waits for them, and re-layouts  0.69 us (2%)
    ppermute x7, starting transfers between devices, to_peer(): return lax.ppermute(x, ('lev', 'sub'), pairs)  8.84 us
    pallas_call x3, Pallas kernels, remap_call(): pl.pallas_call(kernel, out_shape=[jax.ShapeDtypeStruct((rows, PIXELS_DEV)...  7.83 us
    ppermute x5, starting transfers between devices, swap(): return lax.ppermute(x, 'tm', [(0, 1), (1, 0)])  6.71 us
    ppermute x5, waiting for transfers between devices, swap(): return lax.ppermute(x, 'tm', [(0, 1), (1, 0)])  6.1 us
    pallas_call x1, Pallas kernels, hour_sums(): pl.pallas_call(functools.partial(sums_kernel, plain, first, second), out_...  3.88 us
    ppermute x7, waiting for transfers between devices, to_peer(): return lax.ppermute(x, ('lev', 'sub'), pairs)  2.89 us
    pallas_call x1, Pallas kernels, place_tiles(): pl.pallas_call(place_kernel, out_shape=(half, half), in_specs=[smem, smem...  2.65 us
    pallas_call x5, Pallas kernels, small_call(): pl.pallas_call(kernel, out_shape=[jax.ShapeDtypeStruct(shape, jnp.float32...  0.87 us
  transfers between devices with their start and end apart: 12, of which 5 were waited for; matrix products, arithmetic and copies ran while one was open for 0% of the time, Pallas kernels for 26%

profile of v2, /device:TPU:0, one launch (start us, length us, event | category | flops | bytes accessed | tf_op | source)
XLA Modules:
  0.0 41.2 jit_solution(16187638875159217401)
XLA Ops:
  0.0 0.7 %copy-done = s32[8]{0:T(128)S(1)} copy-done((s32[8]{0:T(128)S(1)}, s32[8]{0:T(128)}, u32[]{:S(2)}) %copy-start) | copy-done | bytes 56
  0.7 3.9 %hour_sums.1 = (f32[24,2048]{1,0:T(8,128)S(1)}, f32[24,2048]{1,0:T(8,128)S(1)}, f32[24,2048]{1,0:T(8,128)S(1)}, f32[24,2048]{1,0:T(8,128)S(1)}, f32[24,2048]{1,0...) custom-call(s32[8]{0:T(128)S(1)} %copy-done, ...), custom_call_target="tpu_custom_call" | custom-call | flops 1 | bytes 1 | tf_op jit(solution)/shard_map/hour_sums/pallas_call | solution.py:297
  4.6 0.5 %collective-permute-start = (f32[24,2048]{1,0:T(8,128)S(1)}, f32[24,2048]{1,0:T(8,128)S(1)}, u32[]{:S(2)}, u32[]{:S(2)}) collective-permute-start(f32[24,2048]{1,0:T(8,128)S(1)} %get-tuple-element.23), channel_id=1, source_target_pairs={{0,1},{1,0},{4,5},{5,4},{8,9},{9,8},{12,13},{13,12},{2,3},{3,2},{6... | collective-permute-start | bytes 589832 | tf_op jit(solution)/shard_map/ppermute | solution.py:380
  5.1 3.7 %collective-permute-start.1 = (f32[24,2048]{1,0:T(8,128)S(1)}, f32[24,2048]{1,0:T(8,128)S(1)}, u32[]{:S(2)}, u32[]{:S(2)}) collective-permute-start(f32[24,2048]{1,0:T(8,128)S(1)} %get-tuple-element.24), channel_id=1, source_target_pairs={{0,8},{1,9},{4,12},{5,13},{8,0},{9,1},{12,4},{13,5},{2,10},{3,11},... | collective-permute-start | bytes 589832 | tf_op jit(solution)/shard_map/ppermute | solution.py:380
  8.8 1.6 %collective-permute-start.4 = (f32[24,2048]{1,0:T(8,128)S(1)}, f32[24,2048]{1,0:T(8,128)S(1)}, u32[]{:S(2)}, u32[]{:S(2)}) collective-permute-start(f32[24,2048]{1,0:T(8,128)S(1)} %get-tuple-element.34), channel_id=1, source_target_pairs={{0,4},{1,5},{4,0},{5,1},{8,12},{9,13},{12,8},{13,9},{2,6},{3,7},{6... | collective-permute-start | bytes 589832 | tf_op jit(solution)/shard_map/ppermute | solution.py:380
  10.3 0.0 collective-permute-start.5
  10.3 1.5 %collective-permute-start.2 = (f32[48,1024]{1,0:T(8,128)S(1)}, f32[48,1024]{1,0:T(8,128)S(1)}, u32[]{:S(2)}, u32[]{:S(2)}) collective-permute-start(f32[48,1024]{1,0:T(8,128)S(1)} %get-tuple-element.25.refs_0_), channel_id=1, source_target_pairs={{0,2},{2,0},{1,3},{3,1},{4,6},{6,4},{5,7},{7,5},{8,10},{10,8},{9,1... | collective-permute-start | bytes 589832 | tf_op jit(solution)/shard_map/ppermute | solution.py:383
  12.5 0.0 copy-done.3
  12.5 2.7 %place_tiles.1 = (bf16[1024,2048]{1,0:T(8,128)(2,1)S(1)}, bf16[1024,2048]{1,0:T(8,128)(2,1)S(1)}) custom-call(s32[128]{0:T(128)S(1)} %copy-done.2, s32[128]{0:T(128)S(1)} %copy-done.3, s32[1]{0:T(128)S(6)} %copy.7.count, f32[64,8192]{1,0:T(8,128)S(1)} %copy-done.1, f32[48,1024]{1,0:T(8,128)S(1)} %get-tuple-element.25.refs_0_), custom_call_target="tpu_custom_call" | custom-call | flops 10000000000 | bytes 1 | tf_op jit(solution)/shard_map/place_tiles/pallas_call | solution.py:78
  15.2 0.0 collective-permute-done.refs_1_.sibling
  15.2 2.5 %collective-permute-done.2.got = f32[48,1024]{1,0:T(8,128)S(1)} collective-permute-done((f32[48,1024]{1,0:T(8,128)S(1)}, f32[48,1024]{1,0:T(8,128)S(1)}, u32[]{:S(2)}, u32[]{:S(2)}) %collective-permute-start.2) | collective-permute-done | bytes 196640 | tf_op jit(solution)/shard_map/ppermute | solution.py:383
  17.7 1.4 %collective-permute-start.6 = (f32[24,1024]{1,0:T(8,128)S(1)}, f32[24,1024]{1,0:T(8,128)S(1)}, u32[]{:S(2)}, u32[]{:S(2)}) collective-permute-start(f32[24,1024]{1,0:T(8,128)S(1)} %get-tuple-element.30.refs_1_), channel_id=1, source_target_pairs={{0,12},{1,13},{4,8},{5,9},{8,4},{9,5},{12,0},{13,1},{2,14},{3,15},... | collective-permute-start | bytes 294920 | tf_op jit(solution)/shard_map/ppermute | solution.py:380
  19.1 1.6 %collective-permute-start.7 = (f32[24,1024]{1,0:T(8,128)S(1)}, f32[24,1024]{1,0:T(8,128)S(1)}, u32[]{:S(2)}, u32[]{:S(2)}) collective-permute-start(f32[24,1024]{1,0:T(8,128)S(1)} %get-tuple-element.31.refs_2_), channel_id=1, source_target_pairs={{0,13},{1,12},{4,9},{5,8},{8,5},{9,4},{12,1},{13,0},{2,15},{3,14},... | collective-permute-start | bytes 294920 | tf_op jit(solution)/shard_map/ppermute | solution.py:380
  20.7 0.0 collective-permute-done.1.refs_0_.plain
  20.8 1.6 %collective-permute-start.9 = (f32[24,1024]{1,0:T(8,128)S(1)}, f32[24,1024]{1,0:T(8,128)S(1)}, u32[]{:S(2)}, u32[]{:S(2)}) collective-permute-start(f32[24,1024]{1,0:T(8,128)S(1)} %hold.1.refs_0_), channel_id=1, source_target_pairs={{0,2},{2,0},{1,3},{3,1},{4,6},{6,4},{5,7},{7,5},{8,10},{10,8},{9,1... | collective-permute-start | bytes 294920 | tf_op jit(solution)/shard_map/ppermute | solution.py:383
  22.3 2.7 %remap_both.1 = (f32[48,1024]{1,0:T(8,128)S(1)}, f32[48,1024]{1,0:T(8,128)S(1)}) custom-call(f32[24,2048]{1,0:T(8,128)S(1)} %get-tuple-element.22.own, f32[24,2048]{1,0:T(8,128)S(1)} %collective-permute-done.refs_1_.sibling, f32[24,2048]{1,0:T(8,128)S(1)} %collective-permute-done.1.refs_0_.plain, bf16[1024,2048]{1,0:T(8,128)(2,1)S(1)} %get-tuple-element.26.refs_0_.high, ...), custom_call_target="tpu_custom_call" | custom-call | flops 2500000000 | bytes 1 | tf_op jit(solution)/shard_map/remap_both/pallas_call | solution.py:105
  25.1 0.0 collective-permute-done.4.near_same.refs_1_
  25.1 0.6 %collective-permute-start.3 = (f32[48,1024]{1,0:T(8,128)S(1)}, f32[48,1024]{1,0:T(8,128)S(1)}, u32[]{:S(2)}, u32[]{:S(2)}) collective-permute-start(f32[48,1024]{1,0:T(8,128)S(1)} %get-tuple-element.33), channel_id=1, source_target_pairs={{0,2},{2,0},{1,3},{3,1},{4,6},{6,4},{5,7},{7,5},{8,10},{10,8},{9,1... | collective-permute-start | bytes 589832 | tf_op jit(solution)/shard_map/ppermute | solution.py:383
  25.7 0.8 %collective-permute-done.9.got = f32[24,1024]{1,0:T(8,128)S(1)} collective-permute-done((f32[24,1024]{1,0:T(8,128)S(1)}, f32[24,1024]{1,0:T(8,128)S(1)}, u32[]{:S(2)}, u32[]{:S(2)}) %collective-permute-start.9) | collective-permute-done | bytes 98336 | tf_op jit(solution)/shard_map/ppermute | solution.py:383
  26.5 0.1 collective-permute-start.10
  26.5 0.0 collective-permute-done.6.same_sub
  26.6 1.1 %collective-permute-done.7.other_sub = f32[24,1024]{1,0:T(8,128)S(1)} collective-permute-done((f32[24,1024]{1,0:T(8,128)S(1)}, f32[24,1024]{1,0:T(8,128)S(1)}, u32[]{:S(2)}, u32[]{:S(2)}) %collective-permute-start.7) | collective-permute-done | bytes 98336 | tf_op jit(solution)/shard_map/ppermute | solution.py:380
  27.7 0.0 collective-permute-done.5.near_other
  27.7 2.7 %remap_near.1 = (f32[48,1024]{1,0:T(8,128)S(1)}, f32[48,1024]{1,0:T(8,128)S(1)}) custom-call(f32[24,2048]{1,0:T(8,128)S(1)} %collective-permute-done.4.near_same.refs_1_, f32[24,2048]{1,0:T(8,128)S(1)} %collective-permute-done.5.near_other, f32[24,2048]{1,0:T(8,128)S(1)} %far_rows.1.far, bf16[1024,2048]{1,0:T(8,128)(2,1)S(1)} %get-tuple-element.26.refs_0_.high, ...), custom_call_target="tpu_custom_call" | custom-call | flops 1 | bytes 1 | tf_op jit(solution)/shard_map/remap_near/pallas_call | solution.py:105
  30.4 1.6 %collective-permute-start.8 = (f32[48,1024]{1,0:T(8,128)S(1)}, f32[48,1024]{1,0:T(8,128)S(1)}, u32[]{:S(2)}, u32[]{:S(2)}) collective-permute-start(f32[48,1024]{1,0:T(8,128)S(1)} %get-tuple-element.37), channel_id=1, source_target_pairs={{0,2},{2,0},{1,3},{3,1},{4,6},{6,4},{5,7},{7,5},{8,10},{10,8},{9,1... | collective-permute-start | bytes 589832 | tf_op jit(solution)/shard_map/ppermute | solution.py:383
  32.0 1.8 %collective-permute-done.10.block = f32[24,1024]{1,0:T(8,128)S(1)} collective-permute-done((f32[24,1024]{1,0:T(8,128)S(1)}, f32[24,1024]{1,0:T(8,128)S(1)}, u32[]{:S(2)}, u32[]{:S(2)}) %collective-permute-start.10) | collective-permute-done | bytes 98336 | tf_op jit(solution)/shard_map/ppermute | solution.py:380
  33.8 2.4 %remap_last.1.last = f32[16,1024]{1,0:T(8,128)S(1)} custom-call(f32[24,1024]{1,0:T(8,128)S(1)} %collective-permute-done.10.block, bf16[1024,2048]{1,0:T(8,128)(2,1)S(1)} %get-tuple-element.26.refs_0_.high, bf16[1024,2048]{1,0:T(8,128)(2,1)S(1)} %get-tuple-element.27.low, f32[48,1024]{1,0:T(8,128)S(1)} %get-tuple-element.36.refs_0_.one), custom_call_target="tpu_custom_call" | custom-call | flops 10000000000 | bytes 1 | tf_op jit(solution)/shard_map/remap_last/pallas_call | solution.py:105
  36.1 1.5 %collective-permute-start.11 = (f32[16,1024]{1,0:T(8,128)S(1)}, f32[16,1024]{1,0:T(8,128)S(1)}, u32[]{:S(2)}, u32[]{:S(2)}) collective-permute-start(f32[16,1024]{1,0:T(8,128)S(1)} %remap_last.1.last), channel_id=1, source_target_pairs={{0,2},{2,0},{1,3},{3,1},{4,6},{6,4},{5,7},{7,5},{8,10},{10,8},{9,1... | collective-permute-start | bytes 196616 | tf_op jit(solution)/shard_map/ppermute | solution.py:383
  37.7 0.0 collective-permute-done.3.got_chip
  37.7 2.8 %collective-permute-done.11.got_last = f32[16,1024]{1,0:T(8,128)S(1)} collective-permute-done((f32[16,1024]{1,0:T(8,128)S(1)}, f32[16,1024]{1,0:T(8,128)S(1)}, u32[]{:S(2)}, u32[]{:S(2)}) %collective-permute-start.11) | collective-permute-done | bytes 65568 | tf_op jit(solution)/shard_map/ppermute | solution.py:383
  40.4 0.0 collective-permute-done.8.got_one
  40.4 0.8 %finish.1 = f32[96,1024]{1,0:T(8,128)} custom-call(f32[48,1024]{1,0:T(8,128)S(1)} %get-tuple-element.32.refs_0_.chip, f32[48,1024]{1,0:T(8,128)S(1)} %collective-permute-done.3.got_chip, f32[48,1024]{1,0:T(8,128)S(1)} %get-tuple-element.36.refs_0_.one, f32[48,1024]{1,0:T(8,128)S(1)} %collective-permute-done.8.got_one, f32[16,1024]{1,0:T(8,128)S(1)} %remap_last.1.last, ...), custom_call_target="tpu_custom_call" | custom-call | flops 1 | bytes 1 | tf_op jit(solution)/shard_map/finish/pallas_call | solution.py:331
  (10 shorter events, 0.1 us)
Async XLA Ops:
  0.0 12.5 %copy-start.3 = (s32[128]{0:T(128)S(1)}, s32[128]{0:T(128)}, u32[]{:S(2)}) copy-start(s32[128]{0:T(128)} %columns.1) | copy-start | bytes 1540
  0.0 12.5 %copy-start.2 = (s32[128]{0:T(128)S(1)}, s32[128]{0:T(128)}, u32[]{:S(2)}) copy-start(s32[128]{0:T(128)} %rows.1) | copy-start | bytes 1540
  0.0 0.7 %copy-start = (s32[8]{0:T(128)S(1)}, s32[8]{0:T(128)}, u32[]{:S(2)}) copy-start(s32[8]{0:T(128)} %step_hour.1) | copy-start | bytes 100
  0.7 11.8 %copy-start.1 = (f32[64,8192]{1,0:T(8,128)S(1)}, f32[64,8192]{1,0:T(8,128)}, u32[]{:S(2)}) copy-start(f32[64,8192]{1,0:T(8,128)} %weights.1) | copy-start | bytes 6291460
  4.6 10.6 %collective-permute-start = (f32[24,2048]{1,0:T(8,128)S(1)}, f32[24,2048]{1,0:T(8,128)S(1)}, u32[]{:S(2)}, u32[]{:S(2)}) collective-permute-start(f32[24,2048]{1,0:T(8,128)S(1)} %get-tuple-element.23), channel_id=1, source_target_pairs={{0,1},{1,0},{4,5},{5,4},{8,9},{9,8},{12,13},{13,12},{2,3},{3,2},{6... | collective-permute-start | bytes 589832 | tf_op jit(solution)/shard_map/ppermute | solution.py:380
  5.1 15.6 %collective-permute-start.1 = (f32[24,2048]{1,0:T(8,128)S(1)}, f32[24,2048]{1,0:T(8,128)S(1)}, u32[]{:S(2)}, u32[]{:S(2)}) collective-permute-start(f32[24,2048]{1,0:T(8,128)S(1)} %get-tuple-element.24), channel_id=1, source_target_pairs={{0,8},{1,9},{4,12},{5,13},{8,0},{9,1},{12,4},{13,5},{2,10},{3,11},... | collective-permute-start | bytes 589832 | tf_op jit(solution)/shard_map/ppermute | solution.py:380
  8.8 16.3 %collective-permute-start.4 = (f32[24,2048]{1,0:T(8,128)S(1)}, f32[24,2048]{1,0:T(8,128)S(1)}, u32[]{:S(2)}, u32[]{:S(2)}) collective-permute-start(f32[24,2048]{1,0:T(8,128)S(1)} %get-tuple-element.34), channel_id=1, source_target_pairs={{0,4},{1,5},{4,0},{5,1},{8,12},{9,13},{12,8},{13,9},{2,6},{3,7},{6... | collective-permute-start | bytes 589832 | tf_op jit(solution)/shard_map/ppermute | solution.py:380
  10.3 17.4 %collective-permute-start.5 = (f32[24,2048]{1,0:T(8,128)S(1)}, f32[24,2048]{1,0:T(8,128)S(1)}, u32[]{:S(2)}, u32[]{:S(2)}) collective-permute-start(f32[24,2048]{1,0:T(8,128)S(1)} %get-tuple-element.35), channel_id=1, source_target_pairs={{0,5},{1,4},{4,1},{5,0},{8,13},{9,12},{12,9},{13,8},{2,7},{3,6},{6... | collective-permute-start | bytes 589832 | tf_op jit(solution)/shard_map/ppermute | solution.py:380
  10.3 7.4 %collective-permute-start.2 = (f32[48,1024]{1,0:T(8,128)S(1)}, f32[48,1024]{1,0:T(8,128)S(1)}, u32[]{:S(2)}, u32[]{:S(2)}) collective-permute-start(f32[48,1024]{1,0:T(8,128)S(1)} %get-tuple-element.25.refs_0_), channel_id=1, source_target_pairs={{0,2},{2,0},{1,3},{3,1},{4,6},{6,4},{5,7},{7,5},{8,10},{10,8},{9,1... | collective-permute-start | bytes 589832 | tf_op jit(solution)/shard_map/ppermute | solution.py:383
  17.7 8.8 %collective-permute-start.6 = (f32[24,1024]{1,0:T(8,128)S(1)}, f32[24,1024]{1,0:T(8,128)S(1)}, u32[]{:S(2)}, u32[]{:S(2)}) collective-permute-start(f32[24,1024]{1,0:T(8,128)S(1)} %get-tuple-element.30.refs_1_), channel_id=1, source_target_pairs={{0,12},{1,13},{4,8},{5,9},{8,4},{9,5},{12,0},{13,1},{2,14},{3,15},... | collective-permute-start | bytes 294920 | tf_op jit(solution)/shard_map/ppermute | solution.py:380
  19.1 8.5 %collective-permute-start.7 = (f32[24,1024]{1,0:T(8,128)S(1)}, f32[24,1024]{1,0:T(8,128)S(1)}, u32[]{:S(2)}, u32[]{:S(2)}) collective-permute-start(f32[24,1024]{1,0:T(8,128)S(1)} %get-tuple-element.31.refs_2_), channel_id=1, source_target_pairs={{0,13},{1,12},{4,9},{5,8},{8,5},{9,4},{12,1},{13,0},{2,15},{3,14},... | collective-permute-start | bytes 294920 | tf_op jit(solution)/shard_map/ppermute | solution.py:380
  20.8 5.7 %collective-permute-start.9 = (f32[24,1024]{1,0:T(8,128)S(1)}, f32[24,1024]{1,0:T(8,128)S(1)}, u32[]{:S(2)}, u32[]{:S(2)}) collective-permute-start(f32[24,1024]{1,0:T(8,128)S(1)} %hold.1.refs_0_), channel_id=1, source_target_pairs={{0,2},{2,0},{1,3},{3,1},{4,6},{6,4},{5,7},{7,5},{8,10},{10,8},{9,1... | collective-permute-start | bytes 294920 | tf_op jit(solution)/shard_map/ppermute | solution.py:383
  25.1 12.6 %collective-permute-start.3 = (f32[48,1024]{1,0:T(8,128)S(1)}, f32[48,1024]{1,0:T(8,128)S(1)}, u32[]{:S(2)}, u32[]{:S(2)}) collective-permute-start(f32[48,1024]{1,0:T(8,128)S(1)} %get-tuple-element.33), channel_id=1, source_target_pairs={{0,2},{2,0},{1,3},{3,1},{4,6},{6,4},{5,7},{7,5},{8,10},{10,8},{9,1... | collective-permute-start | bytes 589832 | tf_op jit(solution)/shard_map/ppermute | solution.py:383
  26.5 7.3 %collective-permute-start.10 = (f32[24,1024]{1,0:T(8,128)S(1)}, f32[24,1024]{1,0:T(8,128)S(1)}, u32[]{:S(2)}, u32[]{:S(2)}) collective-permute-start(f32[24,1024]{1,0:T(8,128)S(1)} %merge_last.1), channel_id=1, source_target_pairs={{0,9},{1,8},{4,13},{5,12},{8,1},{9,0},{12,5},{13,4},{2,11},{3,10},... | collective-permute-start | bytes 294920 | tf_op jit(solution)/shard_map/ppermute | solution.py:380
  30.4 10.0 %collective-permute-start.8 = (f32[48,1024]{1,0:T(8,128)S(1)}, f32[48,1024]{1,0:T(8,128)S(1)}, u32[]{:S(2)}, u32[]{:S(2)}) collective-permute-start(f32[48,1024]{1,0:T(8,128)S(1)} %get-tuple-element.37), channel_id=1, source_target_pairs={{0,2},{2,0},{1,3},{3,1},{4,6},{6,4},{5,7},{7,5},{8,10},{10,8},{9,1... | collective-permute-start | bytes 589832 | tf_op jit(solution)/shard_map/ppermute | solution.py:383
  36.1 4.3 %collective-permute-start.11 = (f32[16,1024]{1,0:T(8,128)S(1)}, f32[16,1024]{1,0:T(8,128)S(1)}, u32[]{:S(2)}, u32[]{:S(2)}) collective-permute-start(f32[16,1024]{1,0:T(8,128)S(1)} %remap_last.1.last), channel_id=1, source_target_pairs={{0,2},{2,0},{1,3},{3,1},{4,6},{6,4},{5,7},{7,5},{8,10},{10,8},{9,1... | collective-permute-start | bytes 196616 | tf_op jit(solution)/shard_map/ppermute | solution.py:383

commit v3 on v2

--- a/solution.py
+++ b/solution.py
@@ -90,21 +90,24 @@
 PIXEL_BLOCK = 256
 
 
-def remap_blocks(x, high, low):
+def remap_blocks(x, high, low, cells=slice(None)):
     m = x.shape[0]
     x_high, x_low = split(x)
     both = jnp.concatenate([x_high, x_low], axis=0)
     for start in range(0, PIXELS_DEV, PIXEL_BLOCK):
         at = slice(start, start + PIXEL_BLOCK)
-        first = dot(both, high[at, :], NT)
-        yield at, first[:m] + first[m:] + dot(x_high, low[at, :], NT)
+        first = dot(both, high[at, cells], NT)
+        yield at, first[:m] + first[m:] + dot(x_high, low[at, cells], NT)
 
 
 def remap_call(kernel, inputs, after, out_rows, high, low, cost, name, scratch_rows=()):
     vmem = pl.BlockSpec(memory_space=pltpu.VMEM)
     return pl.pallas_call(
         kernel,
-        out_shape=[jax.ShapeDtypeStruct((rows, PIXELS_DEV), jnp.float32) for rows in out_rows],
+        out_shape=[
+            jax.ShapeDtypeStruct(rows if isinstance(rows, tuple) else (rows, PIXELS_DEV), jnp.float32)
+            for rows in out_rows
+        ],
         in_specs=[vmem] * (len(inputs) + 2) + [pl.BlockSpec(memory_space=pl.ANY)] * len(after),
         out_specs=[vmem] * len(out_rows),
         scratch_shapes=[pltpu.VMEM((rows, PIXELS_DEV), jnp.float32) for rows in scratch_rows],
@@ -178,12 +181,23 @@
     sort_out(near_result, far_result, keep, send)
 
 
-def remap_last_kernel(block, high, low, *refs):
-    out = refs[-1]
+def remap_half(place, block, high, low):
     x = unfold(block[...])
-    x = jnp.concatenate([x, jnp.zeros((out.shape[0] - x.shape[0], x.shape[1]), jnp.float32)], axis=0)
-    for at, result in remap_blocks(x, high, low):
-        out[:, at] = result
+    levels, cells = x.shape
+    x = jnp.concatenate([x, jnp.zeros((-levels % 16, cells), jnp.float32)], axis=0)
+    yield from remap_blocks(x, high, low, slice(place * cells, (place + 1) * cells))
+
+
+def remap_early_kernel(block, high, low, *refs):
+    for at, result in remap_half(0, block, high, low):
+        refs[-1][:, at] = result
+
+
+def remap_last_kernel(block, early, high, low, *refs):
+    out, total = refs[-2:]
+    for at, result in remap_half(1, block, high, low):
+        total[:, at] = result + early[:, at]
+    out[...] = fold(total[: out.shape[0] // 2])
 
 
 def hour_weights(step_hour, steps, hours, width):
@@ -245,10 +259,13 @@
 
 
 def sums_kernel(plain, first, second, step_hour, field, *refs):
-    *outs, buffer, arrived = refs
+    *outs, buffer, arrived, hours, hours_arrived = refs
     _, levels, steps, cells = buffer.shape
     rows, cut = HOURS * levels, cells // 2
     copies = field_copies(field, buffer, arrived, [*plain, *first, second])
+    fetch = pltpu.make_async_copy(step_hour, hours, hours_arrived)
+    fetch.start()
+    fetch.wait()
     me = lax.axis_index("tm")
     groups = range(0, levels, 4)
 
@@ -260,7 +277,7 @@
         for place, x in enumerate(pack(pieces)):
             out[offset + place * 8 : offset + place * 8 + 8, pl.ds(start, width)] = x
 
-    weights = hour_weights(step_hour, steps, range(HOURS), SUM_WIDTH)
+    weights = hour_weights(hours, steps, range(HOURS), SUM_WIDTH)
     for place in range(len(plain)):
         copies[place].wait()
 
@@ -273,7 +290,7 @@
 
     theirs_first, mine_first, theirs_second, mine_second = outs[len(plain) :]
     width = SUM_WIDTH // 2
-    weights = hour_weights(step_hour, steps, (1 - me, me), width)
+    weights = hour_weights(hours, steps, (1 - me, me), width)
     for j in range(len(first) + 1):
         place = len(plain) + j
         copies[place].wait()
@@ -297,11 +314,13 @@
     outs = pl.pallas_call(
         functools.partial(sums_kernel, plain, first, second),
         out_shape=[jax.ShapeDtypeStruct(shape, jnp.float32) for shape in shapes],
-        in_specs=[pl.BlockSpec(memory_space=pltpu.SMEM), pl.BlockSpec(memory_space=pl.ANY)],
+        in_specs=[pl.BlockSpec(memory_space=pl.ANY)] * 2,
         out_specs=[vmem] * len(shapes),
         scratch_shapes=[
             pltpu.VMEM((count, levels, steps, CELLS_DEV), jnp.float32),
             pltpu.SemaphoreType.DMA((count,)),
+            pltpu.SMEM((steps,), jnp.int32),
+            pltpu.SemaphoreType.DMA,
         ],
         compiler_params=pltpu.CompilerParams(vmem_limit_bytes=52 * MIB),
         cost_estimate=LIGHT,
@@ -311,11 +330,24 @@
 
 
 def merge_kernel(mine, got, *refs):
-    outs = refs[-(mine.shape[0] // refs[-1].shape[0]) :]
+    outs = refs[-2:]
     rows = outs[0].shape[0]
     for place, out in enumerate(outs):
         at = slice(place * rows, (place + 1) * rows)
         out[...] = mine[at] + got[at]
+
+
+def fold(x):
+    half = x.shape[1] // 2
+    return jnp.concatenate([x[:, :half], x[:, half:]], axis=0)
+
+
+def merge_last_kernel(mine, got, *refs):
+    outs = refs[-2:]
+    levels = mine.shape[0] // 2
+    total = mine[...] + got[...]
+    for place, out in enumerate(outs):
+        out[...] = fold(total[place * levels : (place + 1) * levels])
 
 
 def hold_kernel(x, *refs):
@@ -357,7 +389,7 @@
         def _():
             here = slice(hour * levels, (hour + 1) * levels)
             plain = chip[here] + got_chip[here]
-            other = jnp.where(me == hour, last[:levels], got_last[:levels])
+            other = unfold(jnp.where(me == hour, last[...], got_last[...]))
             pair = [jnp.where(even, plain, other), jnp.where(even, other, plain)]
             out[same_at, :] = jnp.concatenate(pair, axis=0) / divisor
             out[other_at, :] = jnp.where(me == hour, one[:rows], got_one[:rows]) / divisor
@@ -411,10 +443,12 @@
         [2 * rows] * 2,
     )
     got_both = swap(send)
+    quarter = (folded[0], folded[1] // 2)
     merged = small_call(
-        merge_kernel, [mine_1, got_1], [both, near_got[0]], [folded], HEAVY, "merge_last"
-    )
-    second_got = to_peer(merged[0], *second)
+        merge_last_kernel, [mine_1, got_1], [both, near_got[0]], [quarter] * 2, HEAVY, "merge_last"
+    )
+    late = small_call(hold_kernel, [merged[1]], first_got[:1], [quarter], LIGHT, "hold")
+    second_got = [to_peer(x, *second) for x in (merged[0], late[0])]
     far = small_call(far_rows_kernel, first_got, [], [(rows, CELLS_DEV)], HEAVY, "far_rows")[0]
     one, send = remap_call(
         remap_near_kernel,
@@ -429,7 +463,20 @@
     )
     got_one = swap(send)
     padded = -(-rows // 32) * 16
-    (last,) = remap_call(remap_last_kernel, [second_got], [one], [padded], high, low, HEAVY, "remap_last")
+    (early,) = remap_call(
+        remap_early_kernel, second_got[:1], [one], [padded], high, low, HEAVY, "remap_early"
+    )
+    (last,) = remap_call(
+        remap_last_kernel,
+        [second_got[1], early],
+        [],
+        [(rows, PIXELS_DEV // 2)],
+        high,
+        low,
+        HEAVY,
+        "remap_last",
+        [padded],
+    )
     got_last = swap(last)
     out = finish([both, got_both, one, got_one, last, got_last], rows // 2, divisor)
     return out.reshape(HOURS, out.shape[0] // HOURS, PIXELS_DEV)

time: 41.4 us -> 40.8 us (0.986)
  waiting for transfers between devices: 8.99 us -> 5.61 us
  starting transfers between devices: 15.5 us -> 17.3 us
  Pallas kernels: 15.2 us -> 16.2 us
    ppermute x7 -> x8, waiting for transfers between devices: 2.89 us -> 0.02 us  [to_peer(): return lax.ppermute(x, ('lev', 'sub'), pairs)]
    ppermute x7 -> x8, starting transfers between devices: 8.84 us -> 11.5 us  [to_peer(): return lax.ppermute(x, ('lev', 'sub'), pairs)]
    pallas_call x1, Pallas kernels: 2.65 us -> 3.94 us  [place_tiles(): pl.pallas_call(place_kernel, out_shape=(half, half), in_specs=[smem, smem...]
    ppermute x5, starting transfers between devices: 6.71 us -> 5.81 us  [swap(): return lax.ppermute(x, 'tm', [(0, 1), (1, 0)])]
    ppermute x5, waiting for transfers between devices: 6.1 us -> 5.59 us  [swap(): return lax.ppermute(x, 'tm', [(0, 1), (1, 0)])]
    pallas_call x1, Pallas kernels: 3.88 us -> 3.41 us  [hour_sums(): pl.pallas_call(functools.partial(sums_kernel, plain, first, second), out_...]
    pallas_call x3 -> x4, Pallas kernels: 7.83 us -> 7.96 us  [remap_call(): pl.pallas_call(kernel, out_shape=[jax.ShapeDtypeStruct(rows if isinstance...]
    pallas_call x5 -> x6, Pallas kernels: 0.87 us -> 0.88 us  [small_call(): pl.pallas_call(kernel, out_shape=[jax.ShapeDtypeStruct(shape, jnp.float32...]
  transfers between devices with their start and end apart: 12 -> 13, of which waited for: 5 -> 3; matrix products, arithmetic and copies ran while one was open for 0% -> 0% of each run, Pallas kernels for 26% -> 30%
where the time goes in v3:
time: 40.8 us; the launch traced here: 40.6 us
  starting transfers between devices  17.3 us (42%)
  Pallas kernels  16.2 us (40%)
  waiting for transfers between devices  5.61 us (14%)
  between operations  0.79 us (2%)
  local copies, waits for them, and re-layouts  0.69 us (2%)
    ppermute x8, starting transfers between devices, to_peer(): return lax.ppermute(x, ('lev', 'sub'), pairs)  11.5 us
    pallas_call x4, Pallas kernels, remap_call(): pl.pallas_call(kernel, out_shape=[jax.ShapeDtypeStruct(rows if isinstance...  7.96 us
    ppermute x5, starting transfers between devices, swap(): return lax.ppermute(x, 'tm', [(0, 1), (1, 0)])  5.81 us
    ppermute x5, waiting for transfers between devices, swap(): return lax.ppermute(x, 'tm', [(0, 1), (1, 0)])  5.59 us
    pallas_call x1, Pallas kernels, place_tiles(): pl.pallas_call(place_kernel, out_shape=(half, half), in_specs=[smem, smem...  3.94 us
    pallas_call x1, Pallas kernels, hour_sums(): pl.pallas_call(functools.partial(sums_kernel, plain, first, second), out_...  3.41 us
    pallas_call x6, Pallas kernels, small_call(): pl.pallas_call(kernel, out_shape=[jax.ShapeDtypeStruct(shape, jnp.float32...  0.88 us
  transfers between devices with their start and end apart: 13, of which 3 were waited for; matrix products, arithmetic and copies ran while one was open for 0% of the time, Pallas kernels for 30%

profile of v3, /device:TPU:0, one launch (start us, length us, event | category | flops | bytes accessed | tf_op | source)
XLA Modules:
  0.0 40.6 jit_solution(5926135729938485818)
XLA Ops:
  0.0 0.7 %copy-done = s32[8]{0:T(128)S(1)} copy-done((s32[8]{0:T(128)S(1)}, s32[8]{0:T(128)}, u32[]{:S(2)}) %copy-start) | copy-done | bytes 56
  0.7 3.4 %hour_sums.1 = (f32[24,2048]{1,0:T(8,128)S(1)}, f32[24,2048]{1,0:T(8,128)S(1)}, f32[24,2048]{1,0:T(8,128)S(1)}, f32[24,2048]{1,0:T(8,128)S(1)}, f32[24,2048]{1,0...) custom-call(s32[8]{0:T(128)S(1)} %copy-done, ...), custom_call_target="tpu_custom_call" | custom-call | flops 1 | bytes 1 | tf_op jit(solution)/shard_map/hour_sums/pallas_call | solution.py:314
  4.1 0.5 %collective-permute-start = (f32[24,2048]{1,0:T(8,128)S(1)}, f32[24,2048]{1,0:T(8,128)S(1)}, u32[]{:S(2)}, u32[]{:S(2)}) collective-permute-start(f32[24,2048]{1,0:T(8,128)S(1)} %get-tuple-element.25), channel_id=1, source_target_pairs={{0,1},{1,0},{4,5},{5,4},{8,9},{9,8},{12,13},{13,12},{2,3},{3,2},{6... | collective-permute-start | bytes 589832 | tf_op jit(solution)/shard_map/ppermute | solution.py:412
  4.6 3.7 %collective-permute-start.1 = (f32[24,2048]{1,0:T(8,128)S(1)}, f32[24,2048]{1,0:T(8,128)S(1)}, u32[]{:S(2)}, u32[]{:S(2)}) collective-permute-start(f32[24,2048]{1,0:T(8,128)S(1)} %get-tuple-element.26), channel_id=1, source_target_pairs={{0,8},{1,9},{4,12},{5,13},{8,0},{9,1},{12,4},{13,5},{2,10},{3,11},... | collective-permute-start | bytes 589832 | tf_op jit(solution)/shard_map/ppermute | solution.py:412
  8.3 1.6 %collective-permute-start.4 = (f32[24,2048]{1,0:T(8,128)S(1)}, f32[24,2048]{1,0:T(8,128)S(1)}, u32[]{:S(2)}, u32[]{:S(2)}) collective-permute-start(f32[24,2048]{1,0:T(8,128)S(1)} %get-tuple-element.36), channel_id=1, source_target_pairs={{0,4},{1,5},{4,0},{5,1},{8,12},{9,13},{12,8},{13,9},{2,6},{3,7},{6... | collective-permute-start | bytes 589832 | tf_op jit(solution)/shard_map/ppermute | solution.py:412
  9.9 0.0 collective-permute-start.5
  9.9 1.5 %collective-permute-start.2 = (f32[48,1024]{1,0:T(8,128)S(1)}, f32[48,1024]{1,0:T(8,128)S(1)}, u32[]{:S(2)}, u32[]{:S(2)}) collective-permute-start(f32[48,1024]{1,0:T(8,128)S(1)} %get-tuple-element.27.refs_0_), channel_id=1, source_target_pairs={{0,2},{2,0},{1,3},{3,1},{4,6},{6,4},{5,7},{7,5},{8,10},{10,8},{9,1... | collective-permute-start | bytes 589832 | tf_op jit(solution)/shard_map/ppermute | solution.py:415
  12.0 3.9 %place_tiles.1 = (bf16[1024,2048]{1,0:T(8,128)(2,1)S(1)}, bf16[1024,2048]{1,0:T(8,128)(2,1)S(1)}) custom-call(s32[128]{0:T(128)S(1)} %copy-done.2, s32[128]{0:T(128)S(1)} %copy-done.3, s32[1]{0:T(128)S(6)} %copy.7.count, f32[64,8192]{1,0:T(8,128)S(1)} %copy-done.1, f32[48,1024]{1,0:T(8,128)S(1)} %get-tuple-element.27.refs_0_), custom_call_target="tpu_custom_call" | custom-call | flops 10000000000 | bytes 1 | tf_op jit(solution)/shard_map/place_tiles/pallas_call | solution.py:78
  16.0 0.0 collective-permute-done.refs_1_.sibling
  16.0 1.2 %collective-permute-done.2.got = f32[48,1024]{1,0:T(8,128)S(1)} collective-permute-done((f32[48,1024]{1,0:T(8,128)S(1)}, f32[48,1024]{1,0:T(8,128)S(1)}, u32[]{:S(2)}, u32[]{:S(2)}) %collective-permute-start.2) | collective-permute-done | bytes 196640 | tf_op jit(solution)/shard_map/ppermute | solution.py:415
  17.3 1.4 %collective-permute-start.6 = (f32[24,1024]{1,0:T(8,128)S(1)}, f32[24,1024]{1,0:T(8,128)S(1)}, u32[]{:S(2)}, u32[]{:S(2)}) collective-permute-start(f32[24,1024]{1,0:T(8,128)S(1)} %get-tuple-element.32.refs_1_), channel_id=1, source_target_pairs={{0,12},{1,13},{4,8},{5,9},{8,4},{9,5},{12,0},{13,1},{2,14},{3,15},... | collective-permute-start | bytes 294920 | tf_op jit(solution)/shard_map/ppermute | solution.py:412
  18.7 1.6 %collective-permute-start.7 = (f32[24,1024]{1,0:T(8,128)S(1)}, f32[24,1024]{1,0:T(8,128)S(1)}, u32[]{:S(2)}, u32[]{:S(2)}) collective-permute-start(f32[24,1024]{1,0:T(8,128)S(1)} %get-tuple-element.33.refs_2_), channel_id=1, source_target_pairs={{0,13},{1,12},{4,9},{5,8},{8,5},{9,4},{12,1},{13,0},{2,15},{3,14},... | collective-permute-start | bytes 294920 | tf_op jit(solution)/shard_map/ppermute | solution.py:412
  20.3 0.0 collective-permute-done.1.refs_0_.plain
  20.3 1.6 %collective-permute-start.9 = (f32[24,1024]{1,0:T(8,128)S(1)}, f32[24,1024]{1,0:T(8,128)S(1)}, u32[]{:S(2)}, u32[]{:S(2)}) collective-permute-start(f32[24,1024]{1,0:T(8,128)S(1)} %hold.2.refs_0_), channel_id=1, source_target_pairs={{0,2},{2,0},{1,3},{3,1},{4,6},{6,4},{5,7},{7,5},{8,10},{10,8},{9,1... | collective-permute-start | bytes 294920 | tf_op jit(solution)/shard_map/ppermute | solution.py:415
  21.8 2.7 %remap_both.1 = (f32[48,1024]{1,0:T(8,128)S(1)}, f32[48,1024]{1,0:T(8,128)S(1)}) custom-call(f32[24,2048]{1,0:T(8,128)S(1)} %get-tuple-element.24.own, f32[24,2048]{1,0:T(8,128)S(1)} %collective-permute-done.refs_1_.sibling, f32[24,2048]{1,0:T(8,128)S(1)} %collective-permute-done.1.refs_0_.plain, bf16[1024,2048]{1,0:T(8,128)(2,1)S(1)} %get-tuple-element.28.refs_0_.high, ...), custom_call_target="tpu_custom_call" | custom-call | flops 2500000000 | bytes 1 | tf_op jit(solution)/shard_map/remap_both/pallas_call | solution.py:105
  24.6 0.0 collective-permute-done.4.near_same.refs_1_
  24.6 0.6 %collective-permute-start.3 = (f32[48,1024]{1,0:T(8,128)S(1)}, f32[48,1024]{1,0:T(8,128)S(1)}, u32[]{:S(2)}, u32[]{:S(2)}) collective-permute-start(f32[48,1024]{1,0:T(8,128)S(1)} %get-tuple-element.35), channel_id=1, source_target_pairs={{0,2},{2,0},{1,3},{3,1},{4,6},{6,4},{5,7},{7,5},{8,10},{10,8},{9,1... | collective-permute-start | bytes 589832 | tf_op jit(solution)/shard_map/ppermute | solution.py:415
  25.2 0.8 %collective-permute-done.9.got = f32[24,1024]{1,0:T(8,128)S(1)} collective-permute-done((f32[24,1024]{1,0:T(8,128)S(1)}, f32[24,1024]{1,0:T(8,128)S(1)}, u32[]{:S(2)}, u32[]{:S(2)}) %collective-permute-start.9) | collective-permute-done | bytes 98336 | tf_op jit(solution)/shard_map/ppermute | solution.py:415
  26.0 0.1 collective-permute-start.11
  26.1 0.0 collective-permute-done.6.same_sub.refs_0_
  26.1 2.7 %collective-permute-start.10 = (f32[24,512]{1,0:T(8,128)S(1)}, f32[24,512]{1,0:T(8,128)S(1)}, u32[]{:S(2)}, u32[]{:S(2)}) collective-permute-start(f32[24,512]{1,0:T(8,128)S(1)} %hold.3), channel_id=1, source_target_pairs={{0,9},{1,8},{4,13},{5,12},{8,1},{9,0},{12,5},{13,4},{2,11},{3,10},... | collective-permute-start | bytes 147464 | tf_op jit(solution)/shard_map/ppermute | solution.py:412
  28.8 0.0 collective-permute-done.7.other_sub
  28.8 0.0 collective-permute-done.5.near_other
  28.8 2.7 %remap_near.1 = (f32[48,1024]{1,0:T(8,128)S(1)}, f32[48,1024]{1,0:T(8,128)S(1)}) custom-call(f32[24,2048]{1,0:T(8,128)S(1)} %collective-permute-done.4.near_same.refs_1_, f32[24,2048]{1,0:T(8,128)S(1)} %collective-permute-done.5.near_other, f32[24,2048]{1,0:T(8,128)S(1)} %far_rows.1.far, bf16[1024,2048]{1,0:T(8,128)(2,1)S(1)} %get-tuple-element.28.refs_0_.high, ...), custom_call_target="tpu_custom_call" | custom-call | flops 1 | bytes 1 | tf_op jit(solution)/shard_map/remap_near/pallas_call | solution.py:105
  31.6 1.6 %collective-permute-start.8 = (f32[48,1024]{1,0:T(8,128)S(1)}, f32[48,1024]{1,0:T(8,128)S(1)}, u32[]{:S(2)}, u32[]{:S(2)}) collective-permute-start(f32[48,1024]{1,0:T(8,128)S(1)} %get-tuple-element.39), channel_id=1, source_target_pairs={{0,2},{2,0},{1,3},{3,1},{4,6},{6,4},{5,7},{7,5},{8,10},{10,8},{9,1... | collective-permute-start | bytes 589832 | tf_op jit(solution)/shard_map/ppermute | solution.py:415
  33.1 1.2 %remap_early.1.early = f32[16,1024]{1,0:T(8,128)S(1)} custom-call(f32[24,512]{1,0:T(8,128)S(1)} %collective-permute-done.11.block, bf16[1024,2048]{1,0:T(8,128)(2,1)S(1)} %get-tuple-element.28.refs_0_.high, bf16[1024,2048]{1,0:T(8,128)(2,1)S(1)} %get-tuple-element.29.low, f32[48,1024]{1,0:T(8,128)S(1)} %get-tuple-element.38.refs_0_.one), custom_call_target="tpu_custom_call" | custom-call | flops 10000000000 | bytes 1 | tf_op jit(solution)/shard_map/remap_early/pallas_call | solution.py:105
  34.4 0.0 collective-permute-done.10.block
  34.4 1.3 %remap_last.1.last = f32[24,512]{1,0:T(8,128)S(1)} custom-call(f32[24,512]{1,0:T(8,128)S(1)} %collective-permute-done.10.block, f32[16,1024]{1,0:T(8,128)S(1)} %remap_early.1.early, bf16[1024,2048]{1,0:T(8,128)(2,1)S(1)} %get-tuple-element.28.refs_0_.high, bf16[1024,2048]{1,0:T(8,128)(2,1)S(1)} %get-tuple-element.29.low), custom_call_target="tpu_custom_call" | custom-call | flops 10000000000 | bytes 1 | tf_op jit(solution)/shard_map/remap_last/pallas_call | solution.py:105
  35.6 0.6 %collective-permute-start.12 = (f32[24,512]{1,0:T(8,128)S(1)}, f32[24,512]{1,0:T(8,128)S(1)}, u32[]{:S(2)}, u32[]{:S(2)}) collective-permute-start(f32[24,512]{1,0:T(8,128)S(1)} %remap_last.1.last), channel_id=1, source_target_pairs={{0,2},{2,0},{1,3},{3,1},{4,6},{6,4},{5,7},{7,5},{8,10},{10,8},{9,1... | collective-permute-start | bytes 147464 | tf_op jit(solution)/shard_map/ppermute | solution.py:415
  36.2 3.6 %collective-permute-done.12.got_last = f32[24,512]{1,0:T(8,128)S(1)} collective-permute-done((f32[24,512]{1,0:T(8,128)S(1)}, f32[24,512]{1,0:T(8,128)S(1)}, u32[]{:S(2)}, u32[]{:S(2)}) %collective-permute-start.12) | collective-permute-done | bytes 49184 | tf_op jit(solution)/shard_map/ppermute | solution.py:415
  39.8 0.0 collective-permute-done.3.got_chip
  39.8 0.8 %finish.1 = f32[96,1024]{1,0:T(8,128)} custom-call(f32[48,1024]{1,0:T(8,128)S(1)} %get-tuple-element.34.refs_0_.chip, f32[48,1024]{1,0:T(8,128)S(1)} %collective-permute-done.3.got_chip, f32[48,1024]{1,0:T(8,128)S(1)} %get-tuple-element.38.refs_0_.one, f32[48,1024]{1,0:T(8,128)S(1)} %collective-permute-done.8.got_one, f32[24,512]{1,0:T(8,128)S(1)} %remap_last.1.last, ...), custom_call_target="tpu_custom_call" | custom-call | flops 1 | bytes 1 | tf_op jit(solution)/shard_map/finish/pallas_call | solution.py:363
  (14 shorter events, 0.1 us)
Async XLA Ops:
  0.0 12.0 %copy-start.3 = (s32[128]{0:T(128)S(1)}, s32[128]{0:T(128)}, u32[]{:S(2)}) copy-start(s32[128]{0:T(128)} %columns.1) | copy-start | bytes 1540
  0.0 12.0 %copy-start.2 = (s32[128]{0:T(128)S(1)}, s32[128]{0:T(128)}, u32[]{:S(2)}) copy-start(s32[128]{0:T(128)} %rows.1) | copy-start | bytes 1540
  0.0 0.7 %copy-start = (s32[8]{0:T(128)S(1)}, s32[8]{0:T(128)}, u32[]{:S(2)}) copy-start(s32[8]{0:T(128)} %step_hour.1) | copy-start | bytes 100
  0.7 11.3 %copy-start.1 = (f32[64,8192]{1,0:T(8,128)S(1)}, f32[64,8192]{1,0:T(8,128)}, u32[]{:S(2)}) copy-start(f32[64,8192]{1,0:T(8,128)} %weights.1) | copy-start | bytes 6291460
  4.1 11.9 %collective-permute-start = (f32[24,2048]{1,0:T(8,128)S(1)}, f32[24,2048]{1,0:T(8,128)S(1)}, u32[]{:S(2)}, u32[]{:S(2)}) collective-permute-start(f32[24,2048]{1,0:T(8,128)S(1)} %get-tuple-element.25), channel_id=1, source_target_pairs={{0,1},{1,0},{4,5},{5,4},{8,9},{9,8},{12,13},{13,12},{2,3},{3,2},{6... | collective-permute-start | bytes 589832 | tf_op jit(solution)/shard_map/ppermute | solution.py:412
  4.6 15.6 %collective-permute-start.1 = (f32[24,2048]{1,0:T(8,128)S(1)}, f32[24,2048]{1,0:T(8,128)S(1)}, u32[]{:S(2)}, u32[]{:S(2)}) collective-permute-start(f32[24,2048]{1,0:T(8,128)S(1)} %get-tuple-element.26), channel_id=1, source_target_pairs={{0,8},{1,9},{4,12},{5,13},{8,0},{9,1},{12,4},{13,5},{2,10},{3,11},... | collective-permute-start | bytes 589832 | tf_op jit(solution)/shard_map/ppermute | solution.py:412
  8.3 16.3 %collective-permute-start.4 = (f32[24,2048]{1,0:T(8,128)S(1)}, f32[24,2048]{1,0:T(8,128)S(1)}, u32[]{:S(2)}, u32[]{:S(2)}) collective-permute-start(f32[24,2048]{1,0:T(8,128)S(1)} %get-tuple-element.36), channel_id=1, source_target_pairs={{0,4},{1,5},{4,0},{5,1},{8,12},{9,13},{12,8},{13,9},{2,6},{3,7},{6... | collective-permute-start | bytes 589832 | tf_op jit(solution)/shard_map/ppermute | solution.py:412
  9.9 19.0 %collective-permute-start.5 = (f32[24,2048]{1,0:T(8,128)S(1)}, f32[24,2048]{1,0:T(8,128)S(1)}, u32[]{:S(2)}, u32[]{:S(2)}) collective-permute-start(f32[24,2048]{1,0:T(8,128)S(1)} %get-tuple-element.37), channel_id=1, source_target_pairs={{0,5},{1,4},{4,1},{5,0},{8,13},{9,12},{12,9},{13,8},{2,7},{3,6},{6... | collective-permute-start | bytes 589832 | tf_op jit(solution)/shard_map/ppermute | solution.py:412
  9.9 7.4 %collective-permute-start.2 = (f32[48,1024]{1,0:T(8,128)S(1)}, f32[48,1024]{1,0:T(8,128)S(1)}, u32[]{:S(2)}, u32[]{:S(2)}) collective-permute-start(f32[48,1024]{1,0:T(8,128)S(1)} %get-tuple-element.27.refs_0_), channel_id=1, source_target_pairs={{0,2},{2,0},{1,3},{3,1},{4,6},{6,4},{5,7},{7,5},{8,10},{10,8},{9,1... | collective-permute-start | bytes 589832 | tf_op jit(solution)/shard_map/ppermute | solution.py:415
  17.3 8.8 %collective-permute-start.6 = (f32[24,1024]{1,0:T(8,128)S(1)}, f32[24,1024]{1,0:T(8,128)S(1)}, u32[]{:S(2)}, u32[]{:S(2)}) collective-permute-start(f32[24,1024]{1,0:T(8,128)S(1)} %get-tuple-element.32.refs_1_), channel_id=1, source_target_pairs={{0,12},{1,13},{4,8},{5,9},{8,4},{9,5},{12,0},{13,1},{2,14},{3,15},... | collective-permute-start | bytes 294920 | tf_op jit(solution)/shard_map/ppermute | solution.py:412
  18.7 10.1 %collective-permute-start.7 = (f32[24,1024]{1,0:T(8,128)S(1)}, f32[24,1024]{1,0:T(8,128)S(1)}, u32[]{:S(2)}, u32[]{:S(2)}) collective-permute-start(f32[24,1024]{1,0:T(8,128)S(1)} %get-tuple-element.33.refs_2_), channel_id=1, source_target_pairs={{0,13},{1,12},{4,9},{5,8},{8,5},{9,4},{12,1},{13,0},{2,15},{3,14},... | collective-permute-start | bytes 294920 | tf_op jit(solution)/shard_map/ppermute | solution.py:412
  20.3 5.7 %collective-permute-start.9 = (f32[24,1024]{1,0:T(8,128)S(1)}, f32[24,1024]{1,0:T(8,128)S(1)}, u32[]{:S(2)}, u32[]{:S(2)}) collective-permute-start(f32[24,1024]{1,0:T(8,128)S(1)} %hold.2.refs_0_), channel_id=1, source_target_pairs={{0,2},{2,0},{1,3},{3,1},{4,6},{6,4},{5,7},{7,5},{8,10},{10,8},{9,1... | collective-permute-start | bytes 294920 | tf_op jit(solution)/shard_map/ppermute | solution.py:415
  24.6 15.2 %collective-permute-start.3 = (f32[48,1024]{1,0:T(8,128)S(1)}, f32[48,1024]{1,0:T(8,128)S(1)}, u32[]{:S(2)}, u32[]{:S(2)}) collective-permute-start(f32[48,1024]{1,0:T(8,128)S(1)} %get-tuple-element.35), channel_id=1, source_target_pairs={{0,2},{2,0},{1,3},{3,1},{4,6},{6,4},{5,7},{7,5},{8,10},{10,8},{9,1... | collective-permute-start | bytes 589832 | tf_op jit(solution)/shard_map/ppermute | solution.py:415
  26.0 7.1 %collective-permute-start.11 = (f32[24,512]{1,0:T(8,128)S(1)}, f32[24,512]{1,0:T(8,128)S(1)}, u32[]{:S(2)}, u32[]{:S(2)}) collective-permute-start(f32[24,512]{1,0:T(8,128)S(1)} %get-tuple-element.42), channel_id=1, source_target_pairs={{0,9},{1,8},{4,13},{5,12},{8,1},{9,0},{12,5},{13,4},{2,11},{3,10},... | collective-permute-start | bytes 147464 | tf_op jit(solution)/shard_map/ppermute | solution.py:412
  26.1 8.3 %collective-permute-start.10 = (f32[24,512]{1,0:T(8,128)S(1)}, f32[24,512]{1,0:T(8,128)S(1)}, u32[]{:S(2)}, u32[]{:S(2)}) collective-permute-start(f32[24,512]{1,0:T(8,128)S(1)} %hold.3), channel_id=1, source_target_pairs={{0,9},{1,8},{4,13},{5,12},{8,1},{9,0},{12,5},{13,4},{2,11},{3,10},... | collective-permute-start | bytes 147464 | tf_op jit(solution)/shard_map/ppermute | solution.py:412
  31.6 8.2 %collective-permute-start.8 = (f32[48,1024]{1,0:T(8,128)S(1)}, f32[48,1024]{1,0:T(8,128)S(1)}, u32[]{:S(2)}, u32[]{:S(2)}) collective-permute-start(f32[48,1024]{1,0:T(8,128)S(1)} %get-tuple-element.39), channel_id=1, source_target_pairs={{0,2},{2,0},{1,3},{3,1},{4,6},{6,4},{5,7},{7,5},{8,10},{10,8},{9,1... | collective-permute-start | bytes 589832 | tf_op jit(solution)/shard_map/ppermute | solution.py:415
  35.6 4.2 %collective-permute-start.12 = (f32[24,512]{1,0:T(8,128)S(1)}, f32[24,512]{1,0:T(8,128)S(1)}, u32[]{:S(2)}, u32[]{:S(2)}) collective-permute-start(f32[24,512]{1,0:T(8,128)S(1)} %remap_last.1.last), channel_id=1, source_target_pairs={{0,2},{2,0},{1,3},{3,1},{4,6},{6,4},{5,7},{7,5},{8,10},{10,8},{9,1... | collective-permute-start | bytes 147464 | tf_op jit(solution)/shard_map/ppermute | solution.py:415

commit v4 on v3

--- a/solution.py
+++ b/solution.py
@@ -90,14 +90,14 @@
 PIXEL_BLOCK = 256
 
 
-def remap_blocks(x, high, low, cells=slice(None)):
+def remap_blocks(x, high, low):
     m = x.shape[0]
     x_high, x_low = split(x)
     both = jnp.concatenate([x_high, x_low], axis=0)
     for start in range(0, PIXELS_DEV, PIXEL_BLOCK):
         at = slice(start, start + PIXEL_BLOCK)
-        first = dot(both, high[at, cells], NT)
-        yield at, first[:m] + first[m:] + dot(x_high, low[at, cells], NT)
+        first = dot(both, high[at, :], NT)
+        yield at, first[:m] + first[m:] + dot(x_high, low[at, :], NT)
 
 
 def remap_call(kernel, inputs, after, out_rows, high, low, cost, name, scratch_rows=()):
@@ -181,23 +181,14 @@
     sort_out(near_result, far_result, keep, send)
 
 
-def remap_half(place, block, high, low):
+def remap_last_kernel(block, high, low, *refs):
+    out, total = refs[-2:]
     x = unfold(block[...])
     levels, cells = x.shape
     x = jnp.concatenate([x, jnp.zeros((-levels % 16, cells), jnp.float32)], axis=0)
-    yield from remap_blocks(x, high, low, slice(place * cells, (place + 1) * cells))
-
-
-def remap_early_kernel(block, high, low, *refs):
-    for at, result in remap_half(0, block, high, low):
-        refs[-1][:, at] = result
-
-
-def remap_last_kernel(block, early, high, low, *refs):
-    out, total = refs[-2:]
-    for at, result in remap_half(1, block, high, low):
-        total[:, at] = result + early[:, at]
-    out[...] = fold(total[: out.shape[0] // 2])
+    for at, result in remap_blocks(x, high, low):
+        total[:, at] = result
+    out[...] = fold(total[:levels])
 
 
 def hour_weights(step_hour, steps, hours, width):
@@ -329,25 +320,23 @@
     return outs[: len(plain)], outs[len(plain) :]
 
 
-def merge_kernel(mine, got, *refs):
-    outs = refs[-2:]
-    rows = outs[0].shape[0]
-    for place, out in enumerate(outs):
-        at = slice(place * rows, (place + 1) * rows)
-        out[...] = mine[at] + got[at]
+def merge_first_kernel(mine, got, *refs):
+    rows = refs[-1].shape[0]
+    refs[-1][...] = mine[:rows] + got[:rows]
+
+
+def merge_next_kernel(mine, got, *refs):
+    rows = refs[-1].shape[0]
+    refs[-1][...] = mine[rows:] + got[rows:]
+
+
+def merge_last_kernel(mine, got, *refs):
+    refs[-1][...] = mine[...] + got[...]
 
 
 def fold(x):
     half = x.shape[1] // 2
     return jnp.concatenate([x[:, :half], x[:, half:]], axis=0)
-
-
-def merge_last_kernel(mine, got, *refs):
-    outs = refs[-2:]
-    levels = mine.shape[0] // 2
-    total = mine[...] + got[...]
-    for place, out in enumerate(outs):
-        out[...] = fold(total[place * levels : (place + 1) * levels])
 
 
 def hold_kernel(x, *refs):
@@ -426,15 +415,17 @@
     high, low = place_tiles(tile_rows, tile_columns, live_count, tile_weight, theirs_0)
 
     merged = small_call(
-        merge_kernel, [mine_0, got_0], [high, sibling], [folded] * subs, LIGHT, "merge_first"
-    )
-    first_got = [to_peer(x, *peer) for x, peer in zip(merged, first)]
+        merge_first_kernel, [mine_0, got_0], [high, sibling], [folded], LIGHT, "merge_first"
+    )
+    far_same = to_peer(merged[0], *first[0])
     theirs_1 = small_call(hold_kernel, [theirs_1], [plain_got, *merged], [folded], LIGHT, "hold")[0]
     got_1 = swap(theirs_1)
+    merged = small_call(merge_next_kernel, [mine_0, got_0], [theirs_1], [folded], LIGHT, "merge_next")
+    far_other = to_peer(merged[0], *first[1])
     both, send = remap_call(
         remap_both_kernel,
         [sums[4], sibling, plain_got],
-        [theirs_1],
+        merged,
         [2 * rows] * 2,
         high,
         low,
@@ -443,13 +434,11 @@
         [2 * rows] * 2,
     )
     got_both = swap(send)
-    quarter = (folded[0], folded[1] // 2)
     merged = small_call(
-        merge_last_kernel, [mine_1, got_1], [both, near_got[0]], [quarter] * 2, HEAVY, "merge_last"
-    )
-    late = small_call(hold_kernel, [merged[1]], first_got[:1], [quarter], LIGHT, "hold")
-    second_got = [to_peer(x, *second) for x in (merged[0], late[0])]
-    far = small_call(far_rows_kernel, first_got, [], [(rows, CELLS_DEV)], HEAVY, "far_rows")[0]
+        merge_last_kernel, [mine_1, got_1], [both, near_got[0]], [folded], HEAVY, "merge_last"
+    )
+    second_got = to_peer(merged[0], *second)
+    far = small_call(far_rows_kernel, [far_same, far_other], [], [(rows, CELLS_DEV)], HEAVY, "far_rows")[0]
     one, send = remap_call(
         remap_near_kernel,
         [*near_got, far],
@@ -463,13 +452,10 @@
     )
     got_one = swap(send)
     padded = -(-rows // 32) * 16
-    (early,) = remap_call(
-        remap_early_kernel, second_got[:1], [one], [padded], high, low, HEAVY, "remap_early"
-    )
     (last,) = remap_call(
         remap_last_kernel,
-        [second_got[1], early],
-        [],
+        [second_got],
+        [one],
         [(rows, PIXELS_DEV // 2)],
         high,
         low,

time: 40.8 us -> 41 us (level)
  waiting for transfers between devices: 5.61 us -> 7.58 us
  starting transfers between devices: 17.3 us -> 15.6 us
    ppermute x8 -> x7, waiting for transfers between devices: 0.02 us -> 2.92 us  [to_peer(): return lax.ppermute(x, ('lev', 'sub'), pairs)]
    ppermute x8 -> x7, starting transfers between devices: 11.5 us -> 9.62 us  [to_peer(): return lax.ppermute(x, ('lev', 'sub'), pairs)]
    ppermute x5, waiting for transfers between devices: 5.59 us -> 4.66 us  [swap(): return lax.ppermute(x, 'tm', [(0, 1), (1, 0)])]
    pallas_call x4 -> x3, Pallas kernels: 7.96 us -> 7.83 us  [remap_call(): pl.pallas_call(kernel, out_shape=[jax.ShapeDtypeStruct(rows if isinstance...]
  transfers between devices with their start and end apart: 13 -> 12, of which waited for: 3 -> 4; matrix products, arithmetic and copies ran while one was open for 0% -> 0% of each run, Pallas kernels for 30% -> 29%
where the time goes in v4:
time: 41 us; the launch traced here: 40.5 us
  Pallas kernels  15.8 us (39%)
  starting transfers between devices  15.6 us (38%)
  waiting for transfers between devices  7.58 us (18%)
  between operations  0.77 us (2%)
  local copies, waits for them, and re-layouts  0.69 us (2%)
    ppermute x7, starting transfers between devices, to_peer(): return lax.ppermute(x, ('lev', 'sub'), pairs)  9.62 us
    pallas_call x3, Pallas kernels, remap_call(): pl.pallas_call(kernel, out_shape=[jax.ShapeDtypeStruct(rows if isinstance...  7.83 us
    ppermute x5, starting transfers between devices, swap(): return lax.ppermute(x, 'tm', [(0, 1), (1, 0)])  6.02 us
    ppermute x5, waiting for transfers between devices, swap(): return lax.ppermute(x, 'tm', [(0, 1), (1, 0)])  4.66 us
    pallas_call x1, Pallas kernels, place_tiles(): pl.pallas_call(place_kernel, out_shape=(half, half), in_specs=[smem, smem...  3.68 us
    pallas_call x1, Pallas kernels, hour_sums(): pl.pallas_call(functools.partial(sums_kernel, plain, first, second), out_...  3.41 us
    ppermute x7, waiting for transfers between devices, to_peer(): return lax.ppermute(x, ('lev', 'sub'), pairs)  2.92 us
    pallas_call x6, Pallas kernels, small_call(): pl.pallas_call(kernel, out_shape=[jax.ShapeDtypeStruct(shape, jnp.float32...  0.87 us
  transfers between devices with their start and end apart: 12, of which 4 were waited for; matrix products, arithmetic and copies ran while one was open for 0% of the time, Pallas kernels for 29%

profile of v4, /device:TPU:0, one launch (start us, length us, event | category | flops | bytes accessed | tf_op | source)
XLA Modules:
  0.0 40.5 jit_solution(1823235468674273910)
XLA Ops:
  0.0 0.7 %copy-done = s32[8]{0:T(128)S(1)} copy-done((s32[8]{0:T(128)S(1)}, s32[8]{0:T(128)}, u32[]{:S(2)}) %copy-start) | copy-done | bytes 56
  0.7 3.4 %hour_sums.1 = (f32[24,2048]{1,0:T(8,128)S(1)}, f32[24,2048]{1,0:T(8,128)S(1)}, f32[24,2048]{1,0:T(8,128)S(1)}, f32[24,2048]{1,0:T(8,128)S(1)}, f32[24,2048]{1,0...) custom-call(s32[8]{0:T(128)S(1)} %copy-done, ...), custom_call_target="tpu_custom_call" | custom-call | flops 1 | bytes 1 | tf_op jit(solution)/shard_map/hour_sums/pallas_call | solution.py:305
  4.1 0.5 %collective-permute-start = (f32[24,2048]{1,0:T(8,128)S(1)}, f32[24,2048]{1,0:T(8,128)S(1)}, u32[]{:S(2)}, u32[]{:S(2)}) collective-permute-start(f32[24,2048]{1,0:T(8,128)S(1)} %get-tuple-element.21), channel_id=1, source_target_pairs={{0,1},{1,0},{4,5},{5,4},{8,9},{9,8},{12,13},{13,12},{2,3},{3,2},{6... | collective-permute-start | bytes 589832 | tf_op jit(solution)/shard_map/ppermute | solution.py:401
  4.6 3.7 %collective-permute-start.1 = (f32[24,2048]{1,0:T(8,128)S(1)}, f32[24,2048]{1,0:T(8,128)S(1)}, u32[]{:S(2)}, u32[]{:S(2)}) collective-permute-start(f32[24,2048]{1,0:T(8,128)S(1)} %get-tuple-element.22), channel_id=1, source_target_pairs={{0,8},{1,9},{4,12},{5,13},{8,0},{9,1},{12,4},{13,5},{2,10},{3,11},... | collective-permute-start | bytes 589832 | tf_op jit(solution)/shard_map/ppermute | solution.py:401
  8.3 1.6 %collective-permute-start.4 = (f32[24,2048]{1,0:T(8,128)S(1)}, f32[24,2048]{1,0:T(8,128)S(1)}, u32[]{:S(2)}, u32[]{:S(2)}) collective-permute-start(f32[24,2048]{1,0:T(8,128)S(1)} %get-tuple-element.30), channel_id=1, source_target_pairs={{0,4},{1,5},{4,0},{5,1},{8,12},{9,13},{12,8},{13,9},{2,6},{3,7},{6... | collective-permute-start | bytes 589832 | tf_op jit(solution)/shard_map/ppermute | solution.py:401
  9.9 0.0 collective-permute-start.5
  9.9 1.5 %collective-permute-start.2 = (f32[48,1024]{1,0:T(8,128)S(1)}, f32[48,1024]{1,0:T(8,128)S(1)}, u32[]{:S(2)}, u32[]{:S(2)}) collective-permute-start(f32[48,1024]{1,0:T(8,128)S(1)} %get-tuple-element.23.refs_0_), channel_id=1, source_target_pairs={{0,2},{2,0},{1,3},{3,1},{4,6},{6,4},{5,7},{7,5},{8,10},{10,8},{9,1... | collective-permute-start | bytes 589832 | tf_op jit(solution)/shard_map/ppermute | solution.py:404
  12.0 0.0 copy-done.3
  12.0 3.7 %place_tiles.1 = (bf16[1024,2048]{1,0:T(8,128)(2,1)S(1)}, bf16[1024,2048]{1,0:T(8,128)(2,1)S(1)}) custom-call(s32[128]{0:T(128)S(1)} %copy-done.2, s32[128]{0:T(128)S(1)} %copy-done.3, s32[1]{0:T(128)S(6)} %copy.7.count, f32[64,8192]{1,0:T(8,128)S(1)} %copy-done.1, f32[48,1024]{1,0:T(8,128)S(1)} %get-tuple-element.23.refs_0_), custom_call_target="tpu_custom_call" | custom-call | flops 10000000000 | bytes 1 | tf_op jit(solution)/shard_map/place_tiles/pallas_call | solution.py:78
  15.7 0.0 collective-permute-done.refs_1_.sibling
  15.7 1.5 %collective-permute-done.2.got = f32[48,1024]{1,0:T(8,128)S(1)} collective-permute-done((f32[48,1024]{1,0:T(8,128)S(1)}, f32[48,1024]{1,0:T(8,128)S(1)}, u32[]{:S(2)}, u32[]{:S(2)}) %collective-permute-start.2) | collective-permute-done | bytes 196640 | tf_op jit(solution)/shard_map/ppermute | solution.py:404
  17.2 1.4 %collective-permute-start.6 = (f32[24,1024]{1,0:T(8,128)S(1)}, f32[24,1024]{1,0:T(8,128)S(1)}, u32[]{:S(2)}, u32[]{:S(2)}) collective-permute-start(f32[24,1024]{1,0:T(8,128)S(1)} %merge_first.1.refs_1_), channel_id=1, source_target_pairs={{0,12},{1,13},{4,8},{5,9},{8,4},{9,5},{12,0},{13,1},{2,14},{3,15},... | collective-permute-start | bytes 294920 | tf_op jit(solution)/shard_map/ppermute | solution.py:401
  18.7 0.0 collective-permute-done.1.refs_0_.plain
  18.7 1.6 %collective-permute-start.9 = (f32[24,1024]{1,0:T(8,128)S(1)}, f32[24,1024]{1,0:T(8,128)S(1)}, u32[]{:S(2)}, u32[]{:S(2)}) collective-permute-start(f32[24,1024]{1,0:T(8,128)S(1)} %hold.1.refs_0_), channel_id=1, source_target_pairs={{0,2},{2,0},{1,3},{3,1},{4,6},{6,4},{5,7},{7,5},{8,10},{10,8},{9,1... | collective-permute-start | bytes 294920 | tf_op jit(solution)/shard_map/ppermute | solution.py:404
  20.2 2.4 %collective-permute-start.7 = (f32[24,1024]{1,0:T(8,128)S(1)}, f32[24,1024]{1,0:T(8,128)S(1)}, u32[]{:S(2)}, u32[]{:S(2)}) collective-permute-start(f32[24,1024]{1,0:T(8,128)S(1)} %merge_next.1.refs_0_), channel_id=1, source_target_pairs={{0,13},{1,12},{4,9},{5,8},{8,5},{9,4},{12,1},{13,0},{2,15},{3,14},... | collective-permute-start | bytes 294920 | tf_op jit(solution)/shard_map/ppermute | solution.py:401
  22.6 2.7 %remap_both.1 = (f32[48,1024]{1,0:T(8,128)S(1)}, f32[48,1024]{1,0:T(8,128)S(1)}) custom-call(f32[24,2048]{1,0:T(8,128)S(1)} %get-tuple-element.20.own, f32[24,2048]{1,0:T(8,128)S(1)} %collective-permute-done.refs_1_.sibling, f32[24,2048]{1,0:T(8,128)S(1)} %collective-permute-done.1.refs_0_.plain, bf16[1024,2048]{1,0:T(8,128)(2,1)S(1)} %get-tuple-element.24.refs_0_.high, ...), custom_call_target="tpu_custom_call" | custom-call | flops 2500000000 | bytes 1 | tf_op jit(solution)/shard_map/remap_both/pallas_call | solution.py:105
  25.4 0.0 collective-permute-done.4.near_same.refs_1_
  25.4 0.6 %collective-permute-start.3 = (f32[48,1024]{1,0:T(8,128)S(1)}, f32[48,1024]{1,0:T(8,128)S(1)}, u32[]{:S(2)}, u32[]{:S(2)}) collective-permute-start(f32[48,1024]{1,0:T(8,128)S(1)} %get-tuple-element.29), channel_id=1, source_target_pairs={{0,2},{2,0},{1,3},{3,1},{4,6},{6,4},{5,7},{7,5},{8,10},{10,8},{9,1... | collective-permute-start | bytes 589832 | tf_op jit(solution)/shard_map/ppermute | solution.py:404
  26.0 0.0 collective-permute-done.9.got
  26.0 0.1 collective-permute-start.10
  26.1 1.2 %collective-permute-done.7.other_sub = f32[24,1024]{1,0:T(8,128)S(1)} collective-permute-done((f32[24,1024]{1,0:T(8,128)S(1)}, f32[24,1024]{1,0:T(8,128)S(1)}, u32[]{:S(2)}, u32[]{:S(2)}) %collective-permute-start.7) | collective-permute-done | bytes 98336 | tf_op jit(solution)/shard_map/ppermute | solution.py:401
  27.3 0.0 collective-permute-done.6.same_sub
  27.4 0.0 collective-permute-done.5.near_other
  27.4 2.7 %remap_near.1 = (f32[48,1024]{1,0:T(8,128)S(1)}, f32[48,1024]{1,0:T(8,128)S(1)}) custom-call(f32[24,2048]{1,0:T(8,128)S(1)} %collective-permute-done.4.near_same.refs_1_, f32[24,2048]{1,0:T(8,128)S(1)} %collective-permute-done.5.near_other, f32[24,2048]{1,0:T(8,128)S(1)} %far_rows.1.far, bf16[1024,2048]{1,0:T(8,128)(2,1)S(1)} %get-tuple-element.24.refs_0_.high, ...), custom_call_target="tpu_custom_call" | custom-call | flops 1 | bytes 1 | tf_op jit(solution)/shard_map/remap_near/pallas_call | solution.py:105
  30.1 1.4 %collective-permute-start.8 = (f32[48,1024]{1,0:T(8,128)S(1)}, f32[48,1024]{1,0:T(8,128)S(1)}, u32[]{:S(2)}, u32[]{:S(2)}) collective-permute-start(f32[48,1024]{1,0:T(8,128)S(1)} %get-tuple-element.33), channel_id=1, source_target_pairs={{0,2},{2,0},{1,3},{3,1},{4,6},{6,4},{5,7},{7,5},{8,10},{10,8},{9,1... | collective-permute-start | bytes 589832 | tf_op jit(solution)/shard_map/ppermute | solution.py:404
  31.5 1.7 %collective-permute-done.10.block = f32[24,1024]{1,0:T(8,128)S(1)} collective-permute-done((f32[24,1024]{1,0:T(8,128)S(1)}, f32[24,1024]{1,0:T(8,128)S(1)}, u32[]{:S(2)}, u32[]{:S(2)}) %collective-permute-start.10) | collective-permute-done | bytes 98336 | tf_op jit(solution)/shard_map/ppermute | solution.py:401
  33.2 2.4 %remap_last.1.last = f32[24,512]{1,0:T(8,128)S(1)} custom-call(f32[24,1024]{1,0:T(8,128)S(1)} %collective-permute-done.10.block, bf16[1024,2048]{1,0:T(8,128)(2,1)S(1)} %get-tuple-element.24.refs_0_.high, bf16[1024,2048]{1,0:T(8,128)(2,1)S(1)} %get-tuple-element.25.low, f32[48,1024]{1,0:T(8,128)S(1)} %get-tuple-element.32.refs_0_.one), custom_call_target="tpu_custom_call" | custom-call | flops 10000000000 | bytes 1 | tf_op jit(solution)/shard_map/remap_last/pallas_call | solution.py:105
  35.6 0.9 %collective-permute-start.11 = (f32[24,512]{1,0:T(8,128)S(1)}, f32[24,512]{1,0:T(8,128)S(1)}, u32[]{:S(2)}, u32[]{:S(2)}) collective-permute-start(f32[24,512]{1,0:T(8,128)S(1)} %remap_last.1.last), channel_id=1, source_target_pairs={{0,2},{2,0},{1,3},{3,1},{4,6},{6,4},{5,7},{7,5},{8,10},{10,8},{9,1... | collective-permute-start | bytes 147464 | tf_op jit(solution)/shard_map/ppermute | solution.py:404
  36.5 0.0 collective-permute-done.3.got_chip
  36.5 3.2 %collective-permute-done.11.got_last = f32[24,512]{1,0:T(8,128)S(1)} collective-permute-done((f32[24,512]{1,0:T(8,128)S(1)}, f32[24,512]{1,0:T(8,128)S(1)}, u32[]{:S(2)}, u32[]{:S(2)}) %collective-permute-start.11) | collective-permute-done | bytes 49184 | tf_op jit(solution)/shard_map/ppermute | solution.py:404
  39.7 0.0 collective-permute-done.8.got_one
  39.7 0.8 %finish.1 = f32[96,1024]{1,0:T(8,128)} custom-call(f32[48,1024]{1,0:T(8,128)S(1)} %get-tuple-element.28.refs_0_.chip, f32[48,1024]{1,0:T(8,128)S(1)} %collective-permute-done.3.got_chip, f32[48,1024]{1,0:T(8,128)S(1)} %get-tuple-element.32.refs_0_.one, f32[48,1024]{1,0:T(8,128)S(1)} %collective-permute-done.8.got_one, f32[24,512]{1,0:T(8,128)S(1)} %remap_last.1.last, ...), custom_call_target="tpu_custom_call" | custom-call | flops 1 | bytes 1 | tf_op jit(solution)/shard_map/finish/pallas_call | solution.py:352
  (11 shorter events, 0.1 us)
Async XLA Ops:
  0.0 12.0 %copy-start.3 = (s32[128]{0:T(128)S(1)}, s32[128]{0:T(128)}, u32[]{:S(2)}) copy-start(s32[128]{0:T(128)} %columns.1) | copy-start | bytes 1540
  0.0 12.0 %copy-start.2 = (s32[128]{0:T(128)S(1)}, s32[128]{0:T(128)}, u32[]{:S(2)}) copy-start(s32[128]{0:T(128)} %rows.1) | copy-start | bytes 1540
  0.0 0.7 %copy-start = (s32[8]{0:T(128)S(1)}, s32[8]{0:T(128)}, u32[]{:S(2)}) copy-start(s32[8]{0:T(128)} %step_hour.1) | copy-start | bytes 100
  0.7 11.3 %copy-start.1 = (f32[64,8192]{1,0:T(8,128)S(1)}, f32[64,8192]{1,0:T(8,128)}, u32[]{:S(2)}) copy-start(f32[64,8192]{1,0:T(8,128)} %weights.1) | copy-start | bytes 6291460
  4.1 11.6 %collective-permute-start = (f32[24,2048]{1,0:T(8,128)S(1)}, f32[24,2048]{1,0:T(8,128)S(1)}, u32[]{:S(2)}, u32[]{:S(2)}) collective-permute-start(f32[24,2048]{1,0:T(8,128)S(1)} %get-tuple-element.21), channel_id=1, source_target_pairs={{0,1},{1,0},{4,5},{5,4},{8,9},{9,8},{12,13},{13,12},{2,3},{3,2},{6... | collective-permute-start | bytes 589832 | tf_op jit(solution)/shard_map/ppermute | solution.py:401
  4.6 14.0 %collective-permute-start.1 = (f32[24,2048]{1,0:T(8,128)S(1)}, f32[24,2048]{1,0:T(8,128)S(1)}, u32[]{:S(2)}, u32[]{:S(2)}) collective-permute-start(f32[24,2048]{1,0:T(8,128)S(1)} %get-tuple-element.22), channel_id=1, source_target_pairs={{0,8},{1,9},{4,12},{5,13},{8,0},{9,1},{12,4},{13,5},{2,10},{3,11},... | collective-permute-start | bytes 589832 | tf_op jit(solution)/shard_map/ppermute | solution.py:401
  8.3 17.1 %collective-permute-start.4 = (f32[24,2048]{1,0:T(8,128)S(1)}, f32[24,2048]{1,0:T(8,128)S(1)}, u32[]{:S(2)}, u32[]{:S(2)}) collective-permute-start(f32[24,2048]{1,0:T(8,128)S(1)} %get-tuple-element.30), channel_id=1, source_target_pairs={{0,4},{1,5},{4,0},{5,1},{8,12},{9,13},{12,8},{13,9},{2,6},{3,7},{6... | collective-permute-start | bytes 589832 | tf_op jit(solution)/shard_map/ppermute | solution.py:401
  9.9 17.5 %collective-permute-start.5 = (f32[24,2048]{1,0:T(8,128)S(1)}, f32[24,2048]{1,0:T(8,128)S(1)}, u32[]{:S(2)}, u32[]{:S(2)}) collective-permute-start(f32[24,2048]{1,0:T(8,128)S(1)} %get-tuple-element.31), channel_id=1, source_target_pairs={{0,5},{1,4},{4,1},{5,0},{8,13},{9,12},{12,9},{13,8},{2,7},{3,6},{6... | collective-permute-start | bytes 589832 | tf_op jit(solution)/shard_map/ppermute | solution.py:401
  9.9 7.4 %collective-permute-start.2 = (f32[48,1024]{1,0:T(8,128)S(1)}, f32[48,1024]{1,0:T(8,128)S(1)}, u32[]{:S(2)}, u32[]{:S(2)}) collective-permute-start(f32[48,1024]{1,0:T(8,128)S(1)} %get-tuple-element.23.refs_0_), channel_id=1, source_target_pairs={{0,2},{2,0},{1,3},{3,1},{4,6},{6,4},{5,7},{7,5},{8,10},{10,8},{9,1... | collective-permute-start | bytes 589832 | tf_op jit(solution)/shard_map/ppermute | solution.py:404
  17.2 10.1 %collective-permute-start.6 = (f32[24,1024]{1,0:T(8,128)S(1)}, f32[24,1024]{1,0:T(8,128)S(1)}, u32[]{:S(2)}, u32[]{:S(2)}) collective-permute-start(f32[24,1024]{1,0:T(8,128)S(1)} %merge_first.1.refs_1_), channel_id=1, source_target_pairs={{0,12},{1,13},{4,8},{5,9},{8,4},{9,5},{12,0},{13,1},{2,14},{3,15},... | collective-permute-start | bytes 294920 | tf_op jit(solution)/shard_map/ppermute | solution.py:401
  18.7 7.3 %collective-permute-start.9 = (f32[24,1024]{1,0:T(8,128)S(1)}, f32[24,1024]{1,0:T(8,128)S(1)}, u32[]{:S(2)}, u32[]{:S(2)}) collective-permute-start(f32[24,1024]{1,0:T(8,128)S(1)} %hold.1.refs_0_), channel_id=1, source_target_pairs={{0,2},{2,0},{1,3},{3,1},{4,6},{6,4},{5,7},{7,5},{8,10},{10,8},{9,1... | collective-permute-start | bytes 294920 | tf_op jit(solution)/shard_map/ppermute | solution.py:404
  20.2 7.1 %collective-permute-start.7 = (f32[24,1024]{1,0:T(8,128)S(1)}, f32[24,1024]{1,0:T(8,128)S(1)}, u32[]{:S(2)}, u32[]{:S(2)}) collective-permute-start(f32[24,1024]{1,0:T(8,128)S(1)} %merge_next.1.refs_0_), channel_id=1, source_target_pairs={{0,13},{1,12},{4,9},{5,8},{8,5},{9,4},{12,1},{13,0},{2,15},{3,14},... | collective-permute-start | bytes 294920 | tf_op jit(solution)/shard_map/ppermute | solution.py:401
  25.4 11.1 %collective-permute-start.3 = (f32[48,1024]{1,0:T(8,128)S(1)}, f32[48,1024]{1,0:T(8,128)S(1)}, u32[]{:S(2)}, u32[]{:S(2)}) collective-permute-start(f32[48,1024]{1,0:T(8,128)S(1)} %get-tuple-element.29), channel_id=1, source_target_pairs={{0,2},{2,0},{1,3},{3,1},{4,6},{6,4},{5,7},{7,5},{8,10},{10,8},{9,1... | collective-permute-start | bytes 589832 | tf_op jit(solution)/shard_map/ppermute | solution.py:404
  26.0 7.2 %collective-permute-start.10 = (f32[24,1024]{1,0:T(8,128)S(1)}, f32[24,1024]{1,0:T(8,128)S(1)}, u32[]{:S(2)}, u32[]{:S(2)}) collective-permute-start(f32[24,1024]{1,0:T(8,128)S(1)} %merge_last.1), channel_id=1, source_target_pairs={{0,9},{1,8},{4,13},{5,12},{8,1},{9,0},{12,5},{13,4},{2,11},{3,10},... | collective-permute-start | bytes 294920 | tf_op jit(solution)/shard_map/ppermute | solution.py:401
  30.1 9.6 %collective-permute-start.8 = (f32[48,1024]{1,0:T(8,128)S(1)}, f32[48,1024]{1,0:T(8,128)S(1)}, u32[]{:S(2)}, u32[]{:S(2)}) collective-permute-start(f32[48,1024]{1,0:T(8,128)S(1)} %get-tuple-element.33), channel_id=1, source_target_pairs={{0,2},{2,0},{1,3},{3,1},{4,6},{6,4},{5,7},{7,5},{8,10},{10,8},{9,1... | collective-permute-start | bytes 589832 | tf_op jit(solution)/shard_map/ppermute | solution.py:404
  35.6 4.1 %collective-permute-start.11 = (f32[24,512]{1,0:T(8,128)S(1)}, f32[24,512]{1,0:T(8,128)S(1)}, u32[]{:S(2)}, u32[]{:S(2)}) collective-permute-start(f32[24,512]{1,0:T(8,128)S(1)} %remap_last.1.last), channel_id=1, source_target_pairs={{0,2},{2,0},{1,3},{3,1},{4,6},{6,4},{5,7},{7,5},{8,10},{10,8},{9,1... | collective-permute-start | bytes 147464 | tf_op jit(solution)/shard_map/ppermute | solution.py:404

commit v5 on v4

--- a/solution.py
+++ b/solution.py
@@ -82,7 +82,7 @@
         out_specs=(vmem, vmem),
         scratch_shapes=[pltpu.VMEM((PIXELS_DEV, CELLS_DEV), jnp.float32)],
         compiler_params=pltpu.CompilerParams(vmem_limit_bytes=28 * MIB),
-        cost_estimate=HEAVY,
+        cost_estimate=LIGHT,
         name="place_tiles",
     )(rows, columns, count, weights, *after)
 
@@ -418,14 +418,14 @@
         merge_first_kernel, [mine_0, got_0], [high, sibling], [folded], LIGHT, "merge_first"
     )
     far_same = to_peer(merged[0], *first[0])
+    merged = small_call(merge_next_kernel, [mine_0, got_0], merged, [folded], LIGHT, "merge_next")
+    far_other = to_peer(merged[0], *first[1])
     theirs_1 = small_call(hold_kernel, [theirs_1], [plain_got, *merged], [folded], LIGHT, "hold")[0]
     got_1 = swap(theirs_1)
-    merged = small_call(merge_next_kernel, [mine_0, got_0], [theirs_1], [folded], LIGHT, "merge_next")
-    far_other = to_peer(merged[0], *first[1])
     both, send = remap_call(
         remap_both_kernel,
         [sums[4], sibling, plain_got],
-        merged,
+        [theirs_1],
         [2 * rows] * 2,
         high,
         low,

time: 41 us -> 40.7 us (level)
  Pallas kernels: 15.8 us -> 14.8 us
  waiting for transfers between devices: 7.58 us -> 8.09 us
    ppermute x7, waiting for transfers between devices: 2.92 us -> 4.21 us  [to_peer(): return lax.ppermute(x, ('lev', 'sub'), pairs)]
    pallas_call x1, Pallas kernels: 3.68 us -> 2.79 us  [place_tiles(): pl.pallas_call(place_kernel, out_shape=(half, half), in_specs=[smem, smem...]
    ppermute x5, waiting for transfers between devices: 4.66 us -> 3.88 us  [swap(): return lax.ppermute(x, 'tm', [(0, 1), (1, 0)])]
    ppermute x7, starting transfers between devices: 9.62 us -> 10.1 us  [to_peer(): return lax.ppermute(x, ('lev', 'sub'), pairs)]
  transfers between devices with their start and end apart: 12 -> 12, of which waited for: 4 -> 4; matrix products, arithmetic and copies ran while one was open for 0% -> 0% of each run, Pallas kernels for 29% -> 26%
where the time goes in v5:
time: 40.7 us; the launch traced here: 40.5 us
  starting transfers between devices  16 us (39%)
  Pallas kernels  14.8 us (36%)
  waiting for transfers between devices  8.09 us (20%)
  local copies, waits for them, and re-layouts  0.82 us (2%)
  between operations  0.78 us (2%)
    ppermute x7, starting transfers between devices, to_peer(): return lax.ppermute(x, ('lev', 'sub'), pairs)  10.1 us
    pallas_call x3, Pallas kernels, remap_call(): pl.pallas_call(kernel, out_shape=[jax.ShapeDtypeStruct(rows if isinstance...  7.84 us
    ppermute x5, starting transfers between devices, swap(): return lax.ppermute(x, 'tm', [(0, 1), (1, 0)])  5.89 us
    ppermute x7, waiting for transfers between devices, to_peer(): return lax.ppermute(x, ('lev', 'sub'), pairs)  4.21 us
    ppermute x5, waiting for transfers between devices, swap(): return lax.ppermute(x, 'tm', [(0, 1), (1, 0)])  3.88 us
    pallas_call x1, Pallas kernels, hour_sums(): pl.pallas_call(functools.partial(sums_kernel, plain, first, second), out_...  3.28 us
    pallas_call x1, Pallas kernels, place_tiles(): pl.pallas_call(place_kernel, out_shape=(half, half), in_specs=[smem, smem...  2.79 us
    pallas_call x6, Pallas kernels, small_call(): pl.pallas_call(kernel, out_shape=[jax.ShapeDtypeStruct(shape, jnp.float32...  0.88 us
  transfers between devices with their start and end apart: 12, of which 4 were waited for; matrix products, arithmetic and copies ran while one was open for 0% of the time, Pallas kernels for 26%

profile of v5, /device:TPU:0, one launch (start us, length us, event | category | flops | bytes accessed | tf_op | source)
XLA Modules:
  0.0 40.5 jit_solution(18270319236569316857)
XLA Ops:
  0.0 0.8 %copy-done.1 = s32[8]{0:T(128)S(1)} copy-done((s32[8]{0:T(128)S(1)}, s32[8]{0:T(128)}, u32[]{:S(2)}) %copy-start.1) | copy-done | bytes 56
  0.8 3.3 %hour_sums.1 = (f32[24,2048]{1,0:T(8,128)S(1)}, f32[24,2048]{1,0:T(8,128)S(1)}, f32[24,2048]{1,0:T(8,128)S(1)}, f32[24,2048]{1,0:T(8,128)S(1)}, f32[24,2048]{1,0...) custom-call(s32[8]{0:T(128)S(1)} %copy-done.1, ...), custom_call_target="tpu_custom_call" | custom-call | flops 1 | bytes 1 | tf_op jit(solution)/shard_map/hour_sums/pallas_call | solution.py:305
  4.1 0.5 %collective-permute-start = (f32[24,2048]{1,0:T(8,128)S(1)}, f32[24,2048]{1,0:T(8,128)S(1)}, u32[]{:S(2)}, u32[]{:S(2)}) collective-permute-start(f32[24,2048]{1,0:T(8,128)S(1)} %get-tuple-element.21), channel_id=1, source_target_pairs={{0,1},{1,0},{4,5},{5,4},{8,9},{9,8},{12,13},{13,12},{2,3},{3,2},{6... | collective-permute-start | bytes 589832 | tf_op jit(solution)/shard_map/ppermute | solution.py:401
  4.6 2.6 %collective-permute-start.2 = (f32[48,1024]{1,0:T(8,128)S(1)}, f32[48,1024]{1,0:T(8,128)S(1)}, u32[]{:S(2)}, u32[]{:S(2)}) collective-permute-start(f32[48,1024]{1,0:T(8,128)S(1)} %get-tuple-element.23.refs_0_), channel_id=1, source_target_pairs={{0,2},{2,0},{1,3},{3,1},{4,6},{6,4},{5,7},{7,5},{8,10},{10,8},{9,1... | collective-permute-start | bytes 589832 | tf_op jit(solution)/shard_map/ppermute | solution.py:404
  7.2 2.6 %collective-permute-start.1 = (f32[24,2048]{1,0:T(8,128)S(1)}, f32[24,2048]{1,0:T(8,128)S(1)}, u32[]{:S(2)}, u32[]{:S(2)}) collective-permute-start(f32[24,2048]{1,0:T(8,128)S(1)} %get-tuple-element.22), channel_id=1, source_target_pairs={{0,8},{1,9},{4,12},{5,13},{8,0},{9,1},{12,4},{13,5},{2,10},{3,11},... | collective-permute-start | bytes 589832 | tf_op jit(solution)/shard_map/ppermute | solution.py:401
  9.8 1.6 %collective-permute-start.4 = (f32[24,2048]{1,0:T(8,128)S(1)}, f32[24,2048]{1,0:T(8,128)S(1)}, u32[]{:S(2)}, u32[]{:S(2)}) collective-permute-start(f32[24,2048]{1,0:T(8,128)S(1)} %get-tuple-element.30), channel_id=1, source_target_pairs={{0,4},{1,5},{4,0},{5,1},{8,12},{9,13},{12,8},{13,9},{2,6},{3,7},{6... | collective-permute-start | bytes 589832 | tf_op jit(solution)/shard_map/ppermute | solution.py:401
  11.4 0.0 collective-permute-start.5
  12.0 0.0 copy-done
  12.0 2.8 %place_tiles.1 = (bf16[1024,2048]{1,0:T(8,128)(2,1)S(1)}, bf16[1024,2048]{1,0:T(8,128)(2,1)S(1)}) custom-call(s32[128]{0:T(128)S(1)} %copy-done.2, s32[128]{0:T(128)S(1)} %copy-done.3, s32[1]{0:T(128)S(6)} %copy.7.count, f32[64,8192]{1,0:T(8,128)S(1)} %copy-done, f32[48,1024]{1,0:T(8,128)S(1)} %get-tuple-element.23.refs_0_), custom_call_target="tpu_custom_call" | custom-call | flops 1 | bytes 1 | tf_op jit(solution)/shard_map/place_tiles/pallas_call | solution.py:78
  14.8 0.0 collective-permute-done.refs_1_.sibling
  14.8 0.0 collective-permute-done.2.got
  14.9 1.8 %collective-permute-start.6 = (f32[24,1024]{1,0:T(8,128)S(1)}, f32[24,1024]{1,0:T(8,128)S(1)}, u32[]{:S(2)}, u32[]{:S(2)}) collective-permute-start(f32[24,1024]{1,0:T(8,128)S(1)} %merge_first.1.refs_0_), channel_id=1, source_target_pairs={{0,12},{1,13},{4,8},{5,9},{8,4},{9,5},{12,0},{13,1},{2,14},{3,15},... | collective-permute-start | bytes 294920 | tf_op jit(solution)/shard_map/ppermute | solution.py:401
  16.6 3.6 %collective-permute-start.7 = (f32[24,1024]{1,0:T(8,128)S(1)}, f32[24,1024]{1,0:T(8,128)S(1)}, u32[]{:S(2)}, u32[]{:S(2)}) collective-permute-start(f32[24,1024]{1,0:T(8,128)S(1)} %merge_next.1.refs_1_), channel_id=1, source_target_pairs={{0,13},{1,12},{4,9},{5,8},{8,5},{9,4},{12,1},{13,0},{2,15},{3,14},... | collective-permute-start | bytes 294920 | tf_op jit(solution)/shard_map/ppermute | solution.py:401
  20.3 0.0 collective-permute-done.1.refs_0_.plain
  20.3 0.6 %collective-permute-start.9 = (f32[24,1024]{1,0:T(8,128)S(1)}, f32[24,1024]{1,0:T(8,128)S(1)}, u32[]{:S(2)}, u32[]{:S(2)}) collective-permute-start(f32[24,1024]{1,0:T(8,128)S(1)} %hold.1.refs_0_), channel_id=1, source_target_pairs={{0,2},{2,0},{1,3},{3,1},{4,6},{6,4},{5,7},{7,5},{8,10},{10,8},{9,1... | collective-permute-start | bytes 294920 | tf_op jit(solution)/shard_map/ppermute | solution.py:404
  20.9 2.7 %remap_both.1 = (f32[48,1024]{1,0:T(8,128)S(1)}, f32[48,1024]{1,0:T(8,128)S(1)}) custom-call(f32[24,2048]{1,0:T(8,128)S(1)} %get-tuple-element.20.own, f32[24,2048]{1,0:T(8,128)S(1)} %collective-permute-done.refs_1_.sibling, f32[24,2048]{1,0:T(8,128)S(1)} %collective-permute-done.1.refs_0_.plain, bf16[1024,2048]{1,0:T(8,128)(2,1)S(1)} %get-tuple-element.24.refs_0_.high, ...), custom_call_target="tpu_custom_call" | custom-call | flops 2500000000 | bytes 1 | tf_op jit(solution)/shard_map/remap_both/pallas_call | solution.py:105
  23.6 0.0 collective-permute-done.4.near_same.refs_1_
  23.6 1.6 %collective-permute-start.3 = (f32[48,1024]{1,0:T(8,128)S(1)}, f32[48,1024]{1,0:T(8,128)S(1)}, u32[]{:S(2)}, u32[]{:S(2)}) collective-permute-start(f32[48,1024]{1,0:T(8,128)S(1)} %get-tuple-element.29), channel_id=1, source_target_pairs={{0,2},{2,0},{1,3},{3,1},{4,6},{6,4},{5,7},{7,5},{8,10},{10,8},{9,1... | collective-permute-start | bytes 589832 | tf_op jit(solution)/shard_map/ppermute | solution.py:404
  25.2 0.1 collective-permute-done.9.got
  25.3 0.1 collective-permute-start.10
  25.4 2.7 %collective-permute-done.7.other_sub = f32[24,1024]{1,0:T(8,128)S(1)} collective-permute-done((f32[24,1024]{1,0:T(8,128)S(1)}, f32[24,1024]{1,0:T(8,128)S(1)}, u32[]{:S(2)}, u32[]{:S(2)}) %collective-permute-start.7) | collective-permute-done | bytes 98336 | tf_op jit(solution)/shard_map/ppermute | solution.py:401
  28.0 0.0 collective-permute-done.6.same_sub
  28.1 0.0 collective-permute-done.5.near_other
  28.1 2.7 %remap_near.1 = (f32[48,1024]{1,0:T(8,128)S(1)}, f32[48,1024]{1,0:T(8,128)S(1)}) custom-call(f32[24,2048]{1,0:T(8,128)S(1)} %collective-permute-done.4.near_same.refs_1_, f32[24,2048]{1,0:T(8,128)S(1)} %collective-permute-done.5.near_other, f32[24,2048]{1,0:T(8,128)S(1)} %far_rows.1.far, bf16[1024,2048]{1,0:T(8,128)(2,1)S(1)} %get-tuple-element.24.refs_0_.high, ...), custom_call_target="tpu_custom_call" | custom-call | flops 1 | bytes 1 | tf_op jit(solution)/shard_map/remap_near/pallas_call | solution.py:105
  30.8 0.6 %collective-permute-start.8 = (f32[48,1024]{1,0:T(8,128)S(1)}, f32[48,1024]{1,0:T(8,128)S(1)}, u32[]{:S(2)}, u32[]{:S(2)}) collective-permute-start(f32[48,1024]{1,0:T(8,128)S(1)} %get-tuple-element.33), channel_id=1, source_target_pairs={{0,2},{2,0},{1,3},{3,1},{4,6},{6,4},{5,7},{7,5},{8,10},{10,8},{9,1... | collective-permute-start | bytes 589832 | tf_op jit(solution)/shard_map/ppermute | solution.py:404
  31.4 1.5 %collective-permute-done.10.block = f32[24,1024]{1,0:T(8,128)S(1)} collective-permute-done((f32[24,1024]{1,0:T(8,128)S(1)}, f32[24,1024]{1,0:T(8,128)S(1)}, u32[]{:S(2)}, u32[]{:S(2)}) %collective-permute-start.10) | collective-permute-done | bytes 98336 | tf_op jit(solution)/shard_map/ppermute | solution.py:401
  33.0 2.4 %remap_last.1.last = f32[24,512]{1,0:T(8,128)S(1)} custom-call(f32[24,1024]{1,0:T(8,128)S(1)} %collective-permute-done.10.block, bf16[1024,2048]{1,0:T(8,128)(2,1)S(1)} %get-tuple-element.24.refs_0_.high, bf16[1024,2048]{1,0:T(8,128)(2,1)S(1)} %get-tuple-element.25.low, f32[48,1024]{1,0:T(8,128)S(1)} %get-tuple-element.32.refs_0_.one), custom_call_target="tpu_custom_call" | custom-call | flops 10000000000 | bytes 1 | tf_op jit(solution)/shard_map/remap_last/pallas_call | solution.py:105
  35.3 0.6 %collective-permute-start.11 = (f32[24,512]{1,0:T(8,128)S(1)}, f32[24,512]{1,0:T(8,128)S(1)}, u32[]{:S(2)}, u32[]{:S(2)}) collective-permute-start(f32[24,512]{1,0:T(8,128)S(1)} %remap_last.1.last), channel_id=1, source_target_pairs={{0,2},{2,0},{1,3},{3,1},{4,6},{6,4},{5,7},{7,5},{8,10},{10,8},{9,1... | collective-permute-start | bytes 147464 | tf_op jit(solution)/shard_map/ppermute | solution.py:404
  35.9 0.0 collective-permute-done.3.got_chip
  35.9 3.8 %collective-permute-done.11.got_last = f32[24,512]{1,0:T(8,128)S(1)} collective-permute-done((f32[24,512]{1,0:T(8,128)S(1)}, f32[24,512]{1,0:T(8,128)S(1)}, u32[]{:S(2)}, u32[]{:S(2)}) %collective-permute-start.11) | collective-permute-done | bytes 49184 | tf_op jit(solution)/shard_map/ppermute | solution.py:404
  39.7 0.0 collective-permute-done.8.got_one
  39.7 0.8 %finish.1 = f32[96,1024]{1,0:T(8,128)} custom-call(f32[48,1024]{1,0:T(8,128)S(1)} %get-tuple-element.28.refs_0_.chip, f32[48,1024]{1,0:T(8,128)S(1)} %collective-permute-done.3.got_chip, f32[48,1024]{1,0:T(8,128)S(1)} %get-tuple-element.32.refs_0_.one, f32[48,1024]{1,0:T(8,128)S(1)} %collective-permute-done.8.got_one, f32[24,512]{1,0:T(8,128)S(1)} %remap_last.1.last, ...), custom_call_target="tpu_custom_call" | custom-call | flops 1 | bytes 1 | tf_op jit(solution)/shard_map/finish/pallas_call | solution.py:352
  (11 shorter events, 0.1 us)
Async XLA Ops:
  0.0 12.0 %copy-start = (f32[64,8192]{1,0:T(8,128)S(1)}, f32[64,8192]{1,0:T(8,128)}, u32[]{:S(2)}) copy-start(f32[64,8192]{1,0:T(8,128)} %weights.1) | copy-start | bytes 6291460
  0.0 0.8 %copy-start.1 = (s32[8]{0:T(128)S(1)}, s32[8]{0:T(128)}, u32[]{:S(2)}) copy-start(s32[8]{0:T(128)} %step_hour.1) | copy-start | bytes 100
  0.8 11.2 %copy-start.2 = (s32[128]{0:T(128)S(1)}, s32[128]{0:T(128)}, u32[]{:S(2)}) copy-start(s32[128]{0:T(128)} %rows.1) | copy-start | bytes 1540
  0.8 11.2 %copy-start.3 = (s32[128]{0:T(128)S(1)}, s32[128]{0:T(128)}, u32[]{:S(2)}) copy-start(s32[128]{0:T(128)} %columns.1) | copy-start | bytes 1540
  4.1 10.7 %collective-permute-start = (f32[24,2048]{1,0:T(8,128)S(1)}, f32[24,2048]{1,0:T(8,128)S(1)}, u32[]{:S(2)}, u32[]{:S(2)}) collective-permute-start(f32[24,2048]{1,0:T(8,128)S(1)} %get-tuple-element.21), channel_id=1, source_target_pairs={{0,1},{1,0},{4,5},{5,4},{8,9},{9,8},{12,13},{13,12},{2,3},{3,2},{6... | collective-permute-start | bytes 589832 | tf_op jit(solution)/shard_map/ppermute | solution.py:401
  4.6 10.2 %collective-permute-start.2 = (f32[48,1024]{1,0:T(8,128)S(1)}, f32[48,1024]{1,0:T(8,128)S(1)}, u32[]{:S(2)}, u32[]{:S(2)}) collective-permute-start(f32[48,1024]{1,0:T(8,128)S(1)} %get-tuple-element.23.refs_0_), channel_id=1, source_target_pairs={{0,2},{2,0},{1,3},{3,1},{4,6},{6,4},{5,7},{7,5},{8,10},{10,8},{9,1... | collective-permute-start | bytes 589832 | tf_op jit(solution)/shard_map/ppermute | solution.py:404
  7.2 13.1 %collective-permute-start.1 = (f32[24,2048]{1,0:T(8,128)S(1)}, f32[24,2048]{1,0:T(8,128)S(1)}, u32[]{:S(2)}, u32[]{:S(2)}) collective-permute-start(f32[24,2048]{1,0:T(8,128)S(1)} %get-tuple-element.22), channel_id=1, source_target_pairs={{0,8},{1,9},{4,12},{5,13},{8,0},{9,1},{12,4},{13,5},{2,10},{3,11},... | collective-permute-start | bytes 589832 | tf_op jit(solution)/shard_map/ppermute | solution.py:401
  9.8 13.9 %collective-permute-start.4 = (f32[24,2048]{1,0:T(8,128)S(1)}, f32[24,2048]{1,0:T(8,128)S(1)}, u32[]{:S(2)}, u32[]{:S(2)}) collective-permute-start(f32[24,2048]{1,0:T(8,128)S(1)} %get-tuple-element.30), channel_id=1, source_target_pairs={{0,4},{1,5},{4,0},{5,1},{8,12},{9,13},{12,8},{13,9},{2,6},{3,7},{6... | collective-permute-start | bytes 589832 | tf_op jit(solution)/shard_map/ppermute | solution.py:401
  11.4 16.7 %collective-permute-start.5 = (f32[24,2048]{1,0:T(8,128)S(1)}, f32[24,2048]{1,0:T(8,128)S(1)}, u32[]{:S(2)}, u32[]{:S(2)}) collective-permute-start(f32[24,2048]{1,0:T(8,128)S(1)} %get-tuple-element.31), channel_id=1, source_target_pairs={{0,5},{1,4},{4,1},{5,0},{8,13},{9,12},{12,9},{13,8},{2,7},{3,6},{6... | collective-permute-start | bytes 589832 | tf_op jit(solution)/shard_map/ppermute | solution.py:401
  14.9 13.2 %collective-permute-start.6 = (f32[24,1024]{1,0:T(8,128)S(1)}, f32[24,1024]{1,0:T(8,128)S(1)}, u32[]{:S(2)}, u32[]{:S(2)}) collective-permute-start(f32[24,1024]{1,0:T(8,128)S(1)} %merge_first.1.refs_0_), channel_id=1, source_target_pairs={{0,12},{1,13},{4,8},{5,9},{8,4},{9,5},{12,0},{13,1},{2,14},{3,15},... | collective-permute-start | bytes 294920 | tf_op jit(solution)/shard_map/ppermute | solution.py:401
  16.6 11.4 %collective-permute-start.7 = (f32[24,1024]{1,0:T(8,128)S(1)}, f32[24,1024]{1,0:T(8,128)S(1)}, u32[]{:S(2)}, u32[]{:S(2)}) collective-permute-start(f32[24,1024]{1,0:T(8,128)S(1)} %merge_next.1.refs_1_), channel_id=1, source_target_pairs={{0,13},{1,12},{4,9},{5,8},{8,5},{9,4},{12,1},{13,0},{2,15},{3,14},... | collective-permute-start | bytes 294920 | tf_op jit(solution)/shard_map/ppermute | solution.py:401
  20.3 5.0 %collective-permute-start.9 = (f32[24,1024]{1,0:T(8,128)S(1)}, f32[24,1024]{1,0:T(8,128)S(1)}, u32[]{:S(2)}, u32[]{:S(2)}) collective-permute-start(f32[24,1024]{1,0:T(8,128)S(1)} %hold.1.refs_0_), channel_id=1, source_target_pairs={{0,2},{2,0},{1,3},{3,1},{4,6},{6,4},{5,7},{7,5},{8,10},{10,8},{9,1... | collective-permute-start | bytes 294920 | tf_op jit(solution)/shard_map/ppermute | solution.py:404
  23.6 12.3 %collective-permute-start.3 = (f32[48,1024]{1,0:T(8,128)S(1)}, f32[48,1024]{1,0:T(8,128)S(1)}, u32[]{:S(2)}, u32[]{:S(2)}) collective-permute-start(f32[48,1024]{1,0:T(8,128)S(1)} %get-tuple-element.29), channel_id=1, source_target_pairs={{0,2},{2,0},{1,3},{3,1},{4,6},{6,4},{5,7},{7,5},{8,10},{10,8},{9,1... | collective-permute-start | bytes 589832 | tf_op jit(solution)/shard_map/ppermute | solution.py:404
  25.3 7.7 %collective-permute-start.10 = (f32[24,1024]{1,0:T(8,128)S(1)}, f32[24,1024]{1,0:T(8,128)S(1)}, u32[]{:S(2)}, u32[]{:S(2)}) collective-permute-start(f32[24,1024]{1,0:T(8,128)S(1)} %merge_last.1), channel_id=1, source_target_pairs={{0,9},{1,8},{4,13},{5,12},{8,1},{9,0},{12,5},{13,4},{2,11},{3,10},... | collective-permute-start | bytes 294920 | tf_op jit(solution)/shard_map/ppermute | solution.py:401
  30.8 8.9 %collective-permute-start.8 = (f32[48,1024]{1,0:T(8,128)S(1)}, f32[48,1024]{1,0:T(8,128)S(1)}, u32[]{:S(2)}, u32[]{:S(2)}) collective-permute-start(f32[48,1024]{1,0:T(8,128)S(1)} %get-tuple-element.33), channel_id=1, source_target_pairs={{0,2},{2,0},{1,3},{3,1},{4,6},{6,4},{5,7},{7,5},{8,10},{10,8},{9,1... | collective-permute-start | bytes 589832 | tf_op jit(solution)/shard_map/ppermute | solution.py:404
  35.3 4.4 %collective-permute-start.11 = (f32[24,512]{1,0:T(8,128)S(1)}, f32[24,512]{1,0:T(8,128)S(1)}, u32[]{:S(2)}, u32[]{:S(2)}) collective-permute-start(f32[24,512]{1,0:T(8,128)S(1)} %remap_last.1.last), channel_id=1, source_target_pairs={{0,2},{2,0},{1,3},{3,1},{4,6},{6,4},{5,7},{7,5},{8,10},{10,8},{9,1... | collective-permute-start | bytes 147464 | tf_op jit(solution)/shard_map/ppermute | solution.py:404

commit v6 on v5

--- a/solution.py
+++ b/solution.py
@@ -400,6 +400,10 @@
         pairs = [(a * subs + b, (a ^ k) * subs + (b ^ j)) for a in range(levs) for b in range(subs)]
         return lax.ppermute(x, ("lev", "sub"), pairs)
 
+    def hand_over(x):
+        pairs = [(a * shards_tm + a // half, a * shards_tm + 1 - a // half) for a in range(levs)]
+        return lax.ppermute(x, ("lev", "tm"), pairs)
+
     def swap(x):
         return lax.ppermute(x, "tm", [(0, 1), (1, 0)])
 
@@ -463,7 +467,7 @@
         "remap_last",
         [padded],
     )
-    got_last = swap(last)
+    got_last = hand_over(last)
     out = finish([both, got_both, one, got_one, last, got_last], rows // 2, divisor)
     return out.reshape(HOURS, out.shape[0] // HOURS, PIXELS_DEV)
 

time: 40.7 us -> 40.5 us (level)
  waiting for transfers between devices: 8.09 us -> 7.31 us
  Pallas kernels: 14.8 us -> 15.3 us
    ppermute x5 -> x4, waiting for transfers between devices: 3.88 us -> 0.01 us  [swap(): return lax.ppermute(x, 'tm', [(0, 1), (1, 0)])]
    ppermute x0 -> x1, starting transfers between devices: none -> 2.45 us  [hand_over(): return lax.ppermute(x, ('lev', 'tm'), pairs)]
    ppermute x7, starting transfers between devices: 10.1 us -> 8.34 us  [to_peer(): return lax.ppermute(x, ('lev', 'sub'), pairs)]
    ppermute x0 -> x1, waiting for transfers between devices: none -> 1.72 us  [hand_over(): return lax.ppermute(x, ('lev', 'tm'), pairs)]
    ppermute x7, waiting for transfers between devices: 4.21 us -> 5.58 us  [to_peer(): return lax.ppermute(x, ('lev', 'sub'), pairs)]
    ppermute x5 -> x4, starting transfers between devices: 5.89 us -> 5.33 us  [swap(): return lax.ppermute(x, 'tm', [(0, 1), (1, 0)])]
    pallas_call x1, Pallas kernels: 2.79 us -> 3.3 us  [place_tiles(): pl.pallas_call(place_kernel, out_shape=(half, half), in_specs=[smem, smem...]
  transfers between devices with their start and end apart: 12 -> 12, of which waited for: 4 -> 4; matrix products, arithmetic and copies ran while one was open for 0% -> 0% of each run, Pallas kernels for 26% -> 28%
where the time goes in v6:
time: 40.5 us; the launch traced here: 40.3 us
  starting transfers between devices  16.1 us (40%)
  Pallas kernels  15.3 us (38%)
  waiting for transfers between devices  7.31 us (18%)
  local copies, waits for them, and re-layouts  0.82 us (2%)
  between operations  0.79 us (2%)
    ppermute x7, starting transfers between devices, to_peer(): return lax.ppermute(x, ('lev', 'sub'), pairs)  8.34 us
    pallas_call x3, Pallas kernels, remap_call(): pl.pallas_call(kernel, out_shape=[jax.ShapeDtypeStruct(rows if isinstance...  7.83 us
    ppermute x7, waiting for transfers between devices, to_peer(): return lax.ppermute(x, ('lev', 'sub'), pairs)  5.58 us
    ppermute x4, starting transfers between devices, swap(): return lax.ppermute(x, 'tm', [(0, 1), (1, 0)])  5.33 us
    pallas_call x1, Pallas kernels, place_tiles(): pl.pallas_call(place_kernel, out_shape=(half, half), in_specs=[smem, smem...  3.3 us
    pallas_call x1, Pallas kernels, hour_sums(): pl.pallas_call(functools.partial(sums_kernel, plain, first, second), out_...  3.28 us
    ppermute x1, starting transfers between devices, hand_over(): return lax.ppermute(x, ('lev', 'tm'), pairs)  2.45 us
    ppermute x1, waiting for transfers between devices, hand_over(): return lax.ppermute(x, ('lev', 'tm'), pairs)  1.72 us
  transfers between devices with their start and end apart: 12, of which 4 were waited for; matrix products, arithmetic and copies ran while one was open for 0% of the time, Pallas kernels for 28%

profile of v6, /device:TPU:0, one launch (start us, length us, event | category | flops | bytes accessed | tf_op | source)
XLA Modules:
  0.0 40.3 jit_solution(2642474950576341965)
XLA Ops:
  0.0 0.8 %copy-done.1 = s32[8]{0:T(128)S(1)} copy-done((s32[8]{0:T(128)S(1)}, s32[8]{0:T(128)}, u32[]{:S(2)}) %copy-start.1) | copy-done | bytes 56
  0.8 3.3 %hour_sums.1 = (f32[24,2048]{1,0:T(8,128)S(1)}, f32[24,2048]{1,0:T(8,128)S(1)}, f32[24,2048]{1,0:T(8,128)S(1)}, f32[24,2048]{1,0:T(8,128)S(1)}, f32[24,2048]{1,0...) custom-call(s32[8]{0:T(128)S(1)} %copy-done.1, ...), custom_call_target="tpu_custom_call" | custom-call | flops 1 | bytes 1 | tf_op jit(solution)/shard_map/hour_sums/pallas_call | solution.py:305
  4.1 0.5 %collective-permute-start = (f32[24,2048]{1,0:T(8,128)S(1)}, f32[24,2048]{1,0:T(8,128)S(1)}, u32[]{:S(2)}, u32[]{:S(2)}) collective-permute-start(f32[24,2048]{1,0:T(8,128)S(1)} %get-tuple-element.21), channel_id=1, source_target_pairs={{0,1},{1,0},{4,5},{5,4},{8,9},{9,8},{12,13},{13,12},{2,3},{3,2},{6... | collective-permute-start | bytes 589832 | tf_op jit(solution)/shard_map/ppermute | solution.py:401
  4.6 2.6 %collective-permute-start.2 = (f32[48,1024]{1,0:T(8,128)S(1)}, f32[48,1024]{1,0:T(8,128)S(1)}, u32[]{:S(2)}, u32[]{:S(2)}) collective-permute-start(f32[48,1024]{1,0:T(8,128)S(1)} %get-tuple-element.23.refs_0_), channel_id=1, source_target_pairs={{0,2},{2,0},{1,3},{3,1},{4,6},{6,4},{5,7},{7,5},{8,10},{10,8},{9,1... | collective-permute-start | bytes 589832 | tf_op jit(solution)/shard_map/ppermute | solution.py:408
  7.2 2.6 %collective-permute-start.1 = (f32[24,2048]{1,0:T(8,128)S(1)}, f32[24,2048]{1,0:T(8,128)S(1)}, u32[]{:S(2)}, u32[]{:S(2)}) collective-permute-start(f32[24,2048]{1,0:T(8,128)S(1)} %get-tuple-element.22), channel_id=1, source_target_pairs={{0,8},{1,9},{4,12},{5,13},{8,0},{9,1},{12,4},{13,5},{2,10},{3,11},... | collective-permute-start | bytes 589832 | tf_op jit(solution)/shard_map/ppermute | solution.py:401
  9.8 1.6 %collective-permute-start.4 = (f32[24,2048]{1,0:T(8,128)S(1)}, f32[24,2048]{1,0:T(8,128)S(1)}, u32[]{:S(2)}, u32[]{:S(2)}) collective-permute-start(f32[24,2048]{1,0:T(8,128)S(1)} %get-tuple-element.30), channel_id=1, source_target_pairs={{0,4},{1,5},{4,0},{5,1},{8,12},{9,13},{12,8},{13,9},{2,6},{3,7},{6... | collective-permute-start | bytes 589832 | tf_op jit(solution)/shard_map/ppermute | solution.py:401
  11.4 0.0 collective-permute-start.5
  12.0 0.0 copy-done
  12.0 3.3 %place_tiles.1 = (bf16[1024,2048]{1,0:T(8,128)(2,1)S(1)}, bf16[1024,2048]{1,0:T(8,128)(2,1)S(1)}) custom-call(s32[128]{0:T(128)S(1)} %copy-done.2, s32[128]{0:T(128)S(1)} %copy-done.3, s32[1]{0:T(128)S(6)} %copy.7.count, f32[64,8192]{1,0:T(8,128)S(1)} %copy-done, f32[48,1024]{1,0:T(8,128)S(1)} %get-tuple-element.23.refs_0_), custom_call_target="tpu_custom_call" | custom-call | flops 1 | bytes 1 | tf_op jit(solution)/shard_map/place_tiles/pallas_call | solution.py:78
  15.3 0.0 collective-permute-done.refs_1_.sibling
  15.4 0.0 collective-permute-done.2.got
  15.4 1.6 %collective-permute-start.6 = (f32[24,1024]{1,0:T(8,128)S(1)}, f32[24,1024]{1,0:T(8,128)S(1)}, u32[]{:S(2)}, u32[]{:S(2)}) collective-permute-start(f32[24,1024]{1,0:T(8,128)S(1)} %merge_first.1.refs_0_), channel_id=1, source_target_pairs={{0,12},{1,13},{4,8},{5,9},{8,4},{9,5},{12,0},{13,1},{2,14},{3,15},... | collective-permute-start | bytes 294920 | tf_op jit(solution)/shard_map/ppermute | solution.py:401
  17.0 2.0 %collective-permute-start.7 = (f32[24,1024]{1,0:T(8,128)S(1)}, f32[24,1024]{1,0:T(8,128)S(1)}, u32[]{:S(2)}, u32[]{:S(2)}) collective-permute-start(f32[24,1024]{1,0:T(8,128)S(1)} %merge_next.1.refs_1_), channel_id=1, source_target_pairs={{0,13},{1,12},{4,9},{5,8},{8,5},{9,4},{12,1},{13,0},{2,15},{3,14},... | collective-permute-start | bytes 294920 | tf_op jit(solution)/shard_map/ppermute | solution.py:401
  19.0 0.4 collective-permute-done.1.refs_0_.plain
  19.4 0.6 %collective-permute-start.9 = (f32[24,1024]{1,0:T(8,128)S(1)}, f32[24,1024]{1,0:T(8,128)S(1)}, u32[]{:S(2)}, u32[]{:S(2)}) collective-permute-start(f32[24,1024]{1,0:T(8,128)S(1)} %hold.1.refs_0_), channel_id=1, source_target_pairs={{0,2},{2,0},{1,3},{3,1},{4,6},{6,4},{5,7},{7,5},{8,10},{10,8},{9,1... | collective-permute-start | bytes 294920 | tf_op jit(solution)/shard_map/ppermute | solution.py:408
  19.9 2.7 %remap_both.1 = (f32[48,1024]{1,0:T(8,128)S(1)}, f32[48,1024]{1,0:T(8,128)S(1)}) custom-call(f32[24,2048]{1,0:T(8,128)S(1)} %get-tuple-element.20.own, f32[24,2048]{1,0:T(8,128)S(1)} %collective-permute-done.refs_1_.sibling, f32[24,2048]{1,0:T(8,128)S(1)} %collective-permute-done.1.refs_0_.plain, bf16[1024,2048]{1,0:T(8,128)(2,1)S(1)} %get-tuple-element.24.refs_0_.high, ...), custom_call_target="tpu_custom_call" | custom-call | flops 2500000000 | bytes 1 | tf_op jit(solution)/shard_map/remap_both/pallas_call | solution.py:105
  22.7 0.0 collective-permute-done.4.near_same.refs_1_
  22.7 1.6 %collective-permute-start.3 = (f32[48,1024]{1,0:T(8,128)S(1)}, f32[48,1024]{1,0:T(8,128)S(1)}, u32[]{:S(2)}, u32[]{:S(2)}) collective-permute-start(f32[48,1024]{1,0:T(8,128)S(1)} %get-tuple-element.29), channel_id=1, source_target_pairs={{0,2},{2,0},{1,3},{3,1},{4,6},{6,4},{5,7},{7,5},{8,10},{10,8},{9,1... | collective-permute-start | bytes 589832 | tf_op jit(solution)/shard_map/ppermute | solution.py:408
  24.3 0.0 collective-permute-done.9.got
  24.3 0.1 collective-permute-start.10
  24.4 3.6 %collective-permute-done.7.other_sub = f32[24,1024]{1,0:T(8,128)S(1)} collective-permute-done((f32[24,1024]{1,0:T(8,128)S(1)}, f32[24,1024]{1,0:T(8,128)S(1)}, u32[]{:S(2)}, u32[]{:S(2)}) %collective-permute-start.7) | collective-permute-done | bytes 98336 | tf_op jit(solution)/shard_map/ppermute | solution.py:401
  28.0 0.0 collective-permute-done.6.same_sub
  28.0 0.0 collective-permute-done.5.near_other
  28.0 2.7 %remap_near.1 = (f32[48,1024]{1,0:T(8,128)S(1)}, f32[48,1024]{1,0:T(8,128)S(1)}) custom-call(f32[24,2048]{1,0:T(8,128)S(1)} %collective-permute-done.4.near_same.refs_1_, f32[24,2048]{1,0:T(8,128)S(1)} %collective-permute-done.5.near_other, f32[24,2048]{1,0:T(8,128)S(1)} %far_rows.1.far, bf16[1024,2048]{1,0:T(8,128)(2,1)S(1)} %get-tuple-element.24.refs_0_.high, ...), custom_call_target="tpu_custom_call" | custom-call | flops 1 | bytes 1 | tf_op jit(solution)/shard_map/remap_near/pallas_call | solution.py:105
  30.8 0.6 %collective-permute-start.8 = (f32[48,1024]{1,0:T(8,128)S(1)}, f32[48,1024]{1,0:T(8,128)S(1)}, u32[]{:S(2)}, u32[]{:S(2)}) collective-permute-start(f32[48,1024]{1,0:T(8,128)S(1)} %get-tuple-element.33), channel_id=1, source_target_pairs={{0,2},{2,0},{1,3},{3,1},{4,6},{6,4},{5,7},{7,5},{8,10},{10,8},{9,1... | collective-permute-start | bytes 589832 | tf_op jit(solution)/shard_map/ppermute | solution.py:408
  31.4 1.6 %collective-permute-done.10.block = f32[24,1024]{1,0:T(8,128)S(1)} collective-permute-done((f32[24,1024]{1,0:T(8,128)S(1)}, f32[24,1024]{1,0:T(8,128)S(1)}, u32[]{:S(2)}, u32[]{:S(2)}) %collective-permute-start.10) | collective-permute-done | bytes 98336 | tf_op jit(solution)/shard_map/ppermute | solution.py:401
  33.0 2.4 %remap_last.1.last = f32[24,512]{1,0:T(8,128)S(1)} custom-call(f32[24,1024]{1,0:T(8,128)S(1)} %collective-permute-done.10.block, bf16[1024,2048]{1,0:T(8,128)(2,1)S(1)} %get-tuple-element.24.refs_0_.high, bf16[1024,2048]{1,0:T(8,128)(2,1)S(1)} %get-tuple-element.25.low, f32[48,1024]{1,0:T(8,128)S(1)} %get-tuple-element.32.refs_0_.one), custom_call_target="tpu_custom_call" | custom-call | flops 10000000000 | bytes 1 | tf_op jit(solution)/shard_map/remap_last/pallas_call | solution.py:105
  35.3 2.4 %collective-permute-start.11 = (f32[24,512]{1,0:T(8,128)S(1)}, f32[24,512]{1,0:T(8,128)S(1)}, u32[]{:S(2)}, u32[]{:S(2)}) collective-permute-start(f32[24,512]{1,0:T(8,128)S(1)} %remap_last.1.last), channel_id=1, source_target_pairs={{0,2},{4,6},{10,8},{14,12},{1,3},{5,7},{11,9},{15,13},{16,18},{20,... | collective-permute-start | bytes 147464 | tf_op jit(solution)/shard_map/ppermute | solution.py:405
  37.8 0.0 collective-permute-done.3.got_chip
  37.8 1.7 %collective-permute-done.11.got_last = f32[24,512]{1,0:T(8,128)S(1)} collective-permute-done((f32[24,512]{1,0:T(8,128)S(1)}, f32[24,512]{1,0:T(8,128)S(1)}, u32[]{:S(2)}, u32[]{:S(2)}) %collective-permute-start.11) | collective-permute-done | bytes 49184 | tf_op jit(solution)/shard_map/ppermute | solution.py:405
  39.5 0.0 collective-permute-done.8.got_one
  39.5 0.8 %finish.1 = f32[96,1024]{1,0:T(8,128)} custom-call(f32[48,1024]{1,0:T(8,128)S(1)} %get-tuple-element.28.refs_0_.chip, f32[48,1024]{1,0:T(8,128)S(1)} %collective-permute-done.3.got_chip, f32[48,1024]{1,0:T(8,128)S(1)} %get-tuple-element.32.refs_0_.one, f32[48,1024]{1,0:T(8,128)S(1)} %collective-permute-done.8.got_one, f32[24,512]{1,0:T(8,128)S(1)} %remap_last.1.last, ...), custom_call_target="tpu_custom_call" | custom-call | flops 1 | bytes 1 | tf_op jit(solution)/shard_map/finish/pallas_call | solution.py:352
  (11 shorter events, 0.1 us)
Async XLA Ops:
  0.0 12.0 %copy-start = (f32[64,8192]{1,0:T(8,128)S(1)}, f32[64,8192]{1,0:T(8,128)}, u32[]{:S(2)}) copy-start(f32[64,8192]{1,0:T(8,128)} %weights.1) | copy-start | bytes 6291460
  0.0 0.8 %copy-start.1 = (s32[8]{0:T(128)S(1)}, s32[8]{0:T(128)}, u32[]{:S(2)}) copy-start(s32[8]{0:T(128)} %step_hour.1) | copy-start | bytes 100
  0.8 11.2 %copy-start.2 = (s32[128]{0:T(128)S(1)}, s32[128]{0:T(128)}, u32[]{:S(2)}) copy-start(s32[128]{0:T(128)} %rows.1) | copy-start | bytes 1540
  0.8 11.2 %copy-start.3 = (s32[128]{0:T(128)S(1)}, s32[128]{0:T(128)}, u32[]{:S(2)}) copy-start(s32[128]{0:T(128)} %columns.1) | copy-start | bytes 1540
  4.1 11.2 %collective-permute-start = (f32[24,2048]{1,0:T(8,128)S(1)}, f32[24,2048]{1,0:T(8,128)S(1)}, u32[]{:S(2)}, u32[]{:S(2)}) collective-permute-start(f32[24,2048]{1,0:T(8,128)S(1)} %get-tuple-element.21), channel_id=1, source_target_pairs={{0,1},{1,0},{4,5},{5,4},{8,9},{9,8},{12,13},{13,12},{2,3},{3,2},{6... | collective-permute-start | bytes 589832 | tf_op jit(solution)/shard_map/ppermute | solution.py:401
  4.6 10.7 %collective-permute-start.2 = (f32[48,1024]{1,0:T(8,128)S(1)}, f32[48,1024]{1,0:T(8,128)S(1)}, u32[]{:S(2)}, u32[]{:S(2)}) collective-permute-start(f32[48,1024]{1,0:T(8,128)S(1)} %get-tuple-element.23.refs_0_), channel_id=1, source_target_pairs={{0,2},{2,0},{1,3},{3,1},{4,6},{6,4},{5,7},{7,5},{8,10},{10,8},{9,1... | collective-permute-start | bytes 589832 | tf_op jit(solution)/shard_map/ppermute | solution.py:408
  7.2 12.2 %collective-permute-start.1 = (f32[24,2048]{1,0:T(8,128)S(1)}, f32[24,2048]{1,0:T(8,128)S(1)}, u32[]{:S(2)}, u32[]{:S(2)}) collective-permute-start(f32[24,2048]{1,0:T(8,128)S(1)} %get-tuple-element.22), channel_id=1, source_target_pairs={{0,8},{1,9},{4,12},{5,13},{8,0},{9,1},{12,4},{13,5},{2,10},{3,11},... | collective-permute-start | bytes 589832 | tf_op jit(solution)/shard_map/ppermute | solution.py:401
  9.8 12.9 %collective-permute-start.4 = (f32[24,2048]{1,0:T(8,128)S(1)}, f32[24,2048]{1,0:T(8,128)S(1)}, u32[]{:S(2)}, u32[]{:S(2)}) collective-permute-start(f32[24,2048]{1,0:T(8,128)S(1)} %get-tuple-element.30), channel_id=1, source_target_pairs={{0,4},{1,5},{4,0},{5,1},{8,12},{9,13},{12,8},{13,9},{2,6},{3,7},{6... | collective-permute-start | bytes 589832 | tf_op jit(solution)/shard_map/ppermute | solution.py:401
  11.4 16.7 %collective-permute-start.5 = (f32[24,2048]{1,0:T(8,128)S(1)}, f32[24,2048]{1,0:T(8,128)S(1)}, u32[]{:S(2)}, u32[]{:S(2)}) collective-permute-start(f32[24,2048]{1,0:T(8,128)S(1)} %get-tuple-element.31), channel_id=1, source_target_pairs={{0,5},{1,4},{4,1},{5,0},{8,13},{9,12},{12,9},{13,8},{2,7},{3,6},{6... | collective-permute-start | bytes 589832 | tf_op jit(solution)/shard_map/ppermute | solution.py:401
  15.4 12.6 %collective-permute-start.6 = (f32[24,1024]{1,0:T(8,128)S(1)}, f32[24,1024]{1,0:T(8,128)S(1)}, u32[]{:S(2)}, u32[]{:S(2)}) collective-permute-start(f32[24,1024]{1,0:T(8,128)S(1)} %merge_first.1.refs_0_), channel_id=1, source_target_pairs={{0,12},{1,13},{4,8},{5,9},{8,4},{9,5},{12,0},{13,1},{2,14},{3,15},... | collective-permute-start | bytes 294920 | tf_op jit(solution)/shard_map/ppermute | solution.py:401
  17.0 11.0 %collective-permute-start.7 = (f32[24,1024]{1,0:T(8,128)S(1)}, f32[24,1024]{1,0:T(8,128)S(1)}, u32[]{:S(2)}, u32[]{:S(2)}) collective-permute-start(f32[24,1024]{1,0:T(8,128)S(1)} %merge_next.1.refs_1_), channel_id=1, source_target_pairs={{0,13},{1,12},{4,9},{5,8},{8,5},{9,4},{12,1},{13,0},{2,15},{3,14},... | collective-permute-start | bytes 294920 | tf_op jit(solution)/shard_map/ppermute | solution.py:401
  19.4 4.9 %collective-permute-start.9 = (f32[24,1024]{1,0:T(8,128)S(1)}, f32[24,1024]{1,0:T(8,128)S(1)}, u32[]{:S(2)}, u32[]{:S(2)}) collective-permute-start(f32[24,1024]{1,0:T(8,128)S(1)} %hold.1.refs_0_), channel_id=1, source_target_pairs={{0,2},{2,0},{1,3},{3,1},{4,6},{6,4},{5,7},{7,5},{8,10},{10,8},{9,1... | collective-permute-start | bytes 294920 | tf_op jit(solution)/shard_map/ppermute | solution.py:408
  22.7 15.1 %collective-permute-start.3 = (f32[48,1024]{1,0:T(8,128)S(1)}, f32[48,1024]{1,0:T(8,128)S(1)}, u32[]{:S(2)}, u32[]{:S(2)}) collective-permute-start(f32[48,1024]{1,0:T(8,128)S(1)} %get-tuple-element.29), channel_id=1, source_target_pairs={{0,2},{2,0},{1,3},{3,1},{4,6},{6,4},{5,7},{7,5},{8,10},{10,8},{9,1... | collective-permute-start | bytes 589832 | tf_op jit(solution)/shard_map/ppermute | solution.py:408
  24.3 8.7 %collective-permute-start.10 = (f32[24,1024]{1,0:T(8,128)S(1)}, f32[24,1024]{1,0:T(8,128)S(1)}, u32[]{:S(2)}, u32[]{:S(2)}) collective-permute-start(f32[24,1024]{1,0:T(8,128)S(1)} %merge_last.1), channel_id=1, source_target_pairs={{0,9},{1,8},{4,13},{5,12},{8,1},{9,0},{12,5},{13,4},{2,11},{3,10},... | collective-permute-start | bytes 294920 | tf_op jit(solution)/shard_map/ppermute | solution.py:401
  30.8 8.8 %collective-permute-start.8 = (f32[48,1024]{1,0:T(8,128)S(1)}, f32[48,1024]{1,0:T(8,128)S(1)}, u32[]{:S(2)}, u32[]{:S(2)}) collective-permute-start(f32[48,1024]{1,0:T(8,128)S(1)} %get-tuple-element.33), channel_id=1, source_target_pairs={{0,2},{2,0},{1,3},{3,1},{4,6},{6,4},{5,7},{7,5},{8,10},{10,8},{9,1... | collective-permute-start | bytes 589832 | tf_op jit(solution)/shard_map/ppermute | solution.py:408
  35.3 4.2 %collective-permute-start.11 = (f32[24,512]{1,0:T(8,128)S(1)}, f32[24,512]{1,0:T(8,128)S(1)}, u32[]{:S(2)}, u32[]{:S(2)}) collective-permute-start(f32[24,512]{1,0:T(8,128)S(1)} %remap_last.1.last), channel_id=1, source_target_pairs={{0,2},{4,6},{10,8},{14,12},{1,3},{5,7},{11,9},{15,13},{16,18},{20,... | collective-permute-start | bytes 147464 | tf_op jit(solution)/shard_map/ppermute | solution.py:405

commit v7 on v6

--- a/solution.py
+++ b/solution.py
@@ -360,34 +360,70 @@
     )(*inputs, *after)
 
 
-def finish_kernel(divisor, levels, chip, got_chip, one, got_one, last, got_last, out):
-    me, lev, even = lax.axis_index("tm"), lax.axis_index("lev") % 2, lax.axis_index("sub") == 0
+def output_rows(same_lev, hour, levels):
+    lev = lax.axis_index("lev") % 2
+    start = hour * 2 + (lev if same_lev else 1 - lev)
+    return pl.ds(pl.multiple_of(start * 2 * levels, 2 * levels), 2 * levels)
+
+
+def write_first_kernel(divisor, levels, chip, got_chip, one, got_one, out):
+    me = lax.axis_index("tm")
     rows = 2 * levels
     near = keeps_near()
     for hour in range(HOURS):
-        same_at = pl.ds(pl.multiple_of((hour * 2 + lev) * rows, rows), rows)
-        other_at = pl.ds(pl.multiple_of((hour * 2 + 1 - lev) * rows, rows), rows)
+        here = slice(hour * rows, (hour + 1) * rows)
 
         @pl.when(near)
         def _():
-            here = slice(hour * rows, (hour + 1) * rows)
-            out[same_at, :] = (chip[here] + got_chip[here]) / divisor
-            out[other_at, :] = (one[here] + got_one[here]) / divisor
+            out[output_rows(True, hour, levels), :] = (chip[here] + got_chip[here]) / divisor
+            out[output_rows(False, hour, levels), :] = (one[here] + got_one[here]) / divisor
 
         @pl.when(jnp.logical_not(near))
         def _():
+            out[output_rows(False, hour, levels), :] = jnp.where(me == hour, one[:rows], got_one[:rows]) / divisor
+
+
+def write_last_kernel(divisor, levels, plain, got_plain, last, got_last, begun, out, stage, written):
+    me, even = lax.axis_index("tm"), lax.axis_index("sub") == 0
+
+    @pl.when(jnp.logical_not(keeps_near()))
+    def _():
+        copies = []
+        for hour in range(HOURS):
             here = slice(hour * levels, (hour + 1) * levels)
-            plain = chip[here] + got_chip[here]
+            first = plain[here] + got_plain[here]
             other = unfold(jnp.where(me == hour, last[...], got_last[...]))
-            pair = [jnp.where(even, plain, other), jnp.where(even, other, plain)]
-            out[same_at, :] = jnp.concatenate(pair, axis=0) / divisor
-            out[other_at, :] = jnp.where(me == hour, one[:rows], got_one[:rows]) / divisor
-
-
-def finish(arrays, levels, divisor):
-    call = functools.partial(finish_kernel, divisor, levels)
+            pair = [jnp.where(even, first, other), jnp.where(even, other, first)]
+            stage[hour] = jnp.concatenate(pair, axis=0) / divisor
+            target = out.at[output_rows(True, hour, levels), :]
+            copies.append(pltpu.make_async_copy(stage.at[hour], target, written.at[hour]))
+            copies[-1].start()
+        for copy in copies:
+            copy.wait()
+
+
+def write_first(arrays, levels, divisor):
+    kernel = functools.partial(write_first_kernel, divisor, levels)
     shape = (2 * arrays[0].shape[0], PIXELS_DEV)
-    return small_call(call, arrays, [], [shape], LIGHT, "finish")[0]
+    return small_call(kernel, arrays, [], [shape], LIGHT, "write_first")[0]
+
+
+def write_last(begun, arrays, levels, divisor):
+    vmem, anywhere = pl.BlockSpec(memory_space=pltpu.VMEM), pl.BlockSpec(memory_space=pl.ANY)
+    return pl.pallas_call(
+        functools.partial(write_last_kernel, divisor, levels),
+        out_shape=jax.ShapeDtypeStruct(begun.shape, begun.dtype),
+        in_specs=[vmem] * len(arrays) + [anywhere],
+        out_specs=anywhere,
+        scratch_shapes=[
+            pltpu.VMEM((HOURS, 2 * levels, PIXELS_DEV), jnp.float32),
+            pltpu.SemaphoreType.DMA((HOURS,)),
+        ],
+        input_output_aliases={len(arrays): 0},
+        compiler_params=pltpu.CompilerParams(vmem_limit_bytes=8 * MIB),
+        cost_estimate=LIGHT,
+        name="write_last",
+    )(*arrays, begun)
 
 
 def hour_plan(level_field, tile_weight, tile_rows, tile_columns, live_count, step_hour):
@@ -468,7 +504,9 @@
         [padded],
     )
     got_last = hand_over(last)
-    out = finish([both, got_both, one, got_one, last, got_last], rows // 2, divisor)
+    levels = rows // 2
+    out = write_first([both, got_both, one, got_one], levels, divisor)
+    out = write_last(out, [both, got_both, last, got_last], levels, divisor)
     return out.reshape(HOURS, out.shape[0] // HOURS, PIXELS_DEV)
 
 

time: 40.5 us -> 39.8 us (0.983)
  starting transfers between devices: 16.1 us -> 15.1 us
  Pallas kernels: 15.3 us -> 16.3 us
  waiting for transfers between devices: 7.31 us -> 6.48 us
    ppermute x1, waiting for transfers between devices: 1.72 us -> 0.11 us  [hand_over(): return lax.ppermute(x, ('lev', 'tm'), pairs)]
    ppermute x4, waiting for transfers between devices: 0.01 us -> 1.48 us  [swap(): return lax.ppermute(x, 'tm', [(0, 1), (1, 0)])]
    pallas_call x1, Pallas kernels: 3.3 us -> 4.33 us  [place_tiles(): pl.pallas_call(place_kernel, out_shape=(half, half), in_specs=[smem, smem...]
    ppermute x7, starting transfers between devices: 8.34 us -> 7.31 us  [to_peer(): return lax.ppermute(x, ('lev', 'sub'), pairs)]
    ppermute x7, waiting for transfers between devices: 5.58 us -> 4.89 us  [to_peer(): return lax.ppermute(x, ('lev', 'sub'), pairs)]
  transfers between devices with their start and end apart: 12 -> 12, of which waited for: 4 -> 6; matrix products, arithmetic and copies ran while one was open for 0% -> 0% of each run, Pallas kernels for 28% -> 33%
where the time goes in v7:
time: 39.8 us; the launch traced here: 39.5 us
  Pallas kernels  16.3 us (41%)
  starting transfers between devices  15.1 us (38%)
  waiting for transfers between devices  6.48 us (16%)
  local copies, waits for them, and re-layouts  0.82 us (2%)
  between operations  0.79 us (2%)
    pallas_call x3, Pallas kernels, remap_call(): pl.pallas_call(kernel, out_shape=[jax.ShapeDtypeStruct(rows if isinstance...  7.83 us
    ppermute x7, starting transfers between devices, to_peer(): return lax.ppermute(x, ('lev', 'sub'), pairs)  7.31 us
    ppermute x4, starting transfers between devices, swap(): return lax.ppermute(x, 'tm', [(0, 1), (1, 0)])  5.33 us
    ppermute x7, waiting for transfers between devices, to_peer(): return lax.ppermute(x, ('lev', 'sub'), pairs)  4.89 us
    pallas_call x1, Pallas kernels, place_tiles(): pl.pallas_call(place_kernel, out_shape=(half, half), in_specs=[smem, smem...  4.33 us
    pallas_call x1, Pallas kernels, hour_sums(): pl.pallas_call(functools.partial(sums_kernel, plain, first, second), out_...  3.28 us
    ppermute x1, starting transfers between devices, hand_over(): return lax.ppermute(x, ('lev', 'tm'), pairs)  2.45 us
    ppermute x4, waiting for transfers between devices, swap(): return lax.ppermute(x, 'tm', [(0, 1), (1, 0)])  1.48 us
  transfers between devices with their start and end apart: 12, of which 6 were waited for; matrix products, arithmetic and copies ran while one was open for 0% of the time, Pallas kernels for 33%

profile of v7, /device:TPU:0, one launch (start us, length us, event | category | flops | bytes accessed | tf_op | source)
XLA Modules:
  0.0 39.5 jit_solution(15998024813954569365)
XLA Ops:
  0.0 0.8 %copy-done.1 = s32[8]{0:T(128)S(1)} copy-done((s32[8]{0:T(128)S(1)}, s32[8]{0:T(128)}, u32[]{:S(2)}) %copy-start.1) | copy-done | bytes 56
  0.8 3.3 %hour_sums.1 = (f32[24,2048]{1,0:T(8,128)S(1)}, f32[24,2048]{1,0:T(8,128)S(1)}, f32[24,2048]{1,0:T(8,128)S(1)}, f32[24,2048]{1,0:T(8,128)S(1)}, f32[24,2048]{1,0...) custom-call(s32[8]{0:T(128)S(1)} %copy-done.1, ...), custom_call_target="tpu_custom_call" | custom-call | flops 1 | bytes 1 | tf_op jit(solution)/shard_map/hour_sums/pallas_call | solution.py:305
  4.1 0.5 %collective-permute-start = (f32[24,2048]{1,0:T(8,128)S(1)}, f32[24,2048]{1,0:T(8,128)S(1)}, u32[]{:S(2)}, u32[]{:S(2)}) collective-permute-start(f32[24,2048]{1,0:T(8,128)S(1)} %get-tuple-element.21), channel_id=1, source_target_pairs={{0,1},{1,0},{4,5},{5,4},{8,9},{9,8},{12,13},{13,12},{2,3},{3,2},{6... | collective-permute-start | bytes 589832 | tf_op jit(solution)/shard_map/ppermute | solution.py:437
  4.6 2.6 %collective-permute-start.2 = (f32[48,1024]{1,0:T(8,128)S(1)}, f32[48,1024]{1,0:T(8,128)S(1)}, u32[]{:S(2)}, u32[]{:S(2)}) collective-permute-start(f32[48,1024]{1,0:T(8,128)S(1)} %get-tuple-element.23.refs_0_), channel_id=1, source_target_pairs={{0,2},{2,0},{1,3},{3,1},{4,6},{6,4},{5,7},{7,5},{8,10},{10,8},{9,1... | collective-permute-start | bytes 589832 | tf_op jit(solution)/shard_map/ppermute | solution.py:444
  7.2 2.6 %collective-permute-start.1 = (f32[24,2048]{1,0:T(8,128)S(1)}, f32[24,2048]{1,0:T(8,128)S(1)}, u32[]{:S(2)}, u32[]{:S(2)}) collective-permute-start(f32[24,2048]{1,0:T(8,128)S(1)} %get-tuple-element.22), channel_id=1, source_target_pairs={{0,8},{1,9},{4,12},{5,13},{8,0},{9,1},{12,4},{13,5},{2,10},{3,11},... | collective-permute-start | bytes 589832 | tf_op jit(solution)/shard_map/ppermute | solution.py:437
  9.8 1.6 %collective-permute-start.5 = (f32[24,2048]{1,0:T(8,128)S(1)}, f32[24,2048]{1,0:T(8,128)S(1)}, u32[]{:S(2)}, u32[]{:S(2)}) collective-permute-start(f32[24,2048]{1,0:T(8,128)S(1)} %get-tuple-element.31), channel_id=1, source_target_pairs={{0,4},{1,5},{4,0},{5,1},{8,12},{9,13},{12,8},{13,9},{2,6},{3,7},{6... | collective-permute-start | bytes 589832 | tf_op jit(solution)/shard_map/ppermute | solution.py:437
  11.4 0.0 collective-permute-start.7
  12.0 0.0 copy-done
  12.0 4.3 %place_tiles.1 = (bf16[1024,2048]{1,0:T(8,128)(2,1)S(1)}, bf16[1024,2048]{1,0:T(8,128)(2,1)S(1)}) custom-call(s32[128]{0:T(128)S(1)} %copy-done.2, s32[128]{0:T(128)S(1)} %copy-done.3, s32[1]{0:T(128)S(6)} %copy.9.count, f32[64,8192]{1,0:T(8,128)S(1)} %copy-done, f32[48,1024]{1,0:T(8,128)S(1)} %get-tuple-element.23.refs_0_), custom_call_target="tpu_custom_call" | custom-call | flops 1 | bytes 1 | tf_op jit(solution)/shard_map/place_tiles/pallas_call | solution.py:78
  16.4 0.0 collective-permute-done.refs_1_.sibling
  16.4 0.0 collective-permute-done.2.got
  16.4 0.2 collective-permute-start.8
  16.6 2.3 %collective-permute-start.9 = (f32[24,1024]{1,0:T(8,128)S(1)}, f32[24,1024]{1,0:T(8,128)S(1)}, u32[]{:S(2)}, u32[]{:S(2)}) collective-permute-start(f32[24,1024]{1,0:T(8,128)S(1)} %merge_next.1.refs_1_), channel_id=1, source_target_pairs={{0,13},{1,12},{4,9},{5,8},{8,5},{9,4},{12,1},{13,0},{2,15},{3,14},... | collective-permute-start | bytes 294920 | tf_op jit(solution)/shard_map/ppermute | solution.py:437
  19.0 0.4 collective-permute-done.1.refs_0_.plain
  19.4 0.6 %collective-permute-start.4 = (f32[24,1024]{1,0:T(8,128)S(1)}, f32[24,1024]{1,0:T(8,128)S(1)}, u32[]{:S(2)}, u32[]{:S(2)}) collective-permute-start(f32[24,1024]{1,0:T(8,128)S(1)} %hold.1.refs_0_), channel_id=1, source_target_pairs={{0,2},{2,0},{1,3},{3,1},{4,6},{6,4},{5,7},{7,5},{8,10},{10,8},{9,1... | collective-permute-start | bytes 294920 | tf_op jit(solution)/shard_map/ppermute | solution.py:444
  19.9 2.7 %remap_both.1 = (f32[48,1024]{1,0:T(8,128)S(1)}, f32[48,1024]{1,0:T(8,128)S(1)}) custom-call(f32[24,2048]{1,0:T(8,128)S(1)} %get-tuple-element.20.own, f32[24,2048]{1,0:T(8,128)S(1)} %collective-permute-done.refs_1_.sibling, f32[24,2048]{1,0:T(8,128)S(1)} %collective-permute-done.1.refs_0_.plain, bf16[1024,2048]{1,0:T(8,128)(2,1)S(1)} %get-tuple-element.24.refs_0_.high, ...), custom_call_target="tpu_custom_call" | custom-call | flops 2500000000 | bytes 1 | tf_op jit(solution)/shard_map/remap_both/pallas_call | solution.py:105
  22.7 0.0 collective-permute-done.5.refs_1_.near_same
  22.7 1.6 %collective-permute-start.3 = (f32[48,1024]{1,0:T(8,128)S(1)}, f32[48,1024]{1,0:T(8,128)S(1)}, u32[]{:S(2)}, u32[]{:S(2)}) collective-permute-start(f32[48,1024]{1,0:T(8,128)S(1)} %get-tuple-element.29), channel_id=1, source_target_pairs={{0,2},{2,0},{1,3},{3,1},{4,6},{6,4},{5,7},{7,5},{8,10},{10,8},{9,1... | collective-permute-start | bytes 589832 | tf_op jit(solution)/shard_map/ppermute | solution.py:444
  24.3 0.7 %collective-permute-done.4.got = f32[24,1024]{1,0:T(8,128)S(1)} collective-permute-done((f32[24,1024]{1,0:T(8,128)S(1)}, f32[24,1024]{1,0:T(8,128)S(1)}, u32[]{:S(2)}, u32[]{:S(2)}) %collective-permute-start.4) | collective-permute-done | bytes 98336 | tf_op jit(solution)/shard_map/ppermute | solution.py:444
  25.0 0.1 collective-permute-start.6
  25.1 2.9 %collective-permute-done.9.other_sub = f32[24,1024]{1,0:T(8,128)S(1)} collective-permute-done((f32[24,1024]{1,0:T(8,128)S(1)}, f32[24,1024]{1,0:T(8,128)S(1)}, u32[]{:S(2)}, u32[]{:S(2)}) %collective-permute-start.9) | collective-permute-done | bytes 98336 | tf_op jit(solution)/shard_map/ppermute | solution.py:437
  28.0 0.0 collective-permute-done.8.same_sub
  28.0 0.0 collective-permute-done.7.near_other
  28.0 2.7 %remap_near.1 = (f32[48,1024]{1,0:T(8,128)S(1)}, f32[48,1024]{1,0:T(8,128)S(1)}) custom-call(f32[24,2048]{1,0:T(8,128)S(1)} %collective-permute-done.5.refs_1_.near_same, f32[24,2048]{1,0:T(8,128)S(1)} %collective-permute-done.7.near_other, f32[24,2048]{1,0:T(8,128)S(1)} %far_rows.1.far, bf16[1024,2048]{1,0:T(8,128)(2,1)S(1)} %get-tuple-element.24.refs_0_.high, ...), custom_call_target="tpu_custom_call" | custom-call | flops 1 | bytes 1 | tf_op jit(solution)/shard_map/remap_near/pallas_call | solution.py:105
  30.8 0.6 %collective-permute-start.11 = (f32[48,1024]{1,0:T(8,128)S(1)}, f32[48,1024]{1,0:T(8,128)S(1)}, u32[]{:S(2)}, u32[]{:S(2)}) collective-permute-start(f32[48,1024]{1,0:T(8,128)S(1)} %get-tuple-element.34), channel_id=1, source_target_pairs={{0,2},{2,0},{1,3},{3,1},{4,6},{6,4},{5,7},{7,5},{8,10},{10,8},{9,1... | collective-permute-start | bytes 589832 | tf_op jit(solution)/shard_map/ppermute | solution.py:444
  31.4 1.6 %collective-permute-done.6.block = f32[24,1024]{1,0:T(8,128)S(1)} collective-permute-done((f32[24,1024]{1,0:T(8,128)S(1)}, f32[24,1024]{1,0:T(8,128)S(1)}, u32[]{:S(2)}, u32[]{:S(2)}) %collective-permute-start.6) | collective-permute-done | bytes 98336 | tf_op jit(solution)/shard_map/ppermute | solution.py:437
  32.9 2.4 %remap_last.1.last = f32[24,512]{1,0:T(8,128)S(1)} custom-call(f32[24,1024]{1,0:T(8,128)S(1)} %collective-permute-done.6.block, bf16[1024,2048]{1,0:T(8,128)(2,1)S(1)} %get-tuple-element.24.refs_0_.high, bf16[1024,2048]{1,0:T(8,128)(2,1)S(1)} %get-tuple-element.25.low, f32[48,1024]{1,0:T(8,128)S(1)} %get-tuple-element.33.refs_0_.one), custom_call_target="tpu_custom_call" | custom-call | flops 10000000000 | bytes 1 | tf_op jit(solution)/shard_map/remap_last/pallas_call | solution.py:105
  35.3 2.4 %collective-permute-start.10 = (f32[24,512]{1,0:T(8,128)S(1)}, f32[24,512]{1,0:T(8,128)S(1)}, u32[]{:S(2)}, u32[]{:S(2)}) collective-permute-start(f32[24,512]{1,0:T(8,128)S(1)} %remap_last.1.last), channel_id=1, source_target_pairs={{0,2},{4,6},{10,8},{14,12},{1,3},{5,7},{11,9},{15,13},{16,18},{20,... | collective-permute-start | bytes 147464 | tf_op jit(solution)/shard_map/ppermute | solution.py:441
  37.8 0.0 collective-permute-done.3.got_chip.got_plain
  37.8 0.8 %collective-permute-done.11.got_one = f32[48,1024]{1,0:T(8,128)S(1)} collective-permute-done((f32[48,1024]{1,0:T(8,128)S(1)}, f32[48,1024]{1,0:T(8,128)S(1)}, u32[]{:S(2)}, u32[]{:S(2)}) %collective-permute-start.11) | collective-permute-done | bytes 196640 | tf_op jit(solution)/shard_map/ppermute | solution.py:444
  38.6 0.8 %write_first.1.begun = f32[96,1024]{1,0:T(8,128)} custom-call(f32[48,1024]{1,0:T(8,128)S(1)} %get-tuple-element.28.refs_0_.chip.plain, f32[48,1024]{1,0:T(8,128)S(1)} %collective-permute-done.3.got_chip.got_plain, f32[48,1024]{1,0:T(8,128)S(1)} %get-tuple-element.33.refs_0_.one, f32[48,1024]{1,0:T(8,128)S(1)} %collective-permute-done.11.got_one), custom_call_target="tpu_custom_call" | custom-call | flops 1 | bytes 1 | tf_op jit(solution)/shard_map/write_first/pallas_call | solution.py:352
  39.4 0.1 collective-permute-done.10.got_last
  (12 shorter events, 0.1 us)
Async XLA Ops:
  0.0 12.0 %copy-start = (f32[64,8192]{1,0:T(8,128)S(1)}, f32[64,8192]{1,0:T(8,128)}, u32[]{:S(2)}) copy-start(f32[64,8192]{1,0:T(8,128)} %weights.1) | copy-start | bytes 6291460
  0.0 0.8 %copy-start.1 = (s32[8]{0:T(128)S(1)}, s32[8]{0:T(128)}, u32[]{:S(2)}) copy-start(s32[8]{0:T(128)} %step_hour.1) | copy-start | bytes 100
  0.8 11.2 %copy-start.2 = (s32[128]{0:T(128)S(1)}, s32[128]{0:T(128)}, u32[]{:S(2)}) copy-start(s32[128]{0:T(128)} %rows.1) | copy-start | bytes 1540
  0.8 11.2 %copy-start.3 = (s32[128]{0:T(128)S(1)}, s32[128]{0:T(128)}, u32[]{:S(2)}) copy-start(s32[128]{0:T(128)} %columns.1) | copy-start | bytes 1540
  4.1 12.3 %collective-permute-start = (f32[24,2048]{1,0:T(8,128)S(1)}, f32[24,2048]{1,0:T(8,128)S(1)}, u32[]{:S(2)}, u32[]{:S(2)}) collective-permute-start(f32[24,2048]{1,0:T(8,128)S(1)} %get-tuple-element.21), channel_id=1, source_target_pairs={{0,1},{1,0},{4,5},{5,4},{8,9},{9,8},{12,13},{13,12},{2,3},{3,2},{6... | collective-permute-start | bytes 589832 | tf_op jit(solution)/shard_map/ppermute | solution.py:437
  4.6 11.8 %collective-permute-start.2 = (f32[48,1024]{1,0:T(8,128)S(1)}, f32[48,1024]{1,0:T(8,128)S(1)}, u32[]{:S(2)}, u32[]{:S(2)}) collective-permute-start(f32[48,1024]{1,0:T(8,128)S(1)} %get-tuple-element.23.refs_0_), channel_id=1, source_target_pairs={{0,2},{2,0},{1,3},{3,1},{4,6},{6,4},{5,7},{7,5},{8,10},{10,8},{9,1... | collective-permute-start | bytes 589832 | tf_op jit(solution)/shard_map/ppermute | solution.py:444
  7.2 12.2 %collective-permute-start.1 = (f32[24,2048]{1,0:T(8,128)S(1)}, f32[24,2048]{1,0:T(8,128)S(1)}, u32[]{:S(2)}, u32[]{:S(2)}) collective-permute-start(f32[24,2048]{1,0:T(8,128)S(1)} %get-tuple-element.22), channel_id=1, source_target_pairs={{0,8},{1,9},{4,12},{5,13},{8,0},{9,1},{12,4},{13,5},{2,10},{3,11},... | collective-permute-start | bytes 589832 | tf_op jit(solution)/shard_map/ppermute | solution.py:437
  9.8 12.9 %collective-permute-start.5 = (f32[24,2048]{1,0:T(8,128)S(1)}, f32[24,2048]{1,0:T(8,128)S(1)}, u32[]{:S(2)}, u32[]{:S(2)}) collective-permute-start(f32[24,2048]{1,0:T(8,128)S(1)} %get-tuple-element.31), channel_id=1, source_target_pairs={{0,4},{1,5},{4,0},{5,1},{8,12},{9,13},{12,8},{13,9},{2,6},{3,7},{6... | collective-permute-start | bytes 589832 | tf_op jit(solution)/shard_map/ppermute | solution.py:437
  11.4 16.7 %collective-permute-start.7 = (f32[24,2048]{1,0:T(8,128)S(1)}, f32[24,2048]{1,0:T(8,128)S(1)}, u32[]{:S(2)}, u32[]{:S(2)}) collective-permute-start(f32[24,2048]{1,0:T(8,128)S(1)} %get-tuple-element.32), channel_id=1, source_target_pairs={{0,5},{1,4},{4,1},{5,0},{8,13},{9,12},{12,9},{13,8},{2,7},{3,6},{6... | collective-permute-start | bytes 589832 | tf_op jit(solution)/shard_map/ppermute | solution.py:437
  16.4 11.6 %collective-permute-start.8 = (f32[24,1024]{1,0:T(8,128)S(1)}, f32[24,1024]{1,0:T(8,128)S(1)}, u32[]{:S(2)}, u32[]{:S(2)}) collective-permute-start(f32[24,1024]{1,0:T(8,128)S(1)} %merge_first.1.refs_0_), channel_id=1, source_target_pairs={{0,12},{1,13},{4,8},{5,9},{8,4},{9,5},{12,0},{13,1},{2,14},{3,15},... | collective-permute-start | bytes 294920 | tf_op jit(solution)/shard_map/ppermute | solution.py:437
  16.6 11.3 %collective-permute-start.9 = (f32[24,1024]{1,0:T(8,128)S(1)}, f32[24,1024]{1,0:T(8,128)S(1)}, u32[]{:S(2)}, u32[]{:S(2)}) collective-permute-start(f32[24,1024]{1,0:T(8,128)S(1)} %merge_next.1.refs_1_), channel_id=1, source_target_pairs={{0,13},{1,12},{4,9},{5,8},{8,5},{9,4},{12,1},{13,0},{2,15},{3,14},... | collective-permute-start | bytes 294920 | tf_op jit(solution)/shard_map/ppermute | solution.py:437
  19.4 5.6 %collective-permute-start.4 = (f32[24,1024]{1,0:T(8,128)S(1)}, f32[24,1024]{1,0:T(8,128)S(1)}, u32[]{:S(2)}, u32[]{:S(2)}) collective-permute-start(f32[24,1024]{1,0:T(8,128)S(1)} %hold.1.refs_0_), channel_id=1, source_target_pairs={{0,2},{2,0},{1,3},{3,1},{4,6},{6,4},{5,7},{7,5},{8,10},{10,8},{9,1... | collective-permute-start | bytes 294920 | tf_op jit(solution)/shard_map/ppermute | solution.py:444
  22.7 15.1 %collective-permute-start.3 = (f32[48,1024]{1,0:T(8,128)S(1)}, f32[48,1024]{1,0:T(8,128)S(1)}, u32[]{:S(2)}, u32[]{:S(2)}) collective-permute-start(f32[48,1024]{1,0:T(8,128)S(1)} %get-tuple-element.29), channel_id=1, source_target_pairs={{0,2},{2,0},{1,3},{3,1},{4,6},{6,4},{5,7},{7,5},{8,10},{10,8},{9,1... | collective-permute-start | bytes 589832 | tf_op jit(solution)/shard_map/ppermute | solution.py:444
  25.0 8.0 %collective-permute-start.6 = (f32[24,1024]{1,0:T(8,128)S(1)}, f32[24,1024]{1,0:T(8,128)S(1)}, u32[]{:S(2)}, u32[]{:S(2)}) collective-permute-start(f32[24,1024]{1,0:T(8,128)S(1)} %merge_last.1), channel_id=1, source_target_pairs={{0,9},{1,8},{4,13},{5,12},{8,1},{9,0},{12,5},{13,4},{2,11},{3,10},... | collective-permute-start | bytes 294920 | tf_op jit(solution)/shard_map/ppermute | solution.py:437
  30.8 7.8 %collective-permute-start.11 = (f32[48,1024]{1,0:T(8,128)S(1)}, f32[48,1024]{1,0:T(8,128)S(1)}, u32[]{:S(2)}, u32[]{:S(2)}) collective-permute-start(f32[48,1024]{1,0:T(8,128)S(1)} %get-tuple-element.34), channel_id=1, source_target_pairs={{0,2},{2,0},{1,3},{3,1},{4,6},{6,4},{5,7},{7,5},{8,10},{10,8},{9,1... | collective-permute-start | bytes 589832 | tf_op jit(solution)/shard_map/ppermute | solution.py:444
  35.3 4.2 %collective-permute-start.10 = (f32[24,512]{1,0:T(8,128)S(1)}, f32[24,512]{1,0:T(8,128)S(1)}, u32[]{:S(2)}, u32[]{:S(2)}) collective-permute-start(f32[24,512]{1,0:T(8,128)S(1)} %remap_last.1.last), channel_id=1, source_target_pairs={{0,2},{4,6},{10,8},{14,12},{1,3},{5,7},{11,9},{15,13},{16,18},{20,... | collective-permute-start | bytes 147464 | tf_op jit(solution)/shard_map/ppermute | solution.py:441

commit v8 on v7

--- a/solution.py
+++ b/solution.py
@@ -90,14 +90,14 @@
 PIXEL_BLOCK = 256
 
 
-def remap_blocks(x, high, low):
+def remap_blocks(x, high, low, cells=slice(None)):
     m = x.shape[0]
     x_high, x_low = split(x)
     both = jnp.concatenate([x_high, x_low], axis=0)
     for start in range(0, PIXELS_DEV, PIXEL_BLOCK):
         at = slice(start, start + PIXEL_BLOCK)
-        first = dot(both, high[at, :], NT)
-        yield at, first[:m] + first[m:] + dot(x_high, low[at, :], NT)
+        first = dot(both, high[at, cells], NT)
+        yield at, first[:m] + first[m:] + dot(x_high, low[at, cells], NT)
 
 
 def remap_call(kernel, inputs, after, out_rows, high, low, cost, name, scratch_rows=()):
@@ -181,14 +181,23 @@
     sort_out(near_result, far_result, keep, send)
 
 
-def remap_last_kernel(block, high, low, *refs):
-    out, total = refs[-2:]
+def remap_half(place, block, high, low):
     x = unfold(block[...])
     levels, cells = x.shape
     x = jnp.concatenate([x, jnp.zeros((-levels % 16, cells), jnp.float32)], axis=0)
-    for at, result in remap_blocks(x, high, low):
-        total[:, at] = result
-    out[...] = fold(total[:levels])
+    yield from remap_blocks(x, high, low, slice(place * cells, (place + 1) * cells))
+
+
+def remap_early_kernel(block, high, low, *refs):
+    for at, result in remap_half(0, block, high, low):
+        refs[-1][:, at] = result
+
+
+def remap_last_kernel(block, early, high, low, *refs):
+    out, total = refs[-2:]
+    for at, result in remap_half(1, block, high, low):
+        total[:, at] = result + early[:, at]
+    out[...] = fold(total[: out.shape[0] // 2])
 
 
 def hour_weights(step_hour, steps, hours, width):
@@ -330,13 +339,17 @@
     refs[-1][...] = mine[rows:] + got[rows:]
 
 
-def merge_last_kernel(mine, got, *refs):
-    refs[-1][...] = mine[...] + got[...]
-
-
 def fold(x):
     half = x.shape[1] // 2
     return jnp.concatenate([x[:, :half], x[:, half:]], axis=0)
+
+
+def merge_last_kernel(mine, got, *refs):
+    outs = refs[-2:]
+    levels = mine.shape[0] // 2
+    total = mine[...] + got[...]
+    for place, out in enumerate(outs):
+        out[...] = fold(total[place * levels : (place + 1) * levels])
 
 
 def hold_kernel(x, *refs):
@@ -474,10 +487,12 @@
         [2 * rows] * 2,
     )
     got_both = swap(send)
+    quarter = (folded[0], folded[1] // 2)
     merged = small_call(
-        merge_last_kernel, [mine_1, got_1], [both, near_got[0]], [folded], HEAVY, "merge_last"
-    )
-    second_got = to_peer(merged[0], *second)
+        merge_last_kernel, [mine_1, got_1], [both, *near_got], [quarter] * 2, HEAVY, "merge_last"
+    )
+    late = small_call(hold_kernel, [merged[1]], [merged[0]], [quarter], LIGHT, "hold")
+    second_got = [to_peer(x, *second) for x in (merged[0], late[0])]
     far = small_call(far_rows_kernel, [far_same, far_other], [], [(rows, CELLS_DEV)], HEAVY, "far_rows")[0]
     one, send = remap_call(
         remap_near_kernel,
@@ -492,10 +507,13 @@
     )
     got_one = swap(send)
     padded = -(-rows // 32) * 16
+    (early,) = remap_call(
+        remap_early_kernel, second_got[:1], [one, got_both], [padded], high, low, LIGHT, "remap_early"
+    )
     (last,) = remap_call(
         remap_last_kernel,
-        [second_got],
-        [one],
+        [second_got[1], early],
+        [],
         [(rows, PIXELS_DEV // 2)],
         high,
         low,

time: 39.8 us -> 39.6 us (level)
  starting transfers between devices: 15.1 us -> 19.4 us
  waiting for transfers between devices: 6.48 us -> 2.25 us
    ppermute x7 -> x8, waiting for transfers between devices: 4.89 us -> 0.6 us  [to_peer(): return lax.ppermute(x, ('lev', 'sub'), pairs)]
    ppermute x7 -> x8, starting transfers between devices: 7.31 us -> 11 us  [to_peer(): return lax.ppermute(x, ('lev', 'sub'), pairs)]
    ppermute x1, starting transfers between devices: 2.45 us -> 3.05 us  [hand_over(): return lax.ppermute(x, ('lev', 'tm'), pairs)]
    pallas_call x3 -> x4, Pallas kernels: 7.83 us -> 7.94 us  [remap_call(): pl.pallas_call(kernel, out_shape=[jax.ShapeDtypeStruct(rows if isinstance...]
    pallas_call x6 -> x7, Pallas kernels: 0.88 us -> 0.89 us  [small_call(): pl.pallas_call(kernel, out_shape=[jax.ShapeDtypeStruct(shape, jnp.float32...]
  transfers between devices with their start and end apart: 12 -> 13, of which waited for: 6 -> 4; matrix products, arithmetic and copies ran while one was open for 0% -> 0% of each run, Pallas kernels for 33% -> 33%
where the time goes in v8:
time: 39.6 us; the launch traced here: 39.4 us
  starting transfers between devices  19.4 us (49%)
  Pallas kernels  16.2 us (41%)
  waiting for transfers between devices  2.25 us (6%)
  local copies, waits for them, and re-layouts  0.82 us (2%)
  between operations  0.78 us (2%)
    ppermute x8, starting transfers between devices, to_peer(): return lax.ppermute(x, ('lev', 'sub'), pairs)  11 us
    pallas_call x4, Pallas kernels, remap_call(): pl.pallas_call(kernel, out_shape=[jax.ShapeDtypeStruct(rows if isinstance...  7.94 us
    ppermute x4, starting transfers between devices, swap(): return lax.ppermute(x, 'tm', [(0, 1), (1, 0)])  5.32 us
    pallas_call x1, Pallas kernels, place_tiles(): pl.pallas_call(place_kernel, out_shape=(half, half), in_specs=[smem, smem...  4.07 us
    pallas_call x1, Pallas kernels, hour_sums(): pl.pallas_call(functools.partial(sums_kernel, plain, first, second), out_...  3.28 us
    ppermute x1, starting transfers between devices, hand_over(): return lax.ppermute(x, ('lev', 'tm'), pairs)  3.05 us
    ppermute x4, waiting for transfers between devices, swap(): return lax.ppermute(x, 'tm', [(0, 1), (1, 0)])  1.65 us
    pallas_call x7, Pallas kernels, small_call(): pl.pallas_call(kernel, out_shape=[jax.ShapeDtypeStruct(shape, jnp.float32...  0.89 us
  transfers between devices with their start and end apart: 13, of which 4 were waited for; matrix products, arithmetic and copies ran while one was open for 0% of the time, Pallas kernels for 33%

profile of v8, /device:TPU:0, one launch (start us, length us, event | category | flops | bytes accessed | tf_op | source)
XLA Modules:
  0.0 39.4 jit_solution(16766270782401773383)
XLA Ops:
  0.0 0.8 %copy-done.1 = s32[8]{0:T(128)S(1)} copy-done((s32[8]{0:T(128)S(1)}, s32[8]{0:T(128)}, u32[]{:S(2)}) %copy-start.1) | copy-done | bytes 56
  0.8 3.3 %hour_sums.1 = (f32[24,2048]{1,0:T(8,128)S(1)}, f32[24,2048]{1,0:T(8,128)S(1)}, f32[24,2048]{1,0:T(8,128)S(1)}, f32[24,2048]{1,0:T(8,128)S(1)}, f32[24,2048]{1,0...) custom-call(s32[8]{0:T(128)S(1)} %copy-done.1, ...), custom_call_target="tpu_custom_call" | custom-call | flops 1 | bytes 1 | tf_op jit(solution)/shard_map/hour_sums/pallas_call | solution.py:314
  4.1 0.5 %collective-permute-start = (f32[24,2048]{1,0:T(8,128)S(1)}, f32[24,2048]{1,0:T(8,128)S(1)}, u32[]{:S(2)}, u32[]{:S(2)}) collective-permute-start(f32[24,2048]{1,0:T(8,128)S(1)} %get-tuple-element.23), channel_id=1, source_target_pairs={{0,1},{1,0},{4,5},{5,4},{8,9},{9,8},{12,13},{13,12},{2,3},{3,2},{6... | collective-permute-start | bytes 589832 | tf_op jit(solution)/shard_map/ppermute | solution.py:450
  4.6 2.6 %collective-permute-start.2 = (f32[48,1024]{1,0:T(8,128)S(1)}, f32[48,1024]{1,0:T(8,128)S(1)}, u32[]{:S(2)}, u32[]{:S(2)}) collective-permute-start(f32[48,1024]{1,0:T(8,128)S(1)} %get-tuple-element.25.refs_0_), channel_id=1, source_target_pairs={{0,2},{2,0},{1,3},{3,1},{4,6},{6,4},{5,7},{7,5},{8,10},{10,8},{9,1... | collective-permute-start | bytes 589832 | tf_op jit(solution)/shard_map/ppermute | solution.py:457
  7.2 2.6 %collective-permute-start.1 = (f32[24,2048]{1,0:T(8,128)S(1)}, f32[24,2048]{1,0:T(8,128)S(1)}, u32[]{:S(2)}, u32[]{:S(2)}) collective-permute-start(f32[24,2048]{1,0:T(8,128)S(1)} %get-tuple-element.24), channel_id=1, source_target_pairs={{0,8},{1,9},{4,12},{5,13},{8,0},{9,1},{12,4},{13,5},{2,10},{3,11},... | collective-permute-start | bytes 589832 | tf_op jit(solution)/shard_map/ppermute | solution.py:450
  9.8 1.6 %collective-permute-start.5 = (f32[24,2048]{1,0:T(8,128)S(1)}, f32[24,2048]{1,0:T(8,128)S(1)}, u32[]{:S(2)}, u32[]{:S(2)}) collective-permute-start(f32[24,2048]{1,0:T(8,128)S(1)} %get-tuple-element.33), channel_id=1, source_target_pairs={{0,4},{1,5},{4,0},{5,1},{8,12},{9,13},{12,8},{13,9},{2,6},{3,7},{6... | collective-permute-start | bytes 589832 | tf_op jit(solution)/shard_map/ppermute | solution.py:450
  11.4 0.0 collective-permute-start.6
  12.0 4.1 %place_tiles.1 = (bf16[1024,2048]{1,0:T(8,128)(2,1)S(1)}, bf16[1024,2048]{1,0:T(8,128)(2,1)S(1)}) custom-call(s32[128]{0:T(128)S(1)} %copy-done.2, s32[128]{0:T(128)S(1)} %copy-done.3, s32[1]{0:T(128)S(6)} %copy.9.count, f32[64,8192]{1,0:T(8,128)S(1)} %copy-done, f32[48,1024]{1,0:T(8,128)S(1)} %get-tuple-element.25.refs_0_), custom_call_target="tpu_custom_call" | custom-call | flops 1 | bytes 1 | tf_op jit(solution)/shard_map/place_tiles/pallas_call | solution.py:78
  16.1 0.0 collective-permute-done.refs_1_.sibling
  16.1 0.0 collective-permute-done.2.got
  16.2 1.1 %collective-permute-start.9 = (f32[24,1024]{1,0:T(8,128)S(1)}, f32[24,1024]{1,0:T(8,128)S(1)}, u32[]{:S(2)}, u32[]{:S(2)}) collective-permute-start(f32[24,1024]{1,0:T(8,128)S(1)} %merge_first.1.refs_0_), channel_id=1, source_target_pairs={{0,12},{1,13},{4,8},{5,9},{8,4},{9,5},{12,0},{13,1},{2,14},{3,15},... | collective-permute-start | bytes 294920 | tf_op jit(solution)/shard_map/ppermute | solution.py:450
  17.2 2.5 %collective-permute-start.10 = (f32[24,1024]{1,0:T(8,128)S(1)}, f32[24,1024]{1,0:T(8,128)S(1)}, u32[]{:S(2)}, u32[]{:S(2)}) collective-permute-start(f32[24,1024]{1,0:T(8,128)S(1)} %merge_next.1.refs_1_), channel_id=1, source_target_pairs={{0,13},{1,12},{4,9},{5,8},{8,5},{9,4},{12,1},{13,0},{2,15},{3,14},... | collective-permute-start | bytes 294920 | tf_op jit(solution)/shard_map/ppermute | solution.py:450
  19.8 0.0 collective-permute-done.1.refs_0_.plain
  19.8 0.6 %collective-permute-start.4 = (f32[24,1024]{1,0:T(8,128)S(1)}, f32[24,1024]{1,0:T(8,128)S(1)}, u32[]{:S(2)}, u32[]{:S(2)}) collective-permute-start(f32[24,1024]{1,0:T(8,128)S(1)} %hold.2.refs_0_), channel_id=1, source_target_pairs={{0,2},{2,0},{1,3},{3,1},{4,6},{6,4},{5,7},{7,5},{8,10},{10,8},{9,1... | collective-permute-start | bytes 294920 | tf_op jit(solution)/shard_map/ppermute | solution.py:457
  20.4 2.7 %remap_both.1 = (f32[48,1024]{1,0:T(8,128)S(1)}, f32[48,1024]{1,0:T(8,128)S(1)}) custom-call(f32[24,2048]{1,0:T(8,128)S(1)} %get-tuple-element.22.own, f32[24,2048]{1,0:T(8,128)S(1)} %collective-permute-done.refs_1_.sibling, f32[24,2048]{1,0:T(8,128)S(1)} %collective-permute-done.1.refs_0_.plain, bf16[1024,2048]{1,0:T(8,128)(2,1)S(1)} %get-tuple-element.26.refs_0_.high, ...), custom_call_target="tpu_custom_call" | custom-call | flops 2500000000 | bytes 1 | tf_op jit(solution)/shard_map/remap_both/pallas_call | solution.py:105
  23.1 0.0 collective-permute-done.5.refs_1_.near_same
  23.1 1.6 %collective-permute-start.3 = (f32[48,1024]{1,0:T(8,128)S(1)}, f32[48,1024]{1,0:T(8,128)S(1)}, u32[]{:S(2)}, u32[]{:S(2)}) collective-permute-start(f32[48,1024]{1,0:T(8,128)S(1)} %get-tuple-element.31), channel_id=1, source_target_pairs={{0,2},{2,0},{1,3},{3,1},{4,6},{6,4},{5,7},{7,5},{8,10},{10,8},{9,1... | collective-permute-start | bytes 589832 | tf_op jit(solution)/shard_map/ppermute | solution.py:457
  24.7 0.3 collective-permute-done.4.got
  25.0 0.6 %collective-permute-start.8 = (f32[24,512]{1,0:T(8,128)S(1)}, f32[24,512]{1,0:T(8,128)S(1)}, u32[]{:S(2)}, u32[]{:S(2)}) collective-permute-start(f32[24,512]{1,0:T(8,128)S(1)} %get-tuple-element.36.refs_0_), channel_id=1, source_target_pairs={{0,9},{1,8},{4,13},{5,12},{8,1},{9,0},{12,5},{13,4},{2,11},{3,10},... | collective-permute-start | bytes 147464 | tf_op jit(solution)/shard_map/ppermute | solution.py:450
  25.7 2.1 %collective-permute-start.7 = (f32[24,512]{1,0:T(8,128)S(1)}, f32[24,512]{1,0:T(8,128)S(1)}, u32[]{:S(2)}, u32[]{:S(2)}) collective-permute-start(f32[24,512]{1,0:T(8,128)S(1)} %hold.3), channel_id=1, source_target_pairs={{0,9},{1,8},{4,13},{5,12},{8,1},{9,0},{12,5},{13,4},{2,11},{3,10},... | collective-permute-start | bytes 147464 | tf_op jit(solution)/shard_map/ppermute | solution.py:450
  27.8 0.2 collective-permute-done.10.other_sub
  28.0 0.0 collective-permute-done.9.same_sub
  28.0 2.7 %remap_near.1 = (f32[48,1024]{1,0:T(8,128)S(1)}, f32[48,1024]{1,0:T(8,128)S(1)}) custom-call(f32[24,2048]{1,0:T(8,128)S(1)} %collective-permute-done.5.refs_1_.near_same, f32[24,2048]{1,0:T(8,128)S(1)} %collective-permute-done.6.refs_2_.near_other, f32[24,2048]{1,0:T(8,128)S(1)} %far_rows.1.far, bf16[1024,2048]{1,0:T(8,128)(2,1)S(1)} %get-tuple-element.26.refs_0_.high, ...), custom_call_target="tpu_custom_call" | custom-call | flops 1 | bytes 1 | tf_op jit(solution)/shard_map/remap_near/pallas_call | solution.py:105
  30.8 0.6 %collective-permute-start.12 = (f32[48,1024]{1,0:T(8,128)S(1)}, f32[48,1024]{1,0:T(8,128)S(1)}, u32[]{:S(2)}, u32[]{:S(2)}) collective-permute-start(f32[48,1024]{1,0:T(8,128)S(1)} %get-tuple-element.38), channel_id=1, source_target_pairs={{0,2},{2,0},{1,3},{3,1},{4,6},{6,4},{5,7},{7,5},{8,10},{10,8},{9,1... | collective-permute-start | bytes 589832 | tf_op jit(solution)/shard_map/ppermute | solution.py:457
  31.4 0.0 collective-permute-done.8.block
  31.4 0.0 collective-permute-done.3.refs_1_.got_chip.got_plain
  31.4 1.2 %remap_early.1.early = f32[16,1024]{1,0:T(8,128)S(1)} custom-call(f32[24,512]{1,0:T(8,128)S(1)} %collective-permute-done.8.block, bf16[1024,2048]{1,0:T(8,128)(2,1)S(1)} %get-tuple-element.26.refs_0_.high, bf16[1024,2048]{1,0:T(8,128)(2,1)S(1)} %get-tuple-element.27.low, f32[48,1024]{1,0:T(8,128)S(1)} %get-tuple-element.37.refs_0_.one, ...), custom_call_target="tpu_custom_call" | custom-call | flops 1 | bytes 1 | tf_op jit(solution)/shard_map/remap_early/pallas_call | solution.py:105
  32.6 0.4 collective-permute-done.7.block
  33.0 1.2 %remap_last.1.last = f32[24,512]{1,0:T(8,128)S(1)} custom-call(f32[24,512]{1,0:T(8,128)S(1)} %collective-permute-done.7.block, f32[16,1024]{1,0:T(8,128)S(1)} %remap_early.1.early, bf16[1024,2048]{1,0:T(8,128)(2,1)S(1)} %get-tuple-element.26.refs_0_.high, bf16[1024,2048]{1,0:T(8,128)(2,1)S(1)} %get-tuple-element.27.low), custom_call_target="tpu_custom_call" | custom-call | flops 10000000000 | bytes 1 | tf_op jit(solution)/shard_map/remap_last/pallas_call | solution.py:105
  34.2 3.0 %collective-permute-start.11 = (f32[24,512]{1,0:T(8,128)S(1)}, f32[24,512]{1,0:T(8,128)S(1)}, u32[]{:S(2)}, u32[]{:S(2)}) collective-permute-start(f32[24,512]{1,0:T(8,128)S(1)} %remap_last.1.last), channel_id=1, source_target_pairs={{0,2},{4,6},{10,8},{14,12},{1,3},{5,7},{11,9},{15,13},{16,18},{20,... | collective-permute-start | bytes 147464 | tf_op jit(solution)/shard_map/ppermute | solution.py:454
  37.3 1.3 %collective-permute-done.12.got_one = f32[48,1024]{1,0:T(8,128)S(1)} collective-permute-done((f32[48,1024]{1,0:T(8,128)S(1)}, f32[48,1024]{1,0:T(8,128)S(1)}, u32[]{:S(2)}, u32[]{:S(2)}) %collective-permute-start.12) | collective-permute-done | bytes 196640 | tf_op jit(solution)/shard_map/ppermute | solution.py:457
  38.6 0.8 %write_first.1.begun = f32[96,1024]{1,0:T(8,128)} custom-call(f32[48,1024]{1,0:T(8,128)S(1)} %get-tuple-element.30.refs_0_.chip.plain, f32[48,1024]{1,0:T(8,128)S(1)} %collective-permute-done.3.refs_1_.got_chip.got_plain, f32[48,1024]{1,0:T(8,128)S(1)} %get-tuple-element.37.refs_0_.one, f32[48,1024]{1,0:T(8,128)S(1)} %collective-permute-done.12.got_one), custom_call_target="tpu_custom_call" | custom-call | flops 1 | bytes 1 | tf_op jit(solution)/shard_map/write_first/pallas_call | solution.py:365
  (16 shorter events, 0.1 us)
Async XLA Ops:
  0.0 12.0 %copy-start = (f32[64,8192]{1,0:T(8,128)S(1)}, f32[64,8192]{1,0:T(8,128)}, u32[]{:S(2)}) copy-start(f32[64,8192]{1,0:T(8,128)} %weights.1) | copy-start | bytes 6291460
  0.0 0.8 %copy-start.1 = (s32[8]{0:T(128)S(1)}, s32[8]{0:T(128)}, u32[]{:S(2)}) copy-start(s32[8]{0:T(128)} %step_hour.1) | copy-start | bytes 100
  0.8 11.2 %copy-start.2 = (s32[128]{0:T(128)S(1)}, s32[128]{0:T(128)}, u32[]{:S(2)}) copy-start(s32[128]{0:T(128)} %rows.1) | copy-start | bytes 1540
  0.8 11.2 %copy-start.3 = (s32[128]{0:T(128)S(1)}, s32[128]{0:T(128)}, u32[]{:S(2)}) copy-start(s32[128]{0:T(128)} %columns.1) | copy-start | bytes 1540
  4.1 12.0 %collective-permute-start = (f32[24,2048]{1,0:T(8,128)S(1)}, f32[24,2048]{1,0:T(8,128)S(1)}, u32[]{:S(2)}, u32[]{:S(2)}) collective-permute-start(f32[24,2048]{1,0:T(8,128)S(1)} %get-tuple-element.23), channel_id=1, source_target_pairs={{0,1},{1,0},{4,5},{5,4},{8,9},{9,8},{12,13},{13,12},{2,3},{3,2},{6... | collective-permute-start | bytes 589832 | tf_op jit(solution)/shard_map/ppermute | solution.py:450
  4.6 11.5 %collective-permute-start.2 = (f32[48,1024]{1,0:T(8,128)S(1)}, f32[48,1024]{1,0:T(8,128)S(1)}, u32[]{:S(2)}, u32[]{:S(2)}) collective-permute-start(f32[48,1024]{1,0:T(8,128)S(1)} %get-tuple-element.25.refs_0_), channel_id=1, source_target_pairs={{0,2},{2,0},{1,3},{3,1},{4,6},{6,4},{5,7},{7,5},{8,10},{10,8},{9,1... | collective-permute-start | bytes 589832 | tf_op jit(solution)/shard_map/ppermute | solution.py:457
  7.2 12.6 %collective-permute-start.1 = (f32[24,2048]{1,0:T(8,128)S(1)}, f32[24,2048]{1,0:T(8,128)S(1)}, u32[]{:S(2)}, u32[]{:S(2)}) collective-permute-start(f32[24,2048]{1,0:T(8,128)S(1)} %get-tuple-element.24), channel_id=1, source_target_pairs={{0,8},{1,9},{4,12},{5,13},{8,0},{9,1},{12,4},{13,5},{2,10},{3,11},... | collective-permute-start | bytes 589832 | tf_op jit(solution)/shard_map/ppermute | solution.py:450
  9.8 13.3 %collective-permute-start.5 = (f32[24,2048]{1,0:T(8,128)S(1)}, f32[24,2048]{1,0:T(8,128)S(1)}, u32[]{:S(2)}, u32[]{:S(2)}) collective-permute-start(f32[24,2048]{1,0:T(8,128)S(1)} %get-tuple-element.33), channel_id=1, source_target_pairs={{0,4},{1,5},{4,0},{5,1},{8,12},{9,13},{12,8},{13,9},{2,6},{3,7},{6... | collective-permute-start | bytes 589832 | tf_op jit(solution)/shard_map/ppermute | solution.py:450
  11.4 13.3 %collective-permute-start.6 = (f32[24,2048]{1,0:T(8,128)S(1)}, f32[24,2048]{1,0:T(8,128)S(1)}, u32[]{:S(2)}, u32[]{:S(2)}) collective-permute-start(f32[24,2048]{1,0:T(8,128)S(1)} %get-tuple-element.34), channel_id=1, source_target_pairs={{0,5},{1,4},{4,1},{5,0},{8,13},{9,12},{12,9},{13,8},{2,7},{3,6},{6... | collective-permute-start | bytes 589832 | tf_op jit(solution)/shard_map/ppermute | solution.py:450
  16.2 11.8 %collective-permute-start.9 = (f32[24,1024]{1,0:T(8,128)S(1)}, f32[24,1024]{1,0:T(8,128)S(1)}, u32[]{:S(2)}, u32[]{:S(2)}) collective-permute-start(f32[24,1024]{1,0:T(8,128)S(1)} %merge_first.1.refs_0_), channel_id=1, source_target_pairs={{0,12},{1,13},{4,8},{5,9},{8,4},{9,5},{12,0},{13,1},{2,14},{3,15},... | collective-permute-start | bytes 294920 | tf_op jit(solution)/shard_map/ppermute | solution.py:450
  17.2 10.7 %collective-permute-start.10 = (f32[24,1024]{1,0:T(8,128)S(1)}, f32[24,1024]{1,0:T(8,128)S(1)}, u32[]{:S(2)}, u32[]{:S(2)}) collective-permute-start(f32[24,1024]{1,0:T(8,128)S(1)} %merge_next.1.refs_1_), channel_id=1, source_target_pairs={{0,13},{1,12},{4,9},{5,8},{8,5},{9,4},{12,1},{13,0},{2,15},{3,14},... | collective-permute-start | bytes 294920 | tf_op jit(solution)/shard_map/ppermute | solution.py:450
  19.8 5.2 %collective-permute-start.4 = (f32[24,1024]{1,0:T(8,128)S(1)}, f32[24,1024]{1,0:T(8,128)S(1)}, u32[]{:S(2)}, u32[]{:S(2)}) collective-permute-start(f32[24,1024]{1,0:T(8,128)S(1)} %hold.2.refs_0_), channel_id=1, source_target_pairs={{0,2},{2,0},{1,3},{3,1},{4,6},{6,4},{5,7},{7,5},{8,10},{10,8},{9,1... | collective-permute-start | bytes 294920 | tf_op jit(solution)/shard_map/ppermute | solution.py:457
  23.1 8.2 %collective-permute-start.3 = (f32[48,1024]{1,0:T(8,128)S(1)}, f32[48,1024]{1,0:T(8,128)S(1)}, u32[]{:S(2)}, u32[]{:S(2)}) collective-permute-start(f32[48,1024]{1,0:T(8,128)S(1)} %get-tuple-element.31), channel_id=1, source_target_pairs={{0,2},{2,0},{1,3},{3,1},{4,6},{6,4},{5,7},{7,5},{8,10},{10,8},{9,1... | collective-permute-start | bytes 589832 | tf_op jit(solution)/shard_map/ppermute | solution.py:457
  25.0 6.3 %collective-permute-start.8 = (f32[24,512]{1,0:T(8,128)S(1)}, f32[24,512]{1,0:T(8,128)S(1)}, u32[]{:S(2)}, u32[]{:S(2)}) collective-permute-start(f32[24,512]{1,0:T(8,128)S(1)} %get-tuple-element.36.refs_0_), channel_id=1, source_target_pairs={{0,9},{1,8},{4,13},{5,12},{8,1},{9,0},{12,5},{13,4},{2,11},{3,10},... | collective-permute-start | bytes 147464 | tf_op jit(solution)/shard_map/ppermute | solution.py:450
  25.7 7.3 %collective-permute-start.7 = (f32[24,512]{1,0:T(8,128)S(1)}, f32[24,512]{1,0:T(8,128)S(1)}, u32[]{:S(2)}, u32[]{:S(2)}) collective-permute-start(f32[24,512]{1,0:T(8,128)S(1)} %hold.3), channel_id=1, source_target_pairs={{0,9},{1,8},{4,13},{5,12},{8,1},{9,0},{12,5},{13,4},{2,11},{3,10},... | collective-permute-start | bytes 147464 | tf_op jit(solution)/shard_map/ppermute | solution.py:450
  30.8 7.8 %collective-permute-start.12 = (f32[48,1024]{1,0:T(8,128)S(1)}, f32[48,1024]{1,0:T(8,128)S(1)}, u32[]{:S(2)}, u32[]{:S(2)}) collective-permute-start(f32[48,1024]{1,0:T(8,128)S(1)} %get-tuple-element.38), channel_id=1, source_target_pairs={{0,2},{2,0},{1,3},{3,1},{4,6},{6,4},{5,7},{7,5},{8,10},{10,8},{9,1... | collective-permute-start | bytes 589832 | tf_op jit(solution)/shard_map/ppermute | solution.py:457
  34.2 5.2 %collective-permute-start.11 = (f32[24,512]{1,0:T(8,128)S(1)}, f32[24,512]{1,0:T(8,128)S(1)}, u32[]{:S(2)}, u32[]{:S(2)}) collective-permute-start(f32[24,512]{1,0:T(8,128)S(1)} %remap_last.1.last), channel_id=1, source_target_pairs={{0,2},{4,6},{10,8},{14,12},{1,3},{5,7},{11,9},{15,13},{16,18},{20,... | collective-permute-start | bytes 147464 | tf_op jit(solution)/shard_map/ppermute | solution.py:454

commit v9 on v7

--- a/solution.py
+++ b/solution.py
@@ -170,15 +170,17 @@
     sort_out(near_result, far_result, keep, send)
 
 
-def remap_near_kernel(near_same, near_other, far, high, low, *refs):
-    keep, send, near_result, far_result = refs[-4:]
+def remap_near_kernel(near_same, near_other, high, low, *refs):
     rows = near_same.shape[0]
-    blocks = near_rows(near_same[...], near_other[...]) + [far[...]]
-    for at, result in remap_blocks(jnp.concatenate(blocks, axis=0), high, low):
-        near_result[:, at] = by_hour(result, rows // HOURS)
-        far_result[:rows, at] = result[2 * rows :]
-    far_result[rows:] = jnp.zeros((rows, PIXELS_DEV), jnp.float32)
-    sort_out(near_result, far_result, keep, send)
+    x = jnp.concatenate(near_rows(near_same[...], near_other[...]), axis=0)
+    for at, result in remap_blocks(x, high, low):
+        refs[-1][:, at] = by_hour(result, rows // HOURS)
+
+
+def remap_far_kernel(same, other, high, low, *refs):
+    x = jnp.concatenate(far_rows(same[...], other[...]), axis=0)
+    for at, result in remap_blocks(x, high, low):
+        refs[-1][:, at] = result
 
 
 def remap_last_kernel(block, high, low, *refs):
@@ -343,10 +345,6 @@
     refs[-1][...] = x[...]
 
 
-def far_rows_kernel(same_sub, other_sub, out):
-    out[...] = jnp.concatenate(far_rows(same_sub[...], other_sub[...]), axis=0)
-
-
 def small_call(kernel, inputs, after, shapes, cost, name):
     vmem = pl.BlockSpec(memory_space=pltpu.VMEM)
     return pl.pallas_call(
@@ -366,7 +364,7 @@
     return pl.ds(pl.multiple_of(start * 2 * levels, 2 * levels), 2 * levels)
 
 
-def write_first_kernel(divisor, levels, chip, got_chip, one, got_one, out):
+def write_first_kernel(divisor, levels, chip, got_chip, lev_near, got_near, far, got_far, out):
     me = lax.axis_index("tm")
     rows = 2 * levels
     near = keeps_near()
@@ -376,11 +374,11 @@
         @pl.when(near)
         def _():
             out[output_rows(True, hour, levels), :] = (chip[here] + got_chip[here]) / divisor
-            out[output_rows(False, hour, levels), :] = (one[here] + got_one[here]) / divisor
+            out[output_rows(False, hour, levels), :] = (lev_near[here] + got_near[here]) / divisor
 
         @pl.when(jnp.logical_not(near))
         def _():
-            out[output_rows(False, hour, levels), :] = jnp.where(me == hour, one[:rows], got_one[:rows]) / divisor
+            out[output_rows(False, hour, levels), :] = jnp.where(me == hour, far[...], got_far[...]) / divisor
 
 
 def write_last_kernel(divisor, levels, plain, got_plain, last, got_last, begun, out, stage, written):
@@ -478,24 +476,17 @@
         merge_last_kernel, [mine_1, got_1], [both, near_got[0]], [folded], HEAVY, "merge_last"
     )
     second_got = to_peer(merged[0], *second)
-    far = small_call(far_rows_kernel, [far_same, far_other], [], [(rows, CELLS_DEV)], HEAVY, "far_rows")[0]
-    one, send = remap_call(
-        remap_near_kernel,
-        [*near_got, far],
-        [],
-        [2 * rows] * 2,
-        high,
-        low,
-        LIGHT,
-        "remap_near",
-        [2 * rows] * 2,
-    )
-    got_one = swap(send)
+    (near,) = remap_call(
+        remap_near_kernel, near_got, merged, [2 * rows], high, low, LIGHT, "remap_near"
+    )
+    got_near = swap(near)
+    (far,) = remap_call(remap_far_kernel, [far_same, far_other], [near], [rows], high, low, HEAVY, "remap_far")
+    got_far = swap(far)
     padded = -(-rows // 32) * 16
     (last,) = remap_call(
         remap_last_kernel,
         [second_got],
-        [one],
+        [far],
         [(rows, PIXELS_DEV // 2)],
         high,
         low,
@@ -505,7 +496,7 @@
     )
     got_last = hand_over(last)
     levels = rows // 2
-    out = write_first([both, got_both, one, got_one], levels, divisor)
+    out = write_first([both, got_both, near, got_near, far, got_far], levels, divisor)
     out = write_last(out, [both, got_both, last, got_last], levels, divisor)
     return out.reshape(HOURS, out.shape[0] // HOURS, PIXELS_DEV)
 

time: 39.8 us -> 40.4 us (1.015)
  the two profiles are of different devices: /device:TPU:0 before, /device:TPU:10 now
where the time goes in v9:
time: 40.4 us; the launch traced here: 40.1 us
  Pallas kernels  17.9 us (44%)
  starting transfers between devices  15.1 us (37%)
  waiting for transfers between devices  5.46 us (14%)
  local copies, waits for them, and re-layouts  0.82 us (2%)
  between operations  0.78 us (2%)
    pallas_call x4, Pallas kernels, remap_call(): pl.pallas_call(kernel, out_shape=[jax.ShapeDtypeStruct(rows if isinstance...  10.3 us
    ppermute x7, starting transfers between devices, to_peer(): return lax.ppermute(x, ('lev', 'sub'), pairs)  8.93 us
    ppermute x5, starting transfers between devices, swap(): return lax.ppermute(x, 'tm', [(0, 1), (1, 0)])  4.85 us
    pallas_call x1, Pallas kernels, hour_sums(): pl.pallas_call(functools.partial(sums_kernel, plain, first, second), out_...  3.28 us
    pallas_call x1, Pallas kernels, place_tiles(): pl.pallas_call(place_kernel, out_shape=(half, half), in_specs=[smem, smem...  2.78 us
    ppermute x1, waiting for transfers between devices, hand_over(): return lax.ppermute(x, ('lev', 'tm'), pairs)  2.5 us
    ppermute x5, waiting for transfers between devices, swap(): return lax.ppermute(x, 'tm', [(0, 1), (1, 0)])  1.52 us
    ppermute x7, waiting for transfers between devices, to_peer(): return lax.ppermute(x, ('lev', 'sub'), pairs)  1.44 us
  transfers between devices with their start and end apart: 13, of which 3 were waited for; matrix products, arithmetic and copies ran while one was open for 0% of the time, Pallas kernels for 35%

profile of v9, /device:TPU:10, one launch (start us, length us, event | category | flops | bytes accessed | tf_op | source)
XLA Modules:
  0.0 40.1 jit_solution(6982036372906554865)
XLA Ops:
  0.0 0.8 %copy-done.1 = s32[8]{0:T(128)S(1)} copy-done((s32[8]{0:T(128)S(1)}, s32[8]{0:T(128)}, u32[]{:S(2)}) %copy-start.1) | copy-done | bytes 56
  0.8 3.3 %hour_sums.1 = (f32[24,2048]{1,0:T(8,128)S(1)}, f32[24,2048]{1,0:T(8,128)S(1)}, f32[24,2048]{1,0:T(8,128)S(1)}, f32[24,2048]{1,0:T(8,128)S(1)}, f32[24,2048]{1,0...) custom-call(s32[8]{0:T(128)S(1)} %copy-done.1, ...), custom_call_target="tpu_custom_call" | custom-call | flops 1 | bytes 1 | tf_op jit(solution)/shard_map/hour_sums/pallas_call | solution.py:307
  4.1 0.1 collective-permute-start
  4.2 0.6 %collective-permute-start.2 = (f32[48,1024]{1,0:T(8,128)S(1)}, f32[48,1024]{1,0:T(8,128)S(1)}, u32[]{:S(2)}, u32[]{:S(2)}) collective-permute-start(f32[48,1024]{1,0:T(8,128)S(1)} %get-tuple-element.21.refs_0_), channel_id=1, source_target_pairs={{0,2},{2,0},{1,3},{3,1},{4,6},{6,4},{5,7},{7,5},{8,10},{10,8},{9,1... | collective-permute-start | bytes 589832 | tf_op jit(solution)/shard_map/ppermute | solution.py:442
  4.8 2.6 %collective-permute-start.1 = (f32[24,2048]{1,0:T(8,128)S(1)}, f32[24,2048]{1,0:T(8,128)S(1)}, u32[]{:S(2)}, u32[]{:S(2)}) collective-permute-start(f32[24,2048]{1,0:T(8,128)S(1)} %get-tuple-element.20), channel_id=1, source_target_pairs={{0,8},{1,9},{4,12},{5,13},{8,0},{9,1},{12,4},{13,5},{2,10},{3,11},... | collective-permute-start | bytes 589832 | tf_op jit(solution)/shard_map/ppermute | solution.py:435
  7.4 0.4 %collective-permute-start.5 = (f32[24,2048]{1,0:T(8,128)S(1)}, f32[24,2048]{1,0:T(8,128)S(1)}, u32[]{:S(2)}, u32[]{:S(2)}) collective-permute-start(f32[24,2048]{1,0:T(8,128)S(1)} %get-tuple-element.29), channel_id=1, source_target_pairs={{0,4},{1,5},{4,0},{5,1},{8,12},{9,13},{12,8},{13,9},{2,6},{3,7},{6... | collective-permute-start | bytes 589832 | tf_op jit(solution)/shard_map/ppermute | solution.py:435
  7.8 0.8 %collective-permute-start.9 = (f32[24,2048]{1,0:T(8,128)S(1)}, f32[24,2048]{1,0:T(8,128)S(1)}, u32[]{:S(2)}, u32[]{:S(2)}) collective-permute-start(f32[24,2048]{1,0:T(8,128)S(1)} %get-tuple-element.30), channel_id=1, source_target_pairs={{0,5},{1,4},{4,1},{5,0},{8,13},{9,12},{12,9},{13,8},{2,7},{3,6},{6... | collective-permute-start | bytes 589832 | tf_op jit(solution)/shard_map/ppermute | solution.py:435
  9.3 2.8 %place_tiles.1 = (bf16[1024,2048]{1,0:T(8,128)(2,1)S(1)}, bf16[1024,2048]{1,0:T(8,128)(2,1)S(1)}) custom-call(s32[128]{0:T(128)S(1)} %copy-done.2, s32[128]{0:T(128)S(1)} %copy-done.3, s32[1]{0:T(128)S(6)} %copy.9.count, f32[64,8192]{1,0:T(8,128)S(1)} %copy-done, f32[48,1024]{1,0:T(8,128)S(1)} %get-tuple-element.21.refs_0_), custom_call_target="tpu_custom_call" | custom-call | flops 1 | bytes 1 | tf_op jit(solution)/shard_map/place_tiles/pallas_call | solution.py:78
  12.1 0.0 collective-permute-done.refs_1_.sibling
  12.1 0.0 collective-permute-done.2.got
  12.1 1.3 %collective-permute-start.7 = (f32[24,1024]{1,0:T(8,128)S(1)}, f32[24,1024]{1,0:T(8,128)S(1)}, u32[]{:S(2)}, u32[]{:S(2)}) collective-permute-start(f32[24,1024]{1,0:T(8,128)S(1)} %merge_first.1.refs_0_), channel_id=1, source_target_pairs={{0,12},{1,13},{4,8},{5,9},{8,4},{9,5},{12,0},{13,1},{2,14},{3,15},... | collective-permute-start | bytes 294920 | tf_op jit(solution)/shard_map/ppermute | solution.py:435
  13.4 1.2 %collective-permute-start.8 = (f32[24,1024]{1,0:T(8,128)S(1)}, f32[24,1024]{1,0:T(8,128)S(1)}, u32[]{:S(2)}, u32[]{:S(2)}) collective-permute-start(f32[24,1024]{1,0:T(8,128)S(1)} %merge_next.1.refs_1_), channel_id=1, source_target_pairs={{0,13},{1,12},{4,9},{5,8},{8,5},{9,4},{12,1},{13,0},{2,15},{3,14},... | collective-permute-start | bytes 294920 | tf_op jit(solution)/shard_map/ppermute | solution.py:435
  14.7 1.4 %collective-permute-done.1.refs_0_.plain = f32[24,2048]{1,0:T(8,128)S(1)} collective-permute-done((f32[24,2048]{1,0:T(8,128)S(1)}, f32[24,2048]{1,0:T(8,128)S(1)}, u32[]{:S(2)}, u32[]{:S(2)}) %collective-permute-start.1) | collective-permute-done | bytes 196640 | tf_op jit(solution)/shard_map/ppermute | solution.py:435
  16.1 1.5 %collective-permute-start.4 = (f32[24,1024]{1,0:T(8,128)S(1)}, f32[24,1024]{1,0:T(8,128)S(1)}, u32[]{:S(2)}, u32[]{:S(2)}) collective-permute-start(f32[24,1024]{1,0:T(8,128)S(1)} %hold.1.refs_0_), channel_id=1, source_target_pairs={{0,2},{2,0},{1,3},{3,1},{4,6},{6,4},{5,7},{7,5},{8,10},{10,8},{9,1... | collective-permute-start | bytes 294920 | tf_op jit(solution)/shard_map/ppermute | solution.py:442
  17.6 2.7 %remap_both.1 = (f32[48,1024]{1,0:T(8,128)S(1)}, f32[48,1024]{1,0:T(8,128)S(1)}) custom-call(f32[24,2048]{1,0:T(8,128)S(1)} %get-tuple-element.18.own, f32[24,2048]{1,0:T(8,128)S(1)} %collective-permute-done.refs_1_.sibling, f32[24,2048]{1,0:T(8,128)S(1)} %collective-permute-done.1.refs_0_.plain, bf16[1024,2048]{1,0:T(8,128)(2,1)S(1)} %get-tuple-element.22.refs_0_.high, ...), custom_call_target="tpu_custom_call" | custom-call | flops 2500000000 | bytes 1 | tf_op jit(solution)/shard_map/remap_both/pallas_call | solution.py:105
  20.3 0.0 collective-permute-done.5.refs_1_.near_same
  20.3 0.6 %collective-permute-start.3 = (f32[48,1024]{1,0:T(8,128)S(1)}, f32[48,1024]{1,0:T(8,128)S(1)}, u32[]{:S(2)}, u32[]{:S(2)}) collective-permute-start(f32[48,1024]{1,0:T(8,128)S(1)} %get-tuple-element.27), channel_id=1, source_target_pairs={{0,2},{2,0},{1,3},{3,1},{4,6},{6,4},{5,7},{7,5},{8,10},{10,8},{9,1... | collective-permute-start | bytes 589832 | tf_op jit(solution)/shard_map/ppermute | solution.py:442
  20.9 0.0 collective-permute-done.4.got
  20.9 2.5 %collective-permute-start.6 = (f32[24,1024]{1,0:T(8,128)S(1)}, f32[24,1024]{1,0:T(8,128)S(1)}, u32[]{:S(2)}, u32[]{:S(2)}) collective-permute-start(f32[24,1024]{1,0:T(8,128)S(1)} %merge_last.1.refs_0_), channel_id=1, source_target_pairs={{0,9},{1,8},{4,13},{5,12},{8,1},{9,0},{12,5},{13,4},{2,11},{3,10},... | collective-permute-start | bytes 294920 | tf_op jit(solution)/shard_map/ppermute | solution.py:435
  23.5 2.6 %remap_near.1.refs_0_.lev_near = f32[48,1024]{1,0:T(8,128)S(1)} custom-call(f32[24,2048]{1,0:T(8,128)S(1)} %collective-permute-done.5.refs_1_.near_same, f32[24,2048]{1,0:T(8,128)S(1)} %collective-permute-done.9.near_other, bf16[1024,2048]{1,0:T(8,128)(2,1)S(1)} %get-tuple-element.22.refs_0_.high, bf16[1024,2048]{1,0:T(8,128)(2,1)S(1)} %get-tuple-element.23.low, ...), custom_call_target="tpu_custom_call" | custom-call | flops 1 | bytes 1 | tf_op jit(solution)/shard_map/remap_near/pallas_call | solution.py:105
  26.1 1.6 %collective-permute-start.11 = (f32[48,1024]{1,0:T(8,128)S(1)}, f32[48,1024]{1,0:T(8,128)S(1)}, u32[]{:S(2)}, u32[]{:S(2)}) collective-permute-start(f32[48,1024]{1,0:T(8,128)S(1)} %remap_near.1.refs_0_.lev_near), channel_id=1, source_target_pairs={{0,2},{2,0},{1,3},{3,1},{4,6},{6,4},{5,7},{7,5},{8,10},{10,8},{9,1... | collective-permute-start | bytes 589832 | tf_op jit(solution)/shard_map/ppermute | solution.py:442
  27.7 0.0 collective-permute-done.8.other
  27.7 0.0 collective-permute-done.7.same
  27.7 2.6 %remap_far.1.refs_0_.far = f32[24,1024]{1,0:T(8,128)S(1)} custom-call(f32[24,1024]{1,0:T(8,128)S(1)} %collective-permute-done.7.same, f32[24,1024]{1,0:T(8,128)S(1)} %collective-permute-done.8.other, bf16[1024,2048]{1,0:T(8,128)(2,1)S(1)} %get-tuple-element.22.refs_0_.high, bf16[1024,2048]{1,0:T(8,128)(2,1)S(1)} %get-tuple-element.23.low, ...), custom_call_target="tpu_custom_call" | custom-call | flops 10000000000 | bytes 1 | tf_op jit(solution)/shard_map/remap_far/pallas_call | solution.py:105
  30.3 0.6 %collective-permute-start.12 = (f32[24,1024]{1,0:T(8,128)S(1)}, f32[24,1024]{1,0:T(8,128)S(1)}, u32[]{:S(2)}, u32[]{:S(2)}) collective-permute-start(f32[24,1024]{1,0:T(8,128)S(1)} %remap_far.1.refs_0_.far), channel_id=1, source_target_pairs={{0,2},{2,0},{1,3},{3,1},{4,6},{6,4},{5,7},{7,5},{8,10},{10,8},{9,1... | collective-permute-start | bytes 294920 | tf_op jit(solution)/shard_map/ppermute | solution.py:442
  30.9 2.4 %remap_last.1.last = f32[24,512]{1,0:T(8,128)S(1)} custom-call(f32[24,1024]{1,0:T(8,128)S(1)} %collective-permute-done.6.block, bf16[1024,2048]{1,0:T(8,128)(2,1)S(1)} %get-tuple-element.22.refs_0_.high, bf16[1024,2048]{1,0:T(8,128)(2,1)S(1)} %get-tuple-element.23.low, f32[24,1024]{1,0:T(8,128)S(1)} %remap_far.1.refs_0_.far), custom_call_target="tpu_custom_call" | custom-call | flops 10000000000 | bytes 1 | tf_op jit(solution)/shard_map/remap_last/pallas_call | solution.py:105
  33.3 1.3 %collective-permute-start.10 = (f32[24,512]{1,0:T(8,128)S(1)}, f32[24,512]{1,0:T(8,128)S(1)}, u32[]{:S(2)}, u32[]{:S(2)}) collective-permute-start(f32[24,512]{1,0:T(8,128)S(1)} %remap_last.1.last), channel_id=1, source_target_pairs={{0,2},{4,6},{10,8},{14,12},{1,3},{5,7},{11,9},{15,13},{16,18},{20,... | collective-permute-start | bytes 147464 | tf_op jit(solution)/shard_map/ppermute | solution.py:439
  34.6 1.5 %collective-permute-done.12.got_far = f32[24,1024]{1,0:T(8,128)S(1)} collective-permute-done((f32[24,1024]{1,0:T(8,128)S(1)}, f32[24,1024]{1,0:T(8,128)S(1)}, u32[]{:S(2)}, u32[]{:S(2)}) %collective-permute-start.12) | collective-permute-done | bytes 98336 | tf_op jit(solution)/shard_map/ppermute | solution.py:442
  36.1 0.0 collective-permute-done.3.got_chip.got_plain
  36.1 0.8 %write_first.1.begun = f32[96,1024]{1,0:T(8,128)} custom-call(f32[48,1024]{1,0:T(8,128)S(1)} %get-tuple-element.26.refs_0_.chip.plain, f32[48,1024]{1,0:T(8,128)S(1)} %collective-permute-done.3.got_chip.got_plain, f32[48,1024]{1,0:T(8,128)S(1)} %remap_near.1.refs_0_.lev_near, f32[48,1024]{1,0:T(8,128)S(1)} %collective-permute-done.11.got_near, ...), custom_call_target="tpu_custom_call" | custom-call | flops 1 | bytes 1 | tf_op jit(solution)/shard_map/write_first/pallas_call | solution.py:350
  36.9 2.5 %collective-permute-done.10.got_last = f32[24,512]{1,0:T(8,128)S(1)} collective-permute-done((f32[24,512]{1,0:T(8,128)S(1)}, f32[24,512]{1,0:T(8,128)S(1)}, u32[]{:S(2)}, u32[]{:S(2)}) %collective-permute-start.10) | collective-permute-done | bytes 49184 | tf_op jit(solution)/shard_map/ppermute | solution.py:439
  39.4 0.7 %write_last.1 = f32[96,1024]{1,0:T(8,128)} custom-call(f32[48,1024]{1,0:T(8,128)S(1)} %get-tuple-element.26.refs_0_.chip.plain, f32[48,1024]{1,0:T(8,128)S(1)} %collective-permute-done.3.got_chip.got_plain, f32[24,512]{1,0:T(8,128)S(1)} %remap_last.1.last, f32[24,512]{1,0:T(8,128)S(1)} %collective-permute-done.10.got_last, ...), custom_call_target="tpu_custom_call", output_to_operand_aliasing={{}: (4, {})} | custom-call | flops 1 | bytes 1 | tf_op jit(solution)/shard_map/write_last/pallas_call | solution.py:411
  (14 shorter events, 0.1 us)
Async XLA Ops:
  0.0 9.3 %copy-start = (f32[64,8192]{1,0:T(8,128)S(1)}, f32[64,8192]{1,0:T(8,128)}, u32[]{:S(2)}) copy-start(f32[64,8192]{1,0:T(8,128)} %weights.1) | copy-start | bytes 6291460
  0.0 0.8 %copy-start.1 = (s32[8]{0:T(128)S(1)}, s32[8]{0:T(128)}, u32[]{:S(2)}) copy-start(s32[8]{0:T(128)} %step_hour.1) | copy-start | bytes 100
  0.8 8.5 %copy-start.2 = (s32[128]{0:T(128)S(1)}, s32[128]{0:T(128)}, u32[]{:S(2)}) copy-start(s32[128]{0:T(128)} %rows.1) | copy-start | bytes 1540
  0.8 8.5 %copy-start.3 = (s32[128]{0:T(128)S(1)}, s32[128]{0:T(128)}, u32[]{:S(2)}) copy-start(s32[128]{0:T(128)} %columns.1) | copy-start | bytes 1540
  4.1 8.0 %collective-permute-start = (f32[24,2048]{1,0:T(8,128)S(1)}, f32[24,2048]{1,0:T(8,128)S(1)}, u32[]{:S(2)}, u32[]{:S(2)}) collective-permute-start(f32[24,2048]{1,0:T(8,128)S(1)} %get-tuple-element.19), channel_id=1, source_target_pairs={{0,1},{1,0},{4,5},{5,4},{8,9},{9,8},{12,13},{13,12},{2,3},{3,2},{6... | collective-permute-start | bytes 589832 | tf_op jit(solution)/shard_map/ppermute | solution.py:435
  4.2 7.9 %collective-permute-start.2 = (f32[48,1024]{1,0:T(8,128)S(1)}, f32[48,1024]{1,0:T(8,128)S(1)}, u32[]{:S(2)}, u32[]{:S(2)}) collective-permute-start(f32[48,1024]{1,0:T(8,128)S(1)} %get-tuple-element.21.refs_0_), channel_id=1, source_target_pairs={{0,2},{2,0},{1,3},{3,1},{4,6},{6,4},{5,7},{7,5},{8,10},{10,8},{9,1... | collective-permute-start | bytes 589832 | tf_op jit(solution)/shard_map/ppermute | solution.py:442
  4.8 11.3 %collective-permute-start.1 = (f32[24,2048]{1,0:T(8,128)S(1)}, f32[24,2048]{1,0:T(8,128)S(1)}, u32[]{:S(2)}, u32[]{:S(2)}) collective-permute-start(f32[24,2048]{1,0:T(8,128)S(1)} %get-tuple-element.20), channel_id=1, source_target_pairs={{0,8},{1,9},{4,12},{5,13},{8,0},{9,1},{12,4},{13,5},{2,10},{3,11},... | collective-permute-start | bytes 589832 | tf_op jit(solution)/shard_map/ppermute | solution.py:435
  7.4 12.9 %collective-permute-start.5 = (f32[24,2048]{1,0:T(8,128)S(1)}, f32[24,2048]{1,0:T(8,128)S(1)}, u32[]{:S(2)}, u32[]{:S(2)}) collective-permute-start(f32[24,2048]{1,0:T(8,128)S(1)} %get-tuple-element.29), channel_id=1, source_target_pairs={{0,4},{1,5},{4,0},{5,1},{8,12},{9,13},{12,8},{13,9},{2,6},{3,7},{6... | collective-permute-start | bytes 589832 | tf_op jit(solution)/shard_map/ppermute | solution.py:435
  7.8 15.7 %collective-permute-start.9 = (f32[24,2048]{1,0:T(8,128)S(1)}, f32[24,2048]{1,0:T(8,128)S(1)}, u32[]{:S(2)}, u32[]{:S(2)}) collective-permute-start(f32[24,2048]{1,0:T(8,128)S(1)} %get-tuple-element.30), channel_id=1, source_target_pairs={{0,5},{1,4},{4,1},{5,0},{8,13},{9,12},{12,9},{13,8},{2,7},{3,6},{6... | collective-permute-start | bytes 589832 | tf_op jit(solution)/shard_map/ppermute | solution.py:435
  12.1 15.6 %collective-permute-start.7 = (f32[24,1024]{1,0:T(8,128)S(1)}, f32[24,1024]{1,0:T(8,128)S(1)}, u32[]{:S(2)}, u32[]{:S(2)}) collective-permute-start(f32[24,1024]{1,0:T(8,128)S(1)} %merge_first.1.refs_0_), channel_id=1, source_target_pairs={{0,12},{1,13},{4,8},{5,9},{8,4},{9,5},{12,0},{13,1},{2,14},{3,15},... | collective-permute-start | bytes 294920 | tf_op jit(solution)/shard_map/ppermute | solution.py:435
  13.4 14.3 %collective-permute-start.8 = (f32[24,1024]{1,0:T(8,128)S(1)}, f32[24,1024]{1,0:T(8,128)S(1)}, u32[]{:S(2)}, u32[]{:S(2)}) collective-permute-start(f32[24,1024]{1,0:T(8,128)S(1)} %merge_next.1.refs_1_), channel_id=1, source_target_pairs={{0,13},{1,12},{4,9},{5,8},{8,5},{9,4},{12,1},{13,0},{2,15},{3,14},... | collective-permute-start | bytes 294920 | tf_op jit(solution)/shard_map/ppermute | solution.py:435
  16.1 4.8 %collective-permute-start.4 = (f32[24,1024]{1,0:T(8,128)S(1)}, f32[24,1024]{1,0:T(8,128)S(1)}, u32[]{:S(2)}, u32[]{:S(2)}) collective-permute-start(f32[24,1024]{1,0:T(8,128)S(1)} %hold.1.refs_0_), channel_id=1, source_target_pairs={{0,2},{2,0},{1,3},{3,1},{4,6},{6,4},{5,7},{7,5},{8,10},{10,8},{9,1... | collective-permute-start | bytes 294920 | tf_op jit(solution)/shard_map/ppermute | solution.py:442
  20.3 15.7 %collective-permute-start.3 = (f32[48,1024]{1,0:T(8,128)S(1)}, f32[48,1024]{1,0:T(8,128)S(1)}, u32[]{:S(2)}, u32[]{:S(2)}) collective-permute-start(f32[48,1024]{1,0:T(8,128)S(1)} %get-tuple-element.27), channel_id=1, source_target_pairs={{0,2},{2,0},{1,3},{3,1},{4,6},{6,4},{5,7},{7,5},{8,10},{10,8},{9,1... | collective-permute-start | bytes 589832 | tf_op jit(solution)/shard_map/ppermute | solution.py:442
  20.9 9.9 %collective-permute-start.6 = (f32[24,1024]{1,0:T(8,128)S(1)}, f32[24,1024]{1,0:T(8,128)S(1)}, u32[]{:S(2)}, u32[]{:S(2)}) collective-permute-start(f32[24,1024]{1,0:T(8,128)S(1)} %merge_last.1.refs_0_), channel_id=1, source_target_pairs={{0,9},{1,8},{4,13},{5,12},{8,1},{9,0},{12,5},{13,4},{2,11},{3,10},... | collective-permute-start | bytes 294920 | tf_op jit(solution)/shard_map/ppermute | solution.py:435
  26.1 10.0 %collective-permute-start.11 = (f32[48,1024]{1,0:T(8,128)S(1)}, f32[48,1024]{1,0:T(8,128)S(1)}, u32[]{:S(2)}, u32[]{:S(2)}) collective-permute-start(f32[48,1024]{1,0:T(8,128)S(1)} %remap_near.1.refs_0_.lev_near), channel_id=1, source_target_pairs={{0,2},{2,0},{1,3},{3,1},{4,6},{6,4},{5,7},{7,5},{8,10},{10,8},{9,1... | collective-permute-start | bytes 589832 | tf_op jit(solution)/shard_map/ppermute | solution.py:442
  30.3 5.8 %collective-permute-start.12 = (f32[24,1024]{1,0:T(8,128)S(1)}, f32[24,1024]{1,0:T(8,128)S(1)}, u32[]{:S(2)}, u32[]{:S(2)}) collective-permute-start(f32[24,1024]{1,0:T(8,128)S(1)} %remap_far.1.refs_0_.far), channel_id=1, source_target_pairs={{0,2},{2,0},{1,3},{3,1},{4,6},{6,4},{5,7},{7,5},{8,10},{10,8},{9,1... | collective-permute-start | bytes 294920 | tf_op jit(solution)/shard_map/ppermute | solution.py:442
  33.3 6.1 %collective-permute-start.10 = (f32[24,512]{1,0:T(8,128)S(1)}, f32[24,512]{1,0:T(8,128)S(1)}, u32[]{:S(2)}, u32[]{:S(2)}) collective-permute-start(f32[24,512]{1,0:T(8,128)S(1)} %remap_last.1.last), channel_id=1, source_target_pairs={{0,2},{4,6},{10,8},{14,12},{1,3},{5,7},{11,9},{15,13},{16,18},{20,... | collective-permute-start | bytes 147464 | tf_op jit(solution)/shard_map/ppermute | solution.py:439

commit v10 on v9

--- a/solution.py
+++ b/solution.py
@@ -434,10 +434,6 @@
         pairs = [(a * subs + b, (a ^ k) * subs + (b ^ j)) for a in range(levs) for b in range(subs)]
         return lax.ppermute(x, ("lev", "sub"), pairs)
 
-    def hand_over(x):
-        pairs = [(a * shards_tm + a // half, a * shards_tm + 1 - a // half) for a in range(levs)]
-        return lax.ppermute(x, ("lev", "tm"), pairs)
-
     def swap(x):
         return lax.ppermute(x, "tm", [(0, 1), (1, 0)])
 
@@ -494,7 +490,7 @@
         "remap_last",
         [padded],
     )
-    got_last = hand_over(last)
+    got_last = swap(last)
     levels = rows // 2
     out = write_first([both, got_both, near, got_near, far, got_far], levels, divisor)
     out = write_last(out, [both, got_both, last, got_last], levels, divisor)

time: 40.4 us -> 39.6 us (0.980)
  the two profiles are of different devices: /device:TPU:10 before, /device:TPU:0 now
where the time goes in v10:
time: 39.6 us; the launch traced here: 39.4 us
  Pallas kernels  18.7 us (47%)
  starting transfers between devices  14.9 us (38%)
  waiting for transfers between devices  4.29 us (11%)
  local copies, waits for them, and re-layouts  0.82 us (2%)
  between operations  0.78 us (2%)
    pallas_call x4, Pallas kernels, remap_call(): pl.pallas_call(kernel, out_shape=[jax.ShapeDtypeStruct(rows if isinstance...  10.3 us
    ppermute x6, starting transfers between devices, swap(): return lax.ppermute(x, 'tm', [(0, 1), (1, 0)])  7.44 us
    ppermute x7, starting transfers between devices, to_peer(): return lax.ppermute(x, ('lev', 'sub'), pairs)  7.44 us
    pallas_call x1, Pallas kernels, place_tiles(): pl.pallas_call(place_kernel, out_shape=(half, half), in_specs=[smem, smem...  4.2 us
    ppermute x6, waiting for transfers between devices, swap(): return lax.ppermute(x, 'tm', [(0, 1), (1, 0)])  3.55 us
    pallas_call x1, Pallas kernels, hour_sums(): pl.pallas_call(functools.partial(sums_kernel, plain, first, second), out_...  3.28 us
    pallas_call x5, Pallas kernels, small_call(): pl.pallas_call(kernel, out_shape=[jax.ShapeDtypeStruct(shape, jnp.float32...  0.85 us
    unnamed x8, local copies, waits for them, and re-layouts  0.82 us
  transfers between devices with their start and end apart: 13, of which 5 were waited for; matrix products, arithmetic and copies ran while one was open for 0% of the time, Pallas kernels for 39%

profile of v10, /device:TPU:0, one launch (start us, length us, event | category | flops | bytes accessed | tf_op | source)
XLA Modules:
  0.0 39.4 jit_solution(14216772207716893931)
XLA Ops:
  0.0 0.8 %copy-done.1 = s32[8]{0:T(128)S(1)} copy-done((s32[8]{0:T(128)S(1)}, s32[8]{0:T(128)}, u32[]{:S(2)}) %copy-start.1) | copy-done | bytes 56
  0.8 3.3 %hour_sums.1 = (f32[24,2048]{1,0:T(8,128)S(1)}, f32[24,2048]{1,0:T(8,128)S(1)}, f32[24,2048]{1,0:T(8,128)S(1)}, f32[24,2048]{1,0:T(8,128)S(1)}, f32[24,2048]{1,0...) custom-call(s32[8]{0:T(128)S(1)} %copy-done.1, ...), custom_call_target="tpu_custom_call" | custom-call | flops 1 | bytes 1 | tf_op jit(solution)/shard_map/hour_sums/pallas_call | solution.py:307
  4.1 0.5 %collective-permute-start = (f32[24,2048]{1,0:T(8,128)S(1)}, f32[24,2048]{1,0:T(8,128)S(1)}, u32[]{:S(2)}, u32[]{:S(2)}) collective-permute-start(f32[24,2048]{1,0:T(8,128)S(1)} %get-tuple-element.19), channel_id=1, source_target_pairs={{0,1},{1,0},{4,5},{5,4},{8,9},{9,8},{12,13},{13,12},{2,3},{3,2},{6... | collective-permute-start | bytes 589832 | tf_op jit(solution)/shard_map/ppermute | solution.py:435
  4.6 2.6 %collective-permute-start.2 = (f32[48,1024]{1,0:T(8,128)S(1)}, f32[48,1024]{1,0:T(8,128)S(1)}, u32[]{:S(2)}, u32[]{:S(2)}) collective-permute-start(f32[48,1024]{1,0:T(8,128)S(1)} %get-tuple-element.21.refs_0_), channel_id=1, source_target_pairs={{0,2},{2,0},{1,3},{3,1},{4,6},{6,4},{5,7},{7,5},{8,10},{10,8},{9,1... | collective-permute-start | bytes 589832 | tf_op jit(solution)/shard_map/ppermute | solution.py:438
  7.2 2.6 %collective-permute-start.1 = (f32[24,2048]{1,0:T(8,128)S(1)}, f32[24,2048]{1,0:T(8,128)S(1)}, u32[]{:S(2)}, u32[]{:S(2)}) collective-permute-start(f32[24,2048]{1,0:T(8,128)S(1)} %get-tuple-element.20), channel_id=1, source_target_pairs={{0,8},{1,9},{4,12},{5,13},{8,0},{9,1},{12,4},{13,5},{2,10},{3,11},... | collective-permute-start | bytes 589832 | tf_op jit(solution)/shard_map/ppermute | solution.py:435
  9.8 1.6 %collective-permute-start.5 = (f32[24,2048]{1,0:T(8,128)S(1)}, f32[24,2048]{1,0:T(8,128)S(1)}, u32[]{:S(2)}, u32[]{:S(2)}) collective-permute-start(f32[24,2048]{1,0:T(8,128)S(1)} %get-tuple-element.29), channel_id=1, source_target_pairs={{0,4},{1,5},{4,0},{5,1},{8,12},{9,13},{12,8},{13,9},{2,6},{3,7},{6... | collective-permute-start | bytes 589832 | tf_op jit(solution)/shard_map/ppermute | solution.py:435
  11.4 0.0 collective-permute-start.9
  12.0 4.2 %place_tiles.1 = (bf16[1024,2048]{1,0:T(8,128)(2,1)S(1)}, bf16[1024,2048]{1,0:T(8,128)(2,1)S(1)}) custom-call(s32[128]{0:T(128)S(1)} %copy-done.2, s32[128]{0:T(128)S(1)} %copy-done.3, s32[1]{0:T(128)S(6)} %copy.9.count, f32[64,8192]{1,0:T(8,128)S(1)} %copy-done, f32[48,1024]{1,0:T(8,128)S(1)} %get-tuple-element.21.refs_0_), custom_call_target="tpu_custom_call" | custom-call | flops 1 | bytes 1 | tf_op jit(solution)/shard_map/place_tiles/pallas_call | solution.py:78
  16.2 0.0 collective-permute-done.refs_1_.sibling
  16.3 0.0 collective-permute-done.2.got
  16.3 0.7 %collective-permute-start.7 = (f32[24,1024]{1,0:T(8,128)S(1)}, f32[24,1024]{1,0:T(8,128)S(1)}, u32[]{:S(2)}, u32[]{:S(2)}) collective-permute-start(f32[24,1024]{1,0:T(8,128)S(1)} %merge_first.1.refs_0_), channel_id=1, source_target_pairs={{0,12},{1,13},{4,8},{5,9},{8,4},{9,5},{12,0},{13,1},{2,14},{3,15},... | collective-permute-start | bytes 294920 | tf_op jit(solution)/shard_map/ppermute | solution.py:435
  17.0 2.0 %collective-permute-start.8 = (f32[24,1024]{1,0:T(8,128)S(1)}, f32[24,1024]{1,0:T(8,128)S(1)}, u32[]{:S(2)}, u32[]{:S(2)}) collective-permute-start(f32[24,1024]{1,0:T(8,128)S(1)} %merge_next.1.refs_1_), channel_id=1, source_target_pairs={{0,13},{1,12},{4,9},{5,8},{8,5},{9,4},{12,1},{13,0},{2,15},{3,14},... | collective-permute-start | bytes 294920 | tf_op jit(solution)/shard_map/ppermute | solution.py:435
  19.0 0.4 collective-permute-done.1.refs_0_.plain
  19.4 0.6 %collective-permute-start.4 = (f32[24,1024]{1,0:T(8,128)S(1)}, f32[24,1024]{1,0:T(8,128)S(1)}, u32[]{:S(2)}, u32[]{:S(2)}) collective-permute-start(f32[24,1024]{1,0:T(8,128)S(1)} %hold.1.refs_0_), channel_id=1, source_target_pairs={{0,2},{2,0},{1,3},{3,1},{4,6},{6,4},{5,7},{7,5},{8,10},{10,8},{9,1... | collective-permute-start | bytes 294920 | tf_op jit(solution)/shard_map/ppermute | solution.py:438
  19.9 2.7 %remap_both.1 = (f32[48,1024]{1,0:T(8,128)S(1)}, f32[48,1024]{1,0:T(8,128)S(1)}) custom-call(f32[24,2048]{1,0:T(8,128)S(1)} %get-tuple-element.18.own, f32[24,2048]{1,0:T(8,128)S(1)} %collective-permute-done.refs_1_.sibling, f32[24,2048]{1,0:T(8,128)S(1)} %collective-permute-done.1.refs_0_.plain, bf16[1024,2048]{1,0:T(8,128)(2,1)S(1)} %get-tuple-element.22.refs_0_.high, ...), custom_call_target="tpu_custom_call" | custom-call | flops 2500000000 | bytes 1 | tf_op jit(solution)/shard_map/remap_both/pallas_call | solution.py:105
  22.7 0.0 collective-permute-done.5.refs_1_.near_same
  22.7 1.6 %collective-permute-start.3 = (f32[48,1024]{1,0:T(8,128)S(1)}, f32[48,1024]{1,0:T(8,128)S(1)}, u32[]{:S(2)}, u32[]{:S(2)}) collective-permute-start(f32[48,1024]{1,0:T(8,128)S(1)} %get-tuple-element.27), channel_id=1, source_target_pairs={{0,2},{2,0},{1,3},{3,1},{4,6},{6,4},{5,7},{7,5},{8,10},{10,8},{9,1... | collective-permute-start | bytes 589832 | tf_op jit(solution)/shard_map/ppermute | solution.py:438
  24.3 0.8 %collective-permute-done.4.got = f32[24,1024]{1,0:T(8,128)S(1)} collective-permute-done((f32[24,1024]{1,0:T(8,128)S(1)}, f32[24,1024]{1,0:T(8,128)S(1)}, u32[]{:S(2)}, u32[]{:S(2)}) %collective-permute-start.4) | collective-permute-done | bytes 98336 | tf_op jit(solution)/shard_map/ppermute | solution.py:438
  25.1 0.1 collective-permute-start.6
  25.2 0.0 collective-permute-done.9.near_other
  25.2 2.6 %remap_near.1.refs_0_.lev_near = f32[48,1024]{1,0:T(8,128)S(1)} custom-call(f32[24,2048]{1,0:T(8,128)S(1)} %collective-permute-done.5.refs_1_.near_same, f32[24,2048]{1,0:T(8,128)S(1)} %collective-permute-done.9.near_other, bf16[1024,2048]{1,0:T(8,128)(2,1)S(1)} %get-tuple-element.22.refs_0_.high, bf16[1024,2048]{1,0:T(8,128)(2,1)S(1)} %get-tuple-element.23.low, ...), custom_call_target="tpu_custom_call" | custom-call | flops 1 | bytes 1 | tf_op jit(solution)/shard_map/remap_near/pallas_call | solution.py:105
  27.8 0.5 %collective-permute-start.11 = (f32[48,1024]{1,0:T(8,128)S(1)}, f32[48,1024]{1,0:T(8,128)S(1)}, u32[]{:S(2)}, u32[]{:S(2)}) collective-permute-start(f32[48,1024]{1,0:T(8,128)S(1)} %remap_near.1.refs_0_.lev_near), channel_id=1, source_target_pairs={{0,2},{2,0},{1,3},{3,1},{4,6},{6,4},{5,7},{7,5},{8,10},{10,8},{9,1... | collective-permute-start | bytes 589832 | tf_op jit(solution)/shard_map/ppermute | solution.py:438
  28.3 0.0 collective-permute-done.8.other
  28.3 0.0 collective-permute-done.7.same
  28.3 2.6 %remap_far.1.refs_0_.far = f32[24,1024]{1,0:T(8,128)S(1)} custom-call(f32[24,1024]{1,0:T(8,128)S(1)} %collective-permute-done.7.same, f32[24,1024]{1,0:T(8,128)S(1)} %collective-permute-done.8.other, bf16[1024,2048]{1,0:T(8,128)(2,1)S(1)} %get-tuple-element.22.refs_0_.high, bf16[1024,2048]{1,0:T(8,128)(2,1)S(1)} %get-tuple-element.23.low, ...), custom_call_target="tpu_custom_call" | custom-call | flops 10000000000 | bytes 1 | tf_op jit(solution)/shard_map/remap_far/pallas_call | solution.py:105
  30.9 1.7 %collective-permute-start.12 = (f32[24,1024]{1,0:T(8,128)S(1)}, f32[24,1024]{1,0:T(8,128)S(1)}, u32[]{:S(2)}, u32[]{:S(2)}) collective-permute-start(f32[24,1024]{1,0:T(8,128)S(1)} %remap_far.1.refs_0_.far), channel_id=1, source_target_pairs={{0,2},{2,0},{1,3},{3,1},{4,6},{6,4},{5,7},{7,5},{8,10},{10,8},{9,1... | collective-permute-start | bytes 294920 | tf_op jit(solution)/shard_map/ppermute | solution.py:438
  32.6 0.3 collective-permute-done.6.block
  32.9 2.4 %remap_last.1.last = f32[24,512]{1,0:T(8,128)S(1)} custom-call(f32[24,1024]{1,0:T(8,128)S(1)} %collective-permute-done.6.block, bf16[1024,2048]{1,0:T(8,128)(2,1)S(1)} %get-tuple-element.22.refs_0_.high, bf16[1024,2048]{1,0:T(8,128)(2,1)S(1)} %get-tuple-element.23.low, f32[24,1024]{1,0:T(8,128)S(1)} %remap_far.1.refs_0_.far), custom_call_target="tpu_custom_call" | custom-call | flops 10000000000 | bytes 1 | tf_op jit(solution)/shard_map/remap_last/pallas_call | solution.py:105
  35.3 0.6 %collective-permute-start.10 = (f32[24,512]{1,0:T(8,128)S(1)}, f32[24,512]{1,0:T(8,128)S(1)}, u32[]{:S(2)}, u32[]{:S(2)}) collective-permute-start(f32[24,512]{1,0:T(8,128)S(1)} %remap_last.1.last), channel_id=1, source_target_pairs={{0,2},{2,0},{1,3},{3,1},{4,6},{6,4},{5,7},{7,5},{8,10},{10,8},{9,1... | collective-permute-start | bytes 147464 | tf_op jit(solution)/shard_map/ppermute | solution.py:438
  35.9 1.1 %collective-permute-done.12.got_far = f32[24,1024]{1,0:T(8,128)S(1)} collective-permute-done((f32[24,1024]{1,0:T(8,128)S(1)}, f32[24,1024]{1,0:T(8,128)S(1)}, u32[]{:S(2)}, u32[]{:S(2)}) %collective-permute-start.12) | collective-permute-done | bytes 98336 | tf_op jit(solution)/shard_map/ppermute | solution.py:438
  36.9 0.8 %write_first.1.begun = f32[96,1024]{1,0:T(8,128)} custom-call(f32[48,1024]{1,0:T(8,128)S(1)} %get-tuple-element.26.refs_0_.chip.plain, f32[48,1024]{1,0:T(8,128)S(1)} %collective-permute-done.3.got_chip.got_plain, f32[48,1024]{1,0:T(8,128)S(1)} %remap_near.1.refs_0_.lev_near, f32[48,1024]{1,0:T(8,128)S(1)} %collective-permute-done.11.got_near, ...), custom_call_target="tpu_custom_call" | custom-call | flops 1 | bytes 1 | tf_op jit(solution)/shard_map/write_first/pallas_call | solution.py:350
  37.7 1.7 %collective-permute-done.10.got_last = f32[24,512]{1,0:T(8,128)S(1)} collective-permute-done((f32[24,512]{1,0:T(8,128)S(1)}, f32[24,512]{1,0:T(8,128)S(1)}, u32[]{:S(2)}, u32[]{:S(2)}) %collective-permute-start.10) | collective-permute-done | bytes 49184 | tf_op jit(solution)/shard_map/ppermute | solution.py:438
  (14 shorter events, 0.1 us)
Async XLA Ops:
  0.0 12.0 %copy-start = (f32[64,8192]{1,0:T(8,128)S(1)}, f32[64,8192]{1,0:T(8,128)}, u32[]{:S(2)}) copy-start(f32[64,8192]{1,0:T(8,128)} %weights.1) | copy-start | bytes 6291460
  0.0 0.8 %copy-start.1 = (s32[8]{0:T(128)S(1)}, s32[8]{0:T(128)}, u32[]{:S(2)}) copy-start(s32[8]{0:T(128)} %step_hour.1) | copy-start | bytes 100
  0.8 11.2 %copy-start.2 = (s32[128]{0:T(128)S(1)}, s32[128]{0:T(128)}, u32[]{:S(2)}) copy-start(s32[128]{0:T(128)} %rows.1) | copy-start | bytes 1540
  0.8 11.2 %copy-start.3 = (s32[128]{0:T(128)S(1)}, s32[128]{0:T(128)}, u32[]{:S(2)}) copy-start(s32[128]{0:T(128)} %columns.1) | copy-start | bytes 1540
  4.1 12.1 %collective-permute-start = (f32[24,2048]{1,0:T(8,128)S(1)}, f32[24,2048]{1,0:T(8,128)S(1)}, u32[]{:S(2)}, u32[]{:S(2)}) collective-permute-start(f32[24,2048]{1,0:T(8,128)S(1)} %get-tuple-element.19), channel_id=1, source_target_pairs={{0,1},{1,0},{4,5},{5,4},{8,9},{9,8},{12,13},{13,12},{2,3},{3,2},{6... | collective-permute-start | bytes 589832 | tf_op jit(solution)/shard_map/ppermute | solution.py:435
  4.6 11.6 %collective-permute-start.2 = (f32[48,1024]{1,0:T(8,128)S(1)}, f32[48,1024]{1,0:T(8,128)S(1)}, u32[]{:S(2)}, u32[]{:S(2)}) collective-permute-start(f32[48,1024]{1,0:T(8,128)S(1)} %get-tuple-element.21.refs_0_), channel_id=1, source_target_pairs={{0,2},{2,0},{1,3},{3,1},{4,6},{6,4},{5,7},{7,5},{8,10},{10,8},{9,1... | collective-permute-start | bytes 589832 | tf_op jit(solution)/shard_map/ppermute | solution.py:438
  7.2 12.2 %collective-permute-start.1 = (f32[24,2048]{1,0:T(8,128)S(1)}, f32[24,2048]{1,0:T(8,128)S(1)}, u32[]{:S(2)}, u32[]{:S(2)}) collective-permute-start(f32[24,2048]{1,0:T(8,128)S(1)} %get-tuple-element.20), channel_id=1, source_target_pairs={{0,8},{1,9},{4,12},{5,13},{8,0},{9,1},{12,4},{13,5},{2,10},{3,11},... | collective-permute-start | bytes 589832 | tf_op jit(solution)/shard_map/ppermute | solution.py:435
  9.8 12.9 %collective-permute-start.5 = (f32[24,2048]{1,0:T(8,128)S(1)}, f32[24,2048]{1,0:T(8,128)S(1)}, u32[]{:S(2)}, u32[]{:S(2)}) collective-permute-start(f32[24,2048]{1,0:T(8,128)S(1)} %get-tuple-element.29), channel_id=1, source_target_pairs={{0,4},{1,5},{4,0},{5,1},{8,12},{9,13},{12,8},{13,9},{2,6},{3,7},{6... | collective-permute-start | bytes 589832 | tf_op jit(solution)/shard_map/ppermute | solution.py:435
  11.4 13.8 %collective-permute-start.9 = (f32[24,2048]{1,0:T(8,128)S(1)}, f32[24,2048]{1,0:T(8,128)S(1)}, u32[]{:S(2)}, u32[]{:S(2)}) collective-permute-start(f32[24,2048]{1,0:T(8,128)S(1)} %get-tuple-element.30), channel_id=1, source_target_pairs={{0,5},{1,4},{4,1},{5,0},{8,13},{9,12},{12,9},{13,8},{2,7},{3,6},{6... | collective-permute-start | bytes 589832 | tf_op jit(solution)/shard_map/ppermute | solution.py:435
  16.3 12.1 %collective-permute-start.7 = (f32[24,1024]{1,0:T(8,128)S(1)}, f32[24,1024]{1,0:T(8,128)S(1)}, u32[]{:S(2)}, u32[]{:S(2)}) collective-permute-start(f32[24,1024]{1,0:T(8,128)S(1)} %merge_first.1.refs_0_), channel_id=1, source_target_pairs={{0,12},{1,13},{4,8},{5,9},{8,4},{9,5},{12,0},{13,1},{2,14},{3,15},... | collective-permute-start | bytes 294920 | tf_op jit(solution)/shard_map/ppermute | solution.py:435
  17.0 11.4 %collective-permute-start.8 = (f32[24,1024]{1,0:T(8,128)S(1)}, f32[24,1024]{1,0:T(8,128)S(1)}, u32[]{:S(2)}, u32[]{:S(2)}) collective-permute-start(f32[24,1024]{1,0:T(8,128)S(1)} %merge_next.1.refs_1_), channel_id=1, source_target_pairs={{0,13},{1,12},{4,9},{5,8},{8,5},{9,4},{12,1},{13,0},{2,15},{3,14},... | collective-permute-start | bytes 294920 | tf_op jit(solution)/shard_map/ppermute | solution.py:435
  19.4 5.7 %collective-permute-start.4 = (f32[24,1024]{1,0:T(8,128)S(1)}, f32[24,1024]{1,0:T(8,128)S(1)}, u32[]{:S(2)}, u32[]{:S(2)}) collective-permute-start(f32[24,1024]{1,0:T(8,128)S(1)} %hold.1.refs_0_), channel_id=1, source_target_pairs={{0,2},{2,0},{1,3},{3,1},{4,6},{6,4},{5,7},{7,5},{8,10},{10,8},{9,1... | collective-permute-start | bytes 294920 | tf_op jit(solution)/shard_map/ppermute | solution.py:438
  22.7 14.3 %collective-permute-start.3 = (f32[48,1024]{1,0:T(8,128)S(1)}, f32[48,1024]{1,0:T(8,128)S(1)}, u32[]{:S(2)}, u32[]{:S(2)}) collective-permute-start(f32[48,1024]{1,0:T(8,128)S(1)} %get-tuple-element.27), channel_id=1, source_target_pairs={{0,2},{2,0},{1,3},{3,1},{4,6},{6,4},{5,7},{7,5},{8,10},{10,8},{9,1... | collective-permute-start | bytes 589832 | tf_op jit(solution)/shard_map/ppermute | solution.py:438
  25.1 7.8 %collective-permute-start.6 = (f32[24,1024]{1,0:T(8,128)S(1)}, f32[24,1024]{1,0:T(8,128)S(1)}, u32[]{:S(2)}, u32[]{:S(2)}) collective-permute-start(f32[24,1024]{1,0:T(8,128)S(1)} %merge_last.1.refs_0_), channel_id=1, source_target_pairs={{0,9},{1,8},{4,13},{5,12},{8,1},{9,0},{12,5},{13,4},{2,11},{3,10},... | collective-permute-start | bytes 294920 | tf_op jit(solution)/shard_map/ppermute | solution.py:435
  27.8 9.1 %collective-permute-start.11 = (f32[48,1024]{1,0:T(8,128)S(1)}, f32[48,1024]{1,0:T(8,128)S(1)}, u32[]{:S(2)}, u32[]{:S(2)}) collective-permute-start(f32[48,1024]{1,0:T(8,128)S(1)} %remap_near.1.refs_0_.lev_near), channel_id=1, source_target_pairs={{0,2},{2,0},{1,3},{3,1},{4,6},{6,4},{5,7},{7,5},{8,10},{10,8},{9,1... | collective-permute-start | bytes 589832 | tf_op jit(solution)/shard_map/ppermute | solution.py:438
  30.9 6.0 %collective-permute-start.12 = (f32[24,1024]{1,0:T(8,128)S(1)}, f32[24,1024]{1,0:T(8,128)S(1)}, u32[]{:S(2)}, u32[]{:S(2)}) collective-permute-start(f32[24,1024]{1,0:T(8,128)S(1)} %remap_far.1.refs_0_.far), channel_id=1, source_target_pairs={{0,2},{2,0},{1,3},{3,1},{4,6},{6,4},{5,7},{7,5},{8,10},{10,8},{9,1... | collective-permute-start | bytes 294920 | tf_op jit(solution)/shard_map/ppermute | solution.py:438
  35.3 4.1 %collective-permute-start.10 = (f32[24,512]{1,0:T(8,128)S(1)}, f32[24,512]{1,0:T(8,128)S(1)}, u32[]{:S(2)}, u32[]{:S(2)}) collective-permute-start(f32[24,512]{1,0:T(8,128)S(1)} %remap_last.1.last), channel_id=1, source_target_pairs={{0,2},{2,0},{1,3},{3,1},{4,6},{6,4},{5,7},{7,5},{8,10},{10,8},{9,1... | collective-permute-start | bytes 147464 | tf_op jit(solution)/shard_map/ppermute | solution.py:438

commit v11 on v10

--- a/solution.py
+++ b/solution.py
@@ -171,16 +171,21 @@
 
 
 def remap_near_kernel(near_same, near_other, high, low, *refs):
+    outs = refs[-HOURS:]
     rows = near_same.shape[0]
     x = jnp.concatenate(near_rows(near_same[...], near_other[...]), axis=0)
     for at, result in remap_blocks(x, high, low):
-        refs[-1][:, at] = by_hour(result, rows // HOURS)
-
-
-def remap_far_kernel(same, other, high, low, *refs):
+        result = by_hour(result, rows // HOURS)
+        for hour, out in enumerate(outs):
+            out[:, at] = result[hour * rows : (hour + 1) * rows]
+
+
+def remap_far_kernel(same, other, near, high, low, *refs):
+    far, send = refs[-2:]
     x = jnp.concatenate(far_rows(same[...], other[...]), axis=0)
     for at, result in remap_blocks(x, high, low):
-        refs[-1][:, at] = result
+        far[:, at] = result
+        send[:, at] = jnp.where(keeps_near(), result, near[:, at])
 
 
 def remap_last_kernel(block, high, low, *refs):
@@ -364,21 +369,22 @@
     return pl.ds(pl.multiple_of(start * 2 * levels, 2 * levels), 2 * levels)
 
 
-def write_first_kernel(divisor, levels, chip, got_chip, lev_near, got_near, far, got_far, out):
+def write_first_kernel(divisor, levels, chip, got_chip, first_hour, got_first, second_hour, far, got, out):
     me = lax.axis_index("tm")
     rows = 2 * levels
     near = keeps_near()
+    sums = [(first_hour, got_first), (second_hour, got)]
     for hour in range(HOURS):
         here = slice(hour * rows, (hour + 1) * rows)
 
         @pl.when(near)
         def _():
             out[output_rows(True, hour, levels), :] = (chip[here] + got_chip[here]) / divisor
-            out[output_rows(False, hour, levels), :] = (lev_near[here] + got_near[here]) / divisor
+            out[output_rows(False, hour, levels), :] = (sums[hour][0][...] + sums[hour][1][...]) / divisor
 
         @pl.when(jnp.logical_not(near))
         def _():
-            out[output_rows(False, hour, levels), :] = jnp.where(me == hour, far[...], got_far[...]) / divisor
+            out[output_rows(False, hour, levels), :] = jnp.where(me == hour, far[...], got[...]) / divisor
 
 
 def write_last_kernel(divisor, levels, plain, got_plain, last, got_last, begun, out, stage, written):
@@ -472,12 +478,14 @@
         merge_last_kernel, [mine_1, got_1], [both, near_got[0]], [folded], HEAVY, "merge_last"
     )
     second_got = to_peer(merged[0], *second)
-    (near,) = remap_call(
-        remap_near_kernel, near_got, merged, [2 * rows], high, low, LIGHT, "remap_near"
-    )
-    got_near = swap(near)
-    (far,) = remap_call(remap_far_kernel, [far_same, far_other], [near], [rows], high, low, HEAVY, "remap_far")
-    got_far = swap(far)
+    first_hour, second_hour = remap_call(
+        remap_near_kernel, near_got, merged, [rows] * HOURS, high, low, LIGHT, "remap_near"
+    )
+    got_first = swap(first_hour)
+    far, send = remap_call(
+        remap_far_kernel, [far_same, far_other, second_hour], [], [rows] * 2, high, low, HEAVY, "remap_far"
+    )
+    got = swap(send)
     padded = -(-rows // 32) * 16
     (last,) = remap_call(
         remap_last_kernel,
@@ -492,7 +500,7 @@
     )
     got_last = swap(last)
     levels = rows // 2
-    out = write_first([both, got_both, near, got_near, far, got_far], levels, divisor)
+    out = write_first([both, got_both, first_hour, got_first, second_hour, far, got], levels, divisor)
     out = write_last(out, [both, got_both, last, got_last], levels, divisor)
     return out.reshape(HOURS, out.shape[0] // HOURS, PIXELS_DEV)
 

time: 39.6 us -> 39.6 us (level)
  waiting for transfers between devices: 4.29 us -> 3.16 us
  starting transfers between devices: 14.9 us -> 15.9 us
    ppermute x7, starting transfers between devices: 7.44 us -> 8.47 us  [to_peer(): return lax.ppermute(x, ('lev', 'sub'), pairs)]
    ppermute x6, waiting for transfers between devices: 3.55 us -> 2.97 us  [swap(): return lax.ppermute(x, 'tm', [(0, 1), (1, 0)])]
    ppermute x7, waiting for transfers between devices: 0.74 us -> 0.2 us  [to_peer(): return lax.ppermute(x, ('lev', 'sub'), pairs)]
  transfers between devices with their start and end apart: 13 -> 13, of which waited for: 5 -> 4; matrix products, arithmetic and copies ran while one was open for 0% -> 0% of each run, Pallas kernels for 39% -> 39%
where the time goes in v11:
time: 39.6 us; the launch traced here: 39.5 us
  Pallas kernels  18.8 us (47%)
  starting transfers between devices  15.9 us (40%)
  waiting for transfers between devices  3.16 us (8%)
  local copies, waits for them, and re-layouts  0.82 us (2%)
  between operations  0.78 us (2%)
    pallas_call x4, Pallas kernels, remap_call(): pl.pallas_call(kernel, out_shape=[jax.ShapeDtypeStruct(rows if isinstance...  10.3 us
    ppermute x7, starting transfers between devices, to_peer(): return lax.ppermute(x, ('lev', 'sub'), pairs)  8.47 us
    ppermute x6, starting transfers between devices, swap(): return lax.ppermute(x, 'tm', [(0, 1), (1, 0)])  7.43 us
    pallas_call x1, Pallas kernels, place_tiles(): pl.pallas_call(place_kernel, out_shape=(half, half), in_specs=[smem, smem...  4.32 us
    pallas_call x1, Pallas kernels, hour_sums(): pl.pallas_call(functools.partial(sums_kernel, plain, first, second), out_...  3.28 us
    ppermute x6, waiting for transfers between devices, swap(): return lax.ppermute(x, 'tm', [(0, 1), (1, 0)])  2.97 us
    pallas_call x5, Pallas kernels, small_call(): pl.pallas_call(kernel, out_shape=[jax.ShapeDtypeStruct(shape, jnp.float32...  0.85 us
    unnamed x8, local copies, waits for them, and re-layouts  0.82 us
  transfers between devices with their start and end apart: 13, of which 4 were waited for; matrix products, arithmetic and copies ran while one was open for 0% of the time, Pallas kernels for 39%

profile of v11, /device:TPU:0, one launch (start us, length us, event | category | flops | bytes accessed | tf_op | source)
XLA Modules:
  0.0 39.5 jit_solution(1802224952887876084)
XLA Ops:
  0.0 0.8 %copy-done.1 = s32[8]{0:T(128)S(1)} copy-done((s32[8]{0:T(128)S(1)}, s32[8]{0:T(128)}, u32[]{:S(2)}) %copy-start.1) | copy-done | bytes 56
  0.8 3.3 %hour_sums.1 = (f32[24,2048]{1,0:T(8,128)S(1)}, f32[24,2048]{1,0:T(8,128)S(1)}, f32[24,2048]{1,0:T(8,128)S(1)}, f32[24,2048]{1,0:T(8,128)S(1)}, f32[24,2048]{1,0...) custom-call(s32[8]{0:T(128)S(1)} %copy-done.1, ...), custom_call_target="tpu_custom_call" | custom-call | flops 1 | bytes 1 | tf_op jit(solution)/shard_map/hour_sums/pallas_call | solution.py:312
  4.1 0.5 %collective-permute-start = (f32[24,2048]{1,0:T(8,128)S(1)}, f32[24,2048]{1,0:T(8,128)S(1)}, u32[]{:S(2)}, u32[]{:S(2)}) collective-permute-start(f32[24,2048]{1,0:T(8,128)S(1)} %get-tuple-element.23), channel_id=1, source_target_pairs={{0,1},{1,0},{4,5},{5,4},{8,9},{9,8},{12,13},{13,12},{2,3},{3,2},{6... | collective-permute-start | bytes 589832 | tf_op jit(solution)/shard_map/ppermute | solution.py:441
  4.6 2.6 %collective-permute-start.2 = (f32[48,1024]{1,0:T(8,128)S(1)}, f32[48,1024]{1,0:T(8,128)S(1)}, u32[]{:S(2)}, u32[]{:S(2)}) collective-permute-start(f32[48,1024]{1,0:T(8,128)S(1)} %get-tuple-element.25.refs_0_), channel_id=1, source_target_pairs={{0,2},{2,0},{1,3},{3,1},{4,6},{6,4},{5,7},{7,5},{8,10},{10,8},{9,1... | collective-permute-start | bytes 589832 | tf_op jit(solution)/shard_map/ppermute | solution.py:444
  7.2 2.6 %collective-permute-start.1 = (f32[24,2048]{1,0:T(8,128)S(1)}, f32[24,2048]{1,0:T(8,128)S(1)}, u32[]{:S(2)}, u32[]{:S(2)}) collective-permute-start(f32[24,2048]{1,0:T(8,128)S(1)} %get-tuple-element.24), channel_id=1, source_target_pairs={{0,8},{1,9},{4,12},{5,13},{8,0},{9,1},{12,4},{13,5},{2,10},{3,11},... | collective-permute-start | bytes 589832 | tf_op jit(solution)/shard_map/ppermute | solution.py:441
  9.8 1.6 %collective-permute-start.5 = (f32[24,2048]{1,0:T(8,128)S(1)}, f32[24,2048]{1,0:T(8,128)S(1)}, u32[]{:S(2)}, u32[]{:S(2)}) collective-permute-start(f32[24,2048]{1,0:T(8,128)S(1)} %get-tuple-element.33), channel_id=1, source_target_pairs={{0,4},{1,5},{4,0},{5,1},{8,12},{9,13},{12,8},{13,9},{2,6},{3,7},{6... | collective-permute-start | bytes 589832 | tf_op jit(solution)/shard_map/ppermute | solution.py:441
  11.4 0.0 collective-permute-start.9
  12.0 4.3 %place_tiles.1 = (bf16[1024,2048]{1,0:T(8,128)(2,1)S(1)}, bf16[1024,2048]{1,0:T(8,128)(2,1)S(1)}) custom-call(s32[128]{0:T(128)S(1)} %copy-done.2, s32[128]{0:T(128)S(1)} %copy-done.3, s32[1]{0:T(128)S(6)} %copy.9.count, f32[64,8192]{1,0:T(8,128)S(1)} %copy-done, f32[48,1024]{1,0:T(8,128)S(1)} %get-tuple-element.25.refs_0_), custom_call_target="tpu_custom_call" | custom-call | flops 1 | bytes 1 | tf_op jit(solution)/shard_map/place_tiles/pallas_call | solution.py:78
  16.4 0.0 collective-permute-done.refs_1_.sibling
  16.4 0.0 collective-permute-done.2.got
  16.4 0.2 collective-permute-start.7
  16.6 3.5 %collective-permute-start.8 = (f32[24,1024]{1,0:T(8,128)S(1)}, f32[24,1024]{1,0:T(8,128)S(1)}, u32[]{:S(2)}, u32[]{:S(2)}) collective-permute-start(f32[24,1024]{1,0:T(8,128)S(1)} %merge_next.1.refs_1_), channel_id=1, source_target_pairs={{0,13},{1,12},{4,9},{5,8},{8,5},{9,4},{12,1},{13,0},{2,15},{3,14},... | collective-permute-start | bytes 294920 | tf_op jit(solution)/shard_map/ppermute | solution.py:441
  20.1 0.0 collective-permute-done.1.refs_0_.plain
  20.2 0.6 %collective-permute-start.4 = (f32[24,1024]{1,0:T(8,128)S(1)}, f32[24,1024]{1,0:T(8,128)S(1)}, u32[]{:S(2)}, u32[]{:S(2)}) collective-permute-start(f32[24,1024]{1,0:T(8,128)S(1)} %hold.1.refs_0_), channel_id=1, source_target_pairs={{0,2},{2,0},{1,3},{3,1},{4,6},{6,4},{5,7},{7,5},{8,10},{10,8},{9,1... | collective-permute-start | bytes 294920 | tf_op jit(solution)/shard_map/ppermute | solution.py:444
  20.8 2.7 %remap_both.1 = (f32[48,1024]{1,0:T(8,128)S(1)}, f32[48,1024]{1,0:T(8,128)S(1)}) custom-call(f32[24,2048]{1,0:T(8,128)S(1)} %get-tuple-element.22.own, f32[24,2048]{1,0:T(8,128)S(1)} %collective-permute-done.refs_1_.sibling, f32[24,2048]{1,0:T(8,128)S(1)} %collective-permute-done.1.refs_0_.plain, bf16[1024,2048]{1,0:T(8,128)(2,1)S(1)} %get-tuple-element.26.refs_0_.high, ...), custom_call_target="tpu_custom_call" | custom-call | flops 2500000000 | bytes 1 | tf_op jit(solution)/shard_map/remap_both/pallas_call | solution.py:105
  23.5 0.0 collective-permute-done.5.refs_1_.near_same
  23.5 1.6 %collective-permute-start.3 = (f32[48,1024]{1,0:T(8,128)S(1)}, f32[48,1024]{1,0:T(8,128)S(1)}, u32[]{:S(2)}, u32[]{:S(2)}) collective-permute-start(f32[48,1024]{1,0:T(8,128)S(1)} %get-tuple-element.31), channel_id=1, source_target_pairs={{0,2},{2,0},{1,3},{3,1},{4,6},{6,4},{5,7},{7,5},{8,10},{10,8},{9,1... | collective-permute-start | bytes 589832 | tf_op jit(solution)/shard_map/ppermute | solution.py:444
  25.1 0.2 collective-permute-done.4.got
  25.3 0.1 collective-permute-start.6
  25.4 0.0 collective-permute-done.9.near_other
  25.4 2.6 %remap_near.1 = (f32[24,1024]{1,0:T(8,128)S(1)}, f32[24,1024]{1,0:T(8,128)S(1)}) custom-call(f32[24,2048]{1,0:T(8,128)S(1)} %collective-permute-done.5.refs_1_.near_same, f32[24,2048]{1,0:T(8,128)S(1)} %collective-permute-done.9.near_other, bf16[1024,2048]{1,0:T(8,128)(2,1)S(1)} %get-tuple-element.26.refs_0_.high, ...), custom_call_target="tpu_custom_call" | custom-call | flops 1 | bytes 1 | tf_op jit(solution)/shard_map/remap_near/pallas_call | solution.py:105
  28.0 0.6 %collective-permute-start.11 = (f32[24,1024]{1,0:T(8,128)S(1)}, f32[24,1024]{1,0:T(8,128)S(1)}, u32[]{:S(2)}, u32[]{:S(2)}) collective-permute-start(f32[24,1024]{1,0:T(8,128)S(1)} %get-tuple-element.37.first_hour), channel_id=1, source_target_pairs={{0,2},{2,0},{1,3},{3,1},{4,6},{6,4},{5,7},{7,5},{8,10},{10,8},{9,1... | collective-permute-start | bytes 294920 | tf_op jit(solution)/shard_map/ppermute | solution.py:444
  28.6 0.0 collective-permute-done.8.other
  28.6 2.6 %remap_far.1 = (f32[24,1024]{1,0:T(8,128)S(1)}, f32[24,1024]{1,0:T(8,128)S(1)}) custom-call(f32[24,1024]{1,0:T(8,128)S(1)} %collective-permute-done.7.same, f32[24,1024]{1,0:T(8,128)S(1)} %collective-permute-done.8.other, f32[24,1024]{1,0:T(8,128)S(1)} %get-tuple-element.35.near.second_hour, bf16[1024,2048]{1,0:T(8,128)(2,1)S(1)} %get-tuple-element.26.refs_0_.high, ...), custom_call_target="tpu_custom_call" | custom-call | flops 10000000000 | bytes 1 | tf_op jit(solution)/shard_map/remap_far/pallas_call | solution.py:105
  31.2 1.6 %collective-permute-start.12 = (f32[24,1024]{1,0:T(8,128)S(1)}, f32[24,1024]{1,0:T(8,128)S(1)}, u32[]{:S(2)}, u32[]{:S(2)}) collective-permute-start(f32[24,1024]{1,0:T(8,128)S(1)} %get-tuple-element.38), channel_id=1, source_target_pairs={{0,2},{2,0},{1,3},{3,1},{4,6},{6,4},{5,7},{7,5},{8,10},{10,8},{9,1... | collective-permute-start | bytes 294920 | tf_op jit(solution)/shard_map/ppermute | solution.py:444
  32.8 0.2 collective-permute-done.6.block
  33.0 2.4 %remap_last.1.last = f32[24,512]{1,0:T(8,128)S(1)} custom-call(f32[24,1024]{1,0:T(8,128)S(1)} %collective-permute-done.6.block, bf16[1024,2048]{1,0:T(8,128)(2,1)S(1)} %get-tuple-element.26.refs_0_.high, bf16[1024,2048]{1,0:T(8,128)(2,1)S(1)} %get-tuple-element.27.low, f32[24,1024]{1,0:T(8,128)S(1)} %get-tuple-element.36.refs_0_.far), custom_call_target="tpu_custom_call" | custom-call | flops 10000000000 | bytes 1 | tf_op jit(solution)/shard_map/remap_last/pallas_call | solution.py:105
  35.3 0.6 %collective-permute-start.10 = (f32[24,512]{1,0:T(8,128)S(1)}, f32[24,512]{1,0:T(8,128)S(1)}, u32[]{:S(2)}, u32[]{:S(2)}) collective-permute-start(f32[24,512]{1,0:T(8,128)S(1)} %remap_last.1.last), channel_id=1, source_target_pairs={{0,2},{2,0},{1,3},{3,1},{4,6},{6,4},{5,7},{7,5},{8,10},{10,8},{9,1... | collective-permute-start | bytes 147464 | tf_op jit(solution)/shard_map/ppermute | solution.py:444
  35.9 0.0 collective-permute-done.11.got_first
  35.9 0.3 collective-permute-done.12.got
  36.3 0.8 %write_first.1.begun = f32[96,1024]{1,0:T(8,128)} custom-call(f32[48,1024]{1,0:T(8,128)S(1)} %get-tuple-element.30.refs_0_.chip.plain, f32[48,1024]{1,0:T(8,128)S(1)} %collective-permute-done.3.got_chip.got_plain, f32[24,1024]{1,0:T(8,128)S(1)} %get-tuple-element.37.first_hour, f32[24,1024]{1,0:T(8,128)S(1)} %collective-permute-done.11.got_first, ...), custom_call_target="tpu_custom_call" | custom-call | flops 1 | bytes 1 | tf_op jit(solution)/shard_map/write_first/pallas_call | solution.py:355
  37.0 2.4 %collective-permute-done.10.got_last = f32[24,512]{1,0:T(8,128)S(1)} collective-permute-done((f32[24,512]{1,0:T(8,128)S(1)}, f32[24,512]{1,0:T(8,128)S(1)}, u32[]{:S(2)}, u32[]{:S(2)}) %collective-permute-start.10) | collective-permute-done | bytes 49184 | tf_op jit(solution)/shard_map/ppermute | solution.py:444
  (14 shorter events, 0.1 us)
Async XLA Ops:
  0.0 12.0 %copy-start = (f32[64,8192]{1,0:T(8,128)S(1)}, f32[64,8192]{1,0:T(8,128)}, u32[]{:S(2)}) copy-start(f32[64,8192]{1,0:T(8,128)} %weights.1) | copy-start | bytes 6291460
  0.0 0.8 %copy-start.1 = (s32[8]{0:T(128)S(1)}, s32[8]{0:T(128)}, u32[]{:S(2)}) copy-start(s32[8]{0:T(128)} %step_hour.1) | copy-start | bytes 100
  0.8 11.2 %copy-start.2 = (s32[128]{0:T(128)S(1)}, s32[128]{0:T(128)}, u32[]{:S(2)}) copy-start(s32[128]{0:T(128)} %rows.1) | copy-start | bytes 1540
  0.8 11.2 %copy-start.3 = (s32[128]{0:T(128)S(1)}, s32[128]{0:T(128)}, u32[]{:S(2)}) copy-start(s32[128]{0:T(128)} %columns.1) | copy-start | bytes 1540
  4.1 12.3 %collective-permute-start = (f32[24,2048]{1,0:T(8,128)S(1)}, f32[24,2048]{1,0:T(8,128)S(1)}, u32[]{:S(2)}, u32[]{:S(2)}) collective-permute-start(f32[24,2048]{1,0:T(8,128)S(1)} %get-tuple-element.23), channel_id=1, source_target_pairs={{0,1},{1,0},{4,5},{5,4},{8,9},{9,8},{12,13},{13,12},{2,3},{3,2},{6... | collective-permute-start | bytes 589832 | tf_op jit(solution)/shard_map/ppermute | solution.py:441
  4.6 11.8 %collective-permute-start.2 = (f32[48,1024]{1,0:T(8,128)S(1)}, f32[48,1024]{1,0:T(8,128)S(1)}, u32[]{:S(2)}, u32[]{:S(2)}) collective-permute-start(f32[48,1024]{1,0:T(8,128)S(1)} %get-tuple-element.25.refs_0_), channel_id=1, source_target_pairs={{0,2},{2,0},{1,3},{3,1},{4,6},{6,4},{5,7},{7,5},{8,10},{10,8},{9,1... | collective-permute-start | bytes 589832 | tf_op jit(solution)/shard_map/ppermute | solution.py:444
  7.2 13.0 %collective-permute-start.1 = (f32[24,2048]{1,0:T(8,128)S(1)}, f32[24,2048]{1,0:T(8,128)S(1)}, u32[]{:S(2)}, u32[]{:S(2)}) collective-permute-start(f32[24,2048]{1,0:T(8,128)S(1)} %get-tuple-element.24), channel_id=1, source_target_pairs={{0,8},{1,9},{4,12},{5,13},{8,0},{9,1},{12,4},{13,5},{2,10},{3,11},... | collective-permute-start | bytes 589832 | tf_op jit(solution)/shard_map/ppermute | solution.py:441
  9.8 13.7 %collective-permute-start.5 = (f32[24,2048]{1,0:T(8,128)S(1)}, f32[24,2048]{1,0:T(8,128)S(1)}, u32[]{:S(2)}, u32[]{:S(2)}) collective-permute-start(f32[24,2048]{1,0:T(8,128)S(1)} %get-tuple-element.33), channel_id=1, source_target_pairs={{0,4},{1,5},{4,0},{5,1},{8,12},{9,13},{12,8},{13,9},{2,6},{3,7},{6... | collective-permute-start | bytes 589832 | tf_op jit(solution)/shard_map/ppermute | solution.py:441
  11.4 14.0 %collective-permute-start.9 = (f32[24,2048]{1,0:T(8,128)S(1)}, f32[24,2048]{1,0:T(8,128)S(1)}, u32[]{:S(2)}, u32[]{:S(2)}) collective-permute-start(f32[24,2048]{1,0:T(8,128)S(1)} %get-tuple-element.34), channel_id=1, source_target_pairs={{0,5},{1,4},{4,1},{5,0},{8,13},{9,12},{12,9},{13,8},{2,7},{3,6},{6... | collective-permute-start | bytes 589832 | tf_op jit(solution)/shard_map/ppermute | solution.py:441
  16.4 12.2 %collective-permute-start.7 = (f32[24,1024]{1,0:T(8,128)S(1)}, f32[24,1024]{1,0:T(8,128)S(1)}, u32[]{:S(2)}, u32[]{:S(2)}) collective-permute-start(f32[24,1024]{1,0:T(8,128)S(1)} %merge_first.1.refs_0_), channel_id=1, source_target_pairs={{0,12},{1,13},{4,8},{5,9},{8,4},{9,5},{12,0},{13,1},{2,14},{3,15},... | collective-permute-start | bytes 294920 | tf_op jit(solution)/shard_map/ppermute | solution.py:441
  16.6 12.0 %collective-permute-start.8 = (f32[24,1024]{1,0:T(8,128)S(1)}, f32[24,1024]{1,0:T(8,128)S(1)}, u32[]{:S(2)}, u32[]{:S(2)}) collective-permute-start(f32[24,1024]{1,0:T(8,128)S(1)} %merge_next.1.refs_1_), channel_id=1, source_target_pairs={{0,13},{1,12},{4,9},{5,8},{8,5},{9,4},{12,1},{13,0},{2,15},{3,14},... | collective-permute-start | bytes 294920 | tf_op jit(solution)/shard_map/ppermute | solution.py:441
  20.2 5.1 %collective-permute-start.4 = (f32[24,1024]{1,0:T(8,128)S(1)}, f32[24,1024]{1,0:T(8,128)S(1)}, u32[]{:S(2)}, u32[]{:S(2)}) collective-permute-start(f32[24,1024]{1,0:T(8,128)S(1)} %hold.1.refs_0_), channel_id=1, source_target_pairs={{0,2},{2,0},{1,3},{3,1},{4,6},{6,4},{5,7},{7,5},{8,10},{10,8},{9,1... | collective-permute-start | bytes 294920 | tf_op jit(solution)/shard_map/ppermute | solution.py:444
  23.5 12.7 %collective-permute-start.3 = (f32[48,1024]{1,0:T(8,128)S(1)}, f32[48,1024]{1,0:T(8,128)S(1)}, u32[]{:S(2)}, u32[]{:S(2)}) collective-permute-start(f32[48,1024]{1,0:T(8,128)S(1)} %get-tuple-element.31), channel_id=1, source_target_pairs={{0,2},{2,0},{1,3},{3,1},{4,6},{6,4},{5,7},{7,5},{8,10},{10,8},{9,1... | collective-permute-start | bytes 589832 | tf_op jit(solution)/shard_map/ppermute | solution.py:444
  25.3 7.7 %collective-permute-start.6 = (f32[24,1024]{1,0:T(8,128)S(1)}, f32[24,1024]{1,0:T(8,128)S(1)}, u32[]{:S(2)}, u32[]{:S(2)}) collective-permute-start(f32[24,1024]{1,0:T(8,128)S(1)} %merge_last.1.refs_0_), channel_id=1, source_target_pairs={{0,9},{1,8},{4,13},{5,12},{8,1},{9,0},{12,5},{13,4},{2,11},{3,10},... | collective-permute-start | bytes 294920 | tf_op jit(solution)/shard_map/ppermute | solution.py:441
  28.0 7.9 %collective-permute-start.11 = (f32[24,1024]{1,0:T(8,128)S(1)}, f32[24,1024]{1,0:T(8,128)S(1)}, u32[]{:S(2)}, u32[]{:S(2)}) collective-permute-start(f32[24,1024]{1,0:T(8,128)S(1)} %get-tuple-element.37.first_hour), channel_id=1, source_target_pairs={{0,2},{2,0},{1,3},{3,1},{4,6},{6,4},{5,7},{7,5},{8,10},{10,8},{9,1... | collective-permute-start | bytes 294920 | tf_op jit(solution)/shard_map/ppermute | solution.py:444
  31.2 5.0 %collective-permute-start.12 = (f32[24,1024]{1,0:T(8,128)S(1)}, f32[24,1024]{1,0:T(8,128)S(1)}, u32[]{:S(2)}, u32[]{:S(2)}) collective-permute-start(f32[24,1024]{1,0:T(8,128)S(1)} %get-tuple-element.38), channel_id=1, source_target_pairs={{0,2},{2,0},{1,3},{3,1},{4,6},{6,4},{5,7},{7,5},{8,10},{10,8},{9,1... | collective-permute-start | bytes 294920 | tf_op jit(solution)/shard_map/ppermute | solution.py:444
  35.3 4.1 %collective-permute-start.10 = (f32[24,512]{1,0:T(8,128)S(1)}, f32[24,512]{1,0:T(8,128)S(1)}, u32[]{:S(2)}, u32[]{:S(2)}) collective-permute-start(f32[24,512]{1,0:T(8,128)S(1)} %remap_last.1.last), channel_id=1, source_target_pairs={{0,2},{2,0},{1,3},{3,1},{4,6},{6,4},{5,7},{7,5},{8,10},{10,8},{9,1... | collective-permute-start | bytes 147464 | tf_op jit(solution)/shard_map/ppermute | solution.py:444

commit v12 on v11

--- a/solution.py
+++ b/solution.py
@@ -256,11 +256,12 @@
 SUM_WIDTH = 512
 
 
-def sums_kernel(plain, first, second, step_hour, field, *refs):
-    *outs, buffer, arrived, hours, hours_arrived = refs
+def sums_kernel(plain, chunks, step_hour, field, *refs):
+    buffer, arrived, hours, hours_arrived = refs[-4:]
+    outs = refs[-4 - len(plain) - 2 * len(chunks) : -4]
     _, levels, steps, cells = buffer.shape
     rows, cut = HOURS * levels, cells // 2
-    copies = field_copies(field, buffer, arrived, [*plain, *first, second])
+    copies = field_copies(field, buffer, arrived, [*plain, *sum(chunks, [])])
     fetch = pltpu.make_async_copy(step_hour, hours, hours_arrived)
     fetch.start()
     fetch.wait()
@@ -286,33 +287,36 @@
             pieces = [(x, half) for half in range(HOURS) for x in sums]
             store(outs[place], 0, start, SUM_WIDTH, pieces)
 
-    theirs_first, mine_first, theirs_second, mine_second = outs[len(plain) :]
     width = SUM_WIDTH // 2
     weights = hour_weights(hours, steps, (1 - me, me), width)
-    for j in range(len(first) + 1):
-        place = len(plain) + j
-        copies[place].wait()
-        offset = j * rows if j < len(first) else 0
-        theirs, mine = (theirs_first, mine_first) if j < len(first) else (theirs_second, mine_second)
-
-        @pl.loop(0, cut // width)
-        def _(i):
-            start = pl.multiple_of(i * width, width)
-            sums = summed(place, start, width, weights) + summed(place, cut + start, width, weights)
-            store(theirs, offset, start, width, [(x, 0) for x in sums])
-            store(mine, offset, start, width, [(x, 1) for x in sums])
-
-
-def hour_sums(plain, first, second, step_hour, field):
+    place = len(plain)
+    for chunk, members in enumerate(chunks):
+        theirs, mine = outs[len(plain) + 2 * chunk], outs[len(plain) + 2 * chunk + 1]
+        for j in range(len(members)):
+            copies[place].wait()
+
+            @pl.loop(0, cut // width)
+            def _(i):
+                start = pl.multiple_of(i * width, width)
+                sums = summed(place, start, width, weights) + summed(place, cut + start, width, weights)
+                store(theirs, j * rows, start, width, [(x, 0) for x in sums])
+                store(mine, j * rows, start, width, [(x, 1) for x in sums])
+
+            place += 1
+
+
+def hour_sums(plain, chunks, step_hour, field, *after):
     levels, steps, _ = field.shape
     rows, cut = HOURS * levels, CELLS_DEV // 2
     vmem = pl.BlockSpec(memory_space=pltpu.VMEM)
-    shapes = [(rows, CELLS_DEV)] * len(plain) + [(len(first) * rows, cut)] * 2 + [(rows, cut)] * 2
-    count = len(plain) + len(first) + 1
+    shapes = [(rows, CELLS_DEV)] * len(plain)
+    for members in chunks:
+        shapes += [(len(members) * rows, cut)] * 2
+    count = len(plain) + sum(map(len, chunks))
     outs = pl.pallas_call(
-        functools.partial(sums_kernel, plain, first, second),
+        functools.partial(sums_kernel, plain, chunks),
         out_shape=[jax.ShapeDtypeStruct(shape, jnp.float32) for shape in shapes],
-        in_specs=[pl.BlockSpec(memory_space=pl.ANY)] * 2,
+        in_specs=[pl.BlockSpec(memory_space=pl.ANY)] * (2 + len(after)),
         out_specs=[vmem] * len(shapes),
         scratch_shapes=[
             pltpu.VMEM((count, levels, steps, CELLS_DEV), jnp.float32),
@@ -323,7 +327,7 @@
         compiler_params=pltpu.CompilerParams(vmem_limit_bytes=52 * MIB),
         cost_estimate=LIGHT,
         name="hour_sums",
-    )(step_hour, field)
+    )(step_hour, field, *after)
     return outs[: len(plain)], outs[len(plain) :]
 
 
@@ -443,28 +447,31 @@
     def swap(x):
         return lax.ppermute(x, "tm", [(0, 1), (1, 0)])
 
-    plain = [(half, 0), (1, 0), (1, 1), (0, 1), (0, 0)]
+    plain, lev_near = (half, 0), [(1, j) for j in range(subs)]
     first, second = [(half + 1, j) for j in range(subs)], (half, 1)
-    sums, (theirs_0, mine_0, theirs_1, mine_1) = hour_sums(plain, first, second, step_hour, field)
+    (plain_sums, sibling), (theirs_0, mine_0) = hour_sums([plain, (0, 1)], [first], step_hour, field)
     rows = 2 * field.shape[0]
+    sibling = to_peer(sibling, 0, 1)
+    got_0 = swap(theirs_0)
+    plain_got = to_peer(plain_sums, *plain)
+    (*near_sums, own), (theirs_1, mine_1) = hour_sums(
+        [*lev_near, (0, 0)], [[second]], step_hour, field, theirs_0
+    )
     folded = theirs_1.shape
-    sibling = to_peer(sums[3], *plain[3])
-    near_got = [to_peer(x, *peer) for x, peer in list(zip(sums, plain))[1:3]]
-    got_0 = swap(theirs_0)
-    plain_got = to_peer(sums[0], *plain[0])
-    high, low = place_tiles(tile_rows, tile_columns, live_count, tile_weight, theirs_0)
+    near_got = [to_peer(x, *peer) for x, peer in zip(near_sums, lev_near)]
 
     merged = small_call(
-        merge_first_kernel, [mine_0, got_0], [high, sibling], [folded], LIGHT, "merge_first"
+        merge_first_kernel, [mine_0, got_0], [sibling, theirs_1], [folded], LIGHT, "merge_first"
     )
     far_same = to_peer(merged[0], *first[0])
     merged = small_call(merge_next_kernel, [mine_0, got_0], merged, [folded], LIGHT, "merge_next")
     far_other = to_peer(merged[0], *first[1])
-    theirs_1 = small_call(hold_kernel, [theirs_1], [plain_got, *merged], [folded], LIGHT, "hold")[0]
+    high, low = place_tiles(tile_rows, tile_columns, live_count, tile_weight, *merged)
+    theirs_1 = small_call(hold_kernel, [theirs_1], [plain_got, high], [folded], LIGHT, "hold")[0]
     got_1 = swap(theirs_1)
     both, send = remap_call(
         remap_both_kernel,
-        [sums[4], sibling, plain_got],
+        [own, sibling, plain_got],
         [theirs_1],
         [2 * rows] * 2,
         high,

time: 39.6 us -> 42.4 us (1.071)
  waiting for transfers between devices: 3.16 us -> 4.82 us
  Pallas kernels: 18.8 us -> 19.9 us
    ppermute x7, waiting for transfers between devices: 0.2 us -> 1.5 us  [to_peer(): return lax.ppermute(x, ('lev', 'sub'), pairs)]
    pallas_call x1 -> x2, Pallas kernels: 3.28 us -> 4.41 us  [hour_sums(): pl.pallas_call(functools.partial(sums_kernel, plain, chunks), out_shape=[...]
  transfers between devices with their start and end apart: 13 -> 13, of which waited for: 4 -> 4; matrix products, arithmetic and copies ran while one was open for 0% -> 0% of each run, Pallas kernels for 39% -> 42%
where the time goes in v12:
time: 42.4 us; the launch traced here: 42.2 us
  Pallas kernels  19.9 us (47%)
  starting transfers between devices  16 us (38%)
  waiting for transfers between devices  4.82 us (11%)
  between operations  0.81 us (2%)
  local copies, waits for them, and re-layouts  0.67 us (2%)
    pallas_call x4, Pallas kernels, remap_call(): pl.pallas_call(kernel, out_shape=[jax.ShapeDtypeStruct(rows if isinstance...  10.3 us
    ppermute x7, starting transfers between devices, to_peer(): return lax.ppermute(x, ('lev', 'sub'), pairs)  8.66 us
    ppermute x6, starting transfers between devices, swap(): return lax.ppermute(x, 'tm', [(0, 1), (1, 0)])  7.31 us
    pallas_call x2, Pallas kernels, hour_sums(): pl.pallas_call(functools.partial(sums_kernel, plain, chunks), out_shape=[...  4.41 us
    pallas_call x1, Pallas kernels, place_tiles(): pl.pallas_call(place_kernel, out_shape=(half, half), in_specs=[smem, smem...  4.33 us
    ppermute x6, waiting for transfers between devices, swap(): return lax.ppermute(x, 'tm', [(0, 1), (1, 0)])  3.32 us
    ppermute x7, waiting for transfers between devices, to_peer(): return lax.ppermute(x, ('lev', 'sub'), pairs)  1.5 us
  transfers between devices with their start and end apart: 13, of which 4 were waited for; matrix products, arithmetic and copies ran while one was open for 0% of the time, Pallas kernels for 42%

profile of v12, /device:TPU:0, one launch (start us, length us, event | category | flops | bytes accessed | tf_op | source)
XLA Modules:
  0.0 42.2 jit_solution(9153444671583318347)
XLA Ops:
  0.0 0.7 %copy-done.1 = s32[8]{0:T(128)S(1)} copy-done((s32[8]{0:T(128)S(1)}, s32[8]{0:T(128)}, u32[]{:S(2)}) %copy-start.1) | copy-done | bytes 56
  0.7 2.2 %hour_sums.2 = (f32[24,2048]{1,0:T(8,128)S(1)}, f32[24,2048]{1,0:T(8,128)S(1)}, f32[48,1024]{1,0:T(8,128)S(1)}, f32[48,1024]{1,0:T(8,128)S(1)}) custom-call(s32[8]{0:T(128)S(1)} %copy-done.1, f32[12,8,16384]{2,1,0:T(8,128)} %bitcast.2), custom_call_target="tpu_custom_call" | custom-call | flops 1 | bytes 1 | tf_op jit(solution)/shard_map/hour_sums/pallas_call | solution.py:316
  2.9 0.0 copy-start
  2.9 0.0 copy-start.2
  2.9 0.0 copy-start.3
  2.9 0.5 %collective-permute-start = (f32[24,2048]{1,0:T(8,128)S(1)}, f32[24,2048]{1,0:T(8,128)S(1)}, u32[]{:S(2)}, u32[]{:S(2)}) collective-permute-start(f32[24,2048]{1,0:T(8,128)S(1)} %get-tuple-element.24), channel_id=1, source_target_pairs={{0,1},{1,0},{4,5},{5,4},{8,9},{9,8},{12,13},{13,12},{2,3},{3,2},{6... | collective-permute-start | bytes 589832 | tf_op jit(solution)/shard_map/ppermute | solution.py:445
  3.4 2.6 %collective-permute-start.2 = (f32[48,1024]{1,0:T(8,128)S(1)}, f32[48,1024]{1,0:T(8,128)S(1)}, u32[]{:S(2)}, u32[]{:S(2)}) collective-permute-start(f32[48,1024]{1,0:T(8,128)S(1)} %get-tuple-element.22.refs_0_), channel_id=1, source_target_pairs={{0,2},{2,0},{1,3},{3,1},{4,6},{6,4},{5,7},{7,5},{8,10},{10,8},{9,1... | collective-permute-start | bytes 589832 | tf_op jit(solution)/shard_map/ppermute | solution.py:448
  6.0 2.6 %collective-permute-start.1 = (f32[24,2048]{1,0:T(8,128)S(1)}, f32[24,2048]{1,0:T(8,128)S(1)}, u32[]{:S(2)}, u32[]{:S(2)}) collective-permute-start(f32[24,2048]{1,0:T(8,128)S(1)} %get-tuple-element.25), channel_id=1, source_target_pairs={{0,8},{1,9},{4,12},{5,13},{8,0},{9,1},{12,4},{13,5},{2,10},{3,11},... | collective-permute-start | bytes 589832 | tf_op jit(solution)/shard_map/ppermute | solution.py:445
  8.6 2.2 %hour_sums.3 = (f32[24,2048]{1,0:T(8,128)S(1)}, f32[24,2048]{1,0:T(8,128)S(1)}, f32[24,2048]{1,0:T(8,128)S(1)}, f32[24,1024]{1,0:T(8,128)S(1)}, f32[24,1024]{1,0:T(8,128)S(1)}) custom-call(s32[8]{0:T(128)S(1)} %copy-done.1, f32[12,8,16384]{2,1,0:T(8,128)} %bitcast.3, f32[48,1024]{1,0:T(8,128)S(1)} %get-tuple-element.22.refs_0_), custom_call_target="tpu_custom_call" | custom-call | flops 1 | bytes 1 | tf_op jit(solution)/shard_map/hour_sums/pallas_call | solution.py:316
  10.8 1.6 %collective-permute-start.5 = (f32[24,2048]{1,0:T(8,128)S(1)}, f32[24,2048]{1,0:T(8,128)S(1)}, u32[]{:S(2)}, u32[]{:S(2)}) collective-permute-start(f32[24,2048]{1,0:T(8,128)S(1)} %get-tuple-element.33), channel_id=1, source_target_pairs={{0,4},{1,5},{4,0},{5,1},{8,12},{9,13},{12,8},{13,9},{2,6},{3,7},{6... | collective-permute-start | bytes 589832 | tf_op jit(solution)/shard_map/ppermute | solution.py:445
  12.4 0.0 collective-permute-start.9
  13.1 0.0 collective-permute-done.refs_0_.sibling
  13.1 0.0 collective-permute-done.2.got
  13.1 2.3 %collective-permute-start.7 = (f32[24,1024]{1,0:T(8,128)S(1)}, f32[24,1024]{1,0:T(8,128)S(1)}, u32[]{:S(2)}, u32[]{:S(2)}) collective-permute-start(f32[24,1024]{1,0:T(8,128)S(1)} %merge_first.1.refs_0_), channel_id=1, source_target_pairs={{0,12},{1,13},{4,8},{5,9},{8,4},{9,5},{12,0},{13,1},{2,14},{3,15},... | collective-permute-start | bytes 294920 | tf_op jit(solution)/shard_map/ppermute | solution.py:445
  15.4 1.5 %collective-permute-start.8 = (f32[24,1024]{1,0:T(8,128)S(1)}, f32[24,1024]{1,0:T(8,128)S(1)}, u32[]{:S(2)}, u32[]{:S(2)}) collective-permute-start(f32[24,1024]{1,0:T(8,128)S(1)} %merge_next.1.refs_0_), channel_id=1, source_target_pairs={{0,13},{1,12},{4,9},{5,8},{8,5},{9,4},{12,1},{13,0},{2,15},{3,14},... | collective-permute-start | bytes 294920 | tf_op jit(solution)/shard_map/ppermute | solution.py:445
  17.0 4.3 %place_tiles.1 = (bf16[1024,2048]{1,0:T(8,128)(2,1)S(1)}, bf16[1024,2048]{1,0:T(8,128)(2,1)S(1)}) custom-call(s32[128]{0:T(128)S(1)} %copy-done.2, s32[128]{0:T(128)S(1)} %copy-done.3, s32[1]{0:T(128)S(6)} %copy.9.count, f32[64,8192]{1,0:T(8,128)S(1)} %copy-done, f32[24,1024]{1,0:T(8,128)S(1)} %merge_next.1.refs_0_), custom_call_target="tpu_custom_call" | custom-call | flops 1 | bytes 1 | tf_op jit(solution)/shard_map/place_tiles/pallas_call | solution.py:78
  21.4 0.6 %collective-permute-start.4 = (f32[24,1024]{1,0:T(8,128)S(1)}, f32[24,1024]{1,0:T(8,128)S(1)}, u32[]{:S(2)}, u32[]{:S(2)}) collective-permute-start(f32[24,1024]{1,0:T(8,128)S(1)} %hold.1.refs_0_), channel_id=1, source_target_pairs={{0,2},{2,0},{1,3},{3,1},{4,6},{6,4},{5,7},{7,5},{8,10},{10,8},{9,1... | collective-permute-start | bytes 294920 | tf_op jit(solution)/shard_map/ppermute | solution.py:448
  22.0 2.7 %remap_both.1 = (f32[48,1024]{1,0:T(8,128)S(1)}, f32[48,1024]{1,0:T(8,128)S(1)}) custom-call(f32[24,2048]{1,0:T(8,128)S(1)} %get-tuple-element.23.own, f32[24,2048]{1,0:T(8,128)S(1)} %collective-permute-done.refs_0_.sibling, f32[24,2048]{1,0:T(8,128)S(1)} %collective-permute-done.1.refs_0_.plain, bf16[1024,2048]{1,0:T(8,128)(2,1)S(1)} %get-tuple-element.28.refs_1_.high, ...), custom_call_target="tpu_custom_call" | custom-call | flops 2500000000 | bytes 1 | tf_op jit(solution)/shard_map/remap_both/pallas_call | solution.py:105
  24.7 1.6 %collective-permute-start.3 = (f32[48,1024]{1,0:T(8,128)S(1)}, f32[48,1024]{1,0:T(8,128)S(1)}, u32[]{:S(2)}, u32[]{:S(2)}) collective-permute-start(f32[48,1024]{1,0:T(8,128)S(1)} %get-tuple-element.31), channel_id=1, source_target_pairs={{0,2},{2,0},{1,3},{3,1},{4,6},{6,4},{5,7},{7,5},{8,10},{10,8},{9,1... | collective-permute-start | bytes 589832 | tf_op jit(solution)/shard_map/ppermute | solution.py:448
  26.3 0.2 collective-permute-done.4.got
  26.5 0.1 collective-permute-start.6
  26.6 1.5 %collective-permute-done.9.near_other = f32[24,2048]{1,0:T(8,128)S(1)} collective-permute-done((f32[24,2048]{1,0:T(8,128)S(1)}, f32[24,2048]{1,0:T(8,128)S(1)}, u32[]{:S(2)}, u32[]{:S(2)}) %collective-permute-start.9) | collective-permute-done | bytes 196640 | tf_op jit(solution)/shard_map/ppermute | solution.py:445
  28.1 2.6 %remap_near.1 = (f32[24,1024]{1,0:T(8,128)S(1)}, f32[24,1024]{1,0:T(8,128)S(1)}) custom-call(f32[24,2048]{1,0:T(8,128)S(1)} %collective-permute-done.5.refs_1_.near_same, f32[24,2048]{1,0:T(8,128)S(1)} %collective-permute-done.9.near_other, bf16[1024,2048]{1,0:T(8,128)(2,1)S(1)} %get-tuple-element.28.refs_1_.high, ...), custom_call_target="tpu_custom_call" | custom-call | flops 1 | bytes 1 | tf_op jit(solution)/shard_map/remap_near/pallas_call | solution.py:105
  30.7 2.6 %remap_far.1 = (f32[24,1024]{1,0:T(8,128)S(1)}, f32[24,1024]{1,0:T(8,128)S(1)}) custom-call(f32[24,1024]{1,0:T(8,128)S(1)} %collective-permute-done.7.same, f32[24,1024]{1,0:T(8,128)S(1)} %collective-permute-done.8.other, f32[24,1024]{1,0:T(8,128)S(1)} %get-tuple-element.35.near.second_hour, bf16[1024,2048]{1,0:T(8,128)(2,1)S(1)} %get-tuple-element.28.refs_1_.high, ...), custom_call_target="tpu_custom_call" | custom-call | flops 10000000000 | bytes 1 | tf_op jit(solution)/shard_map/remap_far/pallas_call | solution.py:105
  33.3 0.5 %collective-permute-start.12 = (f32[24,1024]{1,0:T(8,128)S(1)}, f32[24,1024]{1,0:T(8,128)S(1)}, u32[]{:S(2)}, u32[]{:S(2)}) collective-permute-start(f32[24,1024]{1,0:T(8,128)S(1)} %get-tuple-element.38), channel_id=1, source_target_pairs={{0,2},{2,0},{1,3},{3,1},{4,6},{6,4},{5,7},{7,5},{8,10},{10,8},{9,1... | collective-permute-start | bytes 294920 | tf_op jit(solution)/shard_map/ppermute | solution.py:448
  33.9 1.5 %collective-permute-start.11 = (f32[24,1024]{1,0:T(8,128)S(1)}, f32[24,1024]{1,0:T(8,128)S(1)}, u32[]{:S(2)}, u32[]{:S(2)}) collective-permute-start(f32[24,1024]{1,0:T(8,128)S(1)} %get-tuple-element.37.first_hour), channel_id=1, source_target_pairs={{0,2},{2,0},{1,3},{3,1},{4,6},{6,4},{5,7},{7,5},{8,10},{10,8},{9,1... | collective-permute-start | bytes 294920 | tf_op jit(solution)/shard_map/ppermute | solution.py:448
  35.4 2.4 %remap_last.1.last = f32[24,512]{1,0:T(8,128)S(1)} custom-call(f32[24,1024]{1,0:T(8,128)S(1)} %collective-permute-done.6.block, bf16[1024,2048]{1,0:T(8,128)(2,1)S(1)} %get-tuple-element.28.refs_1_.high, bf16[1024,2048]{1,0:T(8,128)(2,1)S(1)} %get-tuple-element.29.low, f32[24,1024]{1,0:T(8,128)S(1)} %get-tuple-element.36.refs_0_.far), custom_call_target="tpu_custom_call" | custom-call | flops 10000000000 | bytes 1 | tf_op jit(solution)/shard_map/remap_last/pallas_call | solution.py:105
  37.8 0.5 %collective-permute-start.10 = (f32[24,512]{1,0:T(8,128)S(1)}, f32[24,512]{1,0:T(8,128)S(1)}, u32[]{:S(2)}, u32[]{:S(2)}) collective-permute-start(f32[24,512]{1,0:T(8,128)S(1)} %remap_last.1.last), channel_id=1, source_target_pairs={{0,2},{2,0},{1,3},{3,1},{4,6},{6,4},{5,7},{7,5},{8,10},{10,8},{9,1... | collective-permute-start | bytes 147464 | tf_op jit(solution)/shard_map/ppermute | solution.py:448
  38.3 0.0 collective-permute-done.12.got
  38.3 2.1 %collective-permute-done.11.got_first = f32[24,1024]{1,0:T(8,128)S(1)} collective-permute-done((f32[24,1024]{1,0:T(8,128)S(1)}, f32[24,1024]{1,0:T(8,128)S(1)}, u32[]{:S(2)}, u32[]{:S(2)}) %collective-permute-start.11) | collective-permute-done | bytes 98336 | tf_op jit(solution)/shard_map/ppermute | solution.py:448
  40.4 0.8 %write_first.1.begun = f32[96,1024]{1,0:T(8,128)} custom-call(f32[48,1024]{1,0:T(8,128)S(1)} %get-tuple-element.30.refs_0_.chip.plain, f32[48,1024]{1,0:T(8,128)S(1)} %collective-permute-done.3.got_chip.got_plain, f32[24,1024]{1,0:T(8,128)S(1)} %get-tuple-element.37.first_hour, f32[24,1024]{1,0:T(8,128)S(1)} %collective-permute-done.11.got_first, ...), custom_call_target="tpu_custom_call" | custom-call | flops 1 | bytes 1 | tf_op jit(solution)/shard_map/write_first/pallas_call | solution.py:359
  41.2 1.0 %collective-permute-done.10.got_last = f32[24,512]{1,0:T(8,128)S(1)} collective-permute-done((f32[24,512]{1,0:T(8,128)S(1)}, f32[24,512]{1,0:T(8,128)S(1)}, u32[]{:S(2)}, u32[]{:S(2)}) %collective-permute-start.10) | collective-permute-done | bytes 49184 | tf_op jit(solution)/shard_map/ppermute | solution.py:448
  (15 shorter events, 0.1 us)
Async XLA Ops:
  0.0 0.7 %copy-start.1 = (s32[8]{0:T(128)S(1)}, s32[8]{0:T(128)}, u32[]{:S(2)}) copy-start(s32[8]{0:T(128)} %step_hour.3) | copy-start | bytes 100
  2.9 14.1 %copy-start = (f32[64,8192]{1,0:T(8,128)S(1)}, f32[64,8192]{1,0:T(8,128)}, u32[]{:S(2)}) copy-start(f32[64,8192]{1,0:T(8,128)} %weights.1) | copy-start | bytes 6291460
  2.9 14.1 %copy-start.2 = (s32[128]{0:T(128)S(1)}, s32[128]{0:T(128)}, u32[]{:S(2)}) copy-start(s32[128]{0:T(128)} %rows.1) | copy-start | bytes 1540
  2.9 14.1 %copy-start.3 = (s32[128]{0:T(128)S(1)}, s32[128]{0:T(128)}, u32[]{:S(2)}) copy-start(s32[128]{0:T(128)} %columns.1) | copy-start | bytes 1540
  2.9 10.2 %collective-permute-start = (f32[24,2048]{1,0:T(8,128)S(1)}, f32[24,2048]{1,0:T(8,128)S(1)}, u32[]{:S(2)}, u32[]{:S(2)}) collective-permute-start(f32[24,2048]{1,0:T(8,128)S(1)} %get-tuple-element.24), channel_id=1, source_target_pairs={{0,1},{1,0},{4,5},{5,4},{8,9},{9,8},{12,13},{13,12},{2,3},{3,2},{6... | collective-permute-start | bytes 589832 | tf_op jit(solution)/shard_map/ppermute | solution.py:445
  3.4 9.7 %collective-permute-start.2 = (f32[48,1024]{1,0:T(8,128)S(1)}, f32[48,1024]{1,0:T(8,128)S(1)}, u32[]{:S(2)}, u32[]{:S(2)}) collective-permute-start(f32[48,1024]{1,0:T(8,128)S(1)} %get-tuple-element.22.refs_0_), channel_id=1, source_target_pairs={{0,2},{2,0},{1,3},{3,1},{4,6},{6,4},{5,7},{7,5},{8,10},{10,8},{9,1... | collective-permute-start | bytes 589832 | tf_op jit(solution)/shard_map/ppermute | solution.py:448
  6.0 15.3 %collective-permute-start.1 = (f32[24,2048]{1,0:T(8,128)S(1)}, f32[24,2048]{1,0:T(8,128)S(1)}, u32[]{:S(2)}, u32[]{:S(2)}) collective-permute-start(f32[24,2048]{1,0:T(8,128)S(1)} %get-tuple-element.25), channel_id=1, source_target_pairs={{0,8},{1,9},{4,12},{5,13},{8,0},{9,1},{12,4},{13,5},{2,10},{3,11},... | collective-permute-start | bytes 589832 | tf_op jit(solution)/shard_map/ppermute | solution.py:445
  10.8 13.9 %collective-permute-start.5 = (f32[24,2048]{1,0:T(8,128)S(1)}, f32[24,2048]{1,0:T(8,128)S(1)}, u32[]{:S(2)}, u32[]{:S(2)}) collective-permute-start(f32[24,2048]{1,0:T(8,128)S(1)} %get-tuple-element.33), channel_id=1, source_target_pairs={{0,4},{1,5},{4,0},{5,1},{8,12},{9,13},{12,8},{13,9},{2,6},{3,7},{6... | collective-permute-start | bytes 589832 | tf_op jit(solution)/shard_map/ppermute | solution.py:445
  12.4 15.6 %collective-permute-start.9 = (f32[24,2048]{1,0:T(8,128)S(1)}, f32[24,2048]{1,0:T(8,128)S(1)}, u32[]{:S(2)}, u32[]{:S(2)}) collective-permute-start(f32[24,2048]{1,0:T(8,128)S(1)} %get-tuple-element.34), channel_id=1, source_target_pairs={{0,5},{1,4},{4,1},{5,0},{8,13},{9,12},{12,9},{13,8},{2,7},{3,6},{6... | collective-permute-start | bytes 589832 | tf_op jit(solution)/shard_map/ppermute | solution.py:445
  13.1 17.6 %collective-permute-start.7 = (f32[24,1024]{1,0:T(8,128)S(1)}, f32[24,1024]{1,0:T(8,128)S(1)}, u32[]{:S(2)}, u32[]{:S(2)}) collective-permute-start(f32[24,1024]{1,0:T(8,128)S(1)} %merge_first.1.refs_0_), channel_id=1, source_target_pairs={{0,12},{1,13},{4,8},{5,9},{8,4},{9,5},{12,0},{13,1},{2,14},{3,15},... | collective-permute-start | bytes 294920 | tf_op jit(solution)/shard_map/ppermute | solution.py:445
  15.4 15.3 %collective-permute-start.8 = (f32[24,1024]{1,0:T(8,128)S(1)}, f32[24,1024]{1,0:T(8,128)S(1)}, u32[]{:S(2)}, u32[]{:S(2)}) collective-permute-start(f32[24,1024]{1,0:T(8,128)S(1)} %merge_next.1.refs_0_), channel_id=1, source_target_pairs={{0,13},{1,12},{4,9},{5,8},{8,5},{9,4},{12,1},{13,0},{2,15},{3,14},... | collective-permute-start | bytes 294920 | tf_op jit(solution)/shard_map/ppermute | solution.py:445
  21.4 5.1 %collective-permute-start.4 = (f32[24,1024]{1,0:T(8,128)S(1)}, f32[24,1024]{1,0:T(8,128)S(1)}, u32[]{:S(2)}, u32[]{:S(2)}) collective-permute-start(f32[24,1024]{1,0:T(8,128)S(1)} %hold.1.refs_0_), channel_id=1, source_target_pairs={{0,2},{2,0},{1,3},{3,1},{4,6},{6,4},{5,7},{7,5},{8,10},{10,8},{9,1... | collective-permute-start | bytes 294920 | tf_op jit(solution)/shard_map/ppermute | solution.py:448
  24.7 15.7 %collective-permute-start.3 = (f32[48,1024]{1,0:T(8,128)S(1)}, f32[48,1024]{1,0:T(8,128)S(1)}, u32[]{:S(2)}, u32[]{:S(2)}) collective-permute-start(f32[48,1024]{1,0:T(8,128)S(1)} %get-tuple-element.31), channel_id=1, source_target_pairs={{0,2},{2,0},{1,3},{3,1},{4,6},{6,4},{5,7},{7,5},{8,10},{10,8},{9,1... | collective-permute-start | bytes 589832 | tf_op jit(solution)/shard_map/ppermute | solution.py:448
  26.5 8.9 %collective-permute-start.6 = (f32[24,1024]{1,0:T(8,128)S(1)}, f32[24,1024]{1,0:T(8,128)S(1)}, u32[]{:S(2)}, u32[]{:S(2)}) collective-permute-start(f32[24,1024]{1,0:T(8,128)S(1)} %merge_last.1.refs_0_), channel_id=1, source_target_pairs={{0,9},{1,8},{4,13},{5,12},{8,1},{9,0},{12,5},{13,4},{2,11},{3,10},... | collective-permute-start | bytes 294920 | tf_op jit(solution)/shard_map/ppermute | solution.py:445
  33.3 5.0 %collective-permute-start.12 = (f32[24,1024]{1,0:T(8,128)S(1)}, f32[24,1024]{1,0:T(8,128)S(1)}, u32[]{:S(2)}, u32[]{:S(2)}) collective-permute-start(f32[24,1024]{1,0:T(8,128)S(1)} %get-tuple-element.38), channel_id=1, source_target_pairs={{0,2},{2,0},{1,3},{3,1},{4,6},{6,4},{5,7},{7,5},{8,10},{10,8},{9,1... | collective-permute-start | bytes 294920 | tf_op jit(solution)/shard_map/ppermute | solution.py:448
  33.9 6.5 %collective-permute-start.11 = (f32[24,1024]{1,0:T(8,128)S(1)}, f32[24,1024]{1,0:T(8,128)S(1)}, u32[]{:S(2)}, u32[]{:S(2)}) collective-permute-start(f32[24,1024]{1,0:T(8,128)S(1)} %get-tuple-element.37.first_hour), channel_id=1, source_target_pairs={{0,2},{2,0},{1,3},{3,1},{4,6},{6,4},{5,7},{7,5},{8,10},{10,8},{9,1... | collective-permute-start | bytes 294920 | tf_op jit(solution)/shard_map/ppermute | solution.py:448
  37.8 4.4 %collective-permute-start.10 = (f32[24,512]{1,0:T(8,128)S(1)}, f32[24,512]{1,0:T(8,128)S(1)}, u32[]{:S(2)}, u32[]{:S(2)}) collective-permute-start(f32[24,512]{1,0:T(8,128)S(1)} %remap_last.1.last), channel_id=1, source_target_pairs={{0,2},{2,0},{1,3},{3,1},{4,6},{6,4},{5,7},{7,5},{8,10},{10,8},{9,1... | collective-permute-start | bytes 147464 | tf_op jit(solution)/shard_map/ppermute | solution.py:448

commit v13 on v11

--- a/solution.py
+++ b/solution.py
@@ -87,7 +87,7 @@
     )(rows, columns, count, weights, *after)
 
 
-PIXEL_BLOCK = 256
+PIXEL_BLOCK = 1024
 
 
 def remap_blocks(x, high, low):

time: 39.6 us -> 39.6 us (level)
  starting transfers between devices: 15.9 us -> 16.7 us
  Pallas kernels: 18.8 us -> 18.1 us
    ppermute x7, starting transfers between devices: 8.47 us -> 9.24 us  [to_peer(): return lax.ppermute(x, ('lev', 'sub'), pairs)]
    pallas_call x1, Pallas kernels: 4.32 us -> 3.56 us  [place_tiles(): pl.pallas_call(place_kernel, out_shape=(half, half), in_specs=[smem, smem...]
  transfers between devices with their start and end apart: 13 -> 13, of which waited for: 4 -> 3; matrix products, arithmetic and copies ran while one was open for 0% -> 0% of each run, Pallas kernels for 39% -> 37%
where the time goes in v13:
time: 39.6 us; the launch traced here: 39.5 us
  Pallas kernels  18.1 us (46%)
  starting transfers between devices  16.7 us (42%)
  waiting for transfers between devices  3.1 us (8%)
  local copies, waits for them, and re-layouts  0.82 us (2%)
  between operations  0.79 us (2%)
    pallas_call x4, Pallas kernels, remap_call(): pl.pallas_call(kernel, out_shape=[jax.ShapeDtypeStruct(rows if isinstance...  10.4 us
    ppermute x7, starting transfers between devices, to_peer(): return lax.ppermute(x, ('lev', 'sub'), pairs)  9.24 us
    ppermute x6, starting transfers between devices, swap(): return lax.ppermute(x, 'tm', [(0, 1), (1, 0)])  7.42 us
    pallas_call x1, Pallas kernels, place_tiles(): pl.pallas_call(place_kernel, out_shape=(half, half), in_specs=[smem, smem...  3.56 us
    pallas_call x1, Pallas kernels, hour_sums(): pl.pallas_call(functools.partial(sums_kernel, plain, first, second), out_...  3.28 us
    ppermute x6, waiting for transfers between devices, swap(): return lax.ppermute(x, 'tm', [(0, 1), (1, 0)])  2.76 us
    pallas_call x5, Pallas kernels, small_call(): pl.pallas_call(kernel, out_shape=[jax.ShapeDtypeStruct(shape, jnp.float32...  0.85 us
    unnamed x8, local copies, waits for them, and re-layouts  0.82 us
  transfers between devices with their start and end apart: 13, of which 3 were waited for; matrix products, arithmetic and copies ran while one was open for 0% of the time, Pallas kernels for 37%

profile of v13, /device:TPU:0, one launch (start us, length us, event | category | flops | bytes accessed | tf_op | source)
XLA Modules:
  0.0 39.5 jit_solution(11152331025728171507)
XLA Ops:
  0.0 0.8 %copy-done.1 = s32[8]{0:T(128)S(1)} copy-done((s32[8]{0:T(128)S(1)}, s32[8]{0:T(128)}, u32[]{:S(2)}) %copy-start.1) | copy-done | bytes 56
  0.8 3.3 %hour_sums.1 = (f32[24,2048]{1,0:T(8,128)S(1)}, f32[24,2048]{1,0:T(8,128)S(1)}, f32[24,2048]{1,0:T(8,128)S(1)}, f32[24,2048]{1,0:T(8,128)S(1)}, f32[24,2048]{1,0...) custom-call(s32[8]{0:T(128)S(1)} %copy-done.1, ...), custom_call_target="tpu_custom_call" | custom-call | flops 1 | bytes 1 | tf_op jit(solution)/shard_map/hour_sums/pallas_call | solution.py:312
  4.1 0.5 %collective-permute-start = (f32[24,2048]{1,0:T(8,128)S(1)}, f32[24,2048]{1,0:T(8,128)S(1)}, u32[]{:S(2)}, u32[]{:S(2)}) collective-permute-start(f32[24,2048]{1,0:T(8,128)S(1)} %get-tuple-element.23), channel_id=1, source_target_pairs={{0,1},{1,0},{4,5},{5,4},{8,9},{9,8},{12,13},{13,12},{2,3},{3,2},{6... | collective-permute-start | bytes 589832 | tf_op jit(solution)/shard_map/ppermute | solution.py:441
  4.6 2.6 %collective-permute-start.2 = (f32[48,1024]{1,0:T(8,128)S(1)}, f32[48,1024]{1,0:T(8,128)S(1)}, u32[]{:S(2)}, u32[]{:S(2)}) collective-permute-start(f32[48,1024]{1,0:T(8,128)S(1)} %get-tuple-element.25.refs_0_), channel_id=1, source_target_pairs={{0,2},{2,0},{1,3},{3,1},{4,6},{6,4},{5,7},{7,5},{8,10},{10,8},{9,1... | collective-permute-start | bytes 589832 | tf_op jit(solution)/shard_map/ppermute | solution.py:444
  7.2 2.6 %collective-permute-start.1 = (f32[24,2048]{1,0:T(8,128)S(1)}, f32[24,2048]{1,0:T(8,128)S(1)}, u32[]{:S(2)}, u32[]{:S(2)}) collective-permute-start(f32[24,2048]{1,0:T(8,128)S(1)} %get-tuple-element.24), channel_id=1, source_target_pairs={{0,8},{1,9},{4,12},{5,13},{8,0},{9,1},{12,4},{13,5},{2,10},{3,11},... | collective-permute-start | bytes 589832 | tf_op jit(solution)/shard_map/ppermute | solution.py:441
  9.8 1.6 %collective-permute-start.5 = (f32[24,2048]{1,0:T(8,128)S(1)}, f32[24,2048]{1,0:T(8,128)S(1)}, u32[]{:S(2)}, u32[]{:S(2)}) collective-permute-start(f32[24,2048]{1,0:T(8,128)S(1)} %get-tuple-element.33), channel_id=1, source_target_pairs={{0,4},{1,5},{4,0},{5,1},{8,12},{9,13},{12,8},{13,9},{2,6},{3,7},{6... | collective-permute-start | bytes 589832 | tf_op jit(solution)/shard_map/ppermute | solution.py:441
  11.4 0.0 collective-permute-start.9
  12.0 3.6 %place_tiles.1 = (bf16[1024,2048]{1,0:T(8,128)(2,1)S(1)}, bf16[1024,2048]{1,0:T(8,128)(2,1)S(1)}) custom-call(s32[128]{0:T(128)S(1)} %copy-done.2, s32[128]{0:T(128)S(1)} %copy-done.3, s32[1]{0:T(128)S(6)} %copy.9.count, f32[64,8192]{1,0:T(8,128)S(1)} %copy-done, f32[48,1024]{1,0:T(8,128)S(1)} %get-tuple-element.25.refs_0_), custom_call_target="tpu_custom_call" | custom-call | flops 1 | bytes 1 | tf_op jit(solution)/shard_map/place_tiles/pallas_call | solution.py:78
  15.6 0.0 collective-permute-done.refs_1_.sibling
  15.6 0.0 collective-permute-done.2.got
  15.6 1.1 %collective-permute-start.7 = (f32[24,1024]{1,0:T(8,128)S(1)}, f32[24,1024]{1,0:T(8,128)S(1)}, u32[]{:S(2)}, u32[]{:S(2)}) collective-permute-start(f32[24,1024]{1,0:T(8,128)S(1)} %merge_first.1.refs_0_), channel_id=1, source_target_pairs={{0,12},{1,13},{4,8},{5,9},{8,4},{9,5},{12,0},{13,1},{2,14},{3,15},... | collective-permute-start | bytes 294920 | tf_op jit(solution)/shard_map/ppermute | solution.py:441
  16.7 3.4 %collective-permute-start.8 = (f32[24,1024]{1,0:T(8,128)S(1)}, f32[24,1024]{1,0:T(8,128)S(1)}, u32[]{:S(2)}, u32[]{:S(2)}) collective-permute-start(f32[24,1024]{1,0:T(8,128)S(1)} %merge_next.1.refs_1_), channel_id=1, source_target_pairs={{0,13},{1,12},{4,9},{5,8},{8,5},{9,4},{12,1},{13,0},{2,15},{3,14},... | collective-permute-start | bytes 294920 | tf_op jit(solution)/shard_map/ppermute | solution.py:441
  20.1 0.0 collective-permute-done.1.refs_0_.plain
  20.2 0.6 %collective-permute-start.4 = (f32[24,1024]{1,0:T(8,128)S(1)}, f32[24,1024]{1,0:T(8,128)S(1)}, u32[]{:S(2)}, u32[]{:S(2)}) collective-permute-start(f32[24,1024]{1,0:T(8,128)S(1)} %hold.1.refs_0_), channel_id=1, source_target_pairs={{0,2},{2,0},{1,3},{3,1},{4,6},{6,4},{5,7},{7,5},{8,10},{10,8},{9,1... | collective-permute-start | bytes 294920 | tf_op jit(solution)/shard_map/ppermute | solution.py:444
  20.8 2.8 %remap_both.1 = (f32[48,1024]{1,0:T(8,128)S(1)}, f32[48,1024]{1,0:T(8,128)S(1)}) custom-call(f32[24,2048]{1,0:T(8,128)S(1)} %get-tuple-element.22.own, f32[24,2048]{1,0:T(8,128)S(1)} %collective-permute-done.refs_1_.sibling, f32[24,2048]{1,0:T(8,128)S(1)} %collective-permute-done.1.refs_0_.plain, bf16[1024,2048]{1,0:T(8,128)(2,1)S(1)} %get-tuple-element.26.refs_0_.high, ...), custom_call_target="tpu_custom_call" | custom-call | flops 2500000000 | bytes 1 | tf_op jit(solution)/shard_map/remap_both/pallas_call | solution.py:105
  23.6 0.0 collective-permute-done.5.refs_1_.near_same
  23.6 1.5 %collective-permute-start.3 = (f32[48,1024]{1,0:T(8,128)S(1)}, f32[48,1024]{1,0:T(8,128)S(1)}, u32[]{:S(2)}, u32[]{:S(2)}) collective-permute-start(f32[48,1024]{1,0:T(8,128)S(1)} %get-tuple-element.31), channel_id=1, source_target_pairs={{0,2},{2,0},{1,3},{3,1},{4,6},{6,4},{5,7},{7,5},{8,10},{10,8},{9,1... | collective-permute-start | bytes 589832 | tf_op jit(solution)/shard_map/ppermute | solution.py:444
  25.1 0.0 collective-permute-done.4.got
  25.1 0.1 collective-permute-start.6
  25.2 2.6 %remap_near.1 = (f32[24,1024]{1,0:T(8,128)S(1)}, f32[24,1024]{1,0:T(8,128)S(1)}) custom-call(f32[24,2048]{1,0:T(8,128)S(1)} %collective-permute-done.5.refs_1_.near_same, f32[24,2048]{1,0:T(8,128)S(1)} %collective-permute-done.9.near_other, bf16[1024,2048]{1,0:T(8,128)(2,1)S(1)} %get-tuple-element.26.refs_0_.high, ...), custom_call_target="tpu_custom_call" | custom-call | flops 1 | bytes 1 | tf_op jit(solution)/shard_map/remap_near/pallas_call | solution.py:105
  27.9 0.6 %collective-permute-start.11 = (f32[24,1024]{1,0:T(8,128)S(1)}, f32[24,1024]{1,0:T(8,128)S(1)}, u32[]{:S(2)}, u32[]{:S(2)}) collective-permute-start(f32[24,1024]{1,0:T(8,128)S(1)} %get-tuple-element.37.first_hour), channel_id=1, source_target_pairs={{0,2},{2,0},{1,3},{3,1},{4,6},{6,4},{5,7},{7,5},{8,10},{10,8},{9,1... | collective-permute-start | bytes 294920 | tf_op jit(solution)/shard_map/ppermute | solution.py:444
  28.5 0.0 collective-permute-done.8.other
  28.5 0.0 collective-permute-done.7.same
  28.5 2.6 %remap_far.1 = (f32[24,1024]{1,0:T(8,128)S(1)}, f32[24,1024]{1,0:T(8,128)S(1)}) custom-call(f32[24,1024]{1,0:T(8,128)S(1)} %collective-permute-done.7.same, f32[24,1024]{1,0:T(8,128)S(1)} %collective-permute-done.8.other, f32[24,1024]{1,0:T(8,128)S(1)} %get-tuple-element.35.near.second_hour, bf16[1024,2048]{1,0:T(8,128)(2,1)S(1)} %get-tuple-element.26.refs_0_.high, ...), custom_call_target="tpu_custom_call" | custom-call | flops 10000000000 | bytes 1 | tf_op jit(solution)/shard_map/remap_far/pallas_call | solution.py:105
  31.1 1.6 %collective-permute-start.12 = (f32[24,1024]{1,0:T(8,128)S(1)}, f32[24,1024]{1,0:T(8,128)S(1)}, u32[]{:S(2)}, u32[]{:S(2)}) collective-permute-start(f32[24,1024]{1,0:T(8,128)S(1)} %get-tuple-element.38), channel_id=1, source_target_pairs={{0,2},{2,0},{1,3},{3,1},{4,6},{6,4},{5,7},{7,5},{8,10},{10,8},{9,1... | collective-permute-start | bytes 294920 | tf_op jit(solution)/shard_map/ppermute | solution.py:444
  32.6 0.3 collective-permute-done.6.block
  33.0 2.4 %remap_last.1.last = f32[24,512]{1,0:T(8,128)S(1)} custom-call(f32[24,1024]{1,0:T(8,128)S(1)} %collective-permute-done.6.block, bf16[1024,2048]{1,0:T(8,128)(2,1)S(1)} %get-tuple-element.26.refs_0_.high, bf16[1024,2048]{1,0:T(8,128)(2,1)S(1)} %get-tuple-element.27.low, f32[24,1024]{1,0:T(8,128)S(1)} %get-tuple-element.36.refs_0_.far), custom_call_target="tpu_custom_call" | custom-call | flops 10000000000 | bytes 1 | tf_op jit(solution)/shard_map/remap_last/pallas_call | solution.py:105
  35.3 0.6 %collective-permute-start.10 = (f32[24,512]{1,0:T(8,128)S(1)}, f32[24,512]{1,0:T(8,128)S(1)}, u32[]{:S(2)}, u32[]{:S(2)}) collective-permute-start(f32[24,512]{1,0:T(8,128)S(1)} %remap_last.1.last), channel_id=1, source_target_pairs={{0,2},{2,0},{1,3},{3,1},{4,6},{6,4},{5,7},{7,5},{8,10},{10,8},{9,1... | collective-permute-start | bytes 147464 | tf_op jit(solution)/shard_map/ppermute | solution.py:444
  35.9 0.4 %collective-permute-done.12.got = f32[24,1024]{1,0:T(8,128)S(1)} collective-permute-done((f32[24,1024]{1,0:T(8,128)S(1)}, f32[24,1024]{1,0:T(8,128)S(1)}, u32[]{:S(2)}, u32[]{:S(2)}) %collective-permute-start.12) | collective-permute-done | bytes 98336 | tf_op jit(solution)/shard_map/ppermute | solution.py:444
  36.3 0.0 collective-permute-done.3.got_chip.got_plain
  36.3 0.8 %write_first.1.begun = f32[96,1024]{1,0:T(8,128)} custom-call(f32[48,1024]{1,0:T(8,128)S(1)} %get-tuple-element.30.refs_0_.chip.plain, f32[48,1024]{1,0:T(8,128)S(1)} %collective-permute-done.3.got_chip.got_plain, f32[24,1024]{1,0:T(8,128)S(1)} %get-tuple-element.37.first_hour, f32[24,1024]{1,0:T(8,128)S(1)} %collective-permute-done.11.got_first, ...), custom_call_target="tpu_custom_call" | custom-call | flops 1 | bytes 1 | tf_op jit(solution)/shard_map/write_first/pallas_call | solution.py:355
  37.1 2.3 %collective-permute-done.10.got_last = f32[24,512]{1,0:T(8,128)S(1)} collective-permute-done((f32[24,512]{1,0:T(8,128)S(1)}, f32[24,512]{1,0:T(8,128)S(1)}, u32[]{:S(2)}, u32[]{:S(2)}) %collective-permute-start.10) | collective-permute-done | bytes 49184 | tf_op jit(solution)/shard_map/ppermute | solution.py:444
  (14 shorter events, 0.1 us)
Async XLA Ops:
  0.0 12.0 %copy-start = (f32[64,8192]{1,0:T(8,128)S(1)}, f32[64,8192]{1,0:T(8,128)}, u32[]{:S(2)}) copy-start(f32[64,8192]{1,0:T(8,128)} %weights.1) | copy-start | bytes 6291460
  0.0 0.8 %copy-start.1 = (s32[8]{0:T(128)S(1)}, s32[8]{0:T(128)}, u32[]{:S(2)}) copy-start(s32[8]{0:T(128)} %step_hour.1) | copy-start | bytes 100
  0.8 11.2 %copy-start.2 = (s32[128]{0:T(128)S(1)}, s32[128]{0:T(128)}, u32[]{:S(2)}) copy-start(s32[128]{0:T(128)} %rows.1) | copy-start | bytes 1540
  0.8 11.2 %copy-start.3 = (s32[128]{0:T(128)S(1)}, s32[128]{0:T(128)}, u32[]{:S(2)}) copy-start(s32[128]{0:T(128)} %columns.1) | copy-start | bytes 1540
  4.1 11.5 %collective-permute-start = (f32[24,2048]{1,0:T(8,128)S(1)}, f32[24,2048]{1,0:T(8,128)S(1)}, u32[]{:S(2)}, u32[]{:S(2)}) collective-permute-start(f32[24,2048]{1,0:T(8,128)S(1)} %get-tuple-element.23), channel_id=1, source_target_pairs={{0,1},{1,0},{4,5},{5,4},{8,9},{9,8},{12,13},{13,12},{2,3},{3,2},{6... | collective-permute-start | bytes 589832 | tf_op jit(solution)/shard_map/ppermute | solution.py:441
  4.6 11.0 %collective-permute-start.2 = (f32[48,1024]{1,0:T(8,128)S(1)}, f32[48,1024]{1,0:T(8,128)S(1)}, u32[]{:S(2)}, u32[]{:S(2)}) collective-permute-start(f32[48,1024]{1,0:T(8,128)S(1)} %get-tuple-element.25.refs_0_), channel_id=1, source_target_pairs={{0,2},{2,0},{1,3},{3,1},{4,6},{6,4},{5,7},{7,5},{8,10},{10,8},{9,1... | collective-permute-start | bytes 589832 | tf_op jit(solution)/shard_map/ppermute | solution.py:444
  7.2 13.0 %collective-permute-start.1 = (f32[24,2048]{1,0:T(8,128)S(1)}, f32[24,2048]{1,0:T(8,128)S(1)}, u32[]{:S(2)}, u32[]{:S(2)}) collective-permute-start(f32[24,2048]{1,0:T(8,128)S(1)} %get-tuple-element.24), channel_id=1, source_target_pairs={{0,8},{1,9},{4,12},{5,13},{8,0},{9,1},{12,4},{13,5},{2,10},{3,11},... | collective-permute-start | bytes 589832 | tf_op jit(solution)/shard_map/ppermute | solution.py:441
  9.8 13.8 %collective-permute-start.5 = (f32[24,2048]{1,0:T(8,128)S(1)}, f32[24,2048]{1,0:T(8,128)S(1)}, u32[]{:S(2)}, u32[]{:S(2)}) collective-permute-start(f32[24,2048]{1,0:T(8,128)S(1)} %get-tuple-element.33), channel_id=1, source_target_pairs={{0,4},{1,5},{4,0},{5,1},{8,12},{9,13},{12,8},{13,9},{2,6},{3,7},{6... | collective-permute-start | bytes 589832 | tf_op jit(solution)/shard_map/ppermute | solution.py:441
  11.4 13.9 %collective-permute-start.9 = (f32[24,2048]{1,0:T(8,128)S(1)}, f32[24,2048]{1,0:T(8,128)S(1)}, u32[]{:S(2)}, u32[]{:S(2)}) collective-permute-start(f32[24,2048]{1,0:T(8,128)S(1)} %get-tuple-element.34), channel_id=1, source_target_pairs={{0,5},{1,4},{4,1},{5,0},{8,13},{9,12},{12,9},{13,8},{2,7},{3,6},{6... | collective-permute-start | bytes 589832 | tf_op jit(solution)/shard_map/ppermute | solution.py:441
  15.6 12.8 %collective-permute-start.7 = (f32[24,1024]{1,0:T(8,128)S(1)}, f32[24,1024]{1,0:T(8,128)S(1)}, u32[]{:S(2)}, u32[]{:S(2)}) collective-permute-start(f32[24,1024]{1,0:T(8,128)S(1)} %merge_first.1.refs_0_), channel_id=1, source_target_pairs={{0,12},{1,13},{4,8},{5,9},{8,4},{9,5},{12,0},{13,1},{2,14},{3,15},... | collective-permute-start | bytes 294920 | tf_op jit(solution)/shard_map/ppermute | solution.py:441
  16.7 11.8 %collective-permute-start.8 = (f32[24,1024]{1,0:T(8,128)S(1)}, f32[24,1024]{1,0:T(8,128)S(1)}, u32[]{:S(2)}, u32[]{:S(2)}) collective-permute-start(f32[24,1024]{1,0:T(8,128)S(1)} %merge_next.1.refs_1_), channel_id=1, source_target_pairs={{0,13},{1,12},{4,9},{5,8},{8,5},{9,4},{12,1},{13,0},{2,15},{3,14},... | collective-permute-start | bytes 294920 | tf_op jit(solution)/shard_map/ppermute | solution.py:441
  20.2 5.0 %collective-permute-start.4 = (f32[24,1024]{1,0:T(8,128)S(1)}, f32[24,1024]{1,0:T(8,128)S(1)}, u32[]{:S(2)}, u32[]{:S(2)}) collective-permute-start(f32[24,1024]{1,0:T(8,128)S(1)} %hold.1.refs_0_), channel_id=1, source_target_pairs={{0,2},{2,0},{1,3},{3,1},{4,6},{6,4},{5,7},{7,5},{8,10},{10,8},{9,1... | collective-permute-start | bytes 294920 | tf_op jit(solution)/shard_map/ppermute | solution.py:444
  23.6 12.8 %collective-permute-start.3 = (f32[48,1024]{1,0:T(8,128)S(1)}, f32[48,1024]{1,0:T(8,128)S(1)}, u32[]{:S(2)}, u32[]{:S(2)}) collective-permute-start(f32[48,1024]{1,0:T(8,128)S(1)} %get-tuple-element.31), channel_id=1, source_target_pairs={{0,2},{2,0},{1,3},{3,1},{4,6},{6,4},{5,7},{7,5},{8,10},{10,8},{9,1... | collective-permute-start | bytes 589832 | tf_op jit(solution)/shard_map/ppermute | solution.py:444
  25.1 7.8 %collective-permute-start.6 = (f32[24,1024]{1,0:T(8,128)S(1)}, f32[24,1024]{1,0:T(8,128)S(1)}, u32[]{:S(2)}, u32[]{:S(2)}) collective-permute-start(f32[24,1024]{1,0:T(8,128)S(1)} %merge_last.1.refs_0_), channel_id=1, source_target_pairs={{0,9},{1,8},{4,13},{5,12},{8,1},{9,0},{12,5},{13,4},{2,11},{3,10},... | collective-permute-start | bytes 294920 | tf_op jit(solution)/shard_map/ppermute | solution.py:441
  27.9 8.0 %collective-permute-start.11 = (f32[24,1024]{1,0:T(8,128)S(1)}, f32[24,1024]{1,0:T(8,128)S(1)}, u32[]{:S(2)}, u32[]{:S(2)}) collective-permute-start(f32[24,1024]{1,0:T(8,128)S(1)} %get-tuple-element.37.first_hour), channel_id=1, source_target_pairs={{0,2},{2,0},{1,3},{3,1},{4,6},{6,4},{5,7},{7,5},{8,10},{10,8},{9,1... | collective-permute-start | bytes 294920 | tf_op jit(solution)/shard_map/ppermute | solution.py:444
  31.1 5.2 %collective-permute-start.12 = (f32[24,1024]{1,0:T(8,128)S(1)}, f32[24,1024]{1,0:T(8,128)S(1)}, u32[]{:S(2)}, u32[]{:S(2)}) collective-permute-start(f32[24,1024]{1,0:T(8,128)S(1)} %get-tuple-element.38), channel_id=1, source_target_pairs={{0,2},{2,0},{1,3},{3,1},{4,6},{6,4},{5,7},{7,5},{8,10},{10,8},{9,1... | collective-permute-start | bytes 294920 | tf_op jit(solution)/shard_map/ppermute | solution.py:444
  35.3 4.1 %collective-permute-start.10 = (f32[24,512]{1,0:T(8,128)S(1)}, f32[24,512]{1,0:T(8,128)S(1)}, u32[]{:S(2)}, u32[]{:S(2)}) collective-permute-start(f32[24,512]{1,0:T(8,128)S(1)} %remap_last.1.last), channel_id=1, source_target_pairs={{0,2},{2,0},{1,3},{3,1},{4,6},{6,4},{5,7},{7,5},{8,10},{10,8},{9,1... | collective-permute-start | bytes 147464 | tf_op jit(solution)/shard_map/ppermute | solution.py:444

commit v14 on v11

--- a/solution.py
+++ b/solution.py
@@ -21,7 +21,6 @@
 MEDIUM = pl.CostEstimate(flops=2_500_000_000, bytes_accessed=1, transcendentals=0)
 HEAVY = pl.CostEstimate(flops=10_000_000_000, bytes_accessed=1, transcendentals=0)
 
-NT = (((1,), (1,)), ((), ()))
 NN = (((1,), (0,)), ((), ()))
 
 
@@ -39,11 +38,11 @@
 
 def place_kernel(rows, columns, count, weights, *refs):
     high, low, total = refs[-3:]
-    band = 128
-
-    @pl.loop(0, PIXELS_DEV // band)
+    band = 256
+
+    @pl.loop(0, CELLS_DEV // band)
     def _(b):
-        total[pl.ds(pl.multiple_of(b * band, band), band), :] = jnp.zeros((band, CELLS_DEV), jnp.float32)
+        total[pl.ds(pl.multiple_of(b * band, band), band), :] = jnp.zeros((band, PIXELS_DEV), jnp.float32)
 
     lane_half = lax.broadcasted_iota(jnp.int32, (TILE, LANES), 1) // TILE
     live = count[0]
@@ -53,19 +52,19 @@
         for pair in range(GROUP // 2):
             lanes = pl.ds(pl.multiple_of((g * (GROUP // 2) + pair) * LANES, LANES), LANES)
             tiles = weights[:, lanes]
-            turned = pltpu.roll(tiles, TILE, 1)
+            turned = jnp.transpose(jnp.concatenate([tiles, tiles], axis=0))
             for i in range(2):
                 k = g * GROUP + pair * 2 + i
                 row, column = rows[k], columns[k]
-                side = jnp.where(k < live, column & 1, -1)
-                tile = jnp.where(lane_half == i, tiles, turned)
+                side = jnp.where(k < live, row & 1, -1)
                 at = (
-                    pl.ds(pl.multiple_of(row * TILE, TILE), TILE),
-                    pl.ds(pl.multiple_of((column >> 1) * LANES, LANES), LANES),
+                    pl.ds(pl.multiple_of(column * TILE, TILE), TILE),
+                    pl.ds(pl.multiple_of((row >> 1) * LANES, LANES), LANES),
                 )
+                tile = turned[i * TILE : (i + 1) * TILE]
                 total[at] = total[at] + jnp.where(lane_half == side, tile, 0.0)
 
-    @pl.loop(0, PIXELS_DEV // band)
+    @pl.loop(0, CELLS_DEV // band)
     def _(b):
         at = pl.ds(pl.multiple_of(b * band, band), band)
         high[at, :], low[at, :] = split(total[at, :])
@@ -74,13 +73,13 @@
 def place_tiles(rows, columns, count, weights, *after):
     smem = pl.BlockSpec(memory_space=pltpu.SMEM)
     vmem = pl.BlockSpec(memory_space=pltpu.VMEM)
-    half = jax.ShapeDtypeStruct((PIXELS_DEV, CELLS_DEV), jnp.bfloat16)
+    half = jax.ShapeDtypeStruct((CELLS_DEV, PIXELS_DEV), jnp.bfloat16)
     return pl.pallas_call(
         place_kernel,
         out_shape=(half, half),
         in_specs=[smem, smem, smem, vmem] + [pl.BlockSpec(memory_space=pl.ANY)] * len(after),
         out_specs=(vmem, vmem),
-        scratch_shapes=[pltpu.VMEM((PIXELS_DEV, CELLS_DEV), jnp.float32)],
+        scratch_shapes=[pltpu.VMEM((CELLS_DEV, PIXELS_DEV), jnp.float32)],
         compiler_params=pltpu.CompilerParams(vmem_limit_bytes=28 * MIB),
         cost_estimate=LIGHT,
         name="place_tiles",
@@ -96,8 +95,8 @@
     both = jnp.concatenate([x_high, x_low], axis=0)
     for start in range(0, PIXELS_DEV, PIXEL_BLOCK):
         at = slice(start, start + PIXEL_BLOCK)
-        first = dot(both, high[at, :], NT)
-        yield at, first[:m] + first[m:] + dot(x_high, low[at, :], NT)
+        first = dot(both, high[:, at], NN)
+        yield at, first[:m] + first[m:] + dot(x_high, low[:, at], NN)
 
 
 def remap_call(kernel, inputs, after, out_rows, high, low, cost, name, scratch_rows=()):

time: 39.6 us -> 38.6 us (0.975)
  waiting for transfers between devices: 3.16 us -> 8.23 us
  Pallas kernels: 18.8 us -> 13.9 us
  starting transfers between devices: 15.9 us -> 14.7 us
    pallas_call x4, Pallas kernels: 10.3 us -> 5.89 us  [remap_call(): pl.pallas_call(kernel, out_shape=[jax.ShapeDtypeStruct(rows if isinstance...]
    ppermute x7, waiting for transfers between devices: 0.2 us -> 3.68 us  [to_peer(): return lax.ppermute(x, ('lev', 'sub'), pairs)]
    ppermute x6, waiting for transfers between devices: 2.97 us -> 4.55 us  [swap(): return lax.ppermute(x, 'tm', [(0, 1), (1, 0)])]
    ppermute x6, starting transfers between devices: 7.43 us -> 6.51 us  [swap(): return lax.ppermute(x, 'tm', [(0, 1), (1, 0)])]
    pallas_call x1, Pallas kernels: 4.32 us -> 3.89 us  [place_tiles(): pl.pallas_call(place_kernel, out_shape=(half, half), in_specs=[smem, smem...]
  transfers between devices with their start and end apart: 13 -> 13, of which waited for: 4 -> 6; matrix products, arithmetic and copies ran while one was open for 0% -> 0% of each run, Pallas kernels for 39% -> 28%
where the time goes in v14:
time: 38.6 us; the launch traced here: 38.4 us
  starting transfers between devices  14.7 us (38%)
  Pallas kernels  13.9 us (36%)
  waiting for transfers between devices  8.23 us (21%)
  local copies, waits for them, and re-layouts  0.82 us (2%)
  between operations  0.78 us (2%)
    ppermute x7, starting transfers between devices, to_peer(): return lax.ppermute(x, ('lev', 'sub'), pairs)  8.15 us
    ppermute x6, starting transfers between devices, swap(): return lax.ppermute(x, 'tm', [(0, 1), (1, 0)])  6.51 us
    pallas_call x4, Pallas kernels, remap_call(): pl.pallas_call(kernel, out_shape=[jax.ShapeDtypeStruct(rows if isinstance...  5.89 us
    ppermute x6, waiting for transfers between devices, swap(): return lax.ppermute(x, 'tm', [(0, 1), (1, 0)])  4.55 us
    pallas_call x1, Pallas kernels, place_tiles(): pl.pallas_call(place_kernel, out_shape=(half, half), in_specs=[smem, smem...  3.89 us
    ppermute x7, waiting for transfers between devices, to_peer(): return lax.ppermute(x, ('lev', 'sub'), pairs)  3.68 us
    pallas_call x1, Pallas kernels, hour_sums(): pl.pallas_call(functools.partial(sums_kernel, plain, first, second), out_...  3.28 us
    pallas_call x5, Pallas kernels, small_call(): pl.pallas_call(kernel, out_shape=[jax.ShapeDtypeStruct(shape, jnp.float32...  0.85 us
  transfers between devices with their start and end apart: 13, of which 6 were waited for; matrix products, arithmetic and copies ran while one was open for 0% of the time, Pallas kernels for 28%

profile of v14, /device:TPU:0, one launch (start us, length us, event | category | flops | bytes accessed | tf_op | source)
XLA Modules:
  0.0 38.4 jit_solution(8128219987094467459)
XLA Ops:
  0.0 0.8 %copy-done.1 = s32[8]{0:T(128)S(1)} copy-done((s32[8]{0:T(128)S(1)}, s32[8]{0:T(128)}, u32[]{:S(2)}) %copy-start.1) | copy-done | bytes 56
  0.8 3.3 %hour_sums.1 = (f32[24,2048]{1,0:T(8,128)S(1)}, f32[24,2048]{1,0:T(8,128)S(1)}, f32[24,2048]{1,0:T(8,128)S(1)}, f32[24,2048]{1,0:T(8,128)S(1)}, f32[24,2048]{1,0...) custom-call(s32[8]{0:T(128)S(1)} %copy-done.1, ...), custom_call_target="tpu_custom_call" | custom-call | flops 1 | bytes 1 | tf_op jit(solution)/shard_map/hour_sums/pallas_call | solution.py:311
  4.1 0.5 %collective-permute-start = (f32[24,2048]{1,0:T(8,128)S(1)}, f32[24,2048]{1,0:T(8,128)S(1)}, u32[]{:S(2)}, u32[]{:S(2)}) collective-permute-start(f32[24,2048]{1,0:T(8,128)S(1)} %get-tuple-element.23), channel_id=1, source_target_pairs={{0,1},{1,0},{4,5},{5,4},{8,9},{9,8},{12,13},{13,12},{2,3},{3,2},{6... | collective-permute-start | bytes 589832 | tf_op jit(solution)/shard_map/ppermute | solution.py:440
  4.6 2.6 %collective-permute-start.2 = (f32[48,1024]{1,0:T(8,128)S(1)}, f32[48,1024]{1,0:T(8,128)S(1)}, u32[]{:S(2)}, u32[]{:S(2)}) collective-permute-start(f32[48,1024]{1,0:T(8,128)S(1)} %get-tuple-element.25.refs_0_), channel_id=1, source_target_pairs={{0,2},{2,0},{1,3},{3,1},{4,6},{6,4},{5,7},{7,5},{8,10},{10,8},{9,1... | collective-permute-start | bytes 589832 | tf_op jit(solution)/shard_map/ppermute | solution.py:443
  7.2 2.6 %collective-permute-start.1 = (f32[24,2048]{1,0:T(8,128)S(1)}, f32[24,2048]{1,0:T(8,128)S(1)}, u32[]{:S(2)}, u32[]{:S(2)}) collective-permute-start(f32[24,2048]{1,0:T(8,128)S(1)} %get-tuple-element.24), channel_id=1, source_target_pairs={{0,8},{1,9},{4,12},{5,13},{8,0},{9,1},{12,4},{13,5},{2,10},{3,11},... | collective-permute-start | bytes 589832 | tf_op jit(solution)/shard_map/ppermute | solution.py:440
  9.8 1.6 %collective-permute-start.5 = (f32[24,2048]{1,0:T(8,128)S(1)}, f32[24,2048]{1,0:T(8,128)S(1)}, u32[]{:S(2)}, u32[]{:S(2)}) collective-permute-start(f32[24,2048]{1,0:T(8,128)S(1)} %get-tuple-element.33), channel_id=1, source_target_pairs={{0,4},{1,5},{4,0},{5,1},{8,12},{9,13},{12,8},{13,9},{2,6},{3,7},{6... | collective-permute-start | bytes 589832 | tf_op jit(solution)/shard_map/ppermute | solution.py:440
  11.4 0.0 collective-permute-start.9
  12.0 3.9 %place_tiles.1 = (bf16[2048,1024]{1,0:T(8,128)(2,1)S(1)}, bf16[2048,1024]{1,0:T(8,128)(2,1)S(1)}) custom-call(s32[128]{0:T(128)S(1)} %copy-done.2, s32[128]{0:T(128)S(1)} %copy-done.3, s32[1]{0:T(128)S(6)} %copy.9.count, f32[64,8192]{1,0:T(8,128)S(1)} %copy-done, f32[48,1024]{1,0:T(8,128)S(1)} %get-tuple-element.25.refs_0_), custom_call_target="tpu_custom_call" | custom-call | flops 1 | bytes 1 | tf_op jit(solution)/shard_map/place_tiles/pallas_call | solution.py:77
  15.9 0.0 collective-permute-done.refs_1_.sibling
  15.9 0.0 collective-permute-done.2.got
  16.0 0.7 %collective-permute-start.7 = (f32[24,1024]{1,0:T(8,128)S(1)}, f32[24,1024]{1,0:T(8,128)S(1)}, u32[]{:S(2)}, u32[]{:S(2)}) collective-permute-start(f32[24,1024]{1,0:T(8,128)S(1)} %merge_first.1.refs_0_), channel_id=1, source_target_pairs={{0,12},{1,13},{4,8},{5,9},{8,4},{9,5},{12,0},{13,1},{2,14},{3,15},... | collective-permute-start | bytes 294920 | tf_op jit(solution)/shard_map/ppermute | solution.py:440
  16.6 2.7 %collective-permute-start.8 = (f32[24,1024]{1,0:T(8,128)S(1)}, f32[24,1024]{1,0:T(8,128)S(1)}, u32[]{:S(2)}, u32[]{:S(2)}) collective-permute-start(f32[24,1024]{1,0:T(8,128)S(1)} %merge_next.1.refs_1_), channel_id=1, source_target_pairs={{0,13},{1,12},{4,9},{5,8},{8,5},{9,4},{12,1},{13,0},{2,15},{3,14},... | collective-permute-start | bytes 294920 | tf_op jit(solution)/shard_map/ppermute | solution.py:440
  19.4 0.2 collective-permute-done.1.refs_0_.plain
  19.6 0.5 %collective-permute-start.4 = (f32[24,1024]{1,0:T(8,128)S(1)}, f32[24,1024]{1,0:T(8,128)S(1)}, u32[]{:S(2)}, u32[]{:S(2)}) collective-permute-start(f32[24,1024]{1,0:T(8,128)S(1)} %hold.1.refs_0_), channel_id=1, source_target_pairs={{0,2},{2,0},{1,3},{3,1},{4,6},{6,4},{5,7},{7,5},{8,10},{10,8},{9,1... | collective-permute-start | bytes 294920 | tf_op jit(solution)/shard_map/ppermute | solution.py:443
  20.1 1.5 %remap_both.1 = (f32[48,1024]{1,0:T(8,128)S(1)}, f32[48,1024]{1,0:T(8,128)S(1)}) custom-call(f32[24,2048]{1,0:T(8,128)S(1)} %get-tuple-element.22.own, f32[24,2048]{1,0:T(8,128)S(1)} %collective-permute-done.refs_1_.sibling, f32[24,2048]{1,0:T(8,128)S(1)} %collective-permute-done.1.refs_0_.plain, bf16[2048,1024]{1,0:T(8,128)(2,1)S(1)} %get-tuple-element.26.refs_0_.high, ...), custom_call_target="tpu_custom_call" | custom-call | flops 2500000000 | bytes 1 | tf_op jit(solution)/shard_map/remap_both/pallas_call | solution.py:104
  21.6 0.0 collective-permute-done.5.refs_1_.near_same
  21.6 1.7 %collective-permute-start.3 = (f32[48,1024]{1,0:T(8,128)S(1)}, f32[48,1024]{1,0:T(8,128)S(1)}, u32[]{:S(2)}, u32[]{:S(2)}) collective-permute-start(f32[48,1024]{1,0:T(8,128)S(1)} %get-tuple-element.31), channel_id=1, source_target_pairs={{0,2},{2,0},{1,3},{3,1},{4,6},{6,4},{5,7},{7,5},{8,10},{10,8},{9,1... | collective-permute-start | bytes 589832 | tf_op jit(solution)/shard_map/ppermute | solution.py:443
  23.3 1.8 %collective-permute-done.4.got = f32[24,1024]{1,0:T(8,128)S(1)} collective-permute-done((f32[24,1024]{1,0:T(8,128)S(1)}, f32[24,1024]{1,0:T(8,128)S(1)}, u32[]{:S(2)}, u32[]{:S(2)}) %collective-permute-start.4) | collective-permute-done | bytes 98336 | tf_op jit(solution)/shard_map/ppermute | solution.py:443
  25.1 0.1 collective-permute-start.6
  25.1 0.0 collective-permute-done.9.near_other
  25.2 1.5 %remap_near.1 = (f32[24,1024]{1,0:T(8,128)S(1)}, f32[24,1024]{1,0:T(8,128)S(1)}) custom-call(f32[24,2048]{1,0:T(8,128)S(1)} %collective-permute-done.5.refs_1_.near_same, f32[24,2048]{1,0:T(8,128)S(1)} %collective-permute-done.9.near_other, bf16[2048,1024]{1,0:T(8,128)(2,1)S(1)} %get-tuple-element.26.refs_0_.high, ...), custom_call_target="tpu_custom_call" | custom-call | flops 1 | bytes 1 | tf_op jit(solution)/shard_map/remap_near/pallas_call | solution.py:104
  26.7 0.4 %collective-permute-start.11 = (f32[24,1024]{1,0:T(8,128)S(1)}, f32[24,1024]{1,0:T(8,128)S(1)}, u32[]{:S(2)}, u32[]{:S(2)}) collective-permute-start(f32[24,1024]{1,0:T(8,128)S(1)} %get-tuple-element.37.first_hour), channel_id=1, source_target_pairs={{0,2},{2,0},{1,3},{3,1},{4,6},{6,4},{5,7},{7,5},{8,10},{10,8},{9,1... | collective-permute-start | bytes 294920 | tf_op jit(solution)/shard_map/ppermute | solution.py:443
  27.1 0.9 %collective-permute-done.8.other = f32[24,1024]{1,0:T(8,128)S(1)} collective-permute-done((f32[24,1024]{1,0:T(8,128)S(1)}, f32[24,1024]{1,0:T(8,128)S(1)}, u32[]{:S(2)}, u32[]{:S(2)}) %collective-permute-start.8) | collective-permute-done | bytes 98336 | tf_op jit(solution)/shard_map/ppermute | solution.py:440
  28.0 0.0 collective-permute-done.7.same
  28.0 1.6 %remap_far.1 = (f32[24,1024]{1,0:T(8,128)S(1)}, f32[24,1024]{1,0:T(8,128)S(1)}) custom-call(f32[24,1024]{1,0:T(8,128)S(1)} %collective-permute-done.7.same, f32[24,1024]{1,0:T(8,128)S(1)} %collective-permute-done.8.other, f32[24,1024]{1,0:T(8,128)S(1)} %get-tuple-element.35.near.second_hour, bf16[2048,1024]{1,0:T(8,128)(2,1)S(1)} %get-tuple-element.26.refs_0_.high, ...), custom_call_target="tpu_custom_call" | custom-call | flops 10000000000 | bytes 1 | tf_op jit(solution)/shard_map/remap_far/pallas_call | solution.py:104
  29.5 0.8 %collective-permute-start.12 = (f32[24,1024]{1,0:T(8,128)S(1)}, f32[24,1024]{1,0:T(8,128)S(1)}, u32[]{:S(2)}, u32[]{:S(2)}) collective-permute-start(f32[24,1024]{1,0:T(8,128)S(1)} %get-tuple-element.38), channel_id=1, source_target_pairs={{0,2},{2,0},{1,3},{3,1},{4,6},{6,4},{5,7},{7,5},{8,10},{10,8},{9,1... | collective-permute-start | bytes 294920 | tf_op jit(solution)/shard_map/ppermute | solution.py:443
  30.4 2.6 %collective-permute-done.6.block = f32[24,1024]{1,0:T(8,128)S(1)} collective-permute-done((f32[24,1024]{1,0:T(8,128)S(1)}, f32[24,1024]{1,0:T(8,128)S(1)}, u32[]{:S(2)}, u32[]{:S(2)}) %collective-permute-start.6) | collective-permute-done | bytes 98336 | tf_op jit(solution)/shard_map/ppermute | solution.py:440
  33.0 1.3 %remap_last.1.last = f32[24,512]{1,0:T(8,128)S(1)} custom-call(f32[24,1024]{1,0:T(8,128)S(1)} %collective-permute-done.6.block, bf16[2048,1024]{1,0:T(8,128)(2,1)S(1)} %get-tuple-element.26.refs_0_.high, bf16[2048,1024]{1,0:T(8,128)(2,1)S(1)} %get-tuple-element.27.low, f32[24,1024]{1,0:T(8,128)S(1)} %get-tuple-element.36.refs_0_.far), custom_call_target="tpu_custom_call" | custom-call | flops 10000000000 | bytes 1 | tf_op jit(solution)/shard_map/remap_last/pallas_call | solution.py:104
  34.3 0.5 %collective-permute-start.10 = (f32[24,512]{1,0:T(8,128)S(1)}, f32[24,512]{1,0:T(8,128)S(1)}, u32[]{:S(2)}, u32[]{:S(2)}) collective-permute-start(f32[24,512]{1,0:T(8,128)S(1)} %remap_last.1.last), channel_id=1, source_target_pairs={{0,2},{2,0},{1,3},{3,1},{4,6},{6,4},{5,7},{7,5},{8,10},{10,8},{9,1... | collective-permute-start | bytes 147464 | tf_op jit(solution)/shard_map/ppermute | solution.py:443
  34.8 0.1 collective-permute-done.12.got
  34.9 0.8 %write_first.1.begun = f32[96,1024]{1,0:T(8,128)} custom-call(f32[48,1024]{1,0:T(8,128)S(1)} %get-tuple-element.30.refs_0_.chip.plain, f32[48,1024]{1,0:T(8,128)S(1)} %collective-permute-done.3.got_chip.got_plain, f32[24,1024]{1,0:T(8,128)S(1)} %get-tuple-element.37.first_hour, f32[24,1024]{1,0:T(8,128)S(1)} %collective-permute-done.11.got_first, ...), custom_call_target="tpu_custom_call" | custom-call | flops 1 | bytes 1 | tf_op jit(solution)/shard_map/write_first/pallas_call | solution.py:354
  35.7 2.7 %collective-permute-done.10.got_last = f32[24,512]{1,0:T(8,128)S(1)} collective-permute-done((f32[24,512]{1,0:T(8,128)S(1)}, f32[24,512]{1,0:T(8,128)S(1)}, u32[]{:S(2)}, u32[]{:S(2)}) %collective-permute-start.10) | collective-permute-done | bytes 49184 | tf_op jit(solution)/shard_map/ppermute | solution.py:443
  (14 shorter events, 0.1 us)
Async XLA Ops:
  0.0 12.0 %copy-start = (f32[64,8192]{1,0:T(8,128)S(1)}, f32[64,8192]{1,0:T(8,128)}, u32[]{:S(2)}) copy-start(f32[64,8192]{1,0:T(8,128)} %weights.1) | copy-start | bytes 6291460
  0.0 0.8 %copy-start.1 = (s32[8]{0:T(128)S(1)}, s32[8]{0:T(128)}, u32[]{:S(2)}) copy-start(s32[8]{0:T(128)} %step_hour.1) | copy-start | bytes 100
  0.8 11.2 %copy-start.2 = (s32[128]{0:T(128)S(1)}, s32[128]{0:T(128)}, u32[]{:S(2)}) copy-start(s32[128]{0:T(128)} %rows.1) | copy-start | bytes 1540
  0.8 11.2 %copy-start.3 = (s32[128]{0:T(128)S(1)}, s32[128]{0:T(128)}, u32[]{:S(2)}) copy-start(s32[128]{0:T(128)} %columns.1) | copy-start | bytes 1540
  4.1 11.8 %collective-permute-start = (f32[24,2048]{1,0:T(8,128)S(1)}, f32[24,2048]{1,0:T(8,128)S(1)}, u32[]{:S(2)}, u32[]{:S(2)}) collective-permute-start(f32[24,2048]{1,0:T(8,128)S(1)} %get-tuple-element.23), channel_id=1, source_target_pairs={{0,1},{1,0},{4,5},{5,4},{8,9},{9,8},{12,13},{13,12},{2,3},{3,2},{6... | collective-permute-start | bytes 589832 | tf_op jit(solution)/shard_map/ppermute | solution.py:440
  4.6 11.3 %collective-permute-start.2 = (f32[48,1024]{1,0:T(8,128)S(1)}, f32[48,1024]{1,0:T(8,128)S(1)}, u32[]{:S(2)}, u32[]{:S(2)}) collective-permute-start(f32[48,1024]{1,0:T(8,128)S(1)} %get-tuple-element.25.refs_0_), channel_id=1, source_target_pairs={{0,2},{2,0},{1,3},{3,1},{4,6},{6,4},{5,7},{7,5},{8,10},{10,8},{9,1... | collective-permute-start | bytes 589832 | tf_op jit(solution)/shard_map/ppermute | solution.py:443
  7.2 12.4 %collective-permute-start.1 = (f32[24,2048]{1,0:T(8,128)S(1)}, f32[24,2048]{1,0:T(8,128)S(1)}, u32[]{:S(2)}, u32[]{:S(2)}) collective-permute-start(f32[24,2048]{1,0:T(8,128)S(1)} %get-tuple-element.24), channel_id=1, source_target_pairs={{0,8},{1,9},{4,12},{5,13},{8,0},{9,1},{12,4},{13,5},{2,10},{3,11},... | collective-permute-start | bytes 589832 | tf_op jit(solution)/shard_map/ppermute | solution.py:440
  9.8 11.8 %collective-permute-start.5 = (f32[24,2048]{1,0:T(8,128)S(1)}, f32[24,2048]{1,0:T(8,128)S(1)}, u32[]{:S(2)}, u32[]{:S(2)}) collective-permute-start(f32[24,2048]{1,0:T(8,128)S(1)} %get-tuple-element.33), channel_id=1, source_target_pairs={{0,4},{1,5},{4,0},{5,1},{8,12},{9,13},{12,8},{13,9},{2,6},{3,7},{6... | collective-permute-start | bytes 589832 | tf_op jit(solution)/shard_map/ppermute | solution.py:440
  11.4 13.8 %collective-permute-start.9 = (f32[24,2048]{1,0:T(8,128)S(1)}, f32[24,2048]{1,0:T(8,128)S(1)}, u32[]{:S(2)}, u32[]{:S(2)}) collective-permute-start(f32[24,2048]{1,0:T(8,128)S(1)} %get-tuple-element.34), channel_id=1, source_target_pairs={{0,5},{1,4},{4,1},{5,0},{8,13},{9,12},{12,9},{13,8},{2,7},{3,6},{6... | collective-permute-start | bytes 589832 | tf_op jit(solution)/shard_map/ppermute | solution.py:440
  16.0 12.0 %collective-permute-start.7 = (f32[24,1024]{1,0:T(8,128)S(1)}, f32[24,1024]{1,0:T(8,128)S(1)}, u32[]{:S(2)}, u32[]{:S(2)}) collective-permute-start(f32[24,1024]{1,0:T(8,128)S(1)} %merge_first.1.refs_0_), channel_id=1, source_target_pairs={{0,12},{1,13},{4,8},{5,9},{8,4},{9,5},{12,0},{13,1},{2,14},{3,15},... | collective-permute-start | bytes 294920 | tf_op jit(solution)/shard_map/ppermute | solution.py:440
  16.6 11.3 %collective-permute-start.8 = (f32[24,1024]{1,0:T(8,128)S(1)}, f32[24,1024]{1,0:T(8,128)S(1)}, u32[]{:S(2)}, u32[]{:S(2)}) collective-permute-start(f32[24,1024]{1,0:T(8,128)S(1)} %merge_next.1.refs_1_), channel_id=1, source_target_pairs={{0,13},{1,12},{4,9},{5,8},{8,5},{9,4},{12,1},{13,0},{2,15},{3,14},... | collective-permute-start | bytes 294920 | tf_op jit(solution)/shard_map/ppermute | solution.py:440
  19.6 5.5 %collective-permute-start.4 = (f32[24,1024]{1,0:T(8,128)S(1)}, f32[24,1024]{1,0:T(8,128)S(1)}, u32[]{:S(2)}, u32[]{:S(2)}) collective-permute-start(f32[24,1024]{1,0:T(8,128)S(1)} %hold.1.refs_0_), channel_id=1, source_target_pairs={{0,2},{2,0},{1,3},{3,1},{4,6},{6,4},{5,7},{7,5},{8,10},{10,8},{9,1... | collective-permute-start | bytes 294920 | tf_op jit(solution)/shard_map/ppermute | solution.py:443
  21.6 13.3 %collective-permute-start.3 = (f32[48,1024]{1,0:T(8,128)S(1)}, f32[48,1024]{1,0:T(8,128)S(1)}, u32[]{:S(2)}, u32[]{:S(2)}) collective-permute-start(f32[48,1024]{1,0:T(8,128)S(1)} %get-tuple-element.31), channel_id=1, source_target_pairs={{0,2},{2,0},{1,3},{3,1},{4,6},{6,4},{5,7},{7,5},{8,10},{10,8},{9,1... | collective-permute-start | bytes 589832 | tf_op jit(solution)/shard_map/ppermute | solution.py:443
  25.1 7.9 %collective-permute-start.6 = (f32[24,1024]{1,0:T(8,128)S(1)}, f32[24,1024]{1,0:T(8,128)S(1)}, u32[]{:S(2)}, u32[]{:S(2)}) collective-permute-start(f32[24,1024]{1,0:T(8,128)S(1)} %merge_last.1.refs_0_), channel_id=1, source_target_pairs={{0,9},{1,8},{4,13},{5,12},{8,1},{9,0},{12,5},{13,4},{2,11},{3,10},... | collective-permute-start | bytes 294920 | tf_op jit(solution)/shard_map/ppermute | solution.py:440
  26.7 8.2 %collective-permute-start.11 = (f32[24,1024]{1,0:T(8,128)S(1)}, f32[24,1024]{1,0:T(8,128)S(1)}, u32[]{:S(2)}, u32[]{:S(2)}) collective-permute-start(f32[24,1024]{1,0:T(8,128)S(1)} %get-tuple-element.37.first_hour), channel_id=1, source_target_pairs={{0,2},{2,0},{1,3},{3,1},{4,6},{6,4},{5,7},{7,5},{8,10},{10,8},{9,1... | collective-permute-start | bytes 294920 | tf_op jit(solution)/shard_map/ppermute | solution.py:443
  29.5 5.4 %collective-permute-start.12 = (f32[24,1024]{1,0:T(8,128)S(1)}, f32[24,1024]{1,0:T(8,128)S(1)}, u32[]{:S(2)}, u32[]{:S(2)}) collective-permute-start(f32[24,1024]{1,0:T(8,128)S(1)} %get-tuple-element.38), channel_id=1, source_target_pairs={{0,2},{2,0},{1,3},{3,1},{4,6},{6,4},{5,7},{7,5},{8,10},{10,8},{9,1... | collective-permute-start | bytes 294920 | tf_op jit(solution)/shard_map/ppermute | solution.py:443
  34.3 4.1 %collective-permute-start.10 = (f32[24,512]{1,0:T(8,128)S(1)}, f32[24,512]{1,0:T(8,128)S(1)}, u32[]{:S(2)}, u32[]{:S(2)}) collective-permute-start(f32[24,512]{1,0:T(8,128)S(1)} %remap_last.1.last), channel_id=1, source_target_pairs={{0,2},{2,0},{1,3},{3,1},{4,6},{6,4},{5,7},{7,5},{8,10},{10,8},{9,1... | collective-permute-start | bytes 147464 | tf_op jit(solution)/shard_map/ppermute | solution.py:443

commit v15 on v14

--- a/solution.py
+++ b/solution.py
@@ -439,6 +439,10 @@
         pairs = [(a * subs + b, (a ^ k) * subs + (b ^ j)) for a in range(levs) for b in range(subs)]
         return lax.ppermute(x, ("lev", "sub"), pairs)
 
+    def hand_over(x):
+        pairs = [(a * shards_tm + a // half, a * shards_tm + 1 - a // half) for a in range(levs)]
+        return lax.ppermute(x, ("lev", "tm"), pairs)
+
     def swap(x):
         return lax.ppermute(x, "tm", [(0, 1), (1, 0)])
 
@@ -497,7 +501,7 @@
         "remap_last",
         [padded],
     )
-    got_last = swap(last)
+    got_last = hand_over(last)
     levels = rows // 2
     out = write_first([both, got_both, first_hour, got_first, second_hour, far, got], levels, divisor)
     out = write_last(out, [both, got_both, last, got_last], levels, divisor)

time: 38.6 us -> 38.8 us (level)
  starting transfers between devices: 14.7 us -> 19.1 us
  waiting for transfers between devices: 8.23 us -> 4.29 us
  Pallas kernels: 13.9 us -> 13.5 us
    ppermute x6 -> x5, waiting for transfers between devices: 4.55 us -> 2.07 us  [swap(): return lax.ppermute(x, 'tm', [(0, 1), (1, 0)])]
    ppermute x0 -> x1, starting transfers between devices: none -> 2.44 us  [hand_over(): return lax.ppermute(x, ('lev', 'tm'), pairs)]
    ppermute x7, waiting for transfers between devices: 3.68 us -> 1.35 us  [to_peer(): return lax.ppermute(x, ('lev', 'sub'), pairs)]
    ppermute x7, starting transfers between devices: 8.15 us -> 9.79 us  [to_peer(): return lax.ppermute(x, ('lev', 'sub'), pairs)]
    ppermute x0 -> x1, waiting for transfers between devices: none -> 0.88 us  [hand_over(): return lax.ppermute(x, ('lev', 'tm'), pairs)]
    pallas_call x1, Pallas kernels: 3.89 us -> 3.44 us  [place_tiles(): pl.pallas_call(place_kernel, out_shape=(half, half), in_specs=[smem, smem...]
    ppermute x6 -> x5, starting transfers between devices: 6.51 us -> 6.83 us  [swap(): return lax.ppermute(x, 'tm', [(0, 1), (1, 0)])]
  transfers between devices with their start and end apart: 13 -> 13, of which waited for: 6 -> 3; matrix products, arithmetic and copies ran while one was open for 0% -> 0% of each run, Pallas kernels for 28% -> 26%
where the time goes in v15:
time: 38.8 us; the launch traced here: 38.5 us
  starting transfers between devices  19.1 us (49%)
  Pallas kernels  13.5 us (35%)
  waiting for transfers between devices  4.29 us (11%)
  local copies, waits for them, and re-layouts  0.82 us (2%)
  between operations  0.82 us (2%)
    ppermute x7, starting transfers between devices, to_peer(): return lax.ppermute(x, ('lev', 'sub'), pairs)  9.79 us
    ppermute x5, starting transfers between devices, swap(): return lax.ppermute(x, 'tm', [(0, 1), (1, 0)])  6.83 us
    pallas_call x4, Pallas kernels, remap_call(): pl.pallas_call(kernel, out_shape=[jax.ShapeDtypeStruct(rows if isinstance...  5.89 us
    pallas_call x1, Pallas kernels, place_tiles(): pl.pallas_call(place_kernel, out_shape=(half, half), in_specs=[smem, smem...  3.44 us
    pallas_call x1, Pallas kernels, hour_sums(): pl.pallas_call(functools.partial(sums_kernel, plain, first, second), out_...  3.28 us
    ppermute x1, starting transfers between devices, hand_over(): return lax.ppermute(x, ('lev', 'tm'), pairs)  2.44 us
    ppermute x5, waiting for transfers between devices, swap(): return lax.ppermute(x, 'tm', [(0, 1), (1, 0)])  2.07 us
    ppermute x7, waiting for transfers between devices, to_peer(): return lax.ppermute(x, ('lev', 'sub'), pairs)  1.35 us
  transfers between devices with their start and end apart: 13, of which 3 were waited for; matrix products, arithmetic and copies ran while one was open for 0% of the time, Pallas kernels for 26%

profile of v15, /device:TPU:0, one launch (start us, length us, event | category | flops | bytes accessed | tf_op | source)
XLA Modules:
  0.0 38.5 jit_solution(9961869619493410682)
XLA Ops:
  0.0 0.8 %copy-done.1 = s32[8]{0:T(128)S(1)} copy-done((s32[8]{0:T(128)S(1)}, s32[8]{0:T(128)}, u32[]{:S(2)}) %copy-start.1) | copy-done | bytes 56
  0.8 3.3 %hour_sums.1 = (f32[24,2048]{1,0:T(8,128)S(1)}, f32[24,2048]{1,0:T(8,128)S(1)}, f32[24,2048]{1,0:T(8,128)S(1)}, f32[24,2048]{1,0:T(8,128)S(1)}, f32[24,2048]{1,0...) custom-call(s32[8]{0:T(128)S(1)} %copy-done.1, ...), custom_call_target="tpu_custom_call" | custom-call | flops 1 | bytes 1 | tf_op jit(solution)/shard_map/hour_sums/pallas_call | solution.py:311
  4.1 0.5 %collective-permute-start = (f32[24,2048]{1,0:T(8,128)S(1)}, f32[24,2048]{1,0:T(8,128)S(1)}, u32[]{:S(2)}, u32[]{:S(2)}) collective-permute-start(f32[24,2048]{1,0:T(8,128)S(1)} %get-tuple-element.23), channel_id=1, source_target_pairs={{0,1},{1,0},{4,5},{5,4},{8,9},{9,8},{12,13},{13,12},{2,3},{3,2},{6... | collective-permute-start | bytes 589832 | tf_op jit(solution)/shard_map/ppermute | solution.py:440
  4.6 2.6 %collective-permute-start.2 = (f32[48,1024]{1,0:T(8,128)S(1)}, f32[48,1024]{1,0:T(8,128)S(1)}, u32[]{:S(2)}, u32[]{:S(2)}) collective-permute-start(f32[48,1024]{1,0:T(8,128)S(1)} %get-tuple-element.25.refs_0_), channel_id=1, source_target_pairs={{0,2},{2,0},{1,3},{3,1},{4,6},{6,4},{5,7},{7,5},{8,10},{10,8},{9,1... | collective-permute-start | bytes 589832 | tf_op jit(solution)/shard_map/ppermute | solution.py:447
  7.2 2.6 %collective-permute-start.1 = (f32[24,2048]{1,0:T(8,128)S(1)}, f32[24,2048]{1,0:T(8,128)S(1)}, u32[]{:S(2)}, u32[]{:S(2)}) collective-permute-start(f32[24,2048]{1,0:T(8,128)S(1)} %get-tuple-element.24), channel_id=1, source_target_pairs={{0,8},{1,9},{4,12},{5,13},{8,0},{9,1},{12,4},{13,5},{2,10},{3,11},... | collective-permute-start | bytes 589832 | tf_op jit(solution)/shard_map/ppermute | solution.py:440
  9.8 1.6 %collective-permute-start.5 = (f32[24,2048]{1,0:T(8,128)S(1)}, f32[24,2048]{1,0:T(8,128)S(1)}, u32[]{:S(2)}, u32[]{:S(2)}) collective-permute-start(f32[24,2048]{1,0:T(8,128)S(1)} %get-tuple-element.33), channel_id=1, source_target_pairs={{0,4},{1,5},{4,0},{5,1},{8,12},{9,13},{12,8},{13,9},{2,6},{3,7},{6... | collective-permute-start | bytes 589832 | tf_op jit(solution)/shard_map/ppermute | solution.py:440
  11.4 0.0 collective-permute-start.9
  12.0 3.4 %place_tiles.1 = (bf16[2048,1024]{1,0:T(8,128)(2,1)S(1)}, bf16[2048,1024]{1,0:T(8,128)(2,1)S(1)}) custom-call(s32[128]{0:T(128)S(1)} %copy-done.2, s32[128]{0:T(128)S(1)} %copy-done.3, s32[1]{0:T(128)S(6)} %copy.9.count, f32[64,8192]{1,0:T(8,128)S(1)} %copy-done, f32[48,1024]{1,0:T(8,128)S(1)} %get-tuple-element.25.refs_0_), custom_call_target="tpu_custom_call" | custom-call | flops 1 | bytes 1 | tf_op jit(solution)/shard_map/place_tiles/pallas_call | solution.py:77
  15.5 0.0 collective-permute-done.refs_1_.sibling
  15.5 0.0 collective-permute-done.2.got
  15.5 1.5 %collective-permute-start.7 = (f32[24,1024]{1,0:T(8,128)S(1)}, f32[24,1024]{1,0:T(8,128)S(1)}, u32[]{:S(2)}, u32[]{:S(2)}) collective-permute-start(f32[24,1024]{1,0:T(8,128)S(1)} %merge_first.1.refs_0_), channel_id=1, source_target_pairs={{0,12},{1,13},{4,8},{5,9},{8,4},{9,5},{12,0},{13,1},{2,14},{3,15},... | collective-permute-start | bytes 294920 | tf_op jit(solution)/shard_map/ppermute | solution.py:440
  17.1 3.5 %collective-permute-start.8 = (f32[24,1024]{1,0:T(8,128)S(1)}, f32[24,1024]{1,0:T(8,128)S(1)}, u32[]{:S(2)}, u32[]{:S(2)}) collective-permute-start(f32[24,1024]{1,0:T(8,128)S(1)} %merge_next.1.refs_1_), channel_id=1, source_target_pairs={{0,13},{1,12},{4,9},{5,8},{8,5},{9,4},{12,1},{13,0},{2,15},{3,14},... | collective-permute-start | bytes 294920 | tf_op jit(solution)/shard_map/ppermute | solution.py:440
  20.6 0.0 collective-permute-done.1.refs_0_.plain
  20.6 0.6 %collective-permute-start.4 = (f32[24,1024]{1,0:T(8,128)S(1)}, f32[24,1024]{1,0:T(8,128)S(1)}, u32[]{:S(2)}, u32[]{:S(2)}) collective-permute-start(f32[24,1024]{1,0:T(8,128)S(1)} %hold.1.refs_0_), channel_id=1, source_target_pairs={{0,2},{2,0},{1,3},{3,1},{4,6},{6,4},{5,7},{7,5},{8,10},{10,8},{9,1... | collective-permute-start | bytes 294920 | tf_op jit(solution)/shard_map/ppermute | solution.py:447
  21.2 1.5 %remap_both.1 = (f32[48,1024]{1,0:T(8,128)S(1)}, f32[48,1024]{1,0:T(8,128)S(1)}) custom-call(f32[24,2048]{1,0:T(8,128)S(1)} %get-tuple-element.22.own, f32[24,2048]{1,0:T(8,128)S(1)} %collective-permute-done.refs_1_.sibling, f32[24,2048]{1,0:T(8,128)S(1)} %collective-permute-done.1.refs_0_.plain, bf16[2048,1024]{1,0:T(8,128)(2,1)S(1)} %get-tuple-element.26.refs_0_.high, ...), custom_call_target="tpu_custom_call" | custom-call | flops 2500000000 | bytes 1 | tf_op jit(solution)/shard_map/remap_both/pallas_call | solution.py:104
  22.7 0.0 collective-permute-done.5.refs_1_.near_same
  22.7 1.6 %collective-permute-start.3 = (f32[48,1024]{1,0:T(8,128)S(1)}, f32[48,1024]{1,0:T(8,128)S(1)}, u32[]{:S(2)}, u32[]{:S(2)}) collective-permute-start(f32[48,1024]{1,0:T(8,128)S(1)} %get-tuple-element.31), channel_id=1, source_target_pairs={{0,2},{2,0},{1,3},{3,1},{4,6},{6,4},{5,7},{7,5},{8,10},{10,8},{9,1... | collective-permute-start | bytes 589832 | tf_op jit(solution)/shard_map/ppermute | solution.py:447
  24.3 2.1 %collective-permute-done.4.got = f32[24,1024]{1,0:T(8,128)S(1)} collective-permute-done((f32[24,1024]{1,0:T(8,128)S(1)}, f32[24,1024]{1,0:T(8,128)S(1)}, u32[]{:S(2)}, u32[]{:S(2)}) %collective-permute-start.4) | collective-permute-done | bytes 98336 | tf_op jit(solution)/shard_map/ppermute | solution.py:447
  26.3 0.1 collective-permute-start.6
  26.4 0.0 collective-permute-done.9.near_other
  26.4 1.5 %remap_near.1 = (f32[24,1024]{1,0:T(8,128)S(1)}, f32[24,1024]{1,0:T(8,128)S(1)}) custom-call(f32[24,2048]{1,0:T(8,128)S(1)} %collective-permute-done.5.refs_1_.near_same, f32[24,2048]{1,0:T(8,128)S(1)} %collective-permute-done.9.near_other, bf16[2048,1024]{1,0:T(8,128)(2,1)S(1)} %get-tuple-element.26.refs_0_.high, ...), custom_call_target="tpu_custom_call" | custom-call | flops 1 | bytes 1 | tf_op jit(solution)/shard_map/remap_near/pallas_call | solution.py:104
  27.9 0.1 collective-permute-start.11
  28.0 0.0 collective-permute-done.8.other
  28.0 0.0 collective-permute-done.7.same
  28.1 1.6 %remap_far.1 = (f32[24,1024]{1,0:T(8,128)S(1)}, f32[24,1024]{1,0:T(8,128)S(1)}) custom-call(f32[24,1024]{1,0:T(8,128)S(1)} %collective-permute-done.7.same, f32[24,1024]{1,0:T(8,128)S(1)} %collective-permute-done.8.other, f32[24,1024]{1,0:T(8,128)S(1)} %get-tuple-element.35.near.second_hour, bf16[2048,1024]{1,0:T(8,128)(2,1)S(1)} %get-tuple-element.26.refs_0_.high, ...), custom_call_target="tpu_custom_call" | custom-call | flops 10000000000 | bytes 1 | tf_op jit(solution)/shard_map/remap_far/pallas_call | solution.py:104
  29.6 2.0 %collective-permute-start.12 = (f32[24,1024]{1,0:T(8,128)S(1)}, f32[24,1024]{1,0:T(8,128)S(1)}, u32[]{:S(2)}, u32[]{:S(2)}) collective-permute-start(f32[24,1024]{1,0:T(8,128)S(1)} %get-tuple-element.38), channel_id=1, source_target_pairs={{0,2},{2,0},{1,3},{3,1},{4,6},{6,4},{5,7},{7,5},{8,10},{10,8},{9,1... | collective-permute-start | bytes 294920 | tf_op jit(solution)/shard_map/ppermute | solution.py:447
  31.7 1.3 %collective-permute-done.6.block = f32[24,1024]{1,0:T(8,128)S(1)} collective-permute-done((f32[24,1024]{1,0:T(8,128)S(1)}, f32[24,1024]{1,0:T(8,128)S(1)}, u32[]{:S(2)}, u32[]{:S(2)}) %collective-permute-start.6) | collective-permute-done | bytes 98336 | tf_op jit(solution)/shard_map/ppermute | solution.py:440
  33.0 1.3 %remap_last.1.last = f32[24,512]{1,0:T(8,128)S(1)} custom-call(f32[24,1024]{1,0:T(8,128)S(1)} %collective-permute-done.6.block, bf16[2048,1024]{1,0:T(8,128)(2,1)S(1)} %get-tuple-element.26.refs_0_.high, bf16[2048,1024]{1,0:T(8,128)(2,1)S(1)} %get-tuple-element.27.low, f32[24,1024]{1,0:T(8,128)S(1)} %get-tuple-element.36.refs_0_.far), custom_call_target="tpu_custom_call" | custom-call | flops 10000000000 | bytes 1 | tf_op jit(solution)/shard_map/remap_last/pallas_call | solution.py:104
  34.3 2.4 %collective-permute-start.10 = (f32[24,512]{1,0:T(8,128)S(1)}, f32[24,512]{1,0:T(8,128)S(1)}, u32[]{:S(2)}, u32[]{:S(2)}) collective-permute-start(f32[24,512]{1,0:T(8,128)S(1)} %remap_last.1.last), channel_id=1, source_target_pairs={{0,2},{4,6},{10,8},{14,12},{1,3},{5,7},{11,9},{15,13},{16,18},{20,... | collective-permute-start | bytes 147464 | tf_op jit(solution)/shard_map/ppermute | solution.py:444
  36.7 0.0 collective-permute-done.11.got_first
  36.8 0.8 %write_first.1.begun = f32[96,1024]{1,0:T(8,128)} custom-call(f32[48,1024]{1,0:T(8,128)S(1)} %get-tuple-element.30.refs_0_.chip.plain, f32[48,1024]{1,0:T(8,128)S(1)} %collective-permute-done.3.got_chip.got_plain, f32[24,1024]{1,0:T(8,128)S(1)} %get-tuple-element.37.first_hour, f32[24,1024]{1,0:T(8,128)S(1)} %collective-permute-done.11.got_first, ...), custom_call_target="tpu_custom_call" | custom-call | flops 1 | bytes 1 | tf_op jit(solution)/shard_map/write_first/pallas_call | solution.py:354
  37.6 0.9 %collective-permute-done.10.got_last = f32[24,512]{1,0:T(8,128)S(1)} collective-permute-done((f32[24,512]{1,0:T(8,128)S(1)}, f32[24,512]{1,0:T(8,128)S(1)}, u32[]{:S(2)}, u32[]{:S(2)}) %collective-permute-start.10) | collective-permute-done | bytes 49184 | tf_op jit(solution)/shard_map/ppermute | solution.py:444
  (14 shorter events, 0.1 us)
Async XLA Ops:
  0.0 12.0 %copy-start = (f32[64,8192]{1,0:T(8,128)S(1)}, f32[64,8192]{1,0:T(8,128)}, u32[]{:S(2)}) copy-start(f32[64,8192]{1,0:T(8,128)} %weights.1) | copy-start | bytes 6291460
  0.0 0.8 %copy-start.1 = (s32[8]{0:T(128)S(1)}, s32[8]{0:T(128)}, u32[]{:S(2)}) copy-start(s32[8]{0:T(128)} %step_hour.1) | copy-start | bytes 100
  0.8 11.2 %copy-start.2 = (s32[128]{0:T(128)S(1)}, s32[128]{0:T(128)}, u32[]{:S(2)}) copy-start(s32[128]{0:T(128)} %rows.1) | copy-start | bytes 1540
  0.8 11.2 %copy-start.3 = (s32[128]{0:T(128)S(1)}, s32[128]{0:T(128)}, u32[]{:S(2)}) copy-start(s32[128]{0:T(128)} %columns.1) | copy-start | bytes 1540
  4.1 11.4 %collective-permute-start = (f32[24,2048]{1,0:T(8,128)S(1)}, f32[24,2048]{1,0:T(8,128)S(1)}, u32[]{:S(2)}, u32[]{:S(2)}) collective-permute-start(f32[24,2048]{1,0:T(8,128)S(1)} %get-tuple-element.23), channel_id=1, source_target_pairs={{0,1},{1,0},{4,5},{5,4},{8,9},{9,8},{12,13},{13,12},{2,3},{3,2},{6... | collective-permute-start | bytes 589832 | tf_op jit(solution)/shard_map/ppermute | solution.py:440
  4.6 10.9 %collective-permute-start.2 = (f32[48,1024]{1,0:T(8,128)S(1)}, f32[48,1024]{1,0:T(8,128)S(1)}, u32[]{:S(2)}, u32[]{:S(2)}) collective-permute-start(f32[48,1024]{1,0:T(8,128)S(1)} %get-tuple-element.25.refs_0_), channel_id=1, source_target_pairs={{0,2},{2,0},{1,3},{3,1},{4,6},{6,4},{5,7},{7,5},{8,10},{10,8},{9,1... | collective-permute-start | bytes 589832 | tf_op jit(solution)/shard_map/ppermute | solution.py:447
  7.2 13.4 %collective-permute-start.1 = (f32[24,2048]{1,0:T(8,128)S(1)}, f32[24,2048]{1,0:T(8,128)S(1)}, u32[]{:S(2)}, u32[]{:S(2)}) collective-permute-start(f32[24,2048]{1,0:T(8,128)S(1)} %get-tuple-element.24), channel_id=1, source_target_pairs={{0,8},{1,9},{4,12},{5,13},{8,0},{9,1},{12,4},{13,5},{2,10},{3,11},... | collective-permute-start | bytes 589832 | tf_op jit(solution)/shard_map/ppermute | solution.py:440
  9.8 12.9 %collective-permute-start.5 = (f32[24,2048]{1,0:T(8,128)S(1)}, f32[24,2048]{1,0:T(8,128)S(1)}, u32[]{:S(2)}, u32[]{:S(2)}) collective-permute-start(f32[24,2048]{1,0:T(8,128)S(1)} %get-tuple-element.33), channel_id=1, source_target_pairs={{0,4},{1,5},{4,0},{5,1},{8,12},{9,13},{12,8},{13,9},{2,6},{3,7},{6... | collective-permute-start | bytes 589832 | tf_op jit(solution)/shard_map/ppermute | solution.py:440
  11.4 15.1 %collective-permute-start.9 = (f32[24,2048]{1,0:T(8,128)S(1)}, f32[24,2048]{1,0:T(8,128)S(1)}, u32[]{:S(2)}, u32[]{:S(2)}) collective-permute-start(f32[24,2048]{1,0:T(8,128)S(1)} %get-tuple-element.34), channel_id=1, source_target_pairs={{0,5},{1,4},{4,1},{5,0},{8,13},{9,12},{12,9},{13,8},{2,7},{3,6},{6... | collective-permute-start | bytes 589832 | tf_op jit(solution)/shard_map/ppermute | solution.py:440
  15.5 12.5 %collective-permute-start.7 = (f32[24,1024]{1,0:T(8,128)S(1)}, f32[24,1024]{1,0:T(8,128)S(1)}, u32[]{:S(2)}, u32[]{:S(2)}) collective-permute-start(f32[24,1024]{1,0:T(8,128)S(1)} %merge_first.1.refs_0_), channel_id=1, source_target_pairs={{0,12},{1,13},{4,8},{5,9},{8,4},{9,5},{12,0},{13,1},{2,14},{3,15},... | collective-permute-start | bytes 294920 | tf_op jit(solution)/shard_map/ppermute | solution.py:440
  17.1 11.0 %collective-permute-start.8 = (f32[24,1024]{1,0:T(8,128)S(1)}, f32[24,1024]{1,0:T(8,128)S(1)}, u32[]{:S(2)}, u32[]{:S(2)}) collective-permute-start(f32[24,1024]{1,0:T(8,128)S(1)} %merge_next.1.refs_1_), channel_id=1, source_target_pairs={{0,13},{1,12},{4,9},{5,8},{8,5},{9,4},{12,1},{13,0},{2,15},{3,14},... | collective-permute-start | bytes 294920 | tf_op jit(solution)/shard_map/ppermute | solution.py:440
  20.6 5.7 %collective-permute-start.4 = (f32[24,1024]{1,0:T(8,128)S(1)}, f32[24,1024]{1,0:T(8,128)S(1)}, u32[]{:S(2)}, u32[]{:S(2)}) collective-permute-start(f32[24,1024]{1,0:T(8,128)S(1)} %hold.1.refs_0_), channel_id=1, source_target_pairs={{0,2},{2,0},{1,3},{3,1},{4,6},{6,4},{5,7},{7,5},{8,10},{10,8},{9,1... | collective-permute-start | bytes 294920 | tf_op jit(solution)/shard_map/ppermute | solution.py:447
  22.7 14.0 %collective-permute-start.3 = (f32[48,1024]{1,0:T(8,128)S(1)}, f32[48,1024]{1,0:T(8,128)S(1)}, u32[]{:S(2)}, u32[]{:S(2)}) collective-permute-start(f32[48,1024]{1,0:T(8,128)S(1)} %get-tuple-element.31), channel_id=1, source_target_pairs={{0,2},{2,0},{1,3},{3,1},{4,6},{6,4},{5,7},{7,5},{8,10},{10,8},{9,1... | collective-permute-start | bytes 589832 | tf_op jit(solution)/shard_map/ppermute | solution.py:447
  26.3 6.6 %collective-permute-start.6 = (f32[24,1024]{1,0:T(8,128)S(1)}, f32[24,1024]{1,0:T(8,128)S(1)}, u32[]{:S(2)}, u32[]{:S(2)}) collective-permute-start(f32[24,1024]{1,0:T(8,128)S(1)} %merge_last.1.refs_0_), channel_id=1, source_target_pairs={{0,9},{1,8},{4,13},{5,12},{8,1},{9,0},{12,5},{13,4},{2,11},{3,10},... | collective-permute-start | bytes 294920 | tf_op jit(solution)/shard_map/ppermute | solution.py:440
  27.9 8.8 %collective-permute-start.11 = (f32[24,1024]{1,0:T(8,128)S(1)}, f32[24,1024]{1,0:T(8,128)S(1)}, u32[]{:S(2)}, u32[]{:S(2)}) collective-permute-start(f32[24,1024]{1,0:T(8,128)S(1)} %get-tuple-element.37.first_hour), channel_id=1, source_target_pairs={{0,2},{2,0},{1,3},{3,1},{4,6},{6,4},{5,7},{7,5},{8,10},{10,8},{9,1... | collective-permute-start | bytes 294920 | tf_op jit(solution)/shard_map/ppermute | solution.py:447
  29.6 7.1 %collective-permute-start.12 = (f32[24,1024]{1,0:T(8,128)S(1)}, f32[24,1024]{1,0:T(8,128)S(1)}, u32[]{:S(2)}, u32[]{:S(2)}) collective-permute-start(f32[24,1024]{1,0:T(8,128)S(1)} %get-tuple-element.38), channel_id=1, source_target_pairs={{0,2},{2,0},{1,3},{3,1},{4,6},{6,4},{5,7},{7,5},{8,10},{10,8},{9,1... | collective-permute-start | bytes 294920 | tf_op jit(solution)/shard_map/ppermute | solution.py:447
  34.3 4.2 %collective-permute-start.10 = (f32[24,512]{1,0:T(8,128)S(1)}, f32[24,512]{1,0:T(8,128)S(1)}, u32[]{:S(2)}, u32[]{:S(2)}) collective-permute-start(f32[24,512]{1,0:T(8,128)S(1)} %remap_last.1.last), channel_id=1, source_target_pairs={{0,2},{4,6},{10,8},{14,12},{1,3},{5,7},{11,9},{15,13},{16,18},{20,... | collective-permute-start | bytes 147464 | tf_op jit(solution)/shard_map/ppermute | solution.py:444

commit v16 on v9

--- a/solution.py
+++ b/solution.py
@@ -21,7 +21,6 @@
 MEDIUM = pl.CostEstimate(flops=2_500_000_000, bytes_accessed=1, transcendentals=0)
 HEAVY = pl.CostEstimate(flops=10_000_000_000, bytes_accessed=1, transcendentals=0)
 
-NT = (((1,), (1,)), ((), ()))
 NN = (((1,), (0,)), ((), ()))
 
 
@@ -39,11 +38,11 @@
 
 def place_kernel(rows, columns, count, weights, *refs):
     high, low, total = refs[-3:]
-    band = 128
-
-    @pl.loop(0, PIXELS_DEV // band)
+    band = 256
+
+    @pl.loop(0, CELLS_DEV // band)
     def _(b):
-        total[pl.ds(pl.multiple_of(b * band, band), band), :] = jnp.zeros((band, CELLS_DEV), jnp.float32)
+        total[pl.ds(pl.multiple_of(b * band, band), band), :] = jnp.zeros((band, PIXELS_DEV), jnp.float32)
 
     lane_half = lax.broadcasted_iota(jnp.int32, (TILE, LANES), 1) // TILE
     live = count[0]
@@ -53,19 +52,19 @@
         for pair in range(GROUP // 2):
             lanes = pl.ds(pl.multiple_of((g * (GROUP // 2) + pair) * LANES, LANES), LANES)
             tiles = weights[:, lanes]
-            turned = pltpu.roll(tiles, TILE, 1)
+            turned = jnp.transpose(jnp.concatenate([tiles, tiles], axis=0))
             for i in range(2):
                 k = g * GROUP + pair * 2 + i
                 row, column = rows[k], columns[k]
-                side = jnp.where(k < live, column & 1, -1)
-                tile = jnp.where(lane_half == i, tiles, turned)
+                side = jnp.where(k < live, row & 1, -1)
                 at = (
-                    pl.ds(pl.multiple_of(row * TILE, TILE), TILE),
-                    pl.ds(pl.multiple_of((column >> 1) * LANES, LANES), LANES),
+                    pl.ds(pl.multiple_of(column * TILE, TILE), TILE),
+                    pl.ds(pl.multiple_of((row >> 1) * LANES, LANES), LANES),
                 )
+                tile = turned[i * TILE : (i + 1) * TILE]
                 total[at] = total[at] + jnp.where(lane_half == side, tile, 0.0)
 
-    @pl.loop(0, PIXELS_DEV // band)
+    @pl.loop(0, CELLS_DEV // band)
     def _(b):
         at = pl.ds(pl.multiple_of(b * band, band), band)
         high[at, :], low[at, :] = split(total[at, :])
@@ -74,13 +73,13 @@
 def place_tiles(rows, columns, count, weights, *after):
     smem = pl.BlockSpec(memory_space=pltpu.SMEM)
     vmem = pl.BlockSpec(memory_space=pltpu.VMEM)
-    half = jax.ShapeDtypeStruct((PIXELS_DEV, CELLS_DEV), jnp.bfloat16)
+    half = jax.ShapeDtypeStruct((CELLS_DEV, PIXELS_DEV), jnp.bfloat16)
     return pl.pallas_call(
         place_kernel,
         out_shape=(half, half),
         in_specs=[smem, smem, smem, vmem] + [pl.BlockSpec(memory_space=pl.ANY)] * len(after),
         out_specs=(vmem, vmem),
-        scratch_shapes=[pltpu.VMEM((PIXELS_DEV, CELLS_DEV), jnp.float32)],
+        scratch_shapes=[pltpu.VMEM((CELLS_DEV, PIXELS_DEV), jnp.float32)],
         compiler_params=pltpu.CompilerParams(vmem_limit_bytes=28 * MIB),
         cost_estimate=LIGHT,
         name="place_tiles",
@@ -96,8 +95,8 @@
     both = jnp.concatenate([x_high, x_low], axis=0)
     for start in range(0, PIXELS_DEV, PIXEL_BLOCK):
         at = slice(start, start + PIXEL_BLOCK)
-        first = dot(both, high[at, :], NT)
-        yield at, first[:m] + first[m:] + dot(x_high, low[at, :], NT)
+        first = dot(both, high[:, at], NN)
+        yield at, first[:m] + first[m:] + dot(x_high, low[:, at], NN)
 
 
 def remap_call(kernel, inputs, after, out_rows, high, low, cost, name, scratch_rows=()):
@@ -481,7 +480,7 @@
     )
     got_near = swap(near)
     (far,) = remap_call(remap_far_kernel, [far_same, far_other], [near], [rows], high, low, HEAVY, "remap_far")
-    got_far = swap(far)
+    got_far = hand_over(far)
     padded = -(-rows // 32) * 16
     (last,) = remap_call(
         remap_last_kernel,
@@ -494,7 +493,7 @@
         "remap_last",
         [padded],
     )
-    got_last = hand_over(last)
+    got_last = swap(last)
     levels = rows // 2
     out = write_first([both, got_both, near, got_near, far, got_far], levels, divisor)
     out = write_last(out, [both, got_both, last, got_last], levels, divisor)

time: 40.4 us -> 38.6 us (0.955)
  the two profiles are of different devices: /device:TPU:10 before, /device:TPU:0 now
where the time goes in v16:
time: 38.6 us; the launch traced here: 38.4 us
  starting transfers between devices  16.5 us (43%)
  Pallas kernels  12.9 us (33%)
  waiting for transfers between devices  7.37 us (19%)
  local copies, waits for them, and re-layouts  0.82 us (2%)
  between operations  0.8 us (2%)
    ppermute x7, starting transfers between devices, to_peer(): return lax.ppermute(x, ('lev', 'sub'), pairs)  8.76 us
    pallas_call x4, Pallas kernels, remap_call(): pl.pallas_call(kernel, out_shape=[jax.ShapeDtypeStruct(rows if isinstance...  5.89 us
    ppermute x5, starting transfers between devices, swap(): return lax.ppermute(x, 'tm', [(0, 1), (1, 0)])  5.34 us
    ppermute x5, waiting for transfers between devices, swap(): return lax.ppermute(x, 'tm', [(0, 1), (1, 0)])  3.92 us
    pallas_call x1, Pallas kernels, hour_sums(): pl.pallas_call(functools.partial(sums_kernel, plain, first, second), out_...  3.28 us
    ppermute x7, waiting for transfers between devices, to_peer(): return lax.ppermute(x, ('lev', 'sub'), pairs)  3.01 us
    pallas_call x1, Pallas kernels, place_tiles(): pl.pallas_call(place_kernel, out_shape=(half, half), in_specs=[smem, smem...  2.84 us
    ppermute x1, starting transfers between devices, hand_over(): return lax.ppermute(x, ('lev', 'tm'), pairs)  2.45 us
  transfers between devices with their start and end apart: 13, of which 6 were waited for; matrix products, arithmetic and copies ran while one was open for 0% of the time, Pallas kernels for 25%

profile of v16, /device:TPU:0, one launch (start us, length us, event | category | flops | bytes accessed | tf_op | source)
XLA Modules:
  0.0 38.4 jit_solution(17293841225465587408)
XLA Ops:
  0.0 0.8 %copy-done.1 = s32[8]{0:T(128)S(1)} copy-done((s32[8]{0:T(128)S(1)}, s32[8]{0:T(128)}, u32[]{:S(2)}) %copy-start.1) | copy-done | bytes 56
  0.8 3.3 %hour_sums.1 = (f32[24,2048]{1,0:T(8,128)S(1)}, f32[24,2048]{1,0:T(8,128)S(1)}, f32[24,2048]{1,0:T(8,128)S(1)}, f32[24,2048]{1,0:T(8,128)S(1)}, f32[24,2048]{1,0...) custom-call(s32[8]{0:T(128)S(1)} %copy-done.1, ...), custom_call_target="tpu_custom_call" | custom-call | flops 1 | bytes 1 | tf_op jit(solution)/shard_map/hour_sums/pallas_call | solution.py:306
  4.1 0.5 %collective-permute-start = (f32[24,2048]{1,0:T(8,128)S(1)}, f32[24,2048]{1,0:T(8,128)S(1)}, u32[]{:S(2)}, u32[]{:S(2)}) collective-permute-start(f32[24,2048]{1,0:T(8,128)S(1)} %get-tuple-element.19), channel_id=1, source_target_pairs={{0,1},{1,0},{4,5},{5,4},{8,9},{9,8},{12,13},{13,12},{2,3},{3,2},{6... | collective-permute-start | bytes 589832 | tf_op jit(solution)/shard_map/ppermute | solution.py:434
  4.6 2.6 %collective-permute-start.2 = (f32[48,1024]{1,0:T(8,128)S(1)}, f32[48,1024]{1,0:T(8,128)S(1)}, u32[]{:S(2)}, u32[]{:S(2)}) collective-permute-start(f32[48,1024]{1,0:T(8,128)S(1)} %get-tuple-element.21.refs_0_), channel_id=1, source_target_pairs={{0,2},{2,0},{1,3},{3,1},{4,6},{6,4},{5,7},{7,5},{8,10},{10,8},{9,1... | collective-permute-start | bytes 589832 | tf_op jit(solution)/shard_map/ppermute | solution.py:441
  7.2 2.6 %collective-permute-start.1 = (f32[24,2048]{1,0:T(8,128)S(1)}, f32[24,2048]{1,0:T(8,128)S(1)}, u32[]{:S(2)}, u32[]{:S(2)}) collective-permute-start(f32[24,2048]{1,0:T(8,128)S(1)} %get-tuple-element.20), channel_id=1, source_target_pairs={{0,8},{1,9},{4,12},{5,13},{8,0},{9,1},{12,4},{13,5},{2,10},{3,11},... | collective-permute-start | bytes 589832 | tf_op jit(solution)/shard_map/ppermute | solution.py:434
  9.8 1.6 %collective-permute-start.5 = (f32[24,2048]{1,0:T(8,128)S(1)}, f32[24,2048]{1,0:T(8,128)S(1)}, u32[]{:S(2)}, u32[]{:S(2)}) collective-permute-start(f32[24,2048]{1,0:T(8,128)S(1)} %get-tuple-element.29), channel_id=1, source_target_pairs={{0,4},{1,5},{4,0},{5,1},{8,12},{9,13},{12,8},{13,9},{2,6},{3,7},{6... | collective-permute-start | bytes 589832 | tf_op jit(solution)/shard_map/ppermute | solution.py:434
  11.4 0.0 collective-permute-start.9
  12.0 2.8 %place_tiles.1 = (bf16[2048,1024]{1,0:T(8,128)(2,1)S(1)}, bf16[2048,1024]{1,0:T(8,128)(2,1)S(1)}) custom-call(s32[128]{0:T(128)S(1)} %copy-done.2, s32[128]{0:T(128)S(1)} %copy-done.3, s32[1]{0:T(128)S(6)} %copy.9.count, f32[64,8192]{1,0:T(8,128)S(1)} %copy-done, f32[48,1024]{1,0:T(8,128)S(1)} %get-tuple-element.21.refs_0_), custom_call_target="tpu_custom_call" | custom-call | flops 1 | bytes 1 | tf_op jit(solution)/shard_map/place_tiles/pallas_call | solution.py:77
  14.9 0.0 collective-permute-done.refs_1_.sibling
  14.9 2.3 %collective-permute-start.7 = (f32[24,1024]{1,0:T(8,128)S(1)}, f32[24,1024]{1,0:T(8,128)S(1)}, u32[]{:S(2)}, u32[]{:S(2)}) collective-permute-start(f32[24,1024]{1,0:T(8,128)S(1)} %merge_first.1.refs_0_), channel_id=1, source_target_pairs={{0,12},{1,13},{4,8},{5,9},{8,4},{9,5},{12,0},{13,1},{2,14},{3,15},... | collective-permute-start | bytes 294920 | tf_op jit(solution)/shard_map/ppermute | solution.py:434
  17.2 1.7 %collective-permute-start.8 = (f32[24,1024]{1,0:T(8,128)S(1)}, f32[24,1024]{1,0:T(8,128)S(1)}, u32[]{:S(2)}, u32[]{:S(2)}) collective-permute-start(f32[24,1024]{1,0:T(8,128)S(1)} %merge_next.1.refs_1_), channel_id=1, source_target_pairs={{0,13},{1,12},{4,9},{5,8},{8,5},{9,4},{12,1},{13,0},{2,15},{3,14},... | collective-permute-start | bytes 294920 | tf_op jit(solution)/shard_map/ppermute | solution.py:434
  18.9 0.4 %collective-permute-done.1.refs_0_.plain = f32[24,2048]{1,0:T(8,128)S(1)} collective-permute-done((f32[24,2048]{1,0:T(8,128)S(1)}, f32[24,2048]{1,0:T(8,128)S(1)}, u32[]{:S(2)}, u32[]{:S(2)}) %collective-permute-start.1) | collective-permute-done | bytes 196640 | tf_op jit(solution)/shard_map/ppermute | solution.py:434
  19.4 0.6 %collective-permute-start.4 = (f32[24,1024]{1,0:T(8,128)S(1)}, f32[24,1024]{1,0:T(8,128)S(1)}, u32[]{:S(2)}, u32[]{:S(2)}) collective-permute-start(f32[24,1024]{1,0:T(8,128)S(1)} %hold.1.refs_0_), channel_id=1, source_target_pairs={{0,2},{2,0},{1,3},{3,1},{4,6},{6,4},{5,7},{7,5},{8,10},{10,8},{9,1... | collective-permute-start | bytes 294920 | tf_op jit(solution)/shard_map/ppermute | solution.py:441
  19.9 1.5 %remap_both.1 = (f32[48,1024]{1,0:T(8,128)S(1)}, f32[48,1024]{1,0:T(8,128)S(1)}) custom-call(f32[24,2048]{1,0:T(8,128)S(1)} %get-tuple-element.18.own, f32[24,2048]{1,0:T(8,128)S(1)} %collective-permute-done.refs_1_.sibling, f32[24,2048]{1,0:T(8,128)S(1)} %collective-permute-done.1.refs_0_.plain, bf16[2048,1024]{1,0:T(8,128)(2,1)S(1)} %get-tuple-element.22.refs_0_.high, ...), custom_call_target="tpu_custom_call" | custom-call | flops 2500000000 | bytes 1 | tf_op jit(solution)/shard_map/remap_both/pallas_call | solution.py:104
  21.5 1.6 %collective-permute-start.3 = (f32[48,1024]{1,0:T(8,128)S(1)}, f32[48,1024]{1,0:T(8,128)S(1)}, u32[]{:S(2)}, u32[]{:S(2)}) collective-permute-start(f32[48,1024]{1,0:T(8,128)S(1)} %get-tuple-element.27), channel_id=1, source_target_pairs={{0,2},{2,0},{1,3},{3,1},{4,6},{6,4},{5,7},{7,5},{8,10},{10,8},{9,1... | collective-permute-start | bytes 589832 | tf_op jit(solution)/shard_map/ppermute | solution.py:441
  23.1 1.6 %collective-permute-done.4.got = f32[24,1024]{1,0:T(8,128)S(1)} collective-permute-done((f32[24,1024]{1,0:T(8,128)S(1)}, f32[24,1024]{1,0:T(8,128)S(1)}, u32[]{:S(2)}, u32[]{:S(2)}) %collective-permute-start.4) | collective-permute-done | bytes 98336 | tf_op jit(solution)/shard_map/ppermute | solution.py:441
  24.7 0.1 collective-permute-start.6
  24.8 0.0 collective-permute-done.9.near_other
  24.8 1.5 %remap_near.1.refs_0_.lev_near = f32[48,1024]{1,0:T(8,128)S(1)} custom-call(f32[24,2048]{1,0:T(8,128)S(1)} %collective-permute-done.5.refs_1_.near_same, f32[24,2048]{1,0:T(8,128)S(1)} %collective-permute-done.9.near_other, bf16[2048,1024]{1,0:T(8,128)(2,1)S(1)} %get-tuple-element.22.refs_0_.high, bf16[2048,1024]{1,0:T(8,128)(2,1)S(1)} %get-tuple-element.23.low, ...), custom_call_target="tpu_custom_call" | custom-call | flops 1 | bytes 1 | tf_op jit(solution)/shard_map/remap_near/pallas_call | solution.py:104
  26.3 0.1 collective-permute-start.11
  26.4 1.7 %collective-permute-done.8.other = f32[24,1024]{1,0:T(8,128)S(1)} collective-permute-done((f32[24,1024]{1,0:T(8,128)S(1)}, f32[24,1024]{1,0:T(8,128)S(1)}, u32[]{:S(2)}, u32[]{:S(2)}) %collective-permute-start.8) | collective-permute-done | bytes 98336 | tf_op jit(solution)/shard_map/ppermute | solution.py:434
  28.1 0.0 collective-permute-done.7.same
  28.1 1.6 %remap_far.1.refs_0_.far = f32[24,1024]{1,0:T(8,128)S(1)} custom-call(f32[24,1024]{1,0:T(8,128)S(1)} %collective-permute-done.7.same, f32[24,1024]{1,0:T(8,128)S(1)} %collective-permute-done.8.other, bf16[2048,1024]{1,0:T(8,128)(2,1)S(1)} %get-tuple-element.22.refs_0_.high, bf16[2048,1024]{1,0:T(8,128)(2,1)S(1)} %get-tuple-element.23.low, ...), custom_call_target="tpu_custom_call" | custom-call | flops 10000000000 | bytes 1 | tf_op jit(solution)/shard_map/remap_far/pallas_call | solution.py:104
  29.6 2.4 %collective-permute-start.12 = (f32[24,1024]{1,0:T(8,128)S(1)}, f32[24,1024]{1,0:T(8,128)S(1)}, u32[]{:S(2)}, u32[]{:S(2)}) collective-permute-start(f32[24,1024]{1,0:T(8,128)S(1)} %remap_far.1.refs_0_.far), channel_id=1, source_target_pairs={{0,2},{4,6},{10,8},{14,12},{1,3},{5,7},{11,9},{15,13},{16,18},{20,... | collective-permute-start | bytes 294920 | tf_op jit(solution)/shard_map/ppermute | solution.py:438
  32.1 0.9 %collective-permute-done.6.block = f32[24,1024]{1,0:T(8,128)S(1)} collective-permute-done((f32[24,1024]{1,0:T(8,128)S(1)}, f32[24,1024]{1,0:T(8,128)S(1)}, u32[]{:S(2)}, u32[]{:S(2)}) %collective-permute-start.6) | collective-permute-done | bytes 98336 | tf_op jit(solution)/shard_map/ppermute | solution.py:434
  33.0 1.3 %remap_last.1.last = f32[24,512]{1,0:T(8,128)S(1)} custom-call(f32[24,1024]{1,0:T(8,128)S(1)} %collective-permute-done.6.block, bf16[2048,1024]{1,0:T(8,128)(2,1)S(1)} %get-tuple-element.22.refs_0_.high, bf16[2048,1024]{1,0:T(8,128)(2,1)S(1)} %get-tuple-element.23.low, f32[24,1024]{1,0:T(8,128)S(1)} %remap_far.1.refs_0_.far), custom_call_target="tpu_custom_call" | custom-call | flops 10000000000 | bytes 1 | tf_op jit(solution)/shard_map/remap_last/pallas_call | solution.py:104
  34.3 0.5 %collective-permute-start.10 = (f32[24,512]{1,0:T(8,128)S(1)}, f32[24,512]{1,0:T(8,128)S(1)}, u32[]{:S(2)}, u32[]{:S(2)}) collective-permute-start(f32[24,512]{1,0:T(8,128)S(1)} %remap_last.1.last), channel_id=1, source_target_pairs={{0,2},{2,0},{1,3},{3,1},{4,6},{6,4},{5,7},{7,5},{8,10},{10,8},{9,1... | collective-permute-start | bytes 147464 | tf_op jit(solution)/shard_map/ppermute | solution.py:441
  34.8 0.4 %collective-permute-done.12.got_far = f32[24,1024]{1,0:T(8,128)S(1)} collective-permute-done((f32[24,1024]{1,0:T(8,128)S(1)}, f32[24,1024]{1,0:T(8,128)S(1)}, u32[]{:S(2)}, u32[]{:S(2)}) %collective-permute-start.12) | collective-permute-done | bytes 98336 | tf_op jit(solution)/shard_map/ppermute | solution.py:438
  35.3 0.0 collective-permute-done.3.got_chip.got_plain
  35.3 0.0 collective-permute-done.11.got_near
  35.3 0.8 %write_first.1.begun = f32[96,1024]{1,0:T(8,128)} custom-call(f32[48,1024]{1,0:T(8,128)S(1)} %get-tuple-element.26.refs_0_.chip.plain, f32[48,1024]{1,0:T(8,128)S(1)} %collective-permute-done.3.got_chip.got_plain, f32[48,1024]{1,0:T(8,128)S(1)} %remap_near.1.refs_0_.lev_near, f32[48,1024]{1,0:T(8,128)S(1)} %collective-permute-done.11.got_near, ...), custom_call_target="tpu_custom_call" | custom-call | flops 1 | bytes 1 | tf_op jit(solution)/shard_map/write_first/pallas_call | solution.py:349
  36.1 2.3 %collective-permute-done.10.got_last = f32[24,512]{1,0:T(8,128)S(1)} collective-permute-done((f32[24,512]{1,0:T(8,128)S(1)}, f32[24,512]{1,0:T(8,128)S(1)}, u32[]{:S(2)}, u32[]{:S(2)}) %collective-permute-start.10) | collective-permute-done | bytes 49184 | tf_op jit(solution)/shard_map/ppermute | solution.py:441
  (14 shorter events, 0.1 us)
Async XLA Ops:
  0.0 12.0 %copy-start = (f32[64,8192]{1,0:T(8,128)S(1)}, f32[64,8192]{1,0:T(8,128)}, u32[]{:S(2)}) copy-start(f32[64,8192]{1,0:T(8,128)} %weights.1) | copy-start | bytes 6291460
  0.0 0.8 %copy-start.1 = (s32[8]{0:T(128)S(1)}, s32[8]{0:T(128)}, u32[]{:S(2)}) copy-start(s32[8]{0:T(128)} %step_hour.1) | copy-start | bytes 100
  0.8 11.2 %copy-start.2 = (s32[128]{0:T(128)S(1)}, s32[128]{0:T(128)}, u32[]{:S(2)}) copy-start(s32[128]{0:T(128)} %rows.1) | copy-start | bytes 1540
  0.8 11.2 %copy-start.3 = (s32[128]{0:T(128)S(1)}, s32[128]{0:T(128)}, u32[]{:S(2)}) copy-start(s32[128]{0:T(128)} %columns.1) | copy-start | bytes 1540
  4.1 10.8 %collective-permute-start = (f32[24,2048]{1,0:T(8,128)S(1)}, f32[24,2048]{1,0:T(8,128)S(1)}, u32[]{:S(2)}, u32[]{:S(2)}) collective-permute-start(f32[24,2048]{1,0:T(8,128)S(1)} %get-tuple-element.19), channel_id=1, source_target_pairs={{0,1},{1,0},{4,5},{5,4},{8,9},{9,8},{12,13},{13,12},{2,3},{3,2},{6... | collective-permute-start | bytes 589832 | tf_op jit(solution)/shard_map/ppermute | solution.py:434
  4.6 10.3 %collective-permute-start.2 = (f32[48,1024]{1,0:T(8,128)S(1)}, f32[48,1024]{1,0:T(8,128)S(1)}, u32[]{:S(2)}, u32[]{:S(2)}) collective-permute-start(f32[48,1024]{1,0:T(8,128)S(1)} %get-tuple-element.21.refs_0_), channel_id=1, source_target_pairs={{0,2},{2,0},{1,3},{3,1},{4,6},{6,4},{5,7},{7,5},{8,10},{10,8},{9,1... | collective-permute-start | bytes 589832 | tf_op jit(solution)/shard_map/ppermute | solution.py:441
  7.2 12.2 %collective-permute-start.1 = (f32[24,2048]{1,0:T(8,128)S(1)}, f32[24,2048]{1,0:T(8,128)S(1)}, u32[]{:S(2)}, u32[]{:S(2)}) collective-permute-start(f32[24,2048]{1,0:T(8,128)S(1)} %get-tuple-element.20), channel_id=1, source_target_pairs={{0,8},{1,9},{4,12},{5,13},{8,0},{9,1},{12,4},{13,5},{2,10},{3,11},... | collective-permute-start | bytes 589832 | tf_op jit(solution)/shard_map/ppermute | solution.py:434
  9.8 11.7 %collective-permute-start.5 = (f32[24,2048]{1,0:T(8,128)S(1)}, f32[24,2048]{1,0:T(8,128)S(1)}, u32[]{:S(2)}, u32[]{:S(2)}) collective-permute-start(f32[24,2048]{1,0:T(8,128)S(1)} %get-tuple-element.29), channel_id=1, source_target_pairs={{0,4},{1,5},{4,0},{5,1},{8,12},{9,13},{12,8},{13,9},{2,6},{3,7},{6... | collective-permute-start | bytes 589832 | tf_op jit(solution)/shard_map/ppermute | solution.py:434
  11.4 13.4 %collective-permute-start.9 = (f32[24,2048]{1,0:T(8,128)S(1)}, f32[24,2048]{1,0:T(8,128)S(1)}, u32[]{:S(2)}, u32[]{:S(2)}) collective-permute-start(f32[24,2048]{1,0:T(8,128)S(1)} %get-tuple-element.30), channel_id=1, source_target_pairs={{0,5},{1,4},{4,1},{5,0},{8,13},{9,12},{12,9},{13,8},{2,7},{3,6},{6... | collective-permute-start | bytes 589832 | tf_op jit(solution)/shard_map/ppermute | solution.py:434
  14.9 13.1 %collective-permute-start.7 = (f32[24,1024]{1,0:T(8,128)S(1)}, f32[24,1024]{1,0:T(8,128)S(1)}, u32[]{:S(2)}, u32[]{:S(2)}) collective-permute-start(f32[24,1024]{1,0:T(8,128)S(1)} %merge_first.1.refs_0_), channel_id=1, source_target_pairs={{0,12},{1,13},{4,8},{5,9},{8,4},{9,5},{12,0},{13,1},{2,14},{3,15},... | collective-permute-start | bytes 294920 | tf_op jit(solution)/shard_map/ppermute | solution.py:434
  17.2 10.9 %collective-permute-start.8 = (f32[24,1024]{1,0:T(8,128)S(1)}, f32[24,1024]{1,0:T(8,128)S(1)}, u32[]{:S(2)}, u32[]{:S(2)}) collective-permute-start(f32[24,1024]{1,0:T(8,128)S(1)} %merge_next.1.refs_1_), channel_id=1, source_target_pairs={{0,13},{1,12},{4,9},{5,8},{8,5},{9,4},{12,1},{13,0},{2,15},{3,14},... | collective-permute-start | bytes 294920 | tf_op jit(solution)/shard_map/ppermute | solution.py:434
  19.4 5.3 %collective-permute-start.4 = (f32[24,1024]{1,0:T(8,128)S(1)}, f32[24,1024]{1,0:T(8,128)S(1)}, u32[]{:S(2)}, u32[]{:S(2)}) collective-permute-start(f32[24,1024]{1,0:T(8,128)S(1)} %hold.1.refs_0_), channel_id=1, source_target_pairs={{0,2},{2,0},{1,3},{3,1},{4,6},{6,4},{5,7},{7,5},{8,10},{10,8},{9,1... | collective-permute-start | bytes 294920 | tf_op jit(solution)/shard_map/ppermute | solution.py:441
  21.5 13.8 %collective-permute-start.3 = (f32[48,1024]{1,0:T(8,128)S(1)}, f32[48,1024]{1,0:T(8,128)S(1)}, u32[]{:S(2)}, u32[]{:S(2)}) collective-permute-start(f32[48,1024]{1,0:T(8,128)S(1)} %get-tuple-element.27), channel_id=1, source_target_pairs={{0,2},{2,0},{1,3},{3,1},{4,6},{6,4},{5,7},{7,5},{8,10},{10,8},{9,1... | collective-permute-start | bytes 589832 | tf_op jit(solution)/shard_map/ppermute | solution.py:441
  24.7 8.3 %collective-permute-start.6 = (f32[24,1024]{1,0:T(8,128)S(1)}, f32[24,1024]{1,0:T(8,128)S(1)}, u32[]{:S(2)}, u32[]{:S(2)}) collective-permute-start(f32[24,1024]{1,0:T(8,128)S(1)} %merge_last.1.refs_0_), channel_id=1, source_target_pairs={{0,9},{1,8},{4,13},{5,12},{8,1},{9,0},{12,5},{13,4},{2,11},{3,10},... | collective-permute-start | bytes 294920 | tf_op jit(solution)/shard_map/ppermute | solution.py:434
  26.3 9.0 %collective-permute-start.11 = (f32[48,1024]{1,0:T(8,128)S(1)}, f32[48,1024]{1,0:T(8,128)S(1)}, u32[]{:S(2)}, u32[]{:S(2)}) collective-permute-start(f32[48,1024]{1,0:T(8,128)S(1)} %remap_near.1.refs_0_.lev_near), channel_id=1, source_target_pairs={{0,2},{2,0},{1,3},{3,1},{4,6},{6,4},{5,7},{7,5},{8,10},{10,8},{9,1... | collective-permute-start | bytes 589832 | tf_op jit(solution)/shard_map/ppermute | solution.py:441
  29.6 5.6 %collective-permute-start.12 = (f32[24,1024]{1,0:T(8,128)S(1)}, f32[24,1024]{1,0:T(8,128)S(1)}, u32[]{:S(2)}, u32[]{:S(2)}) collective-permute-start(f32[24,1024]{1,0:T(8,128)S(1)} %remap_far.1.refs_0_.far), channel_id=1, source_target_pairs={{0,2},{4,6},{10,8},{14,12},{1,3},{5,7},{11,9},{15,13},{16,18},{20,... | collective-permute-start | bytes 294920 | tf_op jit(solution)/shard_map/ppermute | solution.py:438
  34.3 4.1 %collective-permute-start.10 = (f32[24,512]{1,0:T(8,128)S(1)}, f32[24,512]{1,0:T(8,128)S(1)}, u32[]{:S(2)}, u32[]{:S(2)}) collective-permute-start(f32[24,512]{1,0:T(8,128)S(1)} %remap_last.1.last), channel_id=1, source_target_pairs={{0,2},{2,0},{1,3},{3,1},{4,6},{6,4},{5,7},{7,5},{8,10},{10,8},{9,1... | collective-permute-start | bytes 147464 | tf_op jit(solution)/shard_map/ppermute | solution.py:441

commit v17 on v16

--- a/solution.py
+++ b/solution.py
@@ -433,10 +433,6 @@
         pairs = [(a * subs + b, (a ^ k) * subs + (b ^ j)) for a in range(levs) for b in range(subs)]
         return lax.ppermute(x, ("lev", "sub"), pairs)
 
-    def hand_over(x):
-        pairs = [(a * shards_tm + a // half, a * shards_tm + 1 - a // half) for a in range(levs)]
-        return lax.ppermute(x, ("lev", "tm"), pairs)
-
     def swap(x):
         return lax.ppermute(x, "tm", [(0, 1), (1, 0)])
 
@@ -449,15 +445,14 @@
     near_got = [to_peer(x, *peer) for x, peer in list(zip(sums, plain))[1:3]]
     got_0 = swap(theirs_0)
     plain_got = to_peer(sums[0], *plain[0])
-    high, low = place_tiles(tile_rows, tile_columns, live_count, tile_weight, theirs_0)
-
     merged = small_call(
-        merge_first_kernel, [mine_0, got_0], [high, sibling], [folded], LIGHT, "merge_first"
+        merge_first_kernel, [mine_0, got_0], [sibling], [folded], LIGHT, "merge_first"
     )
     far_same = to_peer(merged[0], *first[0])
     merged = small_call(merge_next_kernel, [mine_0, got_0], merged, [folded], LIGHT, "merge_next")
     far_other = to_peer(merged[0], *first[1])
-    theirs_1 = small_call(hold_kernel, [theirs_1], [plain_got, *merged], [folded], LIGHT, "hold")[0]
+    high, low = place_tiles(tile_rows, tile_columns, live_count, tile_weight, *merged)
+    theirs_1 = small_call(hold_kernel, [theirs_1], [plain_got, high], [folded], LIGHT, "hold")[0]
     got_1 = swap(theirs_1)
     both, send = remap_call(
         remap_both_kernel,
@@ -480,7 +475,7 @@
     )
     got_near = swap(near)
     (far,) = remap_call(remap_far_kernel, [far_same, far_other], [near], [rows], high, low, HEAVY, "remap_far")
-    got_far = hand_over(far)
+    got_far = swap(far)
     padded = -(-rows // 32) * 16
     (last,) = remap_call(
         remap_last_kernel,

time: 38.6 us -> 38.8 us (level)
  waiting for transfers between devices: 7.37 us -> 5.35 us
  starting transfers between devices: 16.5 us -> 18 us
  Pallas kernels: 12.9 us -> 13.8 us
    ppermute x5 -> x6, starting transfers between devices: 5.34 us -> 8.05 us  [swap(): return lax.ppermute(x, 'tm', [(0, 1), (1, 0)])]
    ppermute x1 -> x0, starting transfers between devices: 2.45 us -> none  [hand_over(): return lax.ppermute(x, ('lev', 'tm'), pairs)]
    ppermute x7, waiting for transfers between devices: 3.01 us -> 1.2 us  [to_peer(): return lax.ppermute(x, ('lev', 'sub'), pairs)]
    ppermute x7, starting transfers between devices: 8.76 us -> 9.94 us  [to_peer(): return lax.ppermute(x, ('lev', 'sub'), pairs)]
    pallas_call x1, Pallas kernels: 2.84 us -> 3.74 us  [place_tiles(): pl.pallas_call(place_kernel, out_shape=(half, half), in_specs=[smem, smem...]
    ppermute x1 -> x0, waiting for transfers between devices: 0.43 us -> none  [hand_over(): return lax.ppermute(x, ('lev', 'tm'), pairs)]
    ppermute x5 -> x6, waiting for transfers between devices: 3.92 us -> 4.15 us  [swap(): return lax.ppermute(x, 'tm', [(0, 1), (1, 0)])]
  transfers between devices with their start and end apart: 13 -> 13, of which waited for: 6 -> 4; matrix products, arithmetic and copies ran while one was open for 0% -> 0% of each run, Pallas kernels for 25% -> 27%
where the time goes in v17:
time: 38.8 us; the launch traced here: 38.7 us
  starting transfers between devices  18 us (46%)
  Pallas kernels  13.8 us (36%)
  waiting for transfers between devices  5.35 us (14%)
  local copies, waits for them, and re-layouts  0.82 us (2%)
  between operations  0.78 us (2%)
    ppermute x7, starting transfers between devices, to_peer(): return lax.ppermute(x, ('lev', 'sub'), pairs)  9.94 us
    ppermute x6, starting transfers between devices, swap(): return lax.ppermute(x, 'tm', [(0, 1), (1, 0)])  8.05 us
    pallas_call x4, Pallas kernels, remap_call(): pl.pallas_call(kernel, out_shape=[jax.ShapeDtypeStruct(rows if isinstance...  5.89 us
    ppermute x6, waiting for transfers between devices, swap(): return lax.ppermute(x, 'tm', [(0, 1), (1, 0)])  4.15 us
    pallas_call x1, Pallas kernels, place_tiles(): pl.pallas_call(place_kernel, out_shape=(half, half), in_specs=[smem, smem...  3.74 us
    pallas_call x1, Pallas kernels, hour_sums(): pl.pallas_call(functools.partial(sums_kernel, plain, first, second), out_...  3.28 us
    ppermute x7, waiting for transfers between devices, to_peer(): return lax.ppermute(x, ('lev', 'sub'), pairs)  1.2 us
    pallas_call x5, Pallas kernels, small_call(): pl.pallas_call(kernel, out_shape=[jax.ShapeDtypeStruct(shape, jnp.float32...  0.85 us
  transfers between devices with their start and end apart: 13, of which 4 were waited for; matrix products, arithmetic and copies ran while one was open for 0% of the time, Pallas kernels for 27%

profile of v17, /device:TPU:0, one launch (start us, length us, event | category | flops | bytes accessed | tf_op | source)
XLA Modules:
  0.0 38.7 jit_solution(8893649180168606422)
XLA Ops:
  0.0 0.8 %copy-done.1 = s32[8]{0:T(128)S(1)} copy-done((s32[8]{0:T(128)S(1)}, s32[8]{0:T(128)}, u32[]{:S(2)}) %copy-start.1) | copy-done | bytes 56
  0.8 3.3 %hour_sums.1 = (f32[24,2048]{1,0:T(8,128)S(1)}, f32[24,2048]{1,0:T(8,128)S(1)}, f32[24,2048]{1,0:T(8,128)S(1)}, f32[24,2048]{1,0:T(8,128)S(1)}, f32[24,2048]{1,0...) custom-call(s32[8]{0:T(128)S(1)} %copy-done.1, ...), custom_call_target="tpu_custom_call" | custom-call | flops 1 | bytes 1 | tf_op jit(solution)/shard_map/hour_sums/pallas_call | solution.py:306
  4.1 0.5 %collective-permute-start = (f32[24,2048]{1,0:T(8,128)S(1)}, f32[24,2048]{1,0:T(8,128)S(1)}, u32[]{:S(2)}, u32[]{:S(2)}) collective-permute-start(f32[24,2048]{1,0:T(8,128)S(1)} %get-tuple-element.19), channel_id=1, source_target_pairs={{0,1},{1,0},{4,5},{5,4},{8,9},{9,8},{12,13},{13,12},{2,3},{3,2},{6... | collective-permute-start | bytes 589832 | tf_op jit(solution)/shard_map/ppermute | solution.py:434
  4.6 2.6 %collective-permute-start.2 = (f32[48,1024]{1,0:T(8,128)S(1)}, f32[48,1024]{1,0:T(8,128)S(1)}, u32[]{:S(2)}, u32[]{:S(2)}) collective-permute-start(f32[48,1024]{1,0:T(8,128)S(1)} %get-tuple-element.22), channel_id=1, source_target_pairs={{0,2},{2,0},{1,3},{3,1},{4,6},{6,4},{5,7},{7,5},{8,10},{10,8},{9,1... | collective-permute-start | bytes 589832 | tf_op jit(solution)/shard_map/ppermute | solution.py:437
  7.2 2.6 %collective-permute-start.1 = (f32[24,2048]{1,0:T(8,128)S(1)}, f32[24,2048]{1,0:T(8,128)S(1)}, u32[]{:S(2)}, u32[]{:S(2)}) collective-permute-start(f32[24,2048]{1,0:T(8,128)S(1)} %get-tuple-element.20), channel_id=1, source_target_pairs={{0,8},{1,9},{4,12},{5,13},{8,0},{9,1},{12,4},{13,5},{2,10},{3,11},... | collective-permute-start | bytes 589832 | tf_op jit(solution)/shard_map/ppermute | solution.py:434
  9.8 1.6 %collective-permute-start.5 = (f32[24,2048]{1,0:T(8,128)S(1)}, f32[24,2048]{1,0:T(8,128)S(1)}, u32[]{:S(2)}, u32[]{:S(2)}) collective-permute-start(f32[24,2048]{1,0:T(8,128)S(1)} %get-tuple-element.29), channel_id=1, source_target_pairs={{0,4},{1,5},{4,0},{5,1},{8,12},{9,13},{12,8},{13,9},{2,6},{3,7},{6... | collective-permute-start | bytes 589832 | tf_op jit(solution)/shard_map/ppermute | solution.py:434
  11.4 0.0 collective-permute-start.9
  12.0 0.0 collective-permute-done.refs_0_.sibling
  12.0 0.7 %collective-permute-done.2.got = f32[48,1024]{1,0:T(8,128)S(1)} collective-permute-done((f32[48,1024]{1,0:T(8,128)S(1)}, f32[48,1024]{1,0:T(8,128)S(1)}, u32[]{:S(2)}, u32[]{:S(2)}) %collective-permute-start.2) | collective-permute-done | bytes 196640 | tf_op jit(solution)/shard_map/ppermute | solution.py:437
  12.7 3.9 %collective-permute-start.7 = (f32[24,1024]{1,0:T(8,128)S(1)}, f32[24,1024]{1,0:T(8,128)S(1)}, u32[]{:S(2)}, u32[]{:S(2)}) collective-permute-start(f32[24,1024]{1,0:T(8,128)S(1)} %merge_first.1.refs_0_), channel_id=1, source_target_pairs={{0,12},{1,13},{4,8},{5,9},{8,4},{9,5},{12,0},{13,1},{2,14},{3,15},... | collective-permute-start | bytes 294920 | tf_op jit(solution)/shard_map/ppermute | solution.py:434
  16.6 0.1 collective-permute-start.8
  16.8 3.7 %place_tiles.1 = (bf16[2048,1024]{1,0:T(8,128)(2,1)S(1)}, bf16[2048,1024]{1,0:T(8,128)(2,1)S(1)}) custom-call(s32[128]{0:T(128)S(1)} %copy-done.2, s32[128]{0:T(128)S(1)} %copy-done.3, s32[1]{0:T(128)S(6)} %copy.9.count, f32[64,8192]{1,0:T(8,128)S(1)} %copy-done, f32[24,1024]{1,0:T(8,128)S(1)} %merge_next.1.refs_0_), custom_call_target="tpu_custom_call" | custom-call | flops 1 | bytes 1 | tf_op jit(solution)/shard_map/place_tiles/pallas_call | solution.py:77
  20.5 0.0 collective-permute-done.1.refs_0_.plain
  20.5 1.6 %collective-permute-start.4 = (f32[24,1024]{1,0:T(8,128)S(1)}, f32[24,1024]{1,0:T(8,128)S(1)}, u32[]{:S(2)}, u32[]{:S(2)}) collective-permute-start(f32[24,1024]{1,0:T(8,128)S(1)} %hold.1.refs_0_), channel_id=1, source_target_pairs={{0,2},{2,0},{1,3},{3,1},{4,6},{6,4},{5,7},{7,5},{8,10},{10,8},{9,1... | collective-permute-start | bytes 294920 | tf_op jit(solution)/shard_map/ppermute | solution.py:437
  22.1 1.5 %remap_both.1 = (f32[48,1024]{1,0:T(8,128)S(1)}, f32[48,1024]{1,0:T(8,128)S(1)}) custom-call(f32[24,2048]{1,0:T(8,128)S(1)} %get-tuple-element.18.own, f32[24,2048]{1,0:T(8,128)S(1)} %collective-permute-done.refs_0_.sibling, f32[24,2048]{1,0:T(8,128)S(1)} %collective-permute-done.1.refs_0_.plain, bf16[2048,1024]{1,0:T(8,128)(2,1)S(1)} %get-tuple-element.23.refs_1_.high, ...), custom_call_target="tpu_custom_call" | custom-call | flops 2500000000 | bytes 1 | tf_op jit(solution)/shard_map/remap_both/pallas_call | solution.py:104
  23.6 0.0 collective-permute-done.5.refs_1_.near_same
  23.6 0.6 %collective-permute-start.3 = (f32[48,1024]{1,0:T(8,128)S(1)}, f32[48,1024]{1,0:T(8,128)S(1)}, u32[]{:S(2)}, u32[]{:S(2)}) collective-permute-start(f32[48,1024]{1,0:T(8,128)S(1)} %get-tuple-element.27), channel_id=1, source_target_pairs={{0,2},{2,0},{1,3},{3,1},{4,6},{6,4},{5,7},{7,5},{8,10},{10,8},{9,1... | collective-permute-start | bytes 589832 | tf_op jit(solution)/shard_map/ppermute | solution.py:437
  24.2 1.1 %collective-permute-done.4.got = f32[24,1024]{1,0:T(8,128)S(1)} collective-permute-done((f32[24,1024]{1,0:T(8,128)S(1)}, f32[24,1024]{1,0:T(8,128)S(1)}, u32[]{:S(2)}, u32[]{:S(2)}) %collective-permute-start.4) | collective-permute-done | bytes 98336 | tf_op jit(solution)/shard_map/ppermute | solution.py:437
  25.3 1.3 %collective-permute-start.6 = (f32[24,1024]{1,0:T(8,128)S(1)}, f32[24,1024]{1,0:T(8,128)S(1)}, u32[]{:S(2)}, u32[]{:S(2)}) collective-permute-start(f32[24,1024]{1,0:T(8,128)S(1)} %merge_last.1.refs_0_), channel_id=1, source_target_pairs={{0,9},{1,8},{4,13},{5,12},{8,1},{9,0},{12,5},{13,4},{2,11},{3,10},... | collective-permute-start | bytes 294920 | tf_op jit(solution)/shard_map/ppermute | solution.py:434
  26.5 0.0 collective-permute-done.9.near_other
  26.5 1.5 %remap_near.1.refs_0_.lev_near = f32[48,1024]{1,0:T(8,128)S(1)} custom-call(f32[24,2048]{1,0:T(8,128)S(1)} %collective-permute-done.5.refs_1_.near_same, f32[24,2048]{1,0:T(8,128)S(1)} %collective-permute-done.9.near_other, bf16[2048,1024]{1,0:T(8,128)(2,1)S(1)} %get-tuple-element.23.refs_1_.high, bf16[2048,1024]{1,0:T(8,128)(2,1)S(1)} %get-tuple-element.24.low, ...), custom_call_target="tpu_custom_call" | custom-call | flops 1 | bytes 1 | tf_op jit(solution)/shard_map/remap_near/pallas_call | solution.py:104
  28.1 1.5 %collective-permute-start.11 = (f32[48,1024]{1,0:T(8,128)S(1)}, f32[48,1024]{1,0:T(8,128)S(1)}, u32[]{:S(2)}, u32[]{:S(2)}) collective-permute-start(f32[48,1024]{1,0:T(8,128)S(1)} %remap_near.1.refs_0_.lev_near), channel_id=1, source_target_pairs={{0,2},{2,0},{1,3},{3,1},{4,6},{6,4},{5,7},{7,5},{8,10},{10,8},{9,1... | collective-permute-start | bytes 589832 | tf_op jit(solution)/shard_map/ppermute | solution.py:437
  29.6 0.0 collective-permute-done.8.other
  29.6 0.0 collective-permute-done.7.same
  29.6 1.6 %remap_far.1.refs_0_.far = f32[24,1024]{1,0:T(8,128)S(1)} custom-call(f32[24,1024]{1,0:T(8,128)S(1)} %collective-permute-done.7.same, f32[24,1024]{1,0:T(8,128)S(1)} %collective-permute-done.8.other, bf16[2048,1024]{1,0:T(8,128)(2,1)S(1)} %get-tuple-element.23.refs_1_.high, bf16[2048,1024]{1,0:T(8,128)(2,1)S(1)} %get-tuple-element.24.low, ...), custom_call_target="tpu_custom_call" | custom-call | flops 10000000000 | bytes 1 | tf_op jit(solution)/shard_map/remap_far/pallas_call | solution.py:104
  31.1 0.6 %collective-permute-start.12 = (f32[24,1024]{1,0:T(8,128)S(1)}, f32[24,1024]{1,0:T(8,128)S(1)}, u32[]{:S(2)}, u32[]{:S(2)}) collective-permute-start(f32[24,1024]{1,0:T(8,128)S(1)} %remap_far.1.refs_0_.far), channel_id=1, source_target_pairs={{0,2},{2,0},{1,3},{3,1},{4,6},{6,4},{5,7},{7,5},{8,10},{10,8},{9,1... | collective-permute-start | bytes 294920 | tf_op jit(solution)/shard_map/ppermute | solution.py:437
  31.8 1.2 %collective-permute-done.6.block = f32[24,1024]{1,0:T(8,128)S(1)} collective-permute-done((f32[24,1024]{1,0:T(8,128)S(1)}, f32[24,1024]{1,0:T(8,128)S(1)}, u32[]{:S(2)}, u32[]{:S(2)}) %collective-permute-start.6) | collective-permute-done | bytes 98336 | tf_op jit(solution)/shard_map/ppermute | solution.py:434
  33.0 1.3 %remap_last.1.last = f32[24,512]{1,0:T(8,128)S(1)} custom-call(f32[24,1024]{1,0:T(8,128)S(1)} %collective-permute-done.6.block, bf16[2048,1024]{1,0:T(8,128)(2,1)S(1)} %get-tuple-element.23.refs_1_.high, bf16[2048,1024]{1,0:T(8,128)(2,1)S(1)} %get-tuple-element.24.low, f32[24,1024]{1,0:T(8,128)S(1)} %remap_far.1.refs_0_.far), custom_call_target="tpu_custom_call" | custom-call | flops 10000000000 | bytes 1 | tf_op jit(solution)/shard_map/remap_last/pallas_call | solution.py:104
  34.3 1.2 %collective-permute-start.10 = (f32[24,512]{1,0:T(8,128)S(1)}, f32[24,512]{1,0:T(8,128)S(1)}, u32[]{:S(2)}, u32[]{:S(2)}) collective-permute-start(f32[24,512]{1,0:T(8,128)S(1)} %remap_last.1.last), channel_id=1, source_target_pairs={{0,2},{2,0},{1,3},{3,1},{4,6},{6,4},{5,7},{7,5},{8,10},{10,8},{9,1... | collective-permute-start | bytes 147464 | tf_op jit(solution)/shard_map/ppermute | solution.py:437
  35.5 2.4 %collective-permute-done.12.got_far = f32[24,1024]{1,0:T(8,128)S(1)} collective-permute-done((f32[24,1024]{1,0:T(8,128)S(1)}, f32[24,1024]{1,0:T(8,128)S(1)}, u32[]{:S(2)}, u32[]{:S(2)}) %collective-permute-start.12) | collective-permute-done | bytes 98336 | tf_op jit(solution)/shard_map/ppermute | solution.py:437
  37.9 0.8 %write_first.1.begun = f32[96,1024]{1,0:T(8,128)} custom-call(f32[48,1024]{1,0:T(8,128)S(1)} %get-tuple-element.26.refs_0_.chip.plain, f32[48,1024]{1,0:T(8,128)S(1)} %collective-permute-done.3.got_chip.got_plain, f32[48,1024]{1,0:T(8,128)S(1)} %remap_near.1.refs_0_.lev_near, f32[48,1024]{1,0:T(8,128)S(1)} %collective-permute-done.11.got_near, ...), custom_call_target="tpu_custom_call" | custom-call | flops 1 | bytes 1 | tf_op jit(solution)/shard_map/write_first/pallas_call | solution.py:349
  38.7 0.0 collective-permute-done.10.got_last
  (14 shorter events, 0.1 us)
Async XLA Ops:
  0.0 16.7 %copy-start = (f32[64,8192]{1,0:T(8,128)S(1)}, f32[64,8192]{1,0:T(8,128)}, u32[]{:S(2)}) copy-start(f32[64,8192]{1,0:T(8,128)} %weights.1) | copy-start | bytes 6291460
  0.0 0.8 %copy-start.1 = (s32[8]{0:T(128)S(1)}, s32[8]{0:T(128)}, u32[]{:S(2)}) copy-start(s32[8]{0:T(128)} %step_hour.1) | copy-start | bytes 100
  0.8 15.9 %copy-start.2 = (s32[128]{0:T(128)S(1)}, s32[128]{0:T(128)}, u32[]{:S(2)}) copy-start(s32[128]{0:T(128)} %rows.1) | copy-start | bytes 1540
  0.8 15.9 %copy-start.3 = (s32[128]{0:T(128)S(1)}, s32[128]{0:T(128)}, u32[]{:S(2)}) copy-start(s32[128]{0:T(128)} %columns.1) | copy-start | bytes 1540
  4.1 7.9 %collective-permute-start = (f32[24,2048]{1,0:T(8,128)S(1)}, f32[24,2048]{1,0:T(8,128)S(1)}, u32[]{:S(2)}, u32[]{:S(2)}) collective-permute-start(f32[24,2048]{1,0:T(8,128)S(1)} %get-tuple-element.19), channel_id=1, source_target_pairs={{0,1},{1,0},{4,5},{5,4},{8,9},{9,8},{12,13},{13,12},{2,3},{3,2},{6... | collective-permute-start | bytes 589832 | tf_op jit(solution)/shard_map/ppermute | solution.py:434
  4.6 8.1 %collective-permute-start.2 = (f32[48,1024]{1,0:T(8,128)S(1)}, f32[48,1024]{1,0:T(8,128)S(1)}, u32[]{:S(2)}, u32[]{:S(2)}) collective-permute-start(f32[48,1024]{1,0:T(8,128)S(1)} %get-tuple-element.22), channel_id=1, source_target_pairs={{0,2},{2,0},{1,3},{3,1},{4,6},{6,4},{5,7},{7,5},{8,10},{10,8},{9,1... | collective-permute-start | bytes 589832 | tf_op jit(solution)/shard_map/ppermute | solution.py:437
  7.2 13.3 %collective-permute-start.1 = (f32[24,2048]{1,0:T(8,128)S(1)}, f32[24,2048]{1,0:T(8,128)S(1)}, u32[]{:S(2)}, u32[]{:S(2)}) collective-permute-start(f32[24,2048]{1,0:T(8,128)S(1)} %get-tuple-element.20), channel_id=1, source_target_pairs={{0,8},{1,9},{4,12},{5,13},{8,0},{9,1},{12,4},{13,5},{2,10},{3,11},... | collective-permute-start | bytes 589832 | tf_op jit(solution)/shard_map/ppermute | solution.py:434
  9.8 13.8 %collective-permute-start.5 = (f32[24,2048]{1,0:T(8,128)S(1)}, f32[24,2048]{1,0:T(8,128)S(1)}, u32[]{:S(2)}, u32[]{:S(2)}) collective-permute-start(f32[24,2048]{1,0:T(8,128)S(1)} %get-tuple-element.29), channel_id=1, source_target_pairs={{0,4},{1,5},{4,0},{5,1},{8,12},{9,13},{12,8},{13,9},{2,6},{3,7},{6... | collective-permute-start | bytes 589832 | tf_op jit(solution)/shard_map/ppermute | solution.py:434
  11.4 15.2 %collective-permute-start.9 = (f32[24,2048]{1,0:T(8,128)S(1)}, f32[24,2048]{1,0:T(8,128)S(1)}, u32[]{:S(2)}, u32[]{:S(2)}) collective-permute-start(f32[24,2048]{1,0:T(8,128)S(1)} %get-tuple-element.30), channel_id=1, source_target_pairs={{0,5},{1,4},{4,1},{5,0},{8,13},{9,12},{12,9},{13,8},{2,7},{3,6},{6... | collective-permute-start | bytes 589832 | tf_op jit(solution)/shard_map/ppermute | solution.py:434
  12.7 16.9 %collective-permute-start.7 = (f32[24,1024]{1,0:T(8,128)S(1)}, f32[24,1024]{1,0:T(8,128)S(1)}, u32[]{:S(2)}, u32[]{:S(2)}) collective-permute-start(f32[24,1024]{1,0:T(8,128)S(1)} %merge_first.1.refs_0_), channel_id=1, source_target_pairs={{0,12},{1,13},{4,8},{5,9},{8,4},{9,5},{12,0},{13,1},{2,14},{3,15},... | collective-permute-start | bytes 294920 | tf_op jit(solution)/shard_map/ppermute | solution.py:434
  16.6 12.9 %collective-permute-start.8 = (f32[24,1024]{1,0:T(8,128)S(1)}, f32[24,1024]{1,0:T(8,128)S(1)}, u32[]{:S(2)}, u32[]{:S(2)}) collective-permute-start(f32[24,1024]{1,0:T(8,128)S(1)} %merge_next.1.refs_0_), channel_id=1, source_target_pairs={{0,13},{1,12},{4,9},{5,8},{8,5},{9,4},{12,1},{13,0},{2,15},{3,14},... | collective-permute-start | bytes 294920 | tf_op jit(solution)/shard_map/ppermute | solution.py:434
  20.5 4.7 %collective-permute-start.4 = (f32[24,1024]{1,0:T(8,128)S(1)}, f32[24,1024]{1,0:T(8,128)S(1)}, u32[]{:S(2)}, u32[]{:S(2)}) collective-permute-start(f32[24,1024]{1,0:T(8,128)S(1)} %hold.1.refs_0_), channel_id=1, source_target_pairs={{0,2},{2,0},{1,3},{3,1},{4,6},{6,4},{5,7},{7,5},{8,10},{10,8},{9,1... | collective-permute-start | bytes 294920 | tf_op jit(solution)/shard_map/ppermute | solution.py:437
  23.6 14.3 %collective-permute-start.3 = (f32[48,1024]{1,0:T(8,128)S(1)}, f32[48,1024]{1,0:T(8,128)S(1)}, u32[]{:S(2)}, u32[]{:S(2)}) collective-permute-start(f32[48,1024]{1,0:T(8,128)S(1)} %get-tuple-element.27), channel_id=1, source_target_pairs={{0,2},{2,0},{1,3},{3,1},{4,6},{6,4},{5,7},{7,5},{8,10},{10,8},{9,1... | collective-permute-start | bytes 589832 | tf_op jit(solution)/shard_map/ppermute | solution.py:437
  25.3 7.7 %collective-permute-start.6 = (f32[24,1024]{1,0:T(8,128)S(1)}, f32[24,1024]{1,0:T(8,128)S(1)}, u32[]{:S(2)}, u32[]{:S(2)}) collective-permute-start(f32[24,1024]{1,0:T(8,128)S(1)} %merge_last.1.refs_0_), channel_id=1, source_target_pairs={{0,9},{1,8},{4,13},{5,12},{8,1},{9,0},{12,5},{13,4},{2,11},{3,10},... | collective-permute-start | bytes 294920 | tf_op jit(solution)/shard_map/ppermute | solution.py:434
  28.1 9.8 %collective-permute-start.11 = (f32[48,1024]{1,0:T(8,128)S(1)}, f32[48,1024]{1,0:T(8,128)S(1)}, u32[]{:S(2)}, u32[]{:S(2)}) collective-permute-start(f32[48,1024]{1,0:T(8,128)S(1)} %remap_near.1.refs_0_.lev_near), channel_id=1, source_target_pairs={{0,2},{2,0},{1,3},{3,1},{4,6},{6,4},{5,7},{7,5},{8,10},{10,8},{9,1... | collective-permute-start | bytes 589832 | tf_op jit(solution)/shard_map/ppermute | solution.py:437
  31.1 6.7 %collective-permute-start.12 = (f32[24,1024]{1,0:T(8,128)S(1)}, f32[24,1024]{1,0:T(8,128)S(1)}, u32[]{:S(2)}, u32[]{:S(2)}) collective-permute-start(f32[24,1024]{1,0:T(8,128)S(1)} %remap_far.1.refs_0_.far), channel_id=1, source_target_pairs={{0,2},{2,0},{1,3},{3,1},{4,6},{6,4},{5,7},{7,5},{8,10},{10,8},{9,1... | collective-permute-start | bytes 294920 | tf_op jit(solution)/shard_map/ppermute | solution.py:437
  34.3 4.4 %collective-permute-start.10 = (f32[24,512]{1,0:T(8,128)S(1)}, f32[24,512]{1,0:T(8,128)S(1)}, u32[]{:S(2)}, u32[]{:S(2)}) collective-permute-start(f32[24,512]{1,0:T(8,128)S(1)} %remap_last.1.last), channel_id=1, source_target_pairs={{0,2},{2,0},{1,3},{3,1},{4,6},{6,4},{5,7},{7,5},{8,10},{10,8},{9,1... | collective-permute-start | bytes 147464 | tf_op jit(solution)/shard_map/ppermute | solution.py:437
